TPU v7x, 256 devices: a whole 4x4x8 slice. The times are simulated.
256 devices in a mesh: seq: 32 (over x_lo, z, core), expert: 8 (over y, x_hi).
Axes of the slice: x: 4 (x_hi: 2, x_lo: 2; x = x_hi * 2 + x_lo), y: 4, z: 8, core: 2. Of those that a mesh axis runs over, the one named last changes fastest.
Arguments:
- tokens: float32 [1536, 32768], P('expert', 'seq'), as said below
- router: float32 [1536, 64], P('expert'), as said below
- w_in: float32 [32, 1536, 3072], P('expert', 'seq'), may hold values from -0.15625 to 0.15625
- w_out: float32 [32, 1536, 3072], P('expert', 'seq'), may hold values from -0.109375 to 0.109375
- grad_out: float32 [1536, 32768], P('expert', 'seq'), may hold values from -0.6 to 0.6
Outputs:
- grad_tokens: float32 [1536, 32768], P('expert', 'seq')
- grad_router: float32 [1536, 64], P('expert')
- grad_w_in: float32 [32, 1536, 3072], P('expert', 'seq')
- grad_w_out: float32 [32, 1536, 3072], P('expert', 'seq')
Inputs may be any that keep to these rules, and one draw needn't show every extreme that they name: Entries are of order one in most tokens; a few tokens may be far larger. `router`: columns of moderate norm.
All inputs are finite; a program needn't handle non-finite values.
Results may differ from a plain program's by a relative error of at most 0.0003.
Values sent between devices are 32-bit elements; how exact they have to be, the bound alone decides.
No kernel may reach another device: no remote copies, remote signals or barrier semaphores. Data moves between devices by JAX's collectives and lax.ppermute only.
A program may use at most 64 MiB of HBM per device.

v0:
```python
import jax
import jax.numpy as jnp
from jax import lax
from jax.sharding import PartitionSpec as P

PER_EXPERT = 2


HIGH = lax.Precision.HIGHEST


def smooth_gate(values):
    return jax.nn.gelu(values, approximate=True)


def product(left, right):
    return jnp.dot(left, right, precision=HIGH, preferred_element_type=jnp.float32)


def contract(left, right, left_dim, right_dim):
    return lax.dot_general(
        left,
        right,
        (((left_dim,), (right_dim,)), ((), ())),
        precision=HIGH,
        preferred_element_type=jnp.float32,
    )


def to_owners(partial_value):
    summed = lax.psum(partial_value, "seq")
    owned = lax.all_to_all(summed, "expert", split_axis=0, concat_axis=1, tiled=True)
    block = owned.shape[1] // lax.axis_size("seq")
    return lax.dynamic_slice_in_dim(owned, lax.axis_index("seq") * block, block, 1)


def from_owners(block):
    widened = lax.all_gather(block, "seq", axis=1, tiled=True)
    return lax.all_to_all(widened, "expert", split_axis=1, concat_axis=0, tiled=True)


def per_device(tokens, router, w_in, w_out, grad_out):
    local_experts = w_in.shape[0]
    width_block = w_in.shape[1]
    logits = lax.psum(contract(tokens, router, 0, 0), "expert")
    combine = jax.nn.softmax(logits, axis=1)
    column_top = lax.pmax(jnp.max(logits, axis=0), "seq")
    raised = jnp.exp(logits - column_top)
    column_sum = lax.psum(jnp.sum(raised, axis=0), "seq")
    dispatch = raised / column_sum
    slot_in = to_owners(contract(dispatch, tokens, 0, 1))
    inputs = slot_in.reshape(local_experts, PER_EXPERT, width_block)
    pre_part = jnp.einsum(
        "epd,edh->eph", inputs, w_in, precision=HIGH, preferred_element_type=jnp.float32
    )
    pre = lax.psum(pre_part, "seq")
    act, backward = jax.vjp(smooth_gate, pre)
    slot_out = jnp.einsum(
        "eph,edh->epd", act, w_out, precision=HIGH, preferred_element_type=jnp.float32
    )
    out_cols = from_owners(slot_out.reshape(local_experts * PER_EXPERT, width_block))
    combine_part = contract(grad_out, out_cols, 0, 1)
    grad_combine = lax.psum(combine_part, "expert")
    grad_slot_out = to_owners(contract(combine, grad_out, 0, 1)).reshape(
        local_experts, PER_EXPERT, width_block
    )
    act_part = jnp.einsum(
        "epd,edh->eph", grad_slot_out, w_out, precision=HIGH, preferred_element_type=jnp.float32
    )
    grad_act = lax.psum(act_part, "seq")
    grad_pre = backward(grad_act)[0]
    grad_w_out = jnp.einsum(
        "epd,eph->edh", grad_slot_out, act, precision=HIGH, preferred_element_type=jnp.float32
    )
    grad_w_in = jnp.einsum(
        "epd,eph->edh", inputs, grad_pre, precision=HIGH, preferred_element_type=jnp.float32
    )
    grad_slot_in = jnp.einsum(
        "eph,edh->epd", grad_pre, w_in, precision=HIGH, preferred_element_type=jnp.float32
    )
    in_cols = from_owners(grad_slot_in.reshape(local_experts * PER_EXPERT, width_block))
    dispatch_part = contract(tokens, in_cols, 0, 1)
    grad_dispatch = lax.psum(dispatch_part, "expert")
    row_part = combine * (grad_combine - jnp.sum(combine * grad_combine, axis=1, keepdims=True))
    column_total = lax.psum(jnp.sum(dispatch * grad_dispatch, axis=0), "seq")
    grad_logits = row_part + dispatch * (grad_dispatch - column_total)
    grad_tokens = contract(in_cols, dispatch, 0, 1) + contract(router, grad_logits, 1, 1)
    grad_router = lax.psum(product(tokens, grad_logits), "seq")
    return (grad_tokens, grad_router, grad_w_in, grad_w_out)


def solution(mesh):
    placed = (
        P("expert", "seq"),
        P("expert", None),
        P("expert", "seq", None),
        P("expert", "seq", None),
        P("expert", "seq"),
    )
    return jax.shard_map(
        per_device,
        mesh=mesh,
        in_specs=placed,
        out_specs=(
            P("expert", "seq"),
            P("expert", None),
            P("expert", "seq", None),
            P("expert", "seq", None),
        ),
        check_vma=False,
    )
```

profile of v0, /device:TPU:1, one launch (start us, length us, event | category | flops | bytes accessed | tf_op | source)
XLA Modules:
  0.0 995.5 jit_solution(4200245515463678192)
XLA Ops:
  7.2 2.7 fusion.25
  10.0 89.4 %all-reduce.8.cloned.1.call-done = f32[1024,64]{0,1:T(8,128)} async-done(((f32[1024,64]{0,1:T(8,128)}), f32[1024,64]{0,1:T(8,128)}) %all-reduce.8.cloned.1.call-update) | async-done | bytes 262160 | tf_op jit(solution)/shard_map/psum | solution.py:45
  100.4 58.3 %pmax.7 = f32[64]{0:T(128)S(1)} all-reduce(f32[64]{0:T(128)S(1)} %get-tuple-element.9), channel_id=1, replica_groups=mesh['seq'=32,'expert'=8] {'seq'}, use_global_device_ids=true, to_apply=%region_6.0 | all-reduce | flops 64 | bytes 512 | tf_op jit(solution)/shard_map/pmax | solution.py:47
  158.7 1.2 fusion.2
  159.8 53.0 %psum.73 = f32[64]{0:T(128)S(1)} all-reduce(f32[64]{0:T(128)S(1)} %get-tuple-element.7), channel_id=1, replica_groups=mesh['seq'=32,'expert'=8] {'seq'}, use_global_device_ids=true, to_apply=%region_8.0 | all-reduce | flops 64 | bytes 512 | tf_op jit(solution)/shard_map/psum | solution.py:49
  212.8 2.8 convolution_bitcast_fusion.4
  215.6 2.5 convolution_bitcast_fusion.5
  218.1 192.7 %all-reduce.10.cloned.1.call-done = (f32[8,8,192]{2,1,0:T(8,128)}, f32[8,8,192]{2,1,0:T(8,128)}) async-done(((f32[8,8,192]{2,1,0:T(8,128)}, f32[8,8,192]{2,1,0:T(8,128)}), (f32[8,8,192]{2,1,0:T(8,128)}, f32[8,8,192]{2,1,0:T(8,128)})) %all-reduce.10.cloned.1.call-update) | async-done | bytes 98320 | tf_op jit(solution)/shard_map/psum | solution.py:31
  410.8 13.1 %all_to_all.76 = f32[8,8,192]{2,1,0:T(8,128)S(1)} all-to-all(f32[8,8,192]{2,1,0:T(8,128)} %get-tuple-element.10), channel_id=1, replica_groups=mesh['seq'=32,'expert'=8] {'expert'}, dimensions={0} | all-to-all | bytes 98304 | tf_op jit(solution)/shard_map/all_to_all | solution.py:32
  423.9 3.3 all-to-all-start
  427.4 6.5 all-to-all-done
  434.2 1.9 fusion.26
  436.0 1.9 fusion.27
  437.9 205.2 %all-reduce.12.cloned.1.call-done = (f32[4,2,3072]{2,1,0:T(2,128)}, f32[4,2,3072]{2,1,0:T(2,128)}) async-done(((f32[4,2,3072]{2,1,0:T(2,128)}, f32[4,2,3072]{2,1,0:T(2,128)}), (f32[4,2,3072]{2,1,0:T(2,128)}, f32[4,2,3072]{2,1,0:T(2,128)})) %all-reduce.12.cloned.1.call-update) | async-done | bytes 196624 | tf_op jit(solution)/shard_map/psum | solution.py:56
  643.1 3.0 fusion.16
  646.1 32.9 %all-gather.1 = f32[32,48,8]{1,2,0:T(8,128)S(1)} all-gather(f32[1,48,8]{1,2,0:T(8,128)S(1)} %bitcast.68), channel_id=1, replica_groups=mesh['seq'=32,'expert'=8] {'seq'}, dimensions={0}, use_global_device_ids=true | all-gather | bytes 50688 | tf_op jit(solution)/shard_map/all_gather | solution.py:38
  680.0 6.2 all-to-all-start.3
  686.1 4.7 fusion.18
  690.8 3.1 fusion.20
  693.9 33.0 %all-gather = f32[32,48,8]{1,2,0:T(8,128)S(1)} all-gather(f32[1,48,8]{1,2,0:T(8,128)S(1)} %bitcast.71), channel_id=1, replica_groups=mesh['seq'=32,'expert'=8] {'seq'}, dimensions={0}, use_global_device_ids=true | all-gather | bytes 50688 | tf_op jit(solution)/shard_map/all_gather | solution.py:38
  727.8 6.9 all-to-all-start.2
  734.7 1.3 convolution_bitcast_fusion.2
  736.1 5.3 all-to-all-done.2
  741.4 2.5 convolution_bitcast_fusion.1
  743.9 4.4 fusion.15
  748.3 2.4 fusion.13
  750.7 72.3 %all-reduce.14.cloned.1.call-done = (f32[1024,64]{0,1:T(8,128)}, f32[1024,64]{0,1:T(8,128)}) async-done(((f32[1024,64]{0,1:T(8,128)}, f32[1024,64]{0,1:T(8,128)}), (f32[1024,64]{0,1:T(8,128)}, f32[1024,64]{0,1:T(8,128)})) %all-reduce.14.cloned.1.call-update) | async-done | bytes 524304 | tf_op jit(solution)/shard_map/psum | solution.py:83
  823.0 1.3 multiply_reduce_fusion.1
  824.3 58.9 %psum.78 = f32[64]{0:T(128)} all-reduce(f32[64]{0:T(128)S(1)} %get-tuple-element.5), channel_id=1, replica_groups=mesh['seq'=32,'expert'=8] {'seq'}, use_global_device_ids=true, to_apply=%region_15.0 | all-reduce | flops 64 | bytes 512 | tf_op jit(solution)/shard_map/psum | solution.py:85
  883.2 2.0 convolution_bitcast_fusion.3
  885.2 100.6 %psum.79 = f32[192,64]{0,1:T(8,128)} all-reduce(f32[192,64]{0,1:T(8,128)S(1)} %convolution_bitcast_fusion.3), channel_id=1, replica_groups=mesh['seq'=32,'expert'=8] {'seq'}, use_global_device_ids=true, to_apply=%region_16.0 | all-reduce | flops 12288 | bytes 98304 | tf_op jit(solution)/shard_map/psum | solution.py:88
  985.8 3.1 fusion
  (41 shorter events, 3.4 us)
Async XLA Ops:
  7.2 427.0 %copy-start = (f32[4,48,3072]{2,1,0:T(8,128)S(1)}, f32[4,48,3072]{2,1,0:T(8,128)}, u32[]{:S(2)}) copy-start(f32[4,48,3072]{2,1,0:T(8,128)} %param.8) | copy-start | bytes 7077892
  7.2 208.4 %copy-start.2 = (f32[192,1024]{1,0:T(8,128)S(1)}, f32[192,1024]{1,0:T(8,128)}, u32[]{:S(2)}) copy-start(f32[192,1024]{1,0:T(8,128)} %param.9) | copy-start | bytes 2359300
  7.2 92.1 %all-reduce.8.cloned.1.call-start = ((), (), s32[]{:S(2)}) async-start(), calls=%async_computation.4 | async-start | bytes 524288 | tf_op jit(solution)/shard_map/psum | solution.py:45
  9.9 400.9 %all-reduce.10.cloned.1.call-start = ((), (), s32[]{:S(2)}) async-start(), calls=%async_computation.5 | async-start | bytes 262144 | tf_op jit(solution)/shard_map/psum | solution.py:31
  212.8 221.2 %copy-start.8 = (f32[64]{0:T(128)}, f32[64]{0:T(128)S(1)}, u32[]{:S(2)}) copy-start(f32[64]{0:T(128)S(1)} %psum.73) | copy-start | bytes 772
  423.9 10.1 %all-to-all-start = ((f32[8,8,192]{2,1,0:T(8,128)}), f32[8,8,192]{2,1,0:T(8,128)S(1)}, u32[]{:S(2)}, u32[]{:S(2)}) async-start(f32[8,8,192]{2,1,0:T(8,128)} %get-tuple-element.11), calls=%async_computation | async-start | bytes 131072 | tf_op jit(solution)/shard_map/all_to_all | solution.py:32
  427.3 215.8 %all-reduce.12.cloned.1.call-start = ((), (), s32[]{:S(2)}) async-start(), calls=%async_computation.6 | async-start | bytes 393216 | tf_op jit(solution)/shard_map/psum | solution.py:56
  434.1 2.0 copy-start.4
  643.1 43.0 %copy-start.6 = (f32[4,2,3072]{2,1,0:T(2,128)S(1)}, f32[4,2,3072]{2,1,0:T(2,128)}, u32[]{:S(2)}) copy-start(f32[4,2,3072]{2,1,0:T(2,128)} %get-tuple-element.12) | copy-start | bytes 294916
  680.0 47.8 %all-to-all-start.3 = ((f32[8,8,192]{2,0,1:T(8,128)}), f32[8,8,192]{2,0,1:T(8,128)S(1)}, u32[]{:S(2)}, u32[]{:S(2)}) async-start(f32[8,8,192]{2,0,1:T(8,128)} %copy.18), calls=%async_computation.3 | async-start | bytes 131072 | tf_op jit(solution)/shard_map/all_to_all | solution.py:39
  686.1 4.7 copy-start.5
  727.8 13.6 %all-to-all-start.2 = ((f32[8,8,192]{2,0,1:T(8,128)}), f32[8,8,192]{2,0,1:T(8,128)S(1)}, u32[]{:S(2)}, u32[]{:S(2)}) async-start(f32[8,8,192]{2,0,1:T(8,128)} %copy.16), calls=%async_computation.2 | async-start | bytes 131072 | tf_op jit(solution)/shard_map/all_to_all | solution.py:39
  734.7 13.6 %copy-start.1 = (f32[1024,64]{0,1:T(8,128)S(1)}, f32[1024,64]{0,1:T(8,128)}, u32[]{:S(2)}) copy-start(f32[1024,64]{0,1:T(8,128)} %all-reduce.8.cloned.1.call-done) | copy-start | bytes 786436
  734.7 88.3 %all-reduce.14.cloned.1.call-start = ((), (), s32[]{:S(2)}) async-start(), calls=%async_computation.7 | async-start | bytes 1048576 | tf_op jit(solution)/shard_map/psum | solution.py:83
  743.8 139.4 %copy-start.3 = (f32[192,1024]{1,0:T(8,128)S(1)}, f32[192,1024]{1,0:T(8,128)}, u32[]{:S(2)}) copy-start(f32[192,1024]{1,0:T(8,128)} %param.5) | copy-start | bytes 2359300
  748.3 237.5 %copy-start.7 = (f32[192,64]{0,1:T(8,128)S(1)}, f32[192,64]{0,1:T(8,128)}, u32[]{:S(2)}) copy-start(f32[192,64]{0,1:T(8,128)} %param.6) | copy-start | bytes 147460
Sparse Core Ops, SparseCore 0:
  11.2 88.0 all-reduce.7
  218.2 192.5 all-reduce.9
  438.0 204.9 all-reduce.11
  744.0 78.9 all-reduce.13
where the time goes:
time: 999 us; the launch traced here: 995 us
  waiting for transfers between devices  571 us (57%)
  blocking collectives  350 us (35%)
  matrix products  38.1 us (4%)
  starting transfers between devices  16.6 us (2%)
  between operations  13.9 us (1%)
    psum x1, waiting for transfers between devices, per_device(): pre = lax.psum(pre_part, 'seq')  205 us
    psum x1, waiting for transfers between devices, to_owners(): summed = lax.psum(partial_value, 'seq')  193 us
    psum x1, blocking collectives, per_device(): grad_router = lax.psum(product(tokens, grad_logits), 'seq')  101 us
    psum x1, waiting for transfers between devices, per_device(): logits = lax.psum(contract(tokens, router, 0, 0), 'expert')  89.4 us
    psum x1, waiting for transfers between devices, per_device(): grad_dispatch = lax.psum(dispatch_part, 'expert')  72.3 us
    all_gather x2, blocking collectives, from_owners(): widened = lax.all_gather(block, 'seq', axis=1, tiled=True)  65.9 us
    psum x1, blocking collectives, per_device(): column_total = lax.psum(jnp.sum(dispatch * grad_dispatch, axis=0), 'seq')  58.9 us
    pmax x1, blocking collectives, per_device(): column_top = lax.pmax(jnp.max(logits, axis=0), 'seq')  58.3 us
  transfers between devices with their start and end apart: 7, of which 6 were waited for; matrix products, arithmetic and copies ran while one was open for 2% of the time, Pallas kernels for 0%

commit v1 on v0

v1 whole, which is shorter than its diff:
```python
import jax
import jax.numpy as jnp
from jax import lax
from jax.sharding import PartitionSpec as P

HIGH = lax.Precision.HIGHEST
S = "seq"
E = "expert"


def smooth_gate(values):
    return jax.nn.gelu(values, approximate=True)


def contract(left, right, left_dim, right_dim):
    return lax.dot_general(
        left,
        right,
        (((left_dim,), (right_dim,)), ((), ())),
        precision=HIGH,
        preferred_element_type=jnp.float32,
    )


def einsum(form, left, right):
    return jnp.einsum(form, left, right, precision=HIGH, preferred_element_type=jnp.float32)


def exchange(blocks, axis, groups=None):
    return lax.all_to_all(blocks, axis, 0, 0, axis_index_groups=groups, tiled=True)


def gather(block, axis, count, groups=None):
    return exchange(jnp.broadcast_to(block[None], (count,) + block.shape), axis, groups)


def merge(tops, sums, rows):
    top = jnp.max(tops, axis=0)
    scale = jnp.exp(tops - top[None])
    return top, jnp.sum(scale * sums, axis=0), jnp.sum(scale[..., None] * rows, axis=0)


def per_device(tokens, router, w_in, w_out, grad_out):
    n_seq, n_exp = lax.axis_size(S), lax.axis_size(E)
    local_experts, width_block, hidden = w_in.shape
    rows_block, local_tokens = tokens.shape
    slots = router.shape[1]
    own_slots = slots // n_exp
    per_expert = own_slots // local_experts
    width = rows_block * n_exp
    piece = local_tokens // n_exp
    core = lax.axis_index(S) % 2
    chips = n_seq // 2
    partner = [(i, i ^ 1) for i in range(n_seq)]
    groups = [[2 * k + c for k in range(chips)] for c in range(2)]
    half = own_slots // 2

    def by_tokens(values):
        return jnp.transpose(values.reshape(rows_block, n_exp, piece), (1, 0, 2))

    folded = jnp.concatenate([router[: rows_block // 2], router[rows_block // 2 :]], axis=1)
    packed = jnp.concatenate(
        [
            by_tokens(tokens),
            by_tokens(grad_out),
            jnp.broadcast_to(folded[None], (n_exp,) + folded.shape),
        ],
        axis=1,
    )
    got = exchange(packed, E)
    x = got[:, :rows_block].reshape(width, piece)
    g = got[:, rows_block : 2 * rows_block].reshape(width, piece)
    r = got[:, 2 * rows_block :]
    router_full = jnp.concatenate([r[:, :, :slots], r[:, :, slots:]], axis=1).reshape(width, slots)

    logits = contract(router_full, x, 0, 0)
    combine = jax.nn.softmax(logits, axis=0)
    local_top = jnp.max(logits, axis=1)
    raised = jnp.exp(logits - local_top[:, None])
    local_sum = jnp.sum(raised, axis=1)
    rows_in = contract(raised, x, 1, 1).reshape(n_exp, own_slots, width)
    rows_out = contract(combine, g, 1, 1).reshape(n_exp, own_slots, width)
    marks = jnp.stack([local_top, local_sum], axis=1).reshape(n_exp, own_slots, 2)
    marks = jnp.pad(marks, ((0, 0), (0, own_slots), (0, 126)))
    sent = jnp.concatenate([jnp.concatenate([rows_in, rows_out], axis=1), marks], axis=2)
    got = exchange(sent, E)
    top, total, rows = merge(
        got[:, :own_slots, width], got[:, :own_slots, width + 1], got[:, :own_slots, :width]
    )
    outer = jnp.sum(got[:, own_slots:, :width], axis=0)

    def by_width(values):
        return jnp.transpose(values.reshape(own_slots, n_seq, width_block), (1, 0, 2))

    def spread(values):
        return jnp.broadcast_to(values[None, :, None], (n_seq, own_slots, 1))

    sent = jnp.concatenate(
        [
            by_width(rows),
            by_width(outer),
            spread(top),
            spread(total),
            jnp.zeros((n_seq, own_slots, 30), jnp.float32),
        ],
        axis=2,
    )
    got = exchange(sent, S)
    w = width_block
    top, total, rows = merge(got[:, :, 2 * w], got[:, :, 2 * w + 1], got[:, :, :w])
    slot_in = rows / total[:, None]
    grad_slot_out = jnp.sum(got[:, :, w : 2 * w], axis=0)

    inputs = slot_in.reshape(local_experts, per_expert, w)
    outers = grad_slot_out.reshape(local_experts, per_expert, w)
    pre_part = einsum("epd,edh->eph", inputs, w_in).reshape(2, half, hidden)
    act_part = einsum("epd,edh->eph", outers, w_out).reshape(2, half, hidden)
    parts = jnp.stack([pre_part, act_part], axis=1)
    mine = lax.dynamic_index_in_dim(parts, core, 0, keepdims=False)
    theirs = lax.dynamic_index_in_dim(parts, 1 - core, 0, keepdims=False)
    mine = mine + lax.ppermute(theirs, S, partner)
    share = half * hidden // chips
    sent = jnp.transpose(mine.reshape(2, chips, share), (1, 0, 2))
    got = jnp.sum(exchange(sent, S, groups), axis=0)
    act, backward = jax.vjp(smooth_gate, got[0])
    grad_pre = backward(got[1])[0]
    got = gather(jnp.stack([act, grad_pre]), S, chips, groups)
    mine = jnp.transpose(got, (1, 0, 2)).reshape(2, half, hidden)
    theirs = lax.ppermute(mine, S, partner)
    both = jnp.where(core == 0, jnp.stack([mine, theirs], 1), jnp.stack([theirs, mine], 1))
    both = both.reshape(2, local_experts, per_expert, hidden)
    act, grad_pre = both[0], both[1]

    slot_out = einsum("eph,edh->epd", act, w_out).reshape(own_slots, w)
    grad_slot_in = einsum("eph,edh->epd", grad_pre, w_in).reshape(own_slots, w)
    grad_w_out = einsum("epd,eph->edh", outers, act)
    grad_w_in = einsum("epd,eph->edh", inputs, grad_pre)
    column_part = jnp.sum(slot_in * grad_slot_in, axis=1)
    sent = jnp.concatenate(
        [
            slot_out,
            grad_slot_in,
            top[:, None],
            total[:, None],
            column_part[:, None],
            jnp.zeros((own_slots, 29), jnp.float32),
        ],
        axis=1,
    )
    got = gather(sent, S, n_seq)

    def to_rows(values):
        return jnp.transpose(values, (1, 0, 2)).reshape(own_slots, width)

    marks = jnp.stack(
        [got[0, :, 2 * w], got[0, :, 2 * w + 1], jnp.sum(got[:, :, 2 * w + 2], axis=0)], axis=1
    )
    marks = jnp.pad(marks, ((0, own_slots), (0, 125)))
    rows = jnp.concatenate([to_rows(got[:, :, :w]), to_rows(got[:, :, w : 2 * w])], axis=0)
    got = gather(jnp.concatenate([rows, marks], axis=1), E, n_exp)
    slot_out = got[:, :own_slots, :width].reshape(slots, width)
    grad_slot_in = got[:, own_slots:, :width].reshape(slots, width)
    marks = got[:, :own_slots, width:].reshape(slots, 128)
    top, total, column_total = marks[:, 0], marks[:, 1], marks[:, 2]

    grad_combine = contract(slot_out, g, 1, 0)
    grad_dispatch = contract(grad_slot_in, x, 1, 0)
    dispatch = raised * (jnp.exp(local_top - top) / total)[:, None]
    grad_logits = combine * (
        grad_combine - jnp.sum(combine * grad_combine, axis=0, keepdims=True)
    ) + dispatch * (grad_dispatch - column_total[:, None])
    got = gather(jnp.concatenate([dispatch, grad_logits], axis=0), E, n_exp)
    spread_all = jnp.transpose(got, (1, 0, 2)).reshape(2 * slots, local_tokens)
    mine = lax.dynamic_slice_in_dim(
        grad_slot_in, lax.axis_index(E) * rows_block, rows_block, 1
    )
    grad_tokens = contract(jnp.concatenate([mine, router.T], axis=0), spread_all, 0, 0)
    router_part = contract(tokens, spread_all[slots:], 1, 1)
    parts = router_part.reshape(2, rows_block // 2, slots)
    mine = lax.dynamic_index_in_dim(parts, core, 0, keepdims=False)
    theirs = lax.dynamic_index_in_dim(parts, 1 - core, 0, keepdims=False)
    mine = mine + lax.ppermute(theirs, S, partner)
    mine = jnp.sum(gather(mine, S, chips, groups), axis=0)
    theirs = lax.ppermute(mine, S, partner)
    grad_router = jnp.where(
        core == 0, jnp.concatenate([mine, theirs]), jnp.concatenate([theirs, mine])
    )
    return (grad_tokens, grad_router, grad_w_in, grad_w_out)


def solution(mesh):
    placed = (
        P("expert", "seq"),
        P("expert", None),
        P("expert", "seq", None),
        P("expert", "seq", None),
        P("expert", "seq"),
    )
    return jax.shard_map(
        per_device,
        mesh=mesh,
        in_specs=placed,
        out_specs=(
            P("expert", "seq"),
            P("expert", None),
            P("expert", "seq", None),
            P("expert", "seq", None),
        ),
        check_vma=False,
    )
```

time: 999 us -> 226 us (0.23)
  waiting for transfers between devices: 571 us -> 30.6 us
  blocking collectives: 350 us -> 98.3 us
  local copies, waits for them, and re-layouts: 2.08 us -> 28.8 us
  between operations: 13.9 us -> 1.11 us
  starting transfers between devices: 16.6 us -> 28.9 us
    psum x4 -> x0, waiting for transfers between devices: 560 us -> none  [the longest x1 205 us: per_device(): pre = lax.psum(pre_part, 'seq')]
    psum x3 -> x0, blocking collectives: 213 us -> none  [the longest x1 101 us: per_device(): grad_router = lax.psum(product(tokens, grad_logits), 'seq')]
    all_to_all x1 -> x6, blocking collectives: 13.1 us -> 98.3 us  [exchange(): lax.all_to_all(blocks, axis, 0, 0, axis_index_groups=groups, tiled=True)]
    all_gather x2 -> x0, blocking collectives: 65.9 us -> none  [from_owners(): widened = lax.all_gather(block, 'seq', axis=1, tiled=True)]
    pmax x1 -> x0, blocking collectives: 58.3 us -> none  [per_device(): column_top = lax.pmax(jnp.max(logits, axis=0), 'seq')]
    all_to_all x3, waiting for transfers between devices: 11.8 us -> 28.7 us  [exchange(): lax.all_to_all(blocks, axis, 0, 0, axis_index_groups=groups, tiled=True)]
    dot_general x7 -> x6, matrix products: 21 us -> 17.1 us  [einsum(): jnp.einsum(form, left, right, precision=HIGH, preferred_element_type=jnp....]
  transfers between devices with their start and end apart: 7 -> 7, of which waited for: 6 -> 5; matrix products, arithmetic and copies ran while one was open for 2% -> 5% of each run, Pallas kernels for 0% -> 0%
where the time goes in v1:
time: 226 us; the launch traced here: 224 us
  blocking collectives  98.3 us (43%)
  waiting for transfers between devices  30.6 us (14%)
  starting transfers between devices  28.9 us (13%)
  local copies, waits for them, and re-layouts  28.8 us (13%)
  matrix products  28.2 us (12%)
  other arithmetic  8.44 us (4%)
    all_to_all x6, blocking collectives, exchange(): lax.all_to_all(blocks, axis, 0, 0, axis_index_groups=groups, tiled=True)  98.3 us
    all_to_all x3, waiting for transfers between devices, exchange(): lax.all_to_all(blocks, axis, 0, 0, axis_index_groups=groups, tiled=True)  28.7 us
    all_to_all x3, starting transfers between devices, exchange(): lax.all_to_all(blocks, axis, 0, 0, axis_index_groups=groups, tiled=True)  19.6 us
    dot_general x6, matrix products, einsum(): jnp.einsum(form, left, right, precision=HIGH, preferred_element_type=jnp....  17.1 us
    dot_general x7, matrix products, contract(): lax.dot_general(left, right, (((left_dim,), (right_dim,)), ((), ())), pre...  11.1 us
    ppermute x2, starting transfers between devices, per_device(): mine = mine + lax.ppermute(theirs, S, partner)  5.77 us
  transfers between devices with their start and end apart: 7, of which 5 were waited for; matrix products, arithmetic and copies ran while one was open for 5% of the time, Pallas kernels for 0%

profile of v1, /device:TPU:1, one launch (start us, length us, event | category | flops | bytes accessed | tf_op | source)
XLA Modules:
  0.0 224.5 jit_solution(13997149898392580819)
XLA Ops:
  1.8 1.5 bitcast_bitcast_fusion
  3.5 33.4 %all_to_all.45 = f32[8,480,128]{2,1,0:T(8,128)S(1)} all-to-all(f32[8,480,128]{2,1,0:T(8,128)S(1)} %pad_maximum_fusion), channel_id=1, replica_groups=mesh['seq'=32,'expert'=8] {'expert'}, dimensions={0} | all-to-all | bytes 3932160 | tf_op jit(solution)/shard_map/all_to_all | solution.py:30
  38.2 1.5 fusion.38
  40.2 1.5 fusion.39
  43.8 16.1 %all_to_all.46 = f32[8,16,1664]{2,1,0:T(8,128)S(1)} all-to-all(f32[8,16,1664]{2,1,0:T(8,128)S(1)} %select_maximum_fusion), channel_id=1, replica_groups=mesh['seq'=32,'expert'=8] {'expert'}, dimensions={0} | all-to-all | bytes 1703936 | tf_op jit(solution)/shard_map/all_to_all | solution.py:30
  62.6 1.9 concatenate.45
  64.5 1.6 copy.103
  66.2 11.5 %all-to-all-start.2 = ((f32[32,8,128]{2,1,0:T(8,128)}), f32[32,8,128]{2,1,0:T(8,128)S(1)}, u32[]{:S(2)}, u32[]{:S(2)}) async-start(f32[32,8,128]{2,1,0:T(8,128)} %copy.103), calls=%async_computation.2 | async-start | bytes 262144 | tf_op jit(solution)/shard_map/all_to_all | solution.py:30
  77.7 9.0 %all-to-all-done.2 = f32[32,8,128]{2,1,0:T(8,128)S(1)} async-done(((f32[32,8,128]{2,1,0:T(8,128)}), f32[32,8,128]{2,1,0:T(8,128)S(1)}, u32[]{:S(2)}, u32[]{:S(2)}) %all-to-all-start.2) | async-done | bytes 131104 | tf_op jit(solution)/shard_map/all_to_all | solution.py:30
  89.4 2.9 %fusion.44 = f32[4,2,3072]{2,1,0:T(2,128)S(1)} fusion(f32[4,2,48]{2,1,0:T(2,128)S(1)} %bitcast.136, f32[4,48,3072]{2,1,0:T(8,128)} %param.8), kind=kOutput, calls=%fused_computation.100 | convolution fusion | flops 14155776 | bytes 2459136 | tf_op jit(solution)/shard_map/epd,edh->eph/dot_general | solution.py:26
  96.8 1.7 collective-permute-start
  99.6 1.6 bitcast_add_fusion
  102.2 10.1 %all_to_all.47 = f32[16,2,768]{2,1,0:T(2,128)S(1)} all-to-all(f32[16,2,768]{2,1,0:T(2,128)S(1)} %copy.107), channel_id=1, replica_groups={{0,16,32,48,64,80,96,112,128,144,160,176,192,208,224,240},{8,24,40,56,7..., dimensions={0} | all-to-all | bytes 196608 | tf_op jit(solution)/shard_map/all_to_all | solution.py:30
  112.4 10.6 %all_to_all.48 = f32[16,2,768]{2,1,0:T(2,128)S(1)} all-to-all(f32[16,2,768]{2,1,0:T(2,128)S(1)} %broadcast_in_dim.30), channel_id=1, replica_groups={{0,16,32,48,64,80,96,112,128,144,160,176,192,208,224,240},{8,24,40,56,7..., dimensions={0} | all-to-all | bytes 196608 | tf_op jit(solution)/shard_map/all_to_all | solution.py:30
  123.0 2.6 %collective-permute-start.1 = (f32[2,4,3072]{2,1,0:T(4,128)S(1)}, f32[2,4,3072]{2,1,0:T(4,128)}, u32[]{:S(2)}, u32[]{:S(2)}) collective-permute-start(f32[2,4,3072]{2,1,0:T(4,128)S(1)} %reshape.130), channel_id=1, source_target_pairs={{0,8},{8,0},{16,24},{24,16},{32,40},{40,32},{48,56},{56,48},{64,72... | collective-permute-start | bytes 294920 | tf_op jit(solution)/shard_map/ppermute | solution.py:129
  127.9 2.1 multiply_reduce_fusion.1
  130.2 3.7 %fusion.45 = f32[4,2,48]{2,1,0:T(2,128)S(1)} fusion(f32[4,2,3072]{2,1,0:T(2,128)S(1)} %squeeze.43, f32[4,48,3072]{2,1,0:T(8,128)} %param.8), kind=kOutput, calls=%fused_computation.101 | convolution fusion | flops 14155776 | bytes 2459136 | tf_op jit(solution)/shard_map/eph,edh->epd/dot_general | solution.py:26
  134.0 12.2 %all_to_all.49 = f32[32,8,128]{2,1,0:T(8,128)S(1)} all-to-all(f32[32,8,128]{2,1,0:T(8,128)S(1)} %broadcast_in_dim.35), channel_id=1, replica_groups=mesh['seq'=32,'expert'=8] {'seq'}, dimensions={0} | all-to-all | bytes 262144 | tf_op jit(solution)/shard_map/all_to_all | solution.py:30
  149.5 1.6 copy.114
  151.1 1.6 reshape.134
  154.5 16.0 %all_to_all.50 = f32[8,16,1664]{2,1,0:T(8,128)S(1)} all-to-all(f32[8,16,1664]{2,1,0:T(8,128)S(1)} %broadcast_in_dim.36), channel_id=1, replica_groups=mesh['seq'=32,'expert'=8] {'expert'}, dimensions={0} | all-to-all | bytes 1703936 | tf_op jit(solution)/shard_map/all_to_all | solution.py:30
  171.7 1.9 multiply_reduce_fusion
  173.6 1.6 fusion.1
  176.1 3.5 %all-to-all-start.7 = ((f32[8,128,128]{1,2,0:T(8,128)}), f32[8,128,128]{1,2,0:T(8,128)S(1)}, u32[]{:S(2)}, u32[]{:S(2)}) async-start(f32[8,128,128]{1,2,0:T(8,128)} %broadcast_in_dim.37), calls=%async_computation.7 | async-start | bytes 1048576 | tf_op jit(solution)/shard_map/all_to_all | solution.py:30
  179.6 9.1 %all-to-all-done.7 = f32[8,128,128]{1,2,0:T(8,128)S(1)} async-done(((f32[8,128,128]{1,2,0:T(8,128)}), f32[8,128,128]{1,2,0:T(8,128)S(1)}, u32[]{:S(2)}, u32[]{:S(2)}) %all-to-all-start.7) | async-done | bytes 524320 | tf_op jit(solution)/shard_map/all_to_all | solution.py:30
  188.9 2.2 convolution_bitcast_fusion
  191.3 4.1 %collective-permute-start.2 = (f32[96,64]{0,1:T(8,128)S(1)}, f32[96,64]{0,1:T(8,128)S(1)}, u32[]{:S(2)}, u32[]{:S(2)}) collective-permute-start(f32[96,64]{0,1:T(8,128)S(1)} %bitcast.138), channel_id=1, source_target_pairs={{0,8},{8,0},{16,24},{24,16},{32,40},{40,32},{48,56},{56,48},{64,72... | collective-permute-start | bytes 73736 | tf_op jit(solution)/shard_map/ppermute | solution.py:182
  195.4 3.7 %fusion.35 = f32[4,48,3072]{2,1,0:T(8,128)} fusion(f32[4,2,3072]{2,1,0:T(2,128)S(1)} %squeeze.44, f32[4,2,48]{2,1,0:T(2,128)S(1)} %bitcast.135, f32[4,2]{1,0:T(4,128)S(1)} %copy-done.10), kind=kOutput, calls=%fused_computation.91 | convolution fusion | flops 14156160 | bytes 2459168 | tf_op jit(solution)/shard_map/epd,eph->edh/dot_general | solution.py:26
  199.9 4.6 %all-to-all-start.8 = ((f32[16,96,64]{1,2,0:T(8,128)}), f32[16,96,64]{1,2,0:T(8,128)}, u32[]{:S(2)}, u32[]{:S(2)}) async-start(f32[16,96,64]{1,2,0:T(8,128)} %broadcast_in_dim.38), calls=%async_computation.8 | async-start | bytes 1048576 | tf_op jit(solution)/shard_map/all_to_all | solution.py:30
  204.5 3.5 %fusion.46 = f32[4,48,3072]{2,1,0:T(8,128)} fusion(f32[4,2,48]{2,1,0:T(2,128)S(1)} %bitcast.137, f32[4,2,3072]{2,1,0:T(2,128)S(1)} %squeeze.43), kind=kOutput, calls=%fused_computation.102 | convolution fusion | flops 14155776 | bytes 2459136 | tf_op jit(solution)/shard_map/epd,eph->edh/dot_general | solution.py:26
  209.1 10.5 %all-to-all-done.8 = f32[16,96,64]{1,2,0:T(8,128)} async-done(((f32[16,96,64]{1,2,0:T(8,128)}), f32[16,96,64]{1,2,0:T(8,128)}, u32[]{:S(2)}, u32[]{:S(2)}) %all-to-all-start.8) | async-done | bytes 393248 | tf_op jit(solution)/shard_map/all_to_all | solution.py:30
  221.7 2.0 fusion.8
  (121 shorter events, 32.1 us)
Async XLA Ops:
  0.6 92.4 %copy-start = (f32[4,48,3072]{2,1,0:T(8,128)S(1)}, f32[4,48,3072]{2,1,0:T(8,128)}, u32[]{:S(2)}) copy-start(f32[4,48,3072]{2,1,0:T(8,128)} %param.7) | copy-start | bytes 7077892
  36.9 1.3 copy-start.1
  39.7 4.0 %copy-start.11 = (f32[64]{0:T(128)}, f32[64]{0:T(128)S(1)}, u32[]{:S(2)}) copy-start(f32[64]{0:T(128)S(1)} %get-tuple-element.14) | copy-start | bytes 772
  39.7 4.0 %copy-start.13 = (f32[128]{0:T(128)}, f32[128]{0:T(128)S(1)}, u32[]{:S(2)}) copy-start(f32[128]{0:T(128)S(1)} %get-tuple-element.13) | copy-start | bytes 1540
  40.0 3.7 %copy-start.15 = (f32[128]{0:T(128)}, f32[128]{0:T(128)S(1)}, u32[]{:S(2)}) copy-start(f32[128]{0:T(128)S(1)} %get-tuple-element.11) | copy-start | bytes 1540
  41.7 18.2 %copy-start.2 = (f32[8,192,128]{2,1,0:T(8,128)}, f32[8,192,128]{2,1,0:T(8,128)S(1)}, u32[]{:S(2)}) copy-start(f32[8,192,128]{2,1,0:T(8,128)S(1)} %get-tuple-element.16) | copy-start | bytes 2359300
  66.2 20.6 %all-to-all-start.2 = ((f32[32,8,128]{2,1,0:T(8,128)}), f32[32,8,128]{2,1,0:T(8,128)S(1)}, u32[]{:S(2)}, u32[]{:S(2)}) async-start(f32[32,8,128]{2,1,0:T(8,128)} %copy.103), calls=%async_computation.2 | async-start | bytes 262144 | tf_op jit(solution)/shard_map/all_to_all | solution.py:30
  89.1 38.7 %copy-start.9 = (f32[4,2]{1,0:T(4,128)}, f32[4,2]{1,0:T(4,128)S(1)}, u32[]{:S(2)}) copy-start(f32[4,2]{1,0:T(4,128)S(1)} %div.26) | copy-start | bytes 100
  89.3 4.9 %copy-start.7 = (f32[8,48]{1,0:T(8,128)}, f32[8,48]{1,0:T(8,128)S(1)}, u32[]{:S(2)}) copy-start(f32[8,48]{1,0:T(8,128)S(1)} %get-tuple-element.9) | copy-start | bytes 4612
  89.4 38.5 %copy-start.5 = (f32[8,48]{1,0:T(8,128)}, f32[8,48]{1,0:T(8,128)S(1)}, u32[]{:S(2)}) copy-start(f32[8,48]{1,0:T(8,128)S(1)} %get-tuple-element.10) | copy-start | bytes 4612
  96.8 2.8 %collective-permute-start = (f32[2,4,3072]{2,1,0:T(4,128)S(1)}, f32[2,4,3072]{2,1,0:T(4,128)}, u32[]{:S(2)}, u32[]{:S(2)}) collective-permute-start(f32[2,4,3072]{2,1,0:T(4,128)S(1)} %dynamic-slice_bitcast_fusion), channel_id=1, source_target_pairs={{0,8},{8,0},{16,24},{24,16},{32,40},{40,32},{48,56},{56,48},{64,72... | collective-permute-start | bytes 294920 | tf_op jit(solution)/shard_map/ppermute | solution.py:121
  123.0 3.7 %collective-permute-start.1 = (f32[2,4,3072]{2,1,0:T(4,128)S(1)}, f32[2,4,3072]{2,1,0:T(4,128)}, u32[]{:S(2)}, u32[]{:S(2)}) collective-permute-start(f32[2,4,3072]{2,1,0:T(4,128)S(1)} %reshape.130), channel_id=1, source_target_pairs={{0,8},{8,0},{16,24},{24,16},{32,40},{40,32},{48,56},{56,48},{64,72... | collective-permute-start | bytes 294920 | tf_op jit(solution)/shard_map/ppermute | solution.py:129
  152.8 18.8 %copy-start.12 = (f32[64]{0:T(128)S(1)}, f32[64]{0:T(128)}, u32[]{:S(2)}) copy-start(f32[64]{0:T(128)} %copy-done.11) | copy-start | bytes 772
  152.8 18.9 %copy-start.14 = (f32[128]{0:T(128)S(1)}, f32[128]{0:T(128)}, u32[]{:S(2)}) copy-start(f32[128]{0:T(128)} %copy-done.13) | copy-start | bytes 1540
  152.8 18.9 %copy-start.16 = (f32[128]{0:T(128)S(1)}, f32[128]{0:T(128)}, u32[]{:S(2)}) copy-start(f32[128]{0:T(128)} %copy-done.15) | copy-start | bytes 1540
  170.4 0.9 copy-start.3
  175.2 20.2 %copy-start.6 = (f32[8,48]{1,0:T(8,128)S(1)}, f32[8,48]{1,0:T(8,128)}, u32[]{:S(2)}) copy-start(f32[8,48]{1,0:T(8,128)} %copy-done.5) | copy-start | bytes 4612
  175.2 20.2 %copy-start.10 = (f32[4,2]{1,0:T(4,128)S(1)}, f32[4,2]{1,0:T(4,128)}, u32[]{:S(2)}) copy-start(f32[4,2]{1,0:T(4,128)} %copy-done.9) | copy-start | bytes 100
  176.1 12.6 %all-to-all-start.7 = ((f32[8,128,128]{1,2,0:T(8,128)}), f32[8,128,128]{1,2,0:T(8,128)S(1)}, u32[]{:S(2)}, u32[]{:S(2)}) async-start(f32[8,128,128]{1,2,0:T(8,128)} %broadcast_in_dim.37), calls=%async_computation.7 | async-start | bytes 1048576 | tf_op jit(solution)/shard_map/all_to_all | solution.py:30
  191.1 13.4 %copy-start.8 = (f32[8,48]{1,0:T(8,128)S(1)}, f32[8,48]{1,0:T(8,128)}, u32[]{:S(2)}) copy-start(f32[8,48]{1,0:T(8,128)} %copy-done.7) | copy-start | bytes 4612
  191.3 7.8 %collective-permute-start.2 = (f32[96,64]{0,1:T(8,128)S(1)}, f32[96,64]{0,1:T(8,128)S(1)}, u32[]{:S(2)}, u32[]{:S(2)}) collective-permute-start(f32[96,64]{0,1:T(8,128)S(1)} %bitcast.138), channel_id=1, source_target_pairs={{0,8},{8,0},{16,24},{24,16},{32,40},{40,32},{48,56},{56,48},{64,72... | collective-permute-start | bytes 73736 | tf_op jit(solution)/shard_map/ppermute | solution.py:182
  199.9 21.8 %copy-start.4 = (f32[192,64]{0,1:T(8,128)S(1)}, f32[192,64]{0,1:T(8,128)}, u32[]{:S(2)}) copy-start(f32[192,64]{0,1:T(8,128)} %param.6) | copy-start | bytes 147460
  199.9 19.7 %all-to-all-start.8 = ((f32[16,96,64]{1,2,0:T(8,128)}), f32[16,96,64]{1,2,0:T(8,128)}, u32[]{:S(2)}, u32[]{:S(2)}) async-start(f32[16,96,64]{1,2,0:T(8,128)} %broadcast_in_dim.38), calls=%async_computation.8 | async-start | bytes 1048576 | tf_op jit(solution)/shard_map/all_to_all | solution.py:30
  220.7 3.0 %collective-permute-start.3 = (f32[96,64]{0,1:T(8,128)S(1)}, f32[96,64]{0,1:T(8,128)S(1)}, u32[]{:S(2)}, u32[]{:S(2)}) collective-permute-start(f32[96,64]{0,1:T(8,128)S(1)} %reduce_sum.132), channel_id=1, source_target_pairs={{0,8},{8,0},{16,24},{24,16},{32,40},{40,32},{48,56},{56,48},{64,72... | collective-permute-start | bytes 73736 | tf_op jit(solution)/shard_map/ppermute | solution.py:184

commit v2 on v0

v2 whole, which is shorter than its diff:
```python
import functools

import jax
import jax.numpy as jnp
from jax import lax
from jax.experimental import pallas as pl
from jax.experimental.pallas import tpu as pltpu
from jax.sharding import PartitionSpec as P

HIGH = lax.Precision.HIGHEST
S = "seq"
E = "expert"
LANES = 128
F32 = jnp.float32


def contract(left, right, left_dim, right_dim, precision=HIGH):
    return lax.dot_general(
        left,
        right,
        (((left_dim,), (right_dim,)), ((), ())),
        precision=precision,
        preferred_element_type=F32,
    )


def exchange(blocks, axis, groups=None):
    return lax.all_to_all(blocks, axis, 0, 0, axis_index_groups=groups, tiled=True)


def run(kernel, shapes, *values, scratch=(), flops=0):
    single = not isinstance(shapes, list)
    shapes = [shapes] if single else shapes
    size = 4 * sum(v.size for v in values) + 4 * sum(functools.reduce(lambda a, b: a * b, s) for s in shapes)
    spec = pl.BlockSpec(memory_space=pltpu.VMEM)
    out = pl.pallas_call(
        kernel,
        out_shape=[jax.ShapeDtypeStruct(s, F32) for s in shapes],
        in_specs=[spec] * len(values),
        out_specs=[spec] * len(shapes),
        scratch_shapes=[pltpu.VMEM(s, F32) for s in scratch],
        compiler_params=pltpu.CompilerParams(vmem_limit_bytes=40 * 1024 * 1024),
        cost_estimate=pl.CostEstimate(flops=flops, bytes_accessed=size, transcendentals=0),
    )(*values)
    return out[0] if single else out


def row_of(shape):
    return lax.broadcasted_iota(jnp.int32, shape, len(shape) - 2) % 8


def lane_of(shape):
    return lax.broadcasted_iota(jnp.int32, shape, len(shape) - 1)


def swap(values):
    return jnp.concatenate([values[..., 4:8, :], values[..., 0:4, :]], axis=-2)


def core_index():
    return lax.axis_index(S) % 2


def pack_tokens(tokens, grad_out, router, out):
    n, rows = out.shape[0], tokens.shape[0]
    folded = jnp.concatenate([router[: rows // 2], router[rows // 2 :]], axis=1)
    for e in range(n):
        out[e, 0:rows] = tokens[:, e * LANES : (e + 1) * LANES]
        out[e, rows : 2 * rows] = grad_out[:, e * LANES : (e + 1) * LANES]
        out[e, 2 * rows :] = folded


def token_blocks(got):
    n, rows = got.shape[0], got.shape[1] * 2 // 5
    x = got[:, 0:rows].reshape(n * rows, LANES)
    g = got[:, rows : 2 * rows].reshape(n * rows, LANES)
    return x, g


def softmax_rows(got, sent, keep, tops):
    n, rows = got.shape[0], got.shape[1] * 2 // 5
    width = n * rows
    half = rows // 2
    r = got[:, 2 * rows :].reshape(n * half, LANES)
    pair = jnp.concatenate(
        [
            got[:, 0:half].reshape(n * half, LANES),
            got[:, half:rows].reshape(n * half, LANES),
        ],
        axis=1,
    )
    both = contract(r, pair, 0, 0)
    slots = LANES // 2
    logits = both[:slots, :LANES] + both[slots:, LANES:]
    raised = jnp.exp(logits - jnp.max(logits, axis=0, keepdims=True))
    combine = raised / jnp.sum(raised, axis=0, keepdims=True)
    top = jnp.max(logits, axis=1, keepdims=True)
    raised = jnp.exp(logits - top)
    total = jnp.sum(raised, axis=1, keepdims=True)
    x, g = token_blocks(got)
    rows_in = contract(raised, x, 1, 1)
    rows_out = contract(combine, g, 1, 1)
    lane = lane_of((slots, LANES))
    marks = jnp.where(lane == 0, top, jnp.where(lane == 1, total, 0.0))
    plain = jnp.where(lane_of((4, LANES)) == 1, 1.0, 0.0)
    wide_top = jnp.broadcast_to(top, (slots, LANES))
    for j in range(slots // 4):
        e, b, s = j // 2, 8 * (j % 2), slice(4 * j, 4 * j + 4)
        sent[e, b : b + 4, 0:width] = rows_in[s]
        sent[e, b + 4 : b + 8, 0:width] = rows_out[s]
        sent[e, b : b + 4, width:] = marks[s]
        sent[e, b + 4 : b + 8, width:] = plain
        keep[j, 0:4] = combine[s]
        keep[j, 4:8] = raised[s]
        tops[j, 0:4] = wide_top[s]
        tops[j, 4:8] = wide_top[s]


def merge_tokens(got, out):
    n, width = got.shape[0], got.shape[2] - LANES
    wide = out.shape[0] // 2
    piece = width // wide
    marks = [got[e, :, width:] for e in range(n)]
    top = functools.reduce(jnp.maximum, [m[:, 0:1] for m in marks])
    scale = [jnp.exp(m[:, 0:1] - top) for m in marks]
    total = sum(s * m[:, 1:2] for s, m in zip(scale, marks))
    rows = sum(s * got[e, :, 0:width] for e, s in enumerate(scale))
    lane = lane_of((16, LANES))
    tail = jnp.where(lane == piece, top, jnp.where(lane == piece + 1, total, 0.0))
    for c in range(2):
        s = slice(8 * c, 8 * c + 8)
        for k in range(wide):
            out[2 * k + c] = tail[s]
            out[2 * k + c, :, 0:piece] = rows[s, k * piece : (k + 1) * piece]


def hidden_parts(got, w_in, w_out, near_in, near_out, sent, keep, full):
    piece = 2 * w_in.shape[1]
    hidden = w_in.shape[2]
    core = core_index()
    tops = got[:, :, piece : piece + 1]
    top = jnp.max(tops, axis=0)
    rows = jnp.sum(jnp.exp(tops - top[None]) * got[...], axis=0)
    total = rows[:, piece + 1 : piece + 2]
    rows = jnp.where(row_of((8, LANES)) < 4, rows / total, rows)
    lane = lane_of((8, LANES))
    keep[...] = jnp.where(lane == piece, top, jnp.where(lane == piece + 1, total, rows))
    turned = jnp.transpose(rows)
    low, high = turned[0 : piece // 2], turned[piece // 2 : piece]
    own = jnp.where(core == 0, low, high)
    near = jnp.where(core == 0, high, low)
    step = 512
    for a in range(2):
        for kind, mine, theirs in ((0, w_in, near_in), (1, w_out, near_out)):
            for h in range(0, hidden, step):
                left = mine[2 * core + a, :, h : h + step]
                right = theirs[a, :, h : h + step]
                for p in range(2):
                    r = 4 * kind + 2 * a + p
                    part = left * own[:, r : r + 1] + right * near[:, r : r + 1]
                    full[r : r + 1, h : h + step] = jnp.sum(part, axis=0, keepdims=True)
    chips = sent.shape[0]
    share = hidden // chips
    for k in range(chips):
        sent[k, :, 0:share] = full[:, k * share : (k + 1) * share]
        sent[k, :, share:] = jnp.zeros((8, sent.shape[2] - share), F32)


def gate(got, out):
    z = jnp.sum(got[...], axis=0)
    other = swap(z)
    first = row_of(z.shape) < 4
    pre = jnp.where(first, z, other)
    grad = jnp.where(first, other, z)
    c = 0.7978845608028654
    t = jnp.tanh(c * (pre + 0.044715 * (pre * pre * pre)))
    act = 0.5 * pre * (1.0 + t)
    slope = 0.5 * (1.0 + t) + 0.5 * pre * (1.0 - t * t) * (c * (1.0 + 3 * 0.044715 * (pre * pre)))
    both = jnp.where(first, act, grad * slope)
    for k in range(out.shape[0]):
        out[k] = both


def slot_rows(got, keep, w_in, w_out, near_in, near_out, out, full):
    piece = 2 * w_in.shape[1]
    hidden = w_in.shape[2]
    chips = got.shape[0]
    share = hidden // chips
    core = core_index()
    for k in range(chips):
        full[:, k * share : (k + 1) * share] = got[k, :, 0:share]
    lane = lane_of((piece // 2, LANES))
    own = jnp.zeros((piece // 2, LANES), F32)
    near = own
    for a in range(2):
        for kind, mine, theirs in ((0, w_out, near_out), (1, w_in, near_in)):
            for p in range(2):
                r = 4 * kind + 2 * a + p
                line = full[r : r + 1, :]
                col = jnp.sum(mine[2 * core + a] * line, axis=1, keepdims=True)
                own = jnp.where(lane == r, col, own)
                col = jnp.sum(theirs[a] * line, axis=1, keepdims=True)
                near = jnp.where(lane == r, col, near)
    low = jnp.where(core == 0, own, near)
    high = jnp.where(core == 0, near, own)
    square = jnp.concatenate([low, high, jnp.zeros((LANES - piece, LANES), F32)], axis=0)
    rows = jnp.transpose(square)[0:8]
    held = swap(keep[...])
    lane = lane_of((8, LANES))
    column = jnp.sum(jnp.where(lane < piece, held * rows, 0.0), axis=1, keepdims=True)
    tile = jnp.where(lane < piece, rows, jnp.where(lane == piece + 2, column, held))
    for k in range(out.shape[0]):
        out[k] = tile


def join_widths(got, out, line):
    n = got.shape[0] // 2
    width = out.shape[2] - LANES
    piece = width // n
    lane = lane_of((8, LANES))
    for c in range(2):
        s = slice(8 * c, 8 * c + 8)
        for k in range(n):
            line[s, k * piece : (k + 1) * piece] = got[2 * k + c, :, 0:piece]
        added = sum(got[2 * k + c] for k in range(n))
        line[s, width:] = jnp.where(lane == piece + 2, added, got[c])
    for e in range(out.shape[0]):
        out[e] = line[...]


def logit_grads(got, blocks, keep, tops, out, mine):
    n = got.shape[0]
    width = got.shape[2] - LANES
    rows = width // n
    piece = width // 16
    x, g = token_blocks(blocks)
    left = got[:, :, 0:width].reshape(16 * n, width)
    both = contract(left, jnp.concatenate([x, g], axis=1), 1, 0).reshape(2 * n, 8, 2 * LANES)
    first = row_of((2 * n, 8, LANES)) < 4
    grads = jnp.where(first, both[:, :, LANES:], both[:, :, :LANES])
    marks = got[:, :, width:].reshape(2 * n, 8, LANES)
    top = marks[:, :, piece : piece + 1]
    total = marks[:, :, piece + 1 : piece + 2]
    column = marks[:, :, piece + 2 : piece + 3]
    held = keep[...]
    weights = jnp.where(first, held, held * (jnp.exp(tops[...] - top) / total))
    product = jnp.where(first, weights * grads, 0.0)
    line = jnp.sum(jnp.sum(product, axis=0), axis=0, keepdims=True)
    part = weights * (grads - jnp.where(first, line[None], column))
    part = part + swap(part)
    slots = 8 * n
    for e in range(n):
        for j in range(2 * n):
            out[e, 4 * j : 4 * j + 4] = part[j, 0:4]
            out[e, slots + 4 * j : slots + 4 * j + 4] = weights[j, 4:8]
    me = lax.axis_index(E)
    for e in range(n):

        @pl.when(me == e)
        def _():
            for j in range(2 * n):
                mine[4 * j : 4 * j + 4] = got[
                    j // 2, 8 * (j % 2) + 4 : 8 * (j % 2) + 8, e * rows : (e + 1) * rows
                ]


def router_part(got, tokens, mine, theirs):
    n = got.shape[0]
    slots = got.shape[1] // 2
    grads = jnp.concatenate([got[e, 0:slots] for e in range(n)], axis=1)
    part = contract(tokens[...], grads, 1, 1)
    q = part.shape[0] // 4
    low = jnp.concatenate([part[0:q], part[q : 2 * q]], axis=1)
    high = jnp.concatenate([part[2 * q : 3 * q], part[3 * q :]], axis=1)
    core = core_index()
    mine[...] = jnp.where(core == 0, low, high)
    theirs[...] = jnp.where(core == 0, high, low)


def token_grads(got, rows, router, out):
    left = jnp.concatenate([router[...], jnp.transpose(rows[...])], axis=1)
    for e in range(got.shape[0]):
        out[:, e * LANES : (e + 1) * LANES] = contract(left, got[e], 1, 0)


def add_copies(mine, theirs, out):
    both = mine[...] + theirs[...]
    for k in range(out.shape[0]):
        out[k] = both


def add_all(got, out):
    out[...] = jnp.sum(got[...], axis=0)


def unfold(mine, theirs, out):
    core = core_index()
    a, b = mine[...], theirs[...]
    low = jnp.where(core == 0, a, b)
    high = jnp.where(core == 0, b, a)
    q, h = out.shape[0] // 4, LANES // 2
    out[0:q] = low[:, :h]
    out[q : 2 * q] = low[:, h:]
    out[2 * q : 3 * q] = high[:, :h]
    out[3 * q :] = high[:, h:]


def weight_grads(full, near_full, keep, near_keep, grad_in, grad_out):
    w = grad_in.shape[1]
    hidden = grad_in.shape[2]
    core = core_index()
    step = 512
    for base, values, held in ((2 * core, full, keep), (2 - 2 * core, near_full, near_keep)):
        held = held[...]
        part = jnp.where(core == 0, held[:, 0:w], held[:, w : 2 * w])
        cols = jnp.transpose(part)
        for a in range(2):
            for h in range(0, hidden, step):
                s = slice(h, h + step)
                i, j = 2 * a, 2 * a + 1
                grad_out[base + a, :, s] = (
                    cols[:, 4 + i : 5 + i] * values[i : i + 1, s]
                    + cols[:, 4 + j : 5 + j] * values[j : j + 1, s]
                )
                grad_in[base + a, :, s] = (
                    cols[:, i : i + 1] * values[4 + i : 5 + i, s]
                    + cols[:, j : j + 1] * values[4 + j : 5 + j, s]
                )


def per_device(tokens, router, w_in, w_out, grad_out):
    n_seq, n_exp = lax.axis_size(S), lax.axis_size(E)
    experts, width_block, hidden = w_in.shape
    rows_block, local_tokens = tokens.shape
    slots = router.shape[1]
    own_slots = slots // n_exp
    width = rows_block * n_exp
    chips = n_seq // 2
    core = core_index()
    partner = [(i, i ^ 1) for i in range(n_seq)]
    groups = [[2 * k + c for k in range(chips)] for c in range(2)]

    def to_partner(values):
        return lax.ppermute(values, S, partner)

    packed = run(pack_tokens, (n_exp, rows_block * 5 // 2, LANES), tokens, grad_out, router)
    blocks = exchange(packed, E)
    half = experts // 2
    near_in = to_partner(lax.dynamic_slice_in_dim(w_in, half * (1 - core), half, 0))
    near_out = to_partner(lax.dynamic_slice_in_dim(w_out, half * (1 - core), half, 0))

    line = width + LANES
    groups8 = (slots // 4, 8, LANES)
    sent, keep, tops = run(
        softmax_rows, [(n_exp, 2 * own_slots, line), groups8, groups8], blocks
    )
    sent = run(merge_tokens, (n_seq, 8, LANES), exchange(sent, E))
    share = hidden // chips
    cut = -(-share // LANES) * LANES
    sent, held = run(
        hidden_parts,
        [(chips, 8, cut), (8, LANES)],
        exchange(sent, S),
        w_in,
        w_out,
        near_in,
        near_out,
        scratch=[(8, hidden)],
    )
    sent = run(gate, (chips, 8, cut), exchange(sent, S, groups))
    sent, full = run(
        slot_rows,
        [(n_seq, 8, LANES), (8, hidden)],
        exchange(sent, S, groups),
        held,
        w_in,
        w_out,
        near_in,
        near_out,
    )
    near_full = to_partner(full)
    near_held = to_partner(held)
    grad_w_in, grad_w_out = run(
        weight_grads, [w_in.shape, w_out.shape], full, near_full, held, near_held
    )
    sent = run(
        join_widths, (n_exp, 16, line), exchange(sent, S), scratch=[(16, line)]
    )
    sent, mine = run(
        logit_grads,
        [(n_exp, 2 * slots, LANES), (slots, rows_block)],
        exchange(sent, E),
        blocks,
        keep,
        tops,
    )
    spread = exchange(sent, E)
    fold = (rows_block // 4, 2 * slots)
    near, theirs = run(router_part, [fold, fold], spread, tokens)
    grad_tokens = run(token_grads, (rows_block, local_tokens), spread, mine, router)
    sent = run(add_copies, (chips,) + fold, near, to_partner(theirs))
    near = run(add_all, fold, exchange(sent, S, groups))
    grad_router = run(unfold, (rows_block, slots), near, to_partner(near))
    return (grad_tokens, grad_router, grad_w_in, grad_w_out)


def solution(mesh):
    placed = (
        P("expert", "seq"),
        P("expert", None),
        P("expert", "seq", None),
        P("expert", "seq", None),
        P("expert", "seq"),
    )
    return jax.shard_map(
        per_device,
        mesh=mesh,
        in_specs=placed,
        out_specs=(
            P("expert", "seq"),
            P("expert", None),
            P("expert", "seq", None),
            P("expert", "seq", None),
        ),
        check_vma=False,
    )
```

time: 999 us -> 186 us (0.19)
  waiting for transfers between devices: 571 us -> 42.9 us
  blocking collectives: 350 us -> 82.2 us
  matrix products: 38.1 us -> 0 us
  Pallas kernels: 0 us -> 16.6 us
  starting transfers between devices: 16.6 us -> 30.4 us
  between operations: 13.9 us -> 0.76 us
  local copies, waits for them, and re-layouts: 2.08 us -> 12.2 us
    psum x4 -> x0, waiting for transfers between devices: 560 us -> none  [the longest x1 205 us: per_device(): pre = lax.psum(pre_part, 'seq')]
    psum x3 -> x0, blocking collectives: 213 us -> none  [the longest x1 101 us: per_device(): grad_router = lax.psum(product(tokens, grad_logits), 'seq')]
    all_to_all x1 -> x6, blocking collectives: 13.1 us -> 82.2 us  [exchange(): lax.all_to_all(blocks, axis, 0, 0, axis_index_groups=groups, tiled=True)]
    all_gather x2 -> x0, blocking collectives: 65.9 us -> none  [from_owners(): widened = lax.all_gather(block, 'seq', axis=1, tiled=True)]
    pmax x1 -> x0, blocking collectives: 58.3 us -> none  [per_device(): column_top = lax.pmax(jnp.max(logits, axis=0), 'seq')]
    dot_general x14 -> x0, matrix products: 38.1 us -> none  [the longest x7 17.1 us: contract(): lax.dot_general(left, right, (((left_dim,), (right_dim,)), ((), ())), pre...]
    all_to_all x3, waiting for transfers between devices: 11.8 us -> 41 us  [exchange(): lax.all_to_all(blocks, axis, 0, 0, axis_index_groups=groups, tiled=True)]
    pallas_call x0 -> x14, Pallas kernels: none -> 16.6 us  [run(): pl.pallas_call(kernel, out_shape=[jax.ShapeDtypeStruct(s, F32) for s in s...]
  transfers between devices with their start and end apart: 7 -> 9, of which waited for: 6 -> 5; matrix products, arithmetic and copies ran while one was open for 2% -> 2% of each run, Pallas kernels for 0% -> 5%
where the time goes in v2:
time: 186 us; the launch traced here: 185 us
  blocking collectives  82.2 us (44%)
  waiting for transfers between devices  42.9 us (23%)
  starting transfers between devices  30.4 us (16%)
  Pallas kernels  16.6 us (9%)
  local copies, waits for them, and re-layouts  12.2 us (7%)
    all_to_all x6, blocking collectives, exchange(): lax.all_to_all(blocks, axis, 0, 0, axis_index_groups=groups, tiled=True)  82.2 us
    all_to_all x3, waiting for transfers between devices, exchange(): lax.all_to_all(blocks, axis, 0, 0, axis_index_groups=groups, tiled=True)  41 us
    all_to_all x3, starting transfers between devices, exchange(): lax.all_to_all(blocks, axis, 0, 0, axis_index_groups=groups, tiled=True)  22.1 us
    pallas_call x14, Pallas kernels, run(): pl.pallas_call(kernel, out_shape=[jax.ShapeDtypeStruct(s, F32) for s in s...  16.6 us
    unnamed x18, local copies, waits for them, and re-layouts  8.52 us
    ppermute x6, starting transfers between devices, to_partner(): return lax.ppermute(values, S, partner)  8.4 us
  transfers between devices with their start and end apart: 9, of which 5 were waited for; matrix products, arithmetic and copies ran while one was open for 2% of the time, Pallas kernels for 5%

profile of v2, /device:TPU:1, one launch (start us, length us, event | category | flops | bytes accessed | tf_op | source)
XLA Modules:
  0.0 185.0 jit_solution(1788985268032479732)
XLA Ops:
  0.6 0.9 copy.9.router
  1.6 1.1 copy-done.5
  2.7 1.1 copy-done.7
  4.0 1.3 copy-done.4
  5.3 7.5 %all-to-all-start = ((f32[8,480,128]{2,1,0:T(8,128)}), f32[8,480,128]{2,1,0:T(8,128)S(1)}, u32[]{:S(2)}, u32[]{:S(2)}) async-start(f32[8,480,128]{2,1,0:T(8,128)} %copy-done.4), calls=%async_computation | async-start | bytes 3932160 | tf_op jit(solution)/shard_map/all_to_all | solution.py:28
  12.8 2.5 %constant_dynamic-slice_fusion.1 = f32[2,48,3072]{2,1,0:T(8,128)} fusion(f32[4,48,3072]{2,1,0:T(8,128)} %w_in.3, s32[]{:T(128)S(6)} %select_n.12), kind=kLoop, calls=%fused_computation.1 | loop fusion | bytes 2359300 | tf_op jit(solution)/shard_map/dynamic_slice | solution.py:349
  15.3 1.0 collective-permute-start
  16.2 1.1 constant_dynamic-slice_fusion
  17.4 21.5 %all-to-all-done.got.blocks = f32[8,480,128]{2,1,0:T(8,128)S(1)} async-done(((f32[8,480,128]{2,1,0:T(8,128)}), f32[8,480,128]{2,1,0:T(8,128)S(1)}, u32[]{:S(2)}, u32[]{:S(2)}) %all-to-all-start) | async-done | bytes 1966112 | tf_op jit(solution)/shard_map/all_to_all | solution.py:28
  38.9 2.7 %shard_map.85 = (f32[8,16,1664]{2,1,0:T(8,128)S(1)}, f32[16,8,128]{2,1,0:T(8,128)S(1)}, f32[16,8,128]{2,1,0:T(8,128)S(1)}) custom-call(f32[8,480,128]{2,1,0:T(8,128)S(1)} %all-to-all-done.got.blocks), custom_call_target="tpu_custom_call" | custom-call | bytes 2949120 | tf_op jit(solution)/shard_map/pallas_call | solution.py:36
  41.6 17.7 %all_to_all.45.got = f32[8,16,1664]{2,1,0:T(8,128)S(1)} all-to-all(f32[8,16,1664]{2,1,0:T(8,128)S(1)} %get-tuple-element.17), channel_id=1, replica_groups=mesh['seq'=32,'expert'=8] {'expert'}, dimensions={0} | all-to-all | bytes 1703936 | tf_op jit(solution)/shard_map/all_to_all | solution.py:28
  59.3 0.9 shard_map.86
  60.2 10.7 %all-to-all-start.2 = ((f32[32,8,128]{2,1,0:T(8,128)}), f32[32,8,128]{2,1,0:T(8,128)S(1)}, u32[]{:S(2)}, u32[]{:S(2)}) async-start(f32[32,8,128]{2,1,0:T(8,128)} %shard_map.86), calls=%async_computation.2 | async-start | bytes 262144 | tf_op jit(solution)/shard_map/all_to_all | solution.py:28
  70.9 9.0 %all-to-all-done.2.got = f32[32,8,128]{2,1,0:T(8,128)S(1)} async-done(((f32[32,8,128]{2,1,0:T(8,128)}), f32[32,8,128]{2,1,0:T(8,128)S(1)}, u32[]{:S(2)}, u32[]{:S(2)}) %all-to-all-start.2) | async-done | bytes 131104 | tf_op jit(solution)/shard_map/all_to_all | solution.py:28
  80.0 1.7 copy-done
  81.6 1.7 copy-done.2
  83.3 2.7 %shard_map.87 = (f32[16,8,256]{2,1,0:T(8,128)S(1)}, f32[8,128]{1,0:T(8,128)S(1)}) custom-call(f32[32,8,128]{2,1,0:T(8,128)S(1)} %all-to-all-done.2.got, f32[4,48,3072]{2,1,0:T(8,128)S(1)} %copy-done, f32[4,48,3072]{2,1,0:T(8,128)S(1)} %copy-done.2, f32[2,48,3072]{2,1,0:T(8,128)S(1)} %collective-permute-done.near_in, ...), custom_call_target="tpu_custom_call" | custom-call | bytes 7344128 | tf_op jit(solution)/shard_map/pallas_call | solution.py:36
  86.0 10.1 %all_to_all.46.got = f32[16,8,256]{2,1,0:T(8,128)S(1)} all-to-all(f32[16,8,256]{2,1,0:T(8,128)S(1)} %get-tuple-element.18), channel_id=1, replica_groups={{0,16,32,48,64,80,96,112,128,144,160,176,192,208,224,240},{8,24,40,56,7..., dimensions={0} | all-to-all | bytes 262144 | tf_op jit(solution)/shard_map/all_to_all | solution.py:28
  96.1 10.5 %all_to_all.47.got = f32[16,8,256]{2,1,0:T(8,128)S(1)} all-to-all(f32[16,8,256]{2,1,0:T(8,128)S(1)} %shard_map.88), channel_id=1, replica_groups={{0,16,32,48,64,80,96,112,128,144,160,176,192,208,224,240},{8,24,40,56,7..., dimensions={0} | all-to-all | bytes 262144 | tf_op jit(solution)/shard_map/all_to_all | solution.py:28
  106.6 2.4 %shard_map.89 = (f32[32,8,128]{2,1,0:T(8,128)S(1)}, f32[8,3072]{1,0:T(8,128)S(1)}) custom-call(f32[16,8,256]{2,1,0:T(8,128)S(1)} %all_to_all.47.got, f32[8,128]{1,0:T(8,128)S(1)} %get-tuple-element.19.keep, f32[4,48,3072]{2,1,0:T(8,128)S(1)} %copy-done, f32[4,48,3072]{2,1,0:T(8,128)S(1)} %copy-done.3, f32[2,48,3072]{2,1,0:T(8,128)S(1)} %collective-permute-done.near_in, ...), custom_call_target="tpu_custom_call" | custom-call | bytes 7442432 | tf_op jit(solution)/shard_map/pallas_call | solution.py:36
  109.0 16.0 %all_to_all.48.got = f32[32,8,128]{2,1,0:T(8,128)S(1)} all-to-all(f32[32,8,128]{2,1,0:T(8,128)S(1)} %get-tuple-element.20), channel_id=1, replica_groups=mesh['seq'=32,'expert'=8] {'seq'}, dimensions={0} | all-to-all | bytes 262144 | tf_op jit(solution)/shard_map/all_to_all | solution.py:28
  125.2 16.0 %all_to_all.49.got = f32[8,16,1664]{2,1,0:T(8,128)S(1)} all-to-all(f32[8,16,1664]{2,1,0:T(8,128)S(1)} %shard_map.90), channel_id=1, replica_groups=mesh['seq'=32,'expert'=8] {'expert'}, dimensions={0} | all-to-all | bytes 1703936 | tf_op jit(solution)/shard_map/all_to_all | solution.py:28
  141.2 1.1 shard_map.91
  142.3 11.9 %all_to_all.50.got = f32[8,128,128]{2,1,0:T(8,128)S(1)} all-to-all(f32[8,128,128]{2,1,0:T(8,128)S(1)} %get-tuple-element.23), channel_id=1, replica_groups=mesh['seq'=32,'expert'=8] {'expert'}, dimensions={0} | all-to-all | bytes 1048576 | tf_op jit(solution)/shard_map/all_to_all | solution.py:28
  154.1 0.8 shard_map.93
  155.0 3.9 %collective-permute-start.2 = (f32[48,128]{1,0:T(8,128)S(1)}, f32[48,128]{1,0:T(8,128)S(1)}, u32[]{:S(2)}, u32[]{:S(2)}) collective-permute-start(f32[48,128]{1,0:T(8,128)S(1)} %get-tuple-element.26), channel_id=1, source_target_pairs={{0,8},{8,0},{16,24},{24,16},{32,40},{40,32},{48,56},{56,48},{64,72... | collective-permute-start | bytes 73736 | tf_op jit(solution)/shard_map/ppermute | solution.py:344
  160.5 3.8 %all-to-all-start.8 = ((f32[16,48,128]{2,1,0:T(8,128)}), f32[16,48,128]{2,1,0:T(8,128)S(1)}, u32[]{:S(2)}, u32[]{:S(2)}) async-start(f32[16,48,128]{2,1,0:T(8,128)} %shard_map.94), calls=%async_computation.8 | async-start | bytes 786432 | tf_op jit(solution)/shard_map/all_to_all | solution.py:28
  165.0 10.4 %all-to-all-done.8.got = f32[16,48,128]{2,1,0:T(8,128)S(1)} async-done(((f32[16,48,128]{2,1,0:T(8,128)}), f32[16,48,128]{2,1,0:T(8,128)S(1)}, u32[]{:S(2)}, u32[]{:S(2)}) %all-to-all-start.8) | async-done | bytes 393248 | tf_op jit(solution)/shard_map/all_to_all | solution.py:28
  175.5 2.8 %collective-permute-start.3 = (f32[48,128]{1,0:T(8,128)S(1)}, f32[48,128]{1,0:T(8,128)S(1)}, u32[]{:S(2)}, u32[]{:S(2)}) collective-permute-start(f32[48,128]{1,0:T(8,128)S(1)} %shard_map.95.mine), channel_id=1, source_target_pairs={{0,8},{8,0},{16,24},{24,16},{32,40},{40,32},{48,56},{56,48},{64,72... | collective-permute-start | bytes 73736 | tf_op jit(solution)/shard_map/ppermute | solution.py:344
  178.3 1.1 collective-permute-done.5.near_keep
  179.4 3.0 %shard_map.97 = (f32[4,48,3072]{2,1,0:T(8,128)}, f32[4,48,3072]{2,1,0:T(8,128)}) custom-call(f32[8,3072]{1,0:T(8,128)S(1)} %get-tuple-element.27.full, f32[8,3072]{1,0:T(8,128)S(1)} %collective-permute-done.4.near_full, f32[8,128]{1,0:T(8,128)S(1)} %get-tuple-element.19.keep, f32[8,128]{1,0:T(8,128)S(1)} %collective-permute-done.5.near_keep), custom_call_target="tpu_custom_call" | custom-call | bytes 4923392 | tf_op jit(solution)/shard_map/pallas_call | solution.py:36
  182.4 1.8 shard_map.92
  (26 shorter events, 3.6 us)
Async XLA Ops:
  1.6 1.1 copy-start.5
  2.7 1.1 copy-start.7
  4.0 1.3 copy-start.4
  5.3 33.6 %all-to-all-start = ((f32[8,480,128]{2,1,0:T(8,128)}), f32[8,480,128]{2,1,0:T(8,128)S(1)}, u32[]{:S(2)}, u32[]{:S(2)}) async-start(f32[8,480,128]{2,1,0:T(8,128)} %copy-done.4), calls=%async_computation | async-start | bytes 3932160 | tf_op jit(solution)/shard_map/all_to_all | solution.py:28
  12.8 3.5 %copy-start.1 = (f32[4,48,3072]{2,1,0:T(8,128)S(1)}, f32[4,48,3072]{2,1,0:T(8,128)}, u32[]{:S(2)}) copy-start(f32[4,48,3072]{2,1,0:T(8,128)} %w_out.3) | copy-start | bytes 7077892
  15.3 55.6 %collective-permute-start = (f32[2,48,3072]{2,1,0:T(8,128)}, f32[2,48,3072]{2,1,0:T(8,128)S(1)}, u32[]{:S(2)}, u32[]{:S(2)}) collective-permute-start(f32[2,48,3072]{2,1,0:T(8,128)} %constant_dynamic-slice_fusion.1), channel_id=1, source_target_pairs={{0,8},{8,0},{16,24},{24,16},{32,40},{40,32},{48,56},{56,48},{64,72... | collective-permute-start | bytes 3538952 | tf_op jit(solution)/shard_map/ppermute | solution.py:344
  17.4 53.6 %collective-permute-start.1 = (f32[2,48,3072]{2,1,0:T(8,128)}, f32[2,48,3072]{2,1,0:T(8,128)}, u32[]{:S(2)}, u32[]{:S(2)}) collective-permute-start(f32[2,48,3072]{2,1,0:T(8,128)} %constant_dynamic-slice_fusion), channel_id=1, source_target_pairs={{0,8},{8,0},{16,24},{24,16},{32,40},{40,32},{48,56},{56,48},{64,72... | collective-permute-start | bytes 3538952 | tf_op jit(solution)/shard_map/ppermute | solution.py:344
  60.2 19.8 %all-to-all-start.2 = ((f32[32,8,128]{2,1,0:T(8,128)}), f32[32,8,128]{2,1,0:T(8,128)S(1)}, u32[]{:S(2)}, u32[]{:S(2)}) async-start(f32[32,8,128]{2,1,0:T(8,128)} %shard_map.86), calls=%async_computation.2 | async-start | bytes 262144 | tf_op jit(solution)/shard_map/all_to_all | solution.py:28
  80.0 1.7 copy-start
  81.6 1.7 copy-start.2
  83.3 23.3 %copy-start.3 = (f32[4,48,3072]{2,1,0:T(8,128)S(1)}, f32[4,48,3072]{2,1,0:T(8,128)}, u32[]{:S(2)}) copy-start(f32[4,48,3072]{2,1,0:T(8,128)} %w_out.3) | copy-start | bytes 7077892
  141.2 13.0 %copy-start.6 = (f32[192,1024]{1,0:T(8,128)S(1)}, f32[192,1024]{1,0:T(8,128)}, u32[]{:S(2)}) copy-start(f32[192,1024]{1,0:T(8,128)} %tokens.3) | copy-start | bytes 2359300
  155.0 4.7 %collective-permute-start.2 = (f32[48,128]{1,0:T(8,128)S(1)}, f32[48,128]{1,0:T(8,128)S(1)}, u32[]{:S(2)}, u32[]{:S(2)}) collective-permute-start(f32[48,128]{1,0:T(8,128)S(1)} %get-tuple-element.26), channel_id=1, source_target_pairs={{0,8},{8,0},{16,24},{24,16},{32,40},{40,32},{48,56},{56,48},{64,72... | collective-permute-start | bytes 73736 | tf_op jit(solution)/shard_map/ppermute | solution.py:344
  160.5 15.0 %all-to-all-start.8 = ((f32[16,48,128]{2,1,0:T(8,128)}), f32[16,48,128]{2,1,0:T(8,128)S(1)}, u32[]{:S(2)}, u32[]{:S(2)}) async-start(f32[16,48,128]{2,1,0:T(8,128)} %shard_map.94), calls=%async_computation.8 | async-start | bytes 786432 | tf_op jit(solution)/shard_map/all_to_all | solution.py:28
  164.3 15.1 %collective-permute-start.4 = (f32[8,3072]{1,0:T(8,128)S(1)}, f32[8,3072]{1,0:T(8,128)S(1)}, u32[]{:S(2)}, u32[]{:S(2)}) collective-permute-start(f32[8,3072]{1,0:T(8,128)S(1)} %get-tuple-element.27.full), channel_id=1, source_target_pairs={{0,8},{8,0},{16,24},{24,16},{32,40},{40,32},{48,56},{56,48},{64,72... | collective-permute-start | bytes 294920 | tf_op jit(solution)/shard_map/ppermute | solution.py:344
  175.5 8.7 %collective-permute-start.3 = (f32[48,128]{1,0:T(8,128)S(1)}, f32[48,128]{1,0:T(8,128)S(1)}, u32[]{:S(2)}, u32[]{:S(2)}) collective-permute-start(f32[48,128]{1,0:T(8,128)S(1)} %shard_map.95.mine), channel_id=1, source_target_pairs={{0,8},{8,0},{16,24},{24,16},{32,40},{40,32},{48,56},{56,48},{64,72... | collective-permute-start | bytes 73736 | tf_op jit(solution)/shard_map/ppermute | solution.py:344
  178.2 1.2 collective-permute-start.5

commit v3 on v2

v3 whole, which is shorter than its diff:
```python
import functools

import jax
import jax.numpy as jnp
from jax import lax
from jax.experimental import pallas as pl
from jax.experimental.pallas import tpu as pltpu
from jax.sharding import PartitionSpec as P

HIGH = lax.Precision.HIGHEST
S = "seq"
E = "expert"
LANES = 128
F32 = jnp.float32


def contract(left, right, left_dim, right_dim, precision=HIGH):
    return lax.dot_general(
        left,
        right,
        (((left_dim,), (right_dim,)), ((), ())),
        precision=precision,
        preferred_element_type=F32,
    )


def exchange(blocks, axis, groups=None):
    return lax.all_to_all(blocks, axis, 0, 0, axis_index_groups=groups, tiled=True)


def run(kernel, shapes, *values, scratch=(), flops=0):
    single = not isinstance(shapes, list)
    shapes = [shapes] if single else shapes
    size = 4 * sum(v.size for v in values) + 4 * sum(functools.reduce(lambda a, b: a * b, s) for s in shapes)
    spec = pl.BlockSpec(memory_space=pltpu.VMEM)
    out = pl.pallas_call(
        kernel,
        out_shape=[jax.ShapeDtypeStruct(s, F32) for s in shapes],
        in_specs=[spec] * len(values),
        out_specs=[spec] * len(shapes),
        scratch_shapes=[pltpu.VMEM(s, F32) for s in scratch],
        compiler_params=pltpu.CompilerParams(vmem_limit_bytes=40 * 1024 * 1024),
        cost_estimate=pl.CostEstimate(flops=flops, bytes_accessed=size, transcendentals=0),
    )(*values)
    return out[0] if single else out


def row_of(shape):
    return lax.broadcasted_iota(jnp.int32, shape, len(shape) - 2) % 8


def lane_of(shape):
    return lax.broadcasted_iota(jnp.int32, shape, len(shape) - 1)


def swap(values):
    return jnp.concatenate([values[..., 4:8, :], values[..., 0:4, :]], axis=-2)


def core_index():
    return lax.axis_index(S) % 2


def pack_tokens(tokens, grad_out, router, out, held, logits, load, moves, stores):
    n, rows = out.shape[0], tokens.shape[0]
    first = pltpu.make_async_copy(tokens, held, load)
    first.start()
    copies = []
    for e in range(n):
        s = pl.ds(e * LANES, LANES)
        for i, values in enumerate((tokens, grad_out)):
            copy = pltpu.make_async_copy(
                values.at[:, s], out.at[e, pl.ds(i * rows, rows)], moves.at[2 * e + i]
            )
            copy.start()
            copies.append(copy)
    first.wait()
    part = contract(router[...], held[...], 1, 0)
    for e in range(n):
        logits[e] = part[:, e * LANES : (e + 1) * LANES]
        copy = pltpu.make_async_copy(
            logits.at[e], out.at[e, pl.ds(2 * rows, logits.shape[1])], stores.at[e]
        )
        copy.start()
        copies.append(copy)
    for copy in copies:
        copy.wait()


def token_blocks(got):
    n, rows = got.shape[0], got.shape[1] * 3 // 7
    x = got[:, 0:rows].reshape(n * rows, LANES)
    g = got[:, rows : 2 * rows].reshape(n * rows, LANES)
    return x, g


def softmax_rows(got, mine, near, keep, tops, both):
    n, rows = got.shape[0], got.shape[1] * 3 // 7
    width = n * rows
    logits = sum(got[e, 2 * rows :] for e in range(n))
    slots = logits.shape[0]
    raised = jnp.exp(logits - jnp.max(logits, axis=0, keepdims=True))
    combine = raised / jnp.sum(raised, axis=0, keepdims=True)
    top = jnp.max(logits, axis=1, keepdims=True)
    raised = jnp.exp(logits - top)
    total = jnp.sum(raised, axis=1, keepdims=True)
    x, g = token_blocks(got)
    rows_in = contract(raised, x, 1, 1)
    rows_out = contract(combine, g, 1, 1)
    lane = lane_of((slots, LANES))
    marks = jnp.where(lane == 0, top, jnp.where(lane == 1, total, 0.0))
    plain = jnp.where(lane_of((4, LANES)) == 1, 1.0, 0.0)
    wide_top = jnp.broadcast_to(top, (slots, LANES))
    for e in range(n):
        for c in range(2):
            s, j = slice(8 * e + 4 * c, 8 * e + 4 * c + 4), n * c + e
            both[c, e, 0:4, 0:width] = rows_in[s]
            both[c, e, 4:8, 0:width] = rows_out[s]
            both[c, e, 0:4, width:] = marks[s]
            both[c, e, 4:8, width:] = plain
            keep[j, 0:4] = combine[s]
            keep[j, 4:8] = raised[s]
            tops[j, 0:4] = wide_top[s]
            tops[j, 4:8] = wide_top[s]
    core = core_index()
    mine[...] = both[core]
    near[...] = both[1 - core]


def merge(parts, width):
    marks = [p[:, width : width + LANES] for p in parts]
    top = functools.reduce(jnp.maximum, [m[:, 0:1] for m in marks])
    scale = [jnp.exp(m[:, 0:1] - top) for m in marks]
    rows = sum(s * p[:, 0:width] for s, p in zip(scale, parts))
    total = sum(s * m[:, 1:2] for s, m in zip(scale, marks))
    return rows, top, total


def merge_cores(mine, near, out):
    width = out.shape[2] - LANES
    lane = lane_of((8, LANES))
    for e in range(out.shape[0]):
        rows, top, total = merge([mine[e], near[e]], width)
        out[e, :, 0:width] = rows
        out[e, :, width:] = jnp.where(lane == 0, top, jnp.where(lane == 1, total, 0.0))


def merge_tokens(got, out):
    n, width = got.shape[0], got.shape[2] - LANES
    wide = out.shape[0]
    piece = width // wide
    rows, top, total = merge([got[e] for e in range(n)], width)
    lane = lane_of((8, LANES))
    tail = jnp.where(lane == piece, top, jnp.where(lane == piece + 1, total, 0.0))
    for k in range(wide):
        out[k] = tail
        out[k, :, 0:piece] = rows[:, k * piece : (k + 1) * piece]


def hidden_parts(got, own_in, own_out, near_in, near_out, sent, keep, full):
    w = own_in.shape[1]
    piece = 2 * w
    hidden = own_in.shape[2]
    core = core_index()
    tops = got[:, :, piece : piece + 1]
    top = jnp.max(tops, axis=0)
    rows = jnp.sum(jnp.exp(tops - top[None]) * got[...], axis=0)
    total = rows[:, piece + 1 : piece + 2]
    rows = jnp.where(row_of((8, LANES)) < 4, rows / total, rows)
    lane = lane_of((8, LANES))
    keep[...] = jnp.where(lane == piece, top, jnp.where(lane == piece + 1, total, rows))
    turned = jnp.transpose(rows)
    low, high = turned[0:w], turned[w:piece]
    own = jnp.where(core == 0, low, high)
    near = jnp.where(core == 0, high, low)
    for a in range(2):
        for kind, mine, theirs in ((0, own_in, near_in), (1, own_out, near_out)):
            r = 4 * kind + 2 * a
            values = [
                jnp.concatenate(
                    [
                        jnp.broadcast_to(own[:, r + p : r + p + 1], (w, LANES)),
                        jnp.broadcast_to(near[:, r + p : r + p + 1], (w, LANES)),
                    ],
                    axis=0,
                )
                for p in range(2)
            ]
            for h in range(0, hidden, LANES):
                s = slice(h, h + LANES)
                block = jnp.concatenate([mine[a, :, s], theirs[a, :, s]], axis=0)
                for p in range(2):
                    full[r + p : r + p + 1, s] = jnp.sum(block * values[p], axis=0, keepdims=True)
    chips = sent.shape[0]
    share = hidden // chips
    for k in range(chips):
        sent[k, :, 0:share] = full[:, k * share : (k + 1) * share]
        sent[k, :, share:] = jnp.zeros((8, sent.shape[2] - share), F32)


def gate(got, out):
    z = jnp.sum(got[...], axis=0)
    other = swap(z)
    first = row_of(z.shape) < 4
    pre = jnp.where(first, z, other)
    grad = jnp.where(first, other, z)
    c = 0.7978845608028654
    t = jnp.tanh(c * (pre + 0.044715 * (pre * pre * pre)))
    act = 0.5 * pre * (1.0 + t)
    slope = 0.5 * (1.0 + t) + 0.5 * pre * (1.0 - t * t) * (c * (1.0 + 3 * 0.044715 * (pre * pre)))
    both = jnp.where(first, act, grad * slope)
    for k in range(out.shape[0]):
        out[k] = both


def slot_rows(got, keep, own_in, own_out, near_in, near_out, out, full):
    w = own_in.shape[1]
    piece = 2 * w
    hidden = own_in.shape[2]
    chips = got.shape[0]
    share = hidden // chips
    core = core_index()
    for k in range(chips):
        full[:, k * share : (k + 1) * share] = got[k, :, 0:share]
    lane = lane_of((piece, LANES))
    cols = jnp.zeros((piece, LANES), F32)
    for a in range(2):
        for kind, mine, theirs in ((0, own_out, near_out), (1, own_in, near_in)):
            r = 4 * kind + 2 * a
            sums = [jnp.zeros((piece, LANES), F32) for _ in range(2)]
            for h in range(0, hidden, LANES):
                s = slice(h, h + LANES)
                block = jnp.concatenate([mine[a, :, s], theirs[a, :, s]], axis=0)
                for p in range(2):
                    sums[p] = sums[p] + block * full[r + p : r + p + 1, s]
            for p in range(2):
                cols = jnp.where(lane == r + p, jnp.sum(sums[p], axis=1, keepdims=True), cols)
    own, near = cols[0:w], cols[w:]
    low = jnp.where(core == 0, own, near)
    high = jnp.where(core == 0, near, own)
    square = jnp.concatenate([low, high, jnp.zeros((LANES - piece, LANES), F32)], axis=0)
    rows = jnp.transpose(square)[0:8]
    held = swap(keep[...])
    lane = lane_of((8, LANES))
    column = jnp.sum(jnp.where(lane < piece, held * rows, 0.0), axis=1, keepdims=True)
    tile = jnp.where(lane < piece, rows, jnp.where(lane == piece + 2, column, held))
    for k in range(out.shape[0]):
        out[k] = tile


def join_widths(got, out, line):
    n = got.shape[0]
    width = out.shape[2] - LANES
    piece = width // n
    lane = lane_of((8, LANES))
    for k in range(n):
        line[:, k * piece : (k + 1) * piece] = got[k, :, 0:piece]
    added = sum(got[k] for k in range(n))
    line[:, width:] = jnp.where(lane == piece + 2, added, got[0])
    for e in range(out.shape[0]):
        out[e] = line[...]


def row_products(got, blocks, out):
    n = got.shape[0]
    width = got.shape[2] - LANES
    x, g = token_blocks(blocks)
    left = got[:, :, 0:width].reshape(8 * n, width)
    both = contract(left, jnp.concatenate([x, g], axis=1), 1, 0)
    out[...] = both.reshape(n, 8, 2 * LANES)


def logit_grads(near, blocks, got, done, keep, tops, out, mine, line):
    n = got.shape[0]
    width = got.shape[2] - LANES
    rows = width // n
    piece = width // 16
    core = core_index()
    x, g = token_blocks(blocks)
    left = near[:, :, 0:width].reshape(8 * n, width)
    other = contract(left, jnp.concatenate([x, g], axis=1), 1, 0).reshape(n, 8, 2 * LANES)

    def order(own, theirs):
        low = jnp.where(core == 0, own, theirs)
        high = jnp.where(core == 0, theirs, own)
        return jnp.concatenate([low, high], axis=0)

    both = order(done[...], other)
    marks = order(got[:, :, width:], near[:, :, width:])
    first = row_of((2 * n, 8, LANES)) < 4
    grads = jnp.where(first, both[:, :, LANES:], both[:, :, :LANES])
    top = marks[:, :, piece : piece + 1]
    total = marks[:, :, piece + 1 : piece + 2]
    column = marks[:, :, piece + 2 : piece + 3]
    held = keep[...]
    weights = jnp.where(first, held, held * (jnp.exp(tops[...] - top) / total))
    product = jnp.where(first, weights * grads, 0.0)
    sums = jnp.sum(jnp.sum(product, axis=0), axis=0, keepdims=True)
    part = weights * (grads - jnp.where(first, sums[None], column))
    part = part + swap(part)
    slots = 8 * n
    for c in range(2):
        for e in range(n):
            i, j = 8 * e + 4 * c, n * c + e
            line[i : i + 4] = part[j, 0:4]
            line[slots + i : slots + i + 4] = weights[j, 4:8]
    for e in range(n):
        out[e] = line[...]
    me = lax.axis_index(E)
    for b in range(n):

        @pl.when(me == b)
        def _():
            s = slice(b * rows, (b + 1) * rows)
            for c in range(2):
                for e in range(n):
                    i = 8 * e + 4 * c
                    mine[i : i + 4] = jnp.where(core == c, got[e, 4:8, s], near[e, 4:8, s])


def router_part(got, tokens, mine, theirs):
    n = got.shape[0]
    slots = got.shape[1] // 2
    grads = jnp.concatenate([got[e, 0:slots] for e in range(n)], axis=1)
    part = contract(tokens[...], grads, 1, 1)
    q = part.shape[0] // 4
    low = jnp.concatenate([part[0:q], part[q : 2 * q]], axis=1)
    high = jnp.concatenate([part[2 * q : 3 * q], part[3 * q :]], axis=1)
    core = core_index()
    mine[...] = jnp.where(core == 0, low, high)
    theirs[...] = jnp.where(core == 0, high, low)


def token_grads(got, rows, router, out):
    left = jnp.transpose(jnp.concatenate([router[...], rows[...]], axis=0))
    for e in range(got.shape[0]):
        out[:, e * LANES : (e + 1) * LANES] = contract(left, got[e], 1, 0)


def add_copies(mine, theirs, out):
    both = mine[...] + theirs[...]
    for k in range(out.shape[0]):
        out[k] = both


def add_all(got, out):
    out[...] = jnp.sum(got[...], axis=0)


def unfold(mine, theirs, out):
    core = core_index()
    a, b = mine[...], theirs[...]
    q, h = out.shape[1] // 4, LANES // 2
    for i, values in enumerate((jnp.where(core == 0, a, b), jnp.where(core == 0, b, a))):
        turned = jnp.transpose(values)
        out[:, 2 * i * q : (2 * i + 1) * q] = turned[:h]
        out[:, (2 * i + 1) * q : (2 * i + 2) * q] = turned[h:]


def weight_grads(full, near_full, keep, near_keep, grad_in, grad_out):
    w = grad_in.shape[1]
    hidden = grad_in.shape[2]
    core = core_index()
    step = 512
    for base, values, held in ((2 * core, full, keep), (2 - 2 * core, near_full, near_keep)):
        held = held[...]
        part = jnp.where(core == 0, held[:, 0:w], held[:, w : 2 * w])
        cols = jnp.transpose(part)
        for a in range(2):
            for h in range(0, hidden, step):
                s = slice(h, h + step)
                i, j = 2 * a, 2 * a + 1
                grad_out[base + a, :, s] = (
                    cols[:, 4 + i : 5 + i] * values[i : i + 1, s]
                    + cols[:, 4 + j : 5 + j] * values[j : j + 1, s]
                )
                grad_in[base + a, :, s] = (
                    cols[:, i : i + 1] * values[4 + i : 5 + i, s]
                    + cols[:, j : j + 1] * values[4 + j : 5 + j, s]
                )


def per_device(tokens, router, w_in, w_out, grad_out):
    n_seq, n_exp = lax.axis_size(S), lax.axis_size(E)
    experts, width_block, hidden = w_in.shape
    rows_block, local_tokens = tokens.shape
    slots = router.shape[1]
    width = rows_block * n_exp
    chips = n_seq // 2
    core = core_index()
    partner = [(i, i ^ 1) for i in range(n_seq)]
    groups = [[2 * k + c for k in range(chips)] for c in range(2)]
    turned = router.T

    def to_partner(values):
        return lax.ppermute(values, S, partner)

    any_spec = pl.BlockSpec(memory_space=pl.ANY)
    packed = pl.pallas_call(
        pack_tokens,
        out_shape=jax.ShapeDtypeStruct((n_exp, 2 * rows_block + slots, LANES), F32),
        in_specs=[any_spec, any_spec, pl.BlockSpec(memory_space=pltpu.VMEM)],
        out_specs=any_spec,
        scratch_shapes=[
            pltpu.VMEM(tokens.shape, F32),
            pltpu.VMEM((n_exp, slots, LANES), F32),
            pltpu.SemaphoreType.DMA,
            pltpu.SemaphoreType.DMA((2 * n_exp,)),
            pltpu.SemaphoreType.DMA((n_exp,)),
        ],
        compiler_params=pltpu.CompilerParams(vmem_limit_bytes=40 * 1024 * 1024),
    )(tokens, grad_out, turned)
    blocks = exchange(packed, E)
    half = experts // 2

    def split(w):
        own = lax.dynamic_slice_in_dim(w, half * core, half, 0)
        return own, to_partner(lax.dynamic_slice_in_dim(w, half * (1 - core), half, 0))

    own_in, near_in = split(w_in)
    own_out, near_out = split(w_out)
    blocks, own_in, own_out, near_in, near_out = lax.optimization_barrier(
        (blocks, own_in, own_out, near_in, near_out)
    )
    weights = (own_in, own_out, near_in, near_out)

    line = width + LANES
    groups8 = (slots // 4, 8, LANES)
    part = (n_exp, 8, line)
    mine, near, keep, tops = run(
        softmax_rows, [part, part, groups8, groups8], blocks, scratch=[(2,) + part]
    )
    sent = run(merge_cores, part, mine, to_partner(near))
    sent = run(merge_tokens, (chips, 8, LANES), exchange(sent, E))
    share = hidden // chips
    cut = -(-share // LANES) * LANES
    sent, held = run(
        hidden_parts,
        [(chips, 8, cut), (8, LANES)],
        exchange(sent, S, groups),
        *weights,
        scratch=[(8, hidden)],
    )
    sent = run(gate, (chips, 8, cut), exchange(sent, S, groups))
    sent, full = run(
        slot_rows, [(chips, 8, LANES), (8, hidden)], exchange(sent, S, groups), held, *weights
    )
    near_full = to_partner(full)
    near_held = to_partner(held)
    sent = run(join_widths, part, exchange(sent, S, groups), scratch=[(8, line)])
    got = exchange(sent, E)
    near = to_partner(got)
    done = run(row_products, (n_exp, 8, 2 * LANES), got, blocks)
    sent, mine = run(
        logit_grads,
        [(n_exp, 2 * slots, LANES), (slots, rows_block)],
        near,
        blocks,
        got,
        done,
        keep,
        tops,
        scratch=[(2 * slots, LANES)],
    )
    spread = exchange(sent, E)
    fold = (rows_block // 4, 2 * slots)
    near, theirs = run(router_part, [fold, fold], spread, tokens)
    sent = run(add_copies, (chips,) + fold, near, to_partner(theirs))
    sent, spread, full, near_full, near_held = lax.optimization_barrier(
        (sent, spread, full, near_full, near_held)
    )
    got = exchange(sent, S, groups)
    grad_w_in, grad_w_out = run(
        weight_grads, [w_in.shape, w_out.shape], full, near_full, held, near_held
    )
    grad_tokens = run(token_grads, (rows_block, local_tokens), spread, mine, turned)
    got, grad_w_in, grad_w_out, grad_tokens = lax.optimization_barrier(
        (got, grad_w_in, grad_w_out, grad_tokens)
    )
    near = run(add_all, fold, got)
    grad_router = run(unfold, (slots, rows_block), near, to_partner(near)).T
    return (grad_tokens, grad_router, grad_w_in, grad_w_out)


def solution(mesh):
    placed = (
        P("expert", "seq"),
        P("expert", None),
        P("expert", "seq", None),
        P("expert", "seq", None),
        P("expert", "seq"),
    )
    return jax.shard_map(
        per_device,
        mesh=mesh,
        in_specs=placed,
        out_specs=(
            P("expert", "seq"),
            P("expert", None),
            P("expert", "seq", None),
            P("expert", "seq", None),
        ),
        check_vma=False,
    )
```

time: 186 us -> 167 us (0.90)
  blocking collectives: 82.2 us -> 70.7 us
  waiting for transfers between devices: 42.9 us -> 38.5 us
  local copies, waits for them, and re-layouts: 12.2 us -> 9.57 us
    all_to_all x6, blocking collectives: 82.2 us -> 70.7 us  [exchange(): lax.all_to_all(blocks, axis, 0, 0, axis_index_groups=groups, tiled=True)]
    all_to_all x3, waiting for transfers between devices: 41 us -> 33.5 us  [exchange(): lax.all_to_all(blocks, axis, 0, 0, axis_index_groups=groups, tiled=True)]
    ppermute x6 -> x8, starting transfers between devices: 8.4 us -> 15.8 us  [to_partner(): return lax.ppermute(values, S, partner)]
    all_to_all x3, starting transfers between devices: 22.1 us -> 14.7 us  [exchange(): lax.all_to_all(blocks, axis, 0, 0, axis_index_groups=groups, tiled=True)]
    ppermute x6 -> x8, waiting for transfers between devices: 1.93 us -> 4.97 us  [to_partner(): return lax.ppermute(values, S, partner)]
    unnamed x18 -> x24, local copies, waits for them, and re-layouts: 8.52 us -> 6.41 us
    pallas_call x14 -> x15, Pallas kernels: 16.6 us -> 15 us  [run(): pl.pallas_call(kernel, out_shape=[jax.ShapeDtypeStruct(s, F32) for s in s...]
  transfers between devices with their start and end apart: 9 -> 11, of which waited for: 5 -> 9; matrix products, arithmetic and copies ran while one was open for 2% -> 2% of each run, Pallas kernels for 5% -> 4%
where the time goes in v3:
time: 167 us; the launch traced here: 166 us
  blocking collectives  70.7 us (42%)
  waiting for transfers between devices  38.5 us (23%)
  starting transfers between devices  30.5 us (18%)
  Pallas kernels  16.5 us (10%)
  local copies, waits for them, and re-layouts  9.57 us (6%)
    all_to_all x6, blocking collectives, exchange(): lax.all_to_all(blocks, axis, 0, 0, axis_index_groups=groups, tiled=True)  70.7 us
    all_to_all x3, waiting for transfers between devices, exchange(): lax.all_to_all(blocks, axis, 0, 0, axis_index_groups=groups, tiled=True)  33.5 us
    ppermute x8, starting transfers between devices, to_partner(): return lax.ppermute(values, S, partner)  15.8 us
    pallas_call x15, Pallas kernels, run(): pl.pallas_call(kernel, out_shape=[jax.ShapeDtypeStruct(s, F32) for s in s...  15 us
    all_to_all x3, starting transfers between devices, exchange(): lax.all_to_all(blocks, axis, 0, 0, axis_index_groups=groups, tiled=True)  14.7 us
    unnamed x24, local copies, waits for them, and re-layouts  6.41 us
    ppermute x8, waiting for transfers between devices, to_partner(): return lax.ppermute(values, S, partner)  4.97 us
  transfers between devices with their start and end apart: 11, of which 9 were waited for; matrix products, arithmetic and copies ran while one was open for 2% of the time, Pallas kernels for 4%

profile of v3, /device:TPU:1, one launch (start us, length us, event | category | flops | bytes accessed | tf_op | source)
XLA Modules:
  0.0 166.5 jit_solution(2472071617712623501)
XLA Ops:
  0.6 1.1 copy-done.6
  1.8 1.1 copy-done.8
  3.7 1.4 shard_map.84
  5.2 1.2 copy-done.1
  6.4 7.5 %all-to-all-start = ((f32[8,448,128]{2,1,0:T(8,128)}), f32[8,448,128]{2,1,0:T(8,128)S(1)}, u32[]{:S(2)}, u32[]{:S(2)}) async-start(f32[8,448,128]{2,1,0:T(8,128)} %copy-done.1), calls=%async_computation | async-start | bytes 3670016 | tf_op jit(solution)/shard_map/all_to_all | solution.py:28
  13.9 1.9 %constant_dynamic-slice_fusion.1 = (f32[2,48,3072]{2,1,0:T(8,128)S(1)}, f32[2,48,3072]{2,1,0:T(8,128)S(1)}) fusion(f32[4,48,3072]{2,1,0:T(8,128)} %param.7, s32[]{:T(128)S(6)} %select_n.17, s32[]{:T(128)S(6)} %select_n.16), kind=kLoop, calls=%fused_computation.1 | loop fusion | bytes 4718600 | tf_op jit(solution)/shard_map/dynamic_slice | solution.py:418
  15.9 1.0 collective-permute-start
  16.9 1.2 constant_dynamic-slice_fusion
  19.4 1.0 copy-done.2
  21.1 1.0 copy-done.4
  22.1 16.5 %all-to-all-done.got.blocks = f32[8,448,128]{2,1,0:T(8,128)S(1)} async-done(((f32[8,448,128]{2,1,0:T(8,128)}), f32[8,448,128]{2,1,0:T(8,128)S(1)}, u32[]{:S(2)}, u32[]{:S(2)}) %all-to-all-start) | async-done | bytes 1835040 | tf_op jit(solution)/shard_map/all_to_all | solution.py:28
  38.6 1.9 %shard_map.85 = (f32[8,8,1664]{2,1,0:T(8,128)S(1)}, f32[8,8,1664]{2,1,0:T(8,128)S(1)}, f32[16,8,128]{2,1,0:T(8,128)S(1)}, f32[16,8,128]{2,1,0:T(8,128)S(1)}) custom-call(f32[8,448,128]{2,1,0:T(8,128)S(1)} %all-to-all-done.got.blocks), custom_call_target="tpu_custom_call" | custom-call | bytes 2818048 | tf_op jit(solution)/shard_map/pallas_call | solution.py:36
  40.6 2.0 %collective-permute-start.2 = (f32[8,8,1664]{2,1,0:T(8,128)S(1)}, f32[8,8,1664]{2,1,0:T(8,128)S(1)}, u32[]{:S(2)}, u32[]{:S(2)}) collective-permute-start(f32[8,8,1664]{2,1,0:T(8,128)S(1)} %get-tuple-element.34), channel_id=1, source_target_pairs={{0,8},{8,0},{16,24},{24,16},{32,40},{40,32},{48,56},{56,48},{64,72... | collective-permute-start | bytes 1277960 | tf_op jit(solution)/shard_map/ppermute | solution.py:396
  42.6 1.4 collective-permute-done.2.near
  44.1 12.7 %all_to_all.45.got = f32[8,8,1664]{2,1,0:T(8,128)S(1)} all-to-all(f32[8,8,1664]{2,1,0:T(8,128)S(1)} %shard_map.86), channel_id=1, replica_groups=mesh['seq'=32,'expert'=8] {'expert'}, dimensions={0} | all-to-all | bytes 851968 | tf_op jit(solution)/shard_map/all_to_all | solution.py:28
  57.0 15.5 %all_to_all.46.got = f32[16,8,128]{2,1,0:T(8,128)S(1)} all-to-all(f32[16,8,128]{2,1,0:T(8,128)S(1)} %shard_map.87), channel_id=1, replica_groups={{0,16,32,48,64,80,96,112,128,144,160,176,192,208,224,240},{8,24,40,56,7..., dimensions={0} | all-to-all | bytes 131072 | tf_op jit(solution)/shard_map/all_to_all | solution.py:28
  72.5 1.3 shard_map.88
  73.8 10.0 %all_to_all.47.got = f32[16,8,256]{2,1,0:T(8,128)S(1)} all-to-all(f32[16,8,256]{2,1,0:T(8,128)S(1)} %get-tuple-element.39), channel_id=1, replica_groups={{0,16,32,48,64,80,96,112,128,144,160,176,192,208,224,240},{8,24,40,56,7..., dimensions={0} | all-to-all | bytes 262144 | tf_op jit(solution)/shard_map/all_to_all | solution.py:28
  83.9 10.5 %all_to_all.48.got = f32[16,8,256]{2,1,0:T(8,128)S(1)} all-to-all(f32[16,8,256]{2,1,0:T(8,128)S(1)} %shard_map.89), channel_id=1, replica_groups={{0,16,32,48,64,80,96,112,128,144,160,176,192,208,224,240},{8,24,40,56,7..., dimensions={0} | all-to-all | bytes 262144 | tf_op jit(solution)/shard_map/all_to_all | solution.py:28
  94.4 1.2 shard_map.90
  95.6 10.4 %all_to_all.49.got = f32[16,8,128]{2,1,0:T(8,128)S(1)} all-to-all(f32[16,8,128]{2,1,0:T(8,128)S(1)} %get-tuple-element.41), channel_id=1, replica_groups={{0,16,32,48,64,80,96,112,128,144,160,176,192,208,224,240},{8,24,40,56,7..., dimensions={0} | all-to-all | bytes 131072 | tf_op jit(solution)/shard_map/all_to_all | solution.py:28
  106.1 11.6 %all_to_all.50.got = f32[8,8,1664]{2,1,0:T(8,128)S(1)} all-to-all(f32[8,8,1664]{2,1,0:T(8,128)S(1)} %shard_map.91), channel_id=1, replica_groups=mesh['seq'=32,'expert'=8] {'expert'}, dimensions={0} | all-to-all | bytes 851968 | tf_op jit(solution)/shard_map/all_to_all | solution.py:28
  117.7 7.4 %collective-permute-start.3 = (f32[8,8,1664]{2,1,0:T(8,128)S(1)}, f32[8,8,1664]{2,1,0:T(8,128)S(1)}, u32[]{:S(2)}, u32[]{:S(2)}) collective-permute-start(f32[8,8,1664]{2,1,0:T(8,128)S(1)} %all_to_all.50.got), channel_id=1, source_target_pairs={{0,8},{8,0},{16,24},{24,16},{32,40},{40,32},{48,56},{56,48},{64,72... | collective-permute-start | bytes 1277960 | tf_op jit(solution)/shard_map/ppermute | solution.py:396
  126.6 1.9 %shard_map.93 = (f32[8,128,128]{2,1,0:T(8,128)}, f32[64,192]{1,0:T(8,128)S(1)}) custom-call(f32[8,8,1664]{2,1,0:T(8,128)S(1)} %collective-permute-done.3.near, f32[8,448,128]{2,1,0:T(8,128)S(1)} %all-to-all-done.got.blocks, f32[8,8,1664]{2,1,0:T(8,128)S(1)} %all_to_all.50.got, f32[8,8,256]{2,1,0:T(8,128)S(1)} %shard_map.92.done, ...), custom_call_target="tpu_custom_call" | custom-call | bytes 3457024 | tf_op jit(solution)/shard_map/pallas_call | solution.py:36
  128.5 3.6 %all-to-all-start.7 = ((f32[8,128,128]{2,1,0:T(8,128)}), f32[8,128,128]{2,1,0:T(8,128)S(1)}, u32[]{:S(2)}, u32[]{:S(2)}) async-start(f32[8,128,128]{2,1,0:T(8,128)} %get-tuple-element.44), calls=%async_computation.7 | async-start | bytes 1048576 | tf_op jit(solution)/shard_map/all_to_all | solution.py:28
  132.6 10.5 %all-to-all-done.7.got = f32[8,128,128]{2,1,0:T(8,128)S(1)} async-done(((f32[8,128,128]{2,1,0:T(8,128)}), f32[8,128,128]{2,1,0:T(8,128)S(1)}, u32[]{:S(2)}, u32[]{:S(2)}) %all-to-all-start.7) | async-done | bytes 524320 | tf_op jit(solution)/shard_map/all_to_all | solution.py:28
  143.9 1.8 %collective-permute-start.4 = (f32[48,128]{1,0:T(8,128)S(1)}, f32[48,128]{1,0:T(8,128)S(1)}, u32[]{:S(2)}, u32[]{:S(2)}) collective-permute-start(f32[48,128]{1,0:T(8,128)S(1)} %get-tuple-element.46), channel_id=1, source_target_pairs={{0,8},{8,0},{16,24},{24,16},{32,40},{40,32},{48,56},{56,48},{64,72... | collective-permute-start | bytes 73736 | tf_op jit(solution)/shard_map/ppermute | solution.py:396
  147.3 3.6 %all-to-all-start.8 = ((f32[16,48,128]{2,1,0:T(8,128)}), f32[16,48,128]{2,1,0:T(8,128)S(1)}, u32[]{:S(2)}, u32[]{:S(2)}) async-start(f32[16,48,128]{2,1,0:T(8,128)} %shard_map.95), calls=%async_computation.8 | async-start | bytes 786432 | tf_op jit(solution)/shard_map/all_to_all | solution.py:28
  150.9 1.7 %shard_map.97 = f32[192,1024]{1,0:T(8,128)} custom-call(f32[8,128,128]{2,1,0:T(8,128)S(1)} %all-to-all-done.7.got, f32[64,192]{1,0:T(8,128)S(1)} %get-tuple-element.55.rows, f32[64,192]{1,0:T(8,128)S(1)} %bitcast.3), custom_call_target="tpu_custom_call" | custom-call | bytes 1409024 | tf_op jit(solution)/shard_map/pallas_call | solution.py:36
  152.6 3.0 %shard_map.96 = (f32[4,48,3072]{2,1,0:T(8,128)}, f32[4,48,3072]{2,1,0:T(8,128)}) custom-call(f32[8,3072]{1,0:T(8,128)S(1)} %get-tuple-element.49.full, f32[8,3072]{1,0:T(8,128)S(1)} %collective-permute-done.5.near_full, f32[8,128]{1,0:T(8,128)S(1)} %get-tuple-element.40.keep, f32[8,128]{1,0:T(8,128)S(1)} %collective-permute-done.6.near_keep), custom_call_target="tpu_custom_call" | custom-call | bytes 4923392 | tf_op jit(solution)/shard_map/pallas_call | solution.py:36
  155.6 6.5 %all-to-all-done.8.got = f32[16,48,128]{2,1,0:T(8,128)S(1)} async-done(((f32[16,48,128]{2,1,0:T(8,128)}), f32[16,48,128]{2,1,0:T(8,128)S(1)}, u32[]{:S(2)}, u32[]{:S(2)}) %all-to-all-start.8) | async-done | bytes 393248 | tf_op jit(solution)/shard_map/all_to_all | solution.py:28
  162.2 2.6 %collective-permute-start.7 = (f32[48,128]{1,0:T(8,128)S(1)}, f32[48,128]{1,0:T(8,128)S(1)}, u32[]{:S(2)}, u32[]{:S(2)}) collective-permute-start(f32[48,128]{1,0:T(8,128)S(1)} %shard_map.98.mine), channel_id=1, source_target_pairs={{0,8},{8,0},{16,24},{24,16},{32,40},{40,32},{48,56},{56,48},{64,72... | collective-permute-start | bytes 73736 | tf_op jit(solution)/shard_map/ppermute | solution.py:396
  (38 shorter events, 9.3 us)
Async XLA Ops:
  0.6 1.1 copy-start.6
  1.8 1.1 copy-start.8
  2.9 0.8 copy-start.9
  5.2 1.2 copy-start.1
  6.4 32.2 %all-to-all-start = ((f32[8,448,128]{2,1,0:T(8,128)}), f32[8,448,128]{2,1,0:T(8,128)S(1)}, u32[]{:S(2)}, u32[]{:S(2)}) async-start(f32[8,448,128]{2,1,0:T(8,128)} %copy-done.1), calls=%async_computation | async-start | bytes 3670016 | tf_op jit(solution)/shard_map/all_to_all | solution.py:28
  13.9 3.0 %copy-start.11 = (f32[4,48,3072]{2,1,0:T(8,128)S(1)}, f32[4,48,3072]{2,1,0:T(8,128)}, u32[]{:S(2)}) copy-start(f32[4,48,3072]{2,1,0:T(8,128)} %param.8) | copy-start | bytes 7077892
  15.9 3.5 %collective-permute-start = (f32[2,48,3072]{2,1,0:T(8,128)S(1)}, f32[2,48,3072]{2,1,0:T(8,128)S(1)}, u32[]{:S(2)}, u32[]{:S(2)}) collective-permute-start(f32[2,48,3072]{2,1,0:T(8,128)S(1)} %get-tuple-element.62), channel_id=1, source_target_pairs={{0,8},{8,0},{16,24},{24,16},{32,40},{40,32},{48,56},{56,48},{64,72... | collective-permute-start | bytes 3538952 | tf_op jit(solution)/shard_map/ppermute | solution.py:396
  18.1 2.9 %collective-permute-start.1 = (f32[2,48,3072]{2,1,0:T(8,128)S(1)}, f32[2,48,3072]{2,1,0:T(8,128)S(1)}, u32[]{:S(2)}, u32[]{:S(2)}) collective-permute-start(f32[2,48,3072]{2,1,0:T(8,128)S(1)} %get-tuple-element.60), channel_id=1, source_target_pairs={{0,8},{8,0},{16,24},{24,16},{32,40},{40,32},{48,56},{56,48},{64,72... | collective-permute-start | bytes 3538952 | tf_op jit(solution)/shard_map/ppermute | solution.py:396
  19.4 1.0 copy-start.2
  21.1 1.0 copy-start.4
  38.6 33.9 %copy-start.5 = (f32[2,48,3072]{2,1,0:T(8,128)S(1)}, f32[2,48,3072]{2,1,0:T(8,128)}, u32[]{:S(2)}) copy-start(f32[2,48,3072]{2,1,0:T(8,128)} %copy-done.4) | copy-start | bytes 3538948
  40.6 3.4 %collective-permute-start.2 = (f32[8,8,1664]{2,1,0:T(8,128)S(1)}, f32[8,8,1664]{2,1,0:T(8,128)S(1)}, u32[]{:S(2)}, u32[]{:S(2)}) collective-permute-start(f32[8,8,1664]{2,1,0:T(8,128)S(1)} %get-tuple-element.34), channel_id=1, source_target_pairs={{0,8},{8,0},{16,24},{24,16},{32,40},{40,32},{48,56},{56,48},{64,72... | collective-permute-start | bytes 1277960 | tf_op jit(solution)/shard_map/ppermute | solution.py:396
  44.0 28.5 %copy-start = (f32[2,48,3072]{2,1,0:T(8,128)S(1)}, f32[2,48,3072]{2,1,0:T(8,128)}, u32[]{:S(2)}) copy-start(f32[2,48,3072]{2,1,0:T(8,128)} %get-tuple-element.36.own_out) | copy-start | bytes 3538948
  44.0 28.5 %copy-start.3 = (f32[2,48,3072]{2,1,0:T(8,128)S(1)}, f32[2,48,3072]{2,1,0:T(8,128)}, u32[]{:S(2)}) copy-start(f32[2,48,3072]{2,1,0:T(8,128)} %copy-done.2) | copy-start | bytes 3538948
  117.7 8.8 %collective-permute-start.3 = (f32[8,8,1664]{2,1,0:T(8,128)S(1)}, f32[8,8,1664]{2,1,0:T(8,128)S(1)}, u32[]{:S(2)}, u32[]{:S(2)}) collective-permute-start(f32[8,8,1664]{2,1,0:T(8,128)S(1)} %all_to_all.50.got), channel_id=1, source_target_pairs={{0,8},{8,0},{16,24},{24,16},{32,40},{40,32},{48,56},{56,48},{64,72... | collective-permute-start | bytes 1277960 | tf_op jit(solution)/shard_map/ppermute | solution.py:396
  128.5 14.6 %copy-start.7 = (f32[192,1024]{1,0:T(8,128)S(1)}, f32[192,1024]{1,0:T(8,128)}, u32[]{:S(2)}) copy-start(f32[192,1024]{1,0:T(8,128)} %tokens.3) | copy-start | bytes 2359300
  128.5 14.6 %all-to-all-start.7 = ((f32[8,128,128]{2,1,0:T(8,128)}), f32[8,128,128]{2,1,0:T(8,128)S(1)}, u32[]{:S(2)}, u32[]{:S(2)}) async-start(f32[8,128,128]{2,1,0:T(8,128)} %get-tuple-element.44), calls=%async_computation.7 | async-start | bytes 1048576 | tf_op jit(solution)/shard_map/all_to_all | solution.py:28
  132.1 18.8 %copy-start.10 = (f32[192,64]{0,1:T(8,128)S(1)}, f32[192,64]{0,1:T(8,128)}, u32[]{:S(2)}) copy-start(f32[192,64]{0,1:T(8,128)} %param.6) | copy-start | bytes 147460
  132.1 15.2 %collective-permute-start.5 = (f32[8,3072]{1,0:T(8,128)S(1)}, f32[8,3072]{1,0:T(8,128)S(1)}, u32[]{:S(2)}, u32[]{:S(2)}) collective-permute-start(f32[8,3072]{1,0:T(8,128)S(1)} %get-tuple-element.49.full), channel_id=1, source_target_pairs={{0,8},{8,0},{16,24},{24,16},{32,40},{40,32},{48,56},{56,48},{64,72... | collective-permute-start | bytes 294920 | tf_op jit(solution)/shard_map/ppermute | solution.py:396
  143.9 2.6 %collective-permute-start.4 = (f32[48,128]{1,0:T(8,128)S(1)}, f32[48,128]{1,0:T(8,128)S(1)}, u32[]{:S(2)}, u32[]{:S(2)}) collective-permute-start(f32[48,128]{1,0:T(8,128)S(1)} %get-tuple-element.46), channel_id=1, source_target_pairs={{0,8},{8,0},{16,24},{24,16},{32,40},{40,32},{48,56},{56,48},{64,72... | collective-permute-start | bytes 73736 | tf_op jit(solution)/shard_map/ppermute | solution.py:396
  145.7 1.6 collective-permute-start.6
  147.3 14.8 %all-to-all-start.8 = ((f32[16,48,128]{2,1,0:T(8,128)}), f32[16,48,128]{2,1,0:T(8,128)S(1)}, u32[]{:S(2)}, u32[]{:S(2)}) async-start(f32[16,48,128]{2,1,0:T(8,128)} %shard_map.95), calls=%async_computation.8 | async-start | bytes 786432 | tf_op jit(solution)/shard_map/all_to_all | solution.py:28
  162.2 3.5 %collective-permute-start.7 = (f32[48,128]{1,0:T(8,128)S(1)}, f32[48,128]{1,0:T(8,128)S(1)}, u32[]{:S(2)}, u32[]{:S(2)}) collective-permute-start(f32[48,128]{1,0:T(8,128)S(1)} %shard_map.98.mine), channel_id=1, source_target_pairs={{0,8},{8,0},{16,24},{24,16},{32,40},{40,32},{48,56},{56,48},{64,72... | collective-permute-start | bytes 73736 | tf_op jit(solution)/shard_map/ppermute | solution.py:396

commit v4 on v3

v4 whole, which is shorter than its diff:
```python
import functools

import jax
import jax.numpy as jnp
from jax import lax
from jax.experimental import pallas as pl
from jax.experimental.pallas import tpu as pltpu
from jax.sharding import PartitionSpec as P

HIGH = lax.Precision.HIGHEST
S = "seq"
E = "expert"
LANES = 128
F32 = jnp.float32


def contract(left, right, left_dim, right_dim, precision=HIGH):
    return lax.dot_general(
        left,
        right,
        (((left_dim,), (right_dim,)), ((), ())),
        precision=precision,
        preferred_element_type=F32,
    )


def exchange(blocks, axis, groups=None):
    return lax.all_to_all(blocks, axis, 0, 0, axis_index_groups=groups, tiled=True)


def run(kernel, shapes, *values, scratch=(), flops=0):
    single = not isinstance(shapes, list)
    shapes = [shapes] if single else shapes
    size = 4 * sum(v.size for v in values) + 4 * sum(functools.reduce(lambda a, b: a * b, s) for s in shapes)
    spec = pl.BlockSpec(memory_space=pltpu.VMEM)
    out = pl.pallas_call(
        kernel,
        out_shape=[jax.ShapeDtypeStruct(s, F32) for s in shapes],
        in_specs=[spec] * len(values),
        out_specs=[spec] * len(shapes),
        scratch_shapes=[pltpu.VMEM(s, F32) for s in scratch],
        compiler_params=pltpu.CompilerParams(vmem_limit_bytes=40 * 1024 * 1024),
        cost_estimate=pl.CostEstimate(flops=flops, bytes_accessed=size, transcendentals=0),
    )(*values)
    return out[0] if single else out


def row_of(shape):
    return lax.broadcasted_iota(jnp.int32, shape, len(shape) - 2) % 8


def lane_of(shape):
    return lax.broadcasted_iota(jnp.int32, shape, len(shape) - 1)


def swap(values):
    return jnp.concatenate([values[..., 4:8, :], values[..., 0:4, :]], axis=-2)


def core_index():
    return lax.axis_index(S) % 2


def seats(n):
    place = {}
    for b in range(2):
        for e in range(n):
            place[b, e] = (8 * b + 4 * (e >> 1 & 1) + 2 * (e & 1) + (e >> 2)) ^ 1
    return place


def logit_parts(router, tokens, out):
    part = contract(router[...], tokens[...], 1, 0)
    for i in range(out.shape[0]):
        out[i] = part[:, i * LANES : (i + 1) * LANES]


def add_spread(got, out, own):
    total = jnp.sum(got[...], axis=0)
    own[...] = total
    for e in range(out.shape[0]):
        out[e] = total


def partial_rows(got, tokens, grad_out, mine, near, both):
    n, slots = got.shape[0], got.shape[1]
    logits = jnp.concatenate([got[e] for e in range(n)], axis=1)
    raised = jnp.exp(logits - jnp.max(logits, axis=0, keepdims=True))
    combine = raised / jnp.sum(raised, axis=0, keepdims=True)
    top = jnp.max(logits, axis=1, keepdims=True)
    raised = jnp.exp(logits - top)
    total = jnp.sum(raised, axis=1, keepdims=True)
    rows_in = contract(raised, tokens[...], 1, 1)
    rows_out = contract(combine, grad_out[...], 1, 1)
    piece = rows_in.shape[1] // 2
    lane = lane_of((slots, LANES))
    marks = jnp.where(lane == piece, top, jnp.where(lane == piece + 1, total, 0.0))
    plain = jnp.where(lane_of((4, LANES)) == piece + 1, 1.0, 0.0)
    for (b, e), k in seats(n).items():
        for c in range(2):
            s, w = slice(8 * e + 4 * c, 8 * e + 4 * c + 4), slice(b * piece, (b + 1) * piece)
            both[c, k, 0:4] = marks[s]
            both[c, k, 4:8] = plain
            both[c, k, 0:4, 0:piece] = rows_in[s, w]
            both[c, k, 4:8, 0:piece] = rows_out[s, w]
    core = core_index()
    mine[...] = both[core]
    near[...] = both[1 - core]


def merge(parts, piece):
    top = functools.reduce(jnp.maximum, [p[:, piece : piece + 1] for p in parts])
    rows = sum(jnp.exp(p[:, piece : piece + 1] - top) * p for p in parts)
    return jnp.where(lane_of(rows.shape) == piece, top, rows)


def merge_cores(mine, near, out, piece):
    for k in range(out.shape[0]):
        out[k] = merge([mine[k], near[k]], piece)


def merge_chips(got, out, piece):
    out[...] = merge([got[k] for k in range(got.shape[0])], piece)


def hidden_parts(got, own_in, own_out, near_in, near_out, sent, keep, full):
    w = own_in.shape[1]
    piece = 2 * w
    hidden = own_in.shape[2]
    core = core_index()
    rows = got[...]
    scaled = (row_of((8, LANES)) < 4) & (lane_of((8, LANES)) < piece)
    rows = jnp.where(scaled, rows / rows[:, piece + 1 : piece + 2], rows)
    keep[...] = rows
    turned = jnp.transpose(rows)
    low, high = turned[0:w], turned[w:piece]
    own = jnp.where(core == 0, low, high)
    near = jnp.where(core == 0, high, low)
    for a in range(2):
        for kind, mine, theirs in ((0, own_in, near_in), (1, own_out, near_out)):
            r = 4 * kind + 2 * a
            values = [
                jnp.concatenate(
                    [
                        jnp.broadcast_to(own[:, r + p : r + p + 1], (w, LANES)),
                        jnp.broadcast_to(near[:, r + p : r + p + 1], (w, LANES)),
                    ],
                    axis=0,
                )
                for p in range(2)
            ]
            for h in range(0, hidden, LANES):
                s = slice(h, h + LANES)
                block = jnp.concatenate([mine[a, :, s], theirs[a, :, s]], axis=0)
                for p in range(2):
                    full[r + p : r + p + 1, s] = jnp.sum(block * values[p], axis=0, keepdims=True)
    chips = sent.shape[0]
    share = hidden // chips
    for k in range(chips):
        sent[k, :, 0:share] = full[:, k * share : (k + 1) * share]
        sent[k, :, share:] = jnp.zeros((8, sent.shape[2] - share), F32)


def gate(got, out):
    z = jnp.sum(got[...], axis=0)
    other = swap(z)
    first = row_of(z.shape) < 4
    pre = jnp.where(first, z, other)
    grad = jnp.where(first, other, z)
    c = 0.7978845608028654
    t = jnp.tanh(c * (pre + 0.044715 * (pre * pre * pre)))
    act = 0.5 * pre * (1.0 + t)
    slope = 0.5 * (1.0 + t) + 0.5 * pre * (1.0 - t * t) * (c * (1.0 + 3 * 0.044715 * (pre * pre)))
    both = jnp.where(first, act, grad * slope)
    for k in range(out.shape[0]):
        out[k] = both


def slot_rows(got, keep, own_in, own_out, near_in, near_out, out, full):
    w = own_in.shape[1]
    piece = 2 * w
    hidden = own_in.shape[2]
    chips = got.shape[0]
    share = hidden // chips
    core = core_index()
    for k in range(chips):
        full[:, k * share : (k + 1) * share] = got[k, :, 0:share]
    lane = lane_of((piece, LANES))
    cols = jnp.zeros((piece, LANES), F32)
    for a in range(2):
        for kind, mine, theirs in ((0, own_out, near_out), (1, own_in, near_in)):
            r = 4 * kind + 2 * a
            sums = [jnp.zeros((piece, LANES), F32) for _ in range(2)]
            for h in range(0, hidden, LANES):
                s = slice(h, h + LANES)
                block = jnp.concatenate([mine[a, :, s], theirs[a, :, s]], axis=0)
                for p in range(2):
                    sums[p] = sums[p] + block * full[r + p : r + p + 1, s]
            for p in range(2):
                cols = jnp.where(lane == r + p, jnp.sum(sums[p], axis=1, keepdims=True), cols)
    own, near = cols[0:w], cols[w:]
    low = jnp.where(core == 0, own, near)
    high = jnp.where(core == 0, near, own)
    square = jnp.concatenate([low, high, jnp.zeros((LANES - piece, LANES), F32)], axis=0)
    rows = jnp.transpose(square)[0:8]
    held = swap(keep[...])
    lane = lane_of((8, LANES))
    column = jnp.sum(jnp.where(lane < piece, held * rows, 0.0), axis=1, keepdims=True)
    out[...] = jnp.where(lane < piece, rows, jnp.where(lane == piece + 2, column, held))


def copies(tile, out):
    value = tile[...]
    for k in range(out.shape[0]):
        out[k] = value


def width_products(mine, near, tokens, grad_out, out, rows, marks, outs):
    n = out.shape[0]
    slots = rows.shape[0]
    piece = rows.shape[1] // 2
    core = core_index()
    added = []
    for c in range(2):
        for (b, e), k in seats(n).items():
            tile = jnp.where(core == c, mine[k], near[k])
            s, w = slice(8 * e + 4 * c, 8 * e + 4 * c + 4), slice(b * piece, (b + 1) * piece)
            outs[s, w] = tile[0:4, 0:piece]
            rows[s, w] = tile[4:8, 0:piece]
            if b == 0:
                marks[s] = tile[4:8]
            else:
                added.append((s, tile[4:8, piece + 2 : piece + 3]))
    lane = lane_of((4, LANES))
    for s, column in added:
        marks[s] = marks[s] + jnp.where(lane == piece + 2, column, 0.0)
    combine = contract(outs[...], grad_out[...], 1, 0)
    dispatch = contract(rows[...], tokens[...], 1, 0) - marks[:, piece + 2 : piece + 3]
    for i in range(n):
        s = slice(i * LANES, (i + 1) * LANES)
        out[i, 0:slots] = combine[:, s]
        out[i, slots:] = dispatch[:, s]


def logit_grads(got, own, marks, out, piece):
    slots = own.shape[0]
    total = jnp.sum(got[...], axis=0)
    logits = own[...]
    raised = jnp.exp(logits - jnp.max(logits, axis=0, keepdims=True))
    combine = raised / jnp.sum(raised, axis=0, keepdims=True)
    dispatch = jnp.exp(logits - marks[:, piece : piece + 1]) / marks[:, piece + 1 : piece + 2]
    first, second = total[:slots], total[slots:]
    grads = combine * (first - jnp.sum(combine * first, axis=0, keepdims=True)) + dispatch * second
    for e in range(out.shape[0]):
        out[e] = grads


def router_part(got, tokens, mine, theirs):
    n = got.shape[0]
    grads = jnp.concatenate([got[e] for e in range(n)], axis=1)
    part = contract(tokens[...], grads, 1, 1)
    q = part.shape[0] // 4
    low = jnp.concatenate([part[0:q], part[q : 2 * q]], axis=1)
    high = jnp.concatenate([part[2 * q : 3 * q], part[3 * q :]], axis=1)
    core = core_index()
    mine[...] = jnp.where(core == 0, low, high)
    theirs[...] = jnp.where(core == 0, high, low)


def token_grads(got, logits, rows, marks, router, out, piece):
    left = jnp.transpose(jnp.concatenate([router[...], rows[...]], axis=0))
    top, total = marks[:, piece : piece + 1], marks[:, piece + 1 : piece + 2]
    for e in range(got.shape[0]):
        dispatch = jnp.exp(logits[e] - top) / total
        right = jnp.concatenate([got[e], dispatch], axis=0)
        out[:, e * LANES : (e + 1) * LANES] = contract(left, right, 1, 0)


def add_copies(mine, theirs, out):
    both = mine[...] + theirs[...]
    for k in range(out.shape[0]):
        out[k] = both


def add_all(got, out):
    out[...] = jnp.sum(got[...], axis=0)


def unfold(mine, theirs, out):
    core = core_index()
    a, b = mine[...], theirs[...]
    q, h = out.shape[1] // 4, LANES // 2
    for i, values in enumerate((jnp.where(core == 0, a, b), jnp.where(core == 0, b, a))):
        turned = jnp.transpose(values)
        out[:, 2 * i * q : (2 * i + 1) * q] = turned[:h]
        out[:, (2 * i + 1) * q : (2 * i + 2) * q] = turned[h:]


def weight_grads(full, near_full, keep, near_keep, grad_in, grad_out):
    w = grad_in.shape[1]
    hidden = grad_in.shape[2]
    core = core_index()
    step = 512
    for base, values, held in ((2 * core, full, keep), (2 - 2 * core, near_full, near_keep)):
        held = held[...]
        part = jnp.where(core == 0, held[:, 0:w], held[:, w : 2 * w])
        cols = jnp.transpose(part)
        for a in range(2):
            for h in range(0, hidden, step):
                s = slice(h, h + step)
                i, j = 2 * a, 2 * a + 1
                grad_out[base + a, :, s] = (
                    cols[:, 4 + i : 5 + i] * values[i : i + 1, s]
                    + cols[:, 4 + j : 5 + j] * values[j : j + 1, s]
                )
                grad_in[base + a, :, s] = (
                    cols[:, i : i + 1] * values[4 + i : 5 + i, s]
                    + cols[:, j : j + 1] * values[4 + j : 5 + j, s]
                )


def per_device(tokens, router, w_in, w_out, grad_out):
    n_seq, n_exp = lax.axis_size(S), lax.axis_size(E)
    experts, width_block, hidden = w_in.shape
    rows_block, local_tokens = tokens.shape
    slots = router.shape[1]
    chips = n_seq // 2
    piece = 2 * width_block
    core = core_index()
    partner = [(i, i ^ 1) for i in range(n_seq)]
    groups = [[2 * k + c for k in range(chips)] for c in range(2)]
    turned = router.T
    to_owner = [
        ((2 * k + c) * n_exp + f, (2 * (2 * f + b) + c) * n_exp + e)
        for (b, e), k in seats(n_exp).items()
        for c in range(2)
        for f in range(n_exp)
    ]
    from_owner = [(there, here) for here, there in to_owner]

    def to_partner(values):
        return lax.ppermute(values, S, partner)

    sent = run(logit_parts, (n_exp, slots, LANES), turned, tokens)
    sent, own = run(
        add_spread, [(n_exp, slots, LANES), (slots, LANES)], exchange(sent, E)
    )
    logits = exchange(sent, E)
    half = experts // 2

    def split(w):
        own = lax.dynamic_slice_in_dim(w, half * core, half, 0)
        return own, to_partner(lax.dynamic_slice_in_dim(w, half * (1 - core), half, 0))

    own_in, near_in = split(w_in)
    own_out, near_out = split(w_out)
    logits, own_in, own_out, near_in, near_out = lax.optimization_barrier(
        (logits, own_in, own_out, near_in, near_out)
    )
    weights = (own_in, own_out, near_in, near_out)

    tiles = (chips, 8, LANES)
    mine, near = run(
        partial_rows, [tiles, tiles], logits, tokens, grad_out, scratch=[(2,) + tiles]
    )
    sent = run(functools.partial(merge_cores, piece=piece), tiles, mine, to_partner(near))
    tile = run(
        functools.partial(merge_chips, piece=piece), (8, LANES), exchange(sent, S, groups)
    )
    share = hidden // chips
    cut = -(-share // LANES) * LANES
    sent, held = run(
        hidden_parts,
        [(chips, 8, cut), (8, LANES)],
        lax.ppermute(tile, (S, E), to_owner),
        *weights,
        scratch=[(8, hidden)],
    )
    sent = run(gate, (chips, 8, cut), exchange(sent, S, groups))
    tile, full = run(
        slot_rows, [(8, LANES), (8, hidden)], exchange(sent, S, groups), held, *weights
    )
    sent = run(copies, tiles, lax.ppermute(tile, (S, E), from_owner))
    mine = exchange(sent, S, groups)
    near = to_partner(mine)
    sent, rows, marks = run(
        width_products,
        [(n_exp, 2 * slots, LANES), (slots, rows_block), (slots, LANES)],
        mine,
        near,
        tokens,
        grad_out,
        scratch=[(slots, rows_block)],
    )
    sent = run(
        functools.partial(logit_grads, piece=piece),
        (n_exp, slots, LANES),
        exchange(sent, E),
        own,
        marks,
    )
    grads = exchange(sent, E)
    fold = (rows_block // 4, 2 * slots)
    near, theirs = run(router_part, [fold, fold], grads, tokens)
    sent = run(add_copies, (chips,) + fold, near, to_partner(theirs))
    near_full = to_partner(full)
    near_held = to_partner(held)
    sent, grads, full, near_full, near_held = lax.optimization_barrier(
        (sent, grads, full, near_full, near_held)
    )
    got = exchange(sent, S, groups)
    grad_w_in, grad_w_out = run(
        weight_grads, [w_in.shape, w_out.shape], full, near_full, held, near_held
    )
    grad_tokens = run(
        functools.partial(token_grads, piece=piece),
        (rows_block, local_tokens),
        grads,
        logits,
        rows,
        marks,
        turned,
    )
    got, grad_w_in, grad_w_out, grad_tokens = lax.optimization_barrier(
        (got, grad_w_in, grad_w_out, grad_tokens)
    )
    near = run(add_all, fold, got)
    grad_router = run(unfold, (slots, rows_block), near, to_partner(near)).T
    return (grad_tokens, grad_router, grad_w_in, grad_w_out)


def solution(mesh):
    placed = (
        P("expert", "seq"),
        P("expert", None),
        P("expert", "seq", None),
        P("expert", "seq", None),
        P("expert", "seq"),
    )
    return jax.shard_map(
        per_device,
        mesh=mesh,
        in_specs=placed,
        out_specs=(
            P("expert", "seq"),
            P("expert", None),
            P("expert", "seq", None),
            P("expert", "seq", None),
        ),
        check_vma=False,
    )
```

time: 167 us -> 163 us (0.976)
  blocking collectives: 70.7 us -> 94.2 us
  waiting for transfers between devices: 38.5 us -> 20.2 us
  local copies, waits for them, and re-layouts: 9.57 us -> 2.2 us
  Pallas kernels: 16.5 us -> 14.2 us
    all_to_all x6 -> x7, blocking collectives: 70.7 us -> 94.2 us  [exchange(): lax.all_to_all(blocks, axis, 0, 0, axis_index_groups=groups, tiled=True)]
    all_to_all x3 -> x2, waiting for transfers between devices: 33.5 us -> 12.3 us  [exchange(): lax.all_to_all(blocks, axis, 0, 0, axis_index_groups=groups, tiled=True)]
    all_to_all x3 -> x2, starting transfers between devices: 14.7 us -> 6.97 us  [exchange(): lax.all_to_all(blocks, axis, 0, 0, axis_index_groups=groups, tiled=True)]
    unnamed x24 -> x8, local copies, waits for them, and re-layouts: 6.41 us -> 0.02 us
    ppermute x8, starting transfers between devices: 15.8 us -> 22.1 us  [to_partner(): return lax.ppermute(values, S, partner)]
    ppermute x0 -> x2, waiting for transfers between devices: none -> 4.51 us  [the longest x1 2.88 us: per_device(): sent = run(copies, tiles, lax.ppermute(tile, (S, E), from_owner))]
    ppermute x0 -> x2, starting transfers between devices: none -> 2 us  [the longest x1 1.09 us: per_device(): sent = run(copies, tiles, lax.ppermute(tile, (S, E), from_owner))]
    pallas_call x15 -> x17, Pallas kernels: 15 us -> 14.2 us  [run(): pl.pallas_call(kernel, out_shape=[jax.ShapeDtypeStruct(s, F32) for s in s...]
  transfers between devices with their start and end apart: 11 -> 12, of which waited for: 9 -> 8; matrix products, arithmetic and copies ran while one was open for 2% -> 0% of each run, Pallas kernels for 4% -> 4%
where the time goes in v4:
time: 163 us
  blocking collectives  94.2 us (58%)
  starting transfers between devices  31 us (19%)
  waiting for transfers between devices  20.2 us (12%)
  Pallas kernels  14.2 us (9%)
  local copies, waits for them, and re-layouts  2.2 us (1%)
    all_to_all x7, blocking collectives, exchange(): lax.all_to_all(blocks, axis, 0, 0, axis_index_groups=groups, tiled=True)  94.2 us
    ppermute x8, starting transfers between devices, to_partner(): return lax.ppermute(values, S, partner)  22.1 us
    pallas_call x17, Pallas kernels, run(): pl.pallas_call(kernel, out_shape=[jax.ShapeDtypeStruct(s, F32) for s in s...  14.2 us
    all_to_all x2, waiting for transfers between devices, exchange(): lax.all_to_all(blocks, axis, 0, 0, axis_index_groups=groups, tiled=True)  12.3 us
    all_to_all x2, starting transfers between devices, exchange(): lax.all_to_all(blocks, axis, 0, 0, axis_index_groups=groups, tiled=True)  6.97 us
    ppermute x8, waiting for transfers between devices, to_partner(): return lax.ppermute(values, S, partner)  3.41 us
  transfers between devices with their start and end apart: 12, of which 8 were waited for; matrix products, arithmetic and copies ran while one was open for 0% of the time, Pallas kernels for 4%

profile of v4, /device:TPU:1, one launch (start us, length us, event | category | flops | bytes accessed | tf_op | source)
XLA Modules:
  0.0 162.6 jit_solution(6802864927264814906)
XLA Ops:
  0.7 2.0 %constant_dynamic-slice_fusion.1 = (f32[2,48,3072]{2,1,0:T(8,128)S(1)}, f32[2,48,3072]{2,1,0:T(8,128)S(1)}) fusion(f32[4,48,3072]{2,1,0:T(8,128)} %param.7, s32[]{:T(128)S(6)} %select_n.17, s32[]{:T(128)S(6)} %select_n.16), kind=kLoop, calls=%fused_computation.1 | loop fusion | bytes 4718600 | tf_op jit(solution)/shard_map/dynamic_slice | solution.py:353
  2.7 3.3 %collective-permute-start = (f32[2,48,3072]{2,1,0:T(8,128)S(1)}, f32[2,48,3072]{2,1,0:T(8,128)S(1)}, u32[]{:S(2)}, u32[]{:S(2)}) collective-permute-start(f32[2,48,3072]{2,1,0:T(8,128)S(1)} %get-tuple-element.64), channel_id=1, source_target_pairs={{0,8},{8,0},{16,24},{24,16},{32,40},{40,32},{48,56},{56,48},{64,72... | collective-permute-start | bytes 3538952 | tf_op jit(solution)/shard_map/ppermute | solution.py:342
  7.2 12.5 %all_to_all.45.got = f32[8,64,128]{2,1,0:T(8,128)S(1)} all-to-all(f32[8,64,128]{2,1,0:T(8,128)S(1)} %shard_map.84), channel_id=1, replica_groups=mesh['seq'=32,'expert'=8] {'expert'}, dimensions={0} | all-to-all | bytes 524288 | tf_op jit(solution)/shard_map/all_to_all | solution.py:28
  19.7 10.5 %all_to_all.46.got.logits = f32[8,64,128]{2,1,0:T(8,128)S(1)} all-to-all(f32[8,64,128]{2,1,0:T(8,128)S(1)} %get-tuple-element.33), channel_id=1, replica_groups=mesh['seq'=32,'expert'=8] {'expert'}, dimensions={0} | all-to-all | bytes 524288 | tf_op jit(solution)/shard_map/all_to_all | solution.py:28
  30.2 1.7 %shard_map.86 = (f32[16,8,128]{2,1,0:T(8,128)S(1)}, f32[16,8,128]{2,1,0:T(8,128)S(1)}) custom-call(f32[8,64,128]{2,1,0:T(8,128)S(1)} %all_to_all.46.got.logits, f32[192,1024]{1,0:T(8,128)S(1)} %copy-done, f32[192,1024]{1,0:T(8,128)S(1)} %copy-done.1), custom_call_target="tpu_custom_call" | custom-call | bytes 1966080 | tf_op jit(solution)/shard_map/pallas_call | solution.py:36
  31.9 2.8 %collective-permute-start.2 = (f32[16,8,128]{2,1,0:T(8,128)S(1)}, f32[16,8,128]{2,1,0:T(8,128)S(1)}, u32[]{:S(2)}, u32[]{:S(2)}) collective-permute-start(f32[16,8,128]{2,1,0:T(8,128)S(1)} %get-tuple-element.36), channel_id=1, source_target_pairs={{0,8},{8,0},{16,24},{24,16},{32,40},{40,32},{48,56},{56,48},{64,72... | collective-permute-start | bytes 196616 | tf_op jit(solution)/shard_map/ppermute | solution.py:342
  34.8 0.9 collective-permute-done.2.near
  35.8 15.5 %all_to_all.47.got = f32[16,8,128]{2,1,0:T(8,128)S(1)} all-to-all(f32[16,8,128]{2,1,0:T(8,128)S(1)} %shard_map.87), channel_id=1, replica_groups={{0,16,32,48,64,80,96,112,128,144,160,176,192,208,224,240},{8,24,40,56,7..., dimensions={0} | all-to-all | bytes 131072 | tf_op jit(solution)/shard_map/all_to_all | solution.py:28
  51.4 0.9 collective-permute-start.3
  52.3 1.6 collective-permute-done.3.got
  53.9 1.3 shard_map.89
  55.2 16.4 %all_to_all.48.got = f32[16,8,256]{2,1,0:T(8,128)S(1)} all-to-all(f32[16,8,256]{2,1,0:T(8,128)S(1)} %get-tuple-element.41), channel_id=1, replica_groups={{0,16,32,48,64,80,96,112,128,144,160,176,192,208,224,240},{8,24,40,56,7..., dimensions={0} | all-to-all | bytes 262144 | tf_op jit(solution)/shard_map/all_to_all | solution.py:28
  71.7 10.5 %all_to_all.49.got = f32[16,8,256]{2,1,0:T(8,128)S(1)} all-to-all(f32[16,8,256]{2,1,0:T(8,128)S(1)} %shard_map.90), channel_id=1, replica_groups={{0,16,32,48,64,80,96,112,128,144,160,176,192,208,224,240},{8,24,40,56,7..., dimensions={0} | all-to-all | bytes 262144 | tf_op jit(solution)/shard_map/all_to_all | solution.py:28
  82.1 1.2 shard_map.91
  83.3 1.1 collective-permute-start.4
  84.4 2.9 %collective-permute-done.4.tile = f32[8,128]{1,0:T(8,128)S(1)} collective-permute-done((f32[8,128]{1,0:T(8,128)S(1)}, f32[8,128]{1,0:T(8,128)S(1)}, u32[]{:S(2)}, u32[]{:S(2)}) %collective-permute-start.4) | collective-permute-done | bytes 4128 | tf_op jit(solution)/shard_map/ppermute | solution.py:383
  87.3 14.9 %all_to_all.50.mine = f32[16,8,128]{2,1,0:T(8,128)S(1)} all-to-all(f32[16,8,128]{2,1,0:T(8,128)S(1)} %shard_map.92), channel_id=1, replica_groups={{0,16,32,48,64,80,96,112,128,144,160,176,192,208,224,240},{8,24,40,56,7..., dimensions={0} | all-to-all | bytes 131072 | tf_op jit(solution)/shard_map/all_to_all | solution.py:28
  102.3 7.8 %collective-permute-start.5 = (f32[16,8,128]{2,1,0:T(8,128)S(1)}, f32[16,8,128]{2,1,0:T(8,128)S(1)}, u32[]{:S(2)}, u32[]{:S(2)}) collective-permute-start(f32[16,8,128]{2,1,0:T(8,128)S(1)} %all_to_all.50.mine), channel_id=1, source_target_pairs={{0,8},{8,0},{16,24},{24,16},{32,40},{40,32},{48,56},{56,48},{64,72... | collective-permute-start | bytes 196616 | tf_op jit(solution)/shard_map/ppermute | solution.py:342
  110.0 0.9 collective-permute-done.5.near
  110.9 1.1 shard_map.93
  112.0 13.9 %all_to_all.51.got = f32[8,128,128]{2,1,0:T(8,128)S(1)} all-to-all(f32[8,128,128]{2,1,0:T(8,128)S(1)} %get-tuple-element.44), channel_id=1, replica_groups=mesh['seq'=32,'expert'=8] {'expert'}, dimensions={0} | all-to-all | bytes 1048576 | tf_op jit(solution)/shard_map/all_to_all | solution.py:28
  126.8 3.4 %all-to-all-start.7 = ((f32[8,64,128]{2,1,0:T(8,128)}), f32[8,64,128]{2,1,0:T(8,128)S(1)}, u32[]{:S(2)}, u32[]{:S(2)}) async-start(f32[8,64,128]{2,1,0:T(8,128)} %shard_map.94), calls=%async_computation.7 | async-start | bytes 524288 | tf_op jit(solution)/shard_map/all_to_all | solution.py:28
  130.2 1.9 %collective-permute-start.7 = (f32[8,3072]{1,0:T(8,128)S(1)}, f32[8,3072]{1,0:T(8,128)S(1)}, u32[]{:S(2)}, u32[]{:S(2)}) collective-permute-start(f32[8,3072]{1,0:T(8,128)S(1)} %get-tuple-element.51.full), channel_id=1, source_target_pairs={{0,8},{8,0},{16,24},{24,16},{32,40},{40,32},{48,56},{56,48},{64,72... | collective-permute-start | bytes 294920 | tf_op jit(solution)/shard_map/ppermute | solution.py:342
  132.1 5.8 %all-to-all-done.7.got = f32[8,64,128]{2,1,0:T(8,128)S(1)} async-done(((f32[8,64,128]{2,1,0:T(8,128)}), f32[8,64,128]{2,1,0:T(8,128)S(1)}, u32[]{:S(2)}, u32[]{:S(2)}) %all-to-all-start.7) | async-done | bytes 262176 | tf_op jit(solution)/shard_map/all_to_all | solution.py:28
  137.9 0.8 shard_map.95
  138.7 3.1 %collective-permute-start.6 = (f32[48,128]{1,0:T(8,128)S(1)}, f32[48,128]{1,0:T(8,128)S(1)}, u32[]{:S(2)}, u32[]{:S(2)}) collective-permute-start(f32[48,128]{1,0:T(8,128)S(1)} %get-tuple-element.48), channel_id=1, source_target_pairs={{0,8},{8,0},{16,24},{24,16},{32,40},{40,32},{48,56},{56,48},{64,72... | collective-permute-start | bytes 73736 | tf_op jit(solution)/shard_map/ppermute | solution.py:342
  143.5 3.6 %all-to-all-start.8 = ((f32[16,48,128]{2,1,0:T(8,128)}), f32[16,48,128]{2,1,0:T(8,128)S(1)}, u32[]{:S(2)}, u32[]{:S(2)}) async-start(f32[16,48,128]{2,1,0:T(8,128)} %shard_map.96), calls=%async_computation.8 | async-start | bytes 786432 | tf_op jit(solution)/shard_map/all_to_all | solution.py:28
  147.0 1.8 %shard_map.98 = f32[192,1024]{1,0:T(8,128)} custom-call(f32[8,64,128]{2,1,0:T(8,128)S(1)} %all-to-all-done.7.got, f32[8,64,128]{2,1,0:T(8,128)S(1)} %all_to_all.46.got.logits, f32[64,192]{1,0:T(8,128)S(1)} %get-tuple-element.57.rows, f32[64,128]{1,0:T(8,128)S(1)} %get-tuple-element.46.marks, f32[64,192]{1,0:T(8,128)S(1)} %bitcast.3), custom_call_target="tpu_custom_call" | custom-call | bytes 1441792 | tf_op jit(solution)/shard_map/pallas_call | solution.py:36
  148.8 3.0 %shard_map.97 = (f32[4,48,3072]{2,1,0:T(8,128)}, f32[4,48,3072]{2,1,0:T(8,128)}) custom-call(f32[8,3072]{1,0:T(8,128)S(1)} %get-tuple-element.51.full, f32[8,3072]{1,0:T(8,128)S(1)} %collective-permute-done.7.near_full, f32[8,128]{1,0:T(8,128)S(1)} %get-tuple-element.42.keep, f32[8,128]{1,0:T(8,128)S(1)} %collective-permute-done.8.near_keep), custom_call_target="tpu_custom_call" | custom-call | bytes 4923392 | tf_op jit(solution)/shard_map/pallas_call | solution.py:36
  151.8 6.5 %all-to-all-done.8.got = f32[16,48,128]{2,1,0:T(8,128)S(1)} async-done(((f32[16,48,128]{2,1,0:T(8,128)}), f32[16,48,128]{2,1,0:T(8,128)S(1)}, u32[]{:S(2)}, u32[]{:S(2)}) %all-to-all-start.8) | async-done | bytes 393248 | tf_op jit(solution)/shard_map/all_to_all | solution.py:28
  158.3 2.6 %collective-permute-start.9 = (f32[48,128]{1,0:T(8,128)S(1)}, f32[48,128]{1,0:T(8,128)S(1)}, u32[]{:S(2)}, u32[]{:S(2)}) collective-permute-start(f32[48,128]{1,0:T(8,128)S(1)} %shard_map.99.mine), channel_id=1, source_target_pairs={{0,8},{8,0},{16,24},{24,16},{32,40},{40,32},{48,56},{56,48},{64,72... | collective-permute-start | bytes 73736 | tf_op jit(solution)/shard_map/ppermute | solution.py:342
  161.0 0.8 collective-permute-done.9.theirs
  (26 shorter events, 4.8 us)
Async XLA Ops:
  0.7 5.3 %copy-start.3 = (f32[4,48,3072]{2,1,0:T(8,128)S(1)}, f32[4,48,3072]{2,1,0:T(8,128)}, u32[]{:S(2)}) copy-start(f32[4,48,3072]{2,1,0:T(8,128)} %param.8) | copy-start | bytes 7077892
  2.6 4.0 %copy-start = (f32[192,1024]{1,0:T(8,128)S(1)}, f32[192,1024]{1,0:T(8,128)}, u32[]{:S(2)}) copy-start(f32[192,1024]{1,0:T(8,128)} %tokens.7) | copy-start | bytes 2359300
  2.6 4.0 %copy-start.2 = (f32[192,64]{0,1:T(8,128)S(1)}, f32[192,64]{0,1:T(8,128)}, u32[]{:S(2)}) copy-start(f32[192,64]{0,1:T(8,128)} %param.6) | copy-start | bytes 147460
  2.7 27.6 %collective-permute-start = (f32[2,48,3072]{2,1,0:T(8,128)S(1)}, f32[2,48,3072]{2,1,0:T(8,128)S(1)}, u32[]{:S(2)}, u32[]{:S(2)}) collective-permute-start(f32[2,48,3072]{2,1,0:T(8,128)S(1)} %get-tuple-element.64), channel_id=1, source_target_pairs={{0,8},{8,0},{16,24},{24,16},{32,40},{40,32},{48,56},{56,48},{64,72... | collective-permute-start | bytes 3538952 | tf_op jit(solution)/shard_map/ppermute | solution.py:342
  6.2 24.0 %collective-permute-start.1 = (f32[2,48,3072]{2,1,0:T(8,128)S(1)}, f32[2,48,3072]{2,1,0:T(8,128)S(1)}, u32[]{:S(2)}, u32[]{:S(2)}) collective-permute-start(f32[2,48,3072]{2,1,0:T(8,128)S(1)} %get-tuple-element.62), channel_id=1, source_target_pairs={{0,8},{8,0},{16,24},{24,16},{32,40},{40,32},{48,56},{56,48},{64,72... | collective-permute-start | bytes 3538952 | tf_op jit(solution)/shard_map/ppermute | solution.py:342
  6.6 23.6 %copy-start.1 = (f32[192,1024]{1,0:T(8,128)S(1)}, f32[192,1024]{1,0:T(8,128)}, u32[]{:S(2)}) copy-start(f32[192,1024]{1,0:T(8,128)} %grad_out.3) | copy-start | bytes 2359300
  31.9 3.8 %collective-permute-start.2 = (f32[16,8,128]{2,1,0:T(8,128)S(1)}, f32[16,8,128]{2,1,0:T(8,128)S(1)}, u32[]{:S(2)}, u32[]{:S(2)}) collective-permute-start(f32[16,8,128]{2,1,0:T(8,128)S(1)} %get-tuple-element.36), channel_id=1, source_target_pairs={{0,8},{8,0},{16,24},{24,16},{32,40},{40,32},{48,56},{56,48},{64,72... | collective-permute-start | bytes 196616 | tf_op jit(solution)/shard_map/ppermute | solution.py:342
  51.4 2.5 %collective-permute-start.3 = (f32[8,128]{1,0:T(8,128)S(1)}, f32[8,128]{1,0:T(8,128)S(1)}, u32[]{:S(2)}, u32[]{:S(2)}) collective-permute-start(f32[8,128]{1,0:T(8,128)S(1)} %shard_map.88), channel_id=1, source_target_pairs={{16,0},{17,32},{18,64},{19,96},{20,128},{21,160},{22,192},{23,224}... | collective-permute-start | bytes 12296 | tf_op jit(solution)/shard_map/ppermute | solution.py:375
  83.3 4.0 %collective-permute-start.4 = (f32[8,128]{1,0:T(8,128)S(1)}, f32[8,128]{1,0:T(8,128)S(1)}, u32[]{:S(2)}, u32[]{:S(2)}) collective-permute-start(f32[8,128]{1,0:T(8,128)S(1)} %get-tuple-element.43), channel_id=1, source_target_pairs={{0,16},{32,17},{64,18},{96,19},{128,20},{160,21},{192,22},{224,23}... | collective-permute-start | bytes 12296 | tf_op jit(solution)/shard_map/ppermute | solution.py:383
  102.3 8.7 %collective-permute-start.5 = (f32[16,8,128]{2,1,0:T(8,128)S(1)}, f32[16,8,128]{2,1,0:T(8,128)S(1)}, u32[]{:S(2)}, u32[]{:S(2)}) collective-permute-start(f32[16,8,128]{2,1,0:T(8,128)S(1)} %all_to_all.50.mine), channel_id=1, source_target_pairs={{0,8},{8,0},{16,24},{24,16},{32,40},{40,32},{48,56},{56,48},{64,72... | collective-permute-start | bytes 196616 | tf_op jit(solution)/shard_map/ppermute | solution.py:342
  126.8 11.1 %all-to-all-start.7 = ((f32[8,64,128]{2,1,0:T(8,128)}), f32[8,64,128]{2,1,0:T(8,128)S(1)}, u32[]{:S(2)}, u32[]{:S(2)}) async-start(f32[8,64,128]{2,1,0:T(8,128)} %shard_map.94), calls=%async_computation.7 | async-start | bytes 524288 | tf_op jit(solution)/shard_map/all_to_all | solution.py:28
  130.2 13.3 %collective-permute-start.7 = (f32[8,3072]{1,0:T(8,128)S(1)}, f32[8,3072]{1,0:T(8,128)S(1)}, u32[]{:S(2)}, u32[]{:S(2)}) collective-permute-start(f32[8,3072]{1,0:T(8,128)S(1)} %get-tuple-element.51.full), channel_id=1, source_target_pairs={{0,8},{8,0},{16,24},{24,16},{32,40},{40,32},{48,56},{56,48},{64,72... | collective-permute-start | bytes 294920 | tf_op jit(solution)/shard_map/ppermute | solution.py:342
  138.7 3.9 %collective-permute-start.6 = (f32[48,128]{1,0:T(8,128)S(1)}, f32[48,128]{1,0:T(8,128)S(1)}, u32[]{:S(2)}, u32[]{:S(2)}) collective-permute-start(f32[48,128]{1,0:T(8,128)S(1)} %get-tuple-element.48), channel_id=1, source_target_pairs={{0,8},{8,0},{16,24},{24,16},{32,40},{40,32},{48,56},{56,48},{64,72... | collective-permute-start | bytes 73736 | tf_op jit(solution)/shard_map/ppermute | solution.py:342
  141.8 1.6 %collective-permute-start.8 = (f32[8,128]{1,0:T(8,128)S(1)}, f32[8,128]{1,0:T(8,128)S(1)}, u32[]{:S(2)}, u32[]{:S(2)}) collective-permute-start(f32[8,128]{1,0:T(8,128)S(1)} %get-tuple-element.42.keep), channel_id=1, source_target_pairs={{0,8},{8,0},{16,24},{24,16},{32,40},{40,32},{48,56},{56,48},{64,72... | collective-permute-start | bytes 12296 | tf_op jit(solution)/shard_map/ppermute | solution.py:342
  143.5 14.8 %all-to-all-start.8 = ((f32[16,48,128]{2,1,0:T(8,128)}), f32[16,48,128]{2,1,0:T(8,128)S(1)}, u32[]{:S(2)}, u32[]{:S(2)}) async-start(f32[16,48,128]{2,1,0:T(8,128)} %shard_map.96), calls=%async_computation.8 | async-start | bytes 786432 | tf_op jit(solution)/shard_map/all_to_all | solution.py:28
  158.3 3.5 %collective-permute-start.9 = (f32[48,128]{1,0:T(8,128)S(1)}, f32[48,128]{1,0:T(8,128)S(1)}, u32[]{:S(2)}, u32[]{:S(2)}) collective-permute-start(f32[48,128]{1,0:T(8,128)S(1)} %shard_map.99.mine), channel_id=1, source_target_pairs={{0,8},{8,0},{16,24},{24,16},{32,40},{40,32},{48,56},{56,48},{64,72... | collective-permute-start | bytes 73736 | tf_op jit(solution)/shard_map/ppermute | solution.py:342

commit v5 on v4

--- a/solution.py
+++ b/solution.py
@@ -7,14 +7,15 @@
 from jax.experimental.pallas import tpu as pltpu
 from jax.sharding import PartitionSpec as P
 
-HIGH = lax.Precision.HIGHEST
+FULL = lax.Precision.HIGHEST
+THREE = lax.Precision.HIGH
 S = "seq"
 E = "expert"
 LANES = 128
 F32 = jnp.float32
 
 
-def contract(left, right, left_dim, right_dim, precision=HIGH):
+def contract(left, right, left_dim, right_dim, precision=FULL):
     return lax.dot_general(
         left,
         right,
@@ -61,42 +62,77 @@
     return lax.axis_index(S) % 2
 
 
+SEATS = (0xE680F7D5, 0xB291A3C4)
+
+
+def seat(b, e, column):
+    index = 2 * (((e >> 1) - (column >> 1)) & 3) + ((e ^ column) & 1)
+    if isinstance(column, int):
+        value = SEATS[b] >> (4 * index) & 15
+    else:
+        word = SEATS[b] - (1 << 32 if SEATS[b] >> 31 else 0)
+        value = lax.shift_right_logical(jnp.int32(word), 4 * index) & 15
+    return (((value >> 3) ^ (column >> 2)) << 3) | (((value & 7) + 2 * (column & 3)) & 7)
+
+
 def seats(n):
-    place = {}
-    for b in range(2):
-        for e in range(n):
-            place[b, e] = (8 * b + 4 * (e >> 1 & 1) + 2 * (e & 1) + (e >> 2)) ^ 1
-    return place
-
-
-def logit_parts(router, tokens, out):
-    part = contract(router[...], tokens[...], 1, 0)
-    for i in range(out.shape[0]):
-        out[i] = part[:, i * LANES : (i + 1) * LANES]
-
-
-def add_spread(got, out, own):
+    column = lax.axis_index(E)
+    return [(b, e, seat(b, e, column)) for b in range(2) for e in range(n)]
+
+
+def logit_parts(router, tokens, out, left, right, sems):
+    n = right.shape[0]
+    cut = right.shape[2]
+    copies = [pltpu.make_async_copy(router, left, sems.at[n])]
+    for i in range(n):
+        block = tokens.at[:, pl.ds(i * cut, cut)]
+        copies.append(pltpu.make_async_copy(block, right.at[i], sems.at[i]))
+    for copy in copies:
+        copy.start()
+    copies[0].wait()
+    for i in range(n):
+        copies[i + 1].wait()
+        part = contract(left[...], right[i], 1, 0)
+        for j in range(cut // LANES):
+            out[i * (cut // LANES) + j] = part[:, j * LANES : (j + 1) * LANES]
+
+
+def split_weights(w_in, w_out, own_in, own_out, far_in, far_out, sems):
+    core = core_index()
+    half = own_in.shape[0]
+    copies = []
+    for i, (whole, own, far) in enumerate(((w_in, own_in, far_in), (w_out, own_out, far_out))):
+        for j, (part, place) in enumerate(((far, 1 - core), (own, core))):
+            block = whole.at[pl.ds(half * place, half)]
+            copies.append(pltpu.make_async_copy(block, part, sems.at[2 * i + j]))
+    for copy in copies:
+        copy.start()
+    for copy in copies:
+        copy.wait()
+
+
+def add_spread(got, out):
     total = jnp.sum(got[...], axis=0)
-    own[...] = total
     for e in range(out.shape[0]):
         out[e] = total
 
 
-def partial_rows(got, tokens, grad_out, mine, near, both):
+def partial_rows(got, tokens, grad_out, mine, near, shares, both):
     n, slots = got.shape[0], got.shape[1]
     logits = jnp.concatenate([got[e] for e in range(n)], axis=1)
     raised = jnp.exp(logits - jnp.max(logits, axis=0, keepdims=True))
     combine = raised / jnp.sum(raised, axis=0, keepdims=True)
+    shares[...] = combine
     top = jnp.max(logits, axis=1, keepdims=True)
     raised = jnp.exp(logits - top)
     total = jnp.sum(raised, axis=1, keepdims=True)
     rows_in = contract(raised, tokens[...], 1, 1)
-    rows_out = contract(combine, grad_out[...], 1, 1)
+    rows_out = contract(combine, grad_out[...], 1, 1, THREE)
     piece = rows_in.shape[1] // 2
     lane = lane_of((slots, LANES))
     marks = jnp.where(lane == piece, top, jnp.where(lane == piece + 1, total, 0.0))
     plain = jnp.where(lane_of((4, LANES)) == piece + 1, 1.0, 0.0)
-    for (b, e), k in seats(n).items():
+    for b, e, k in seats(n):
         for c in range(2):
             s, w = slice(8 * e + 4 * c, 8 * e + 4 * c + 4), slice(b * piece, (b + 1) * piece)
             both[c, k, 0:4] = marks[s]
@@ -215,14 +251,13 @@
         out[k] = value
 
 
-def width_products(mine, near, tokens, grad_out, out, rows, marks, outs):
+def width_products(mine, near, tokens, grad_out, logits, shares, out, weights, rows, outs, marks):
     n = out.shape[0]
-    slots = rows.shape[0]
     piece = rows.shape[1] // 2
     core = core_index()
     added = []
     for c in range(2):
-        for (b, e), k in seats(n).items():
+        for b, e, k in seats(n):
             tile = jnp.where(core == c, mine[k], near[k])
             s, w = slice(8 * e + 4 * c, 8 * e + 4 * c + 4), slice(b * piece, (b + 1) * piece)
             outs[s, w] = tile[0:4, 0:piece]
@@ -234,31 +269,23 @@
     lane = lane_of((4, LANES))
     for s, column in added:
         marks[s] = marks[s] + jnp.where(lane == piece + 2, column, 0.0)
-    combine = contract(outs[...], grad_out[...], 1, 0)
-    dispatch = contract(rows[...], tokens[...], 1, 0) - marks[:, piece + 2 : piece + 3]
+    top, total, column = (marks[:, piece + i : piece + i + 1] for i in range(3))
+    first = contract(outs[...], grad_out[...], 1, 0, THREE)
+    second = contract(rows[...], tokens[...], 1, 0) - column
     for i in range(n):
         s = slice(i * LANES, (i + 1) * LANES)
-        out[i, 0:slots] = combine[:, s]
-        out[i, slots:] = dispatch[:, s]
-
-
-def logit_grads(got, own, marks, out, piece):
-    slots = own.shape[0]
-    total = jnp.sum(got[...], axis=0)
-    logits = own[...]
-    raised = jnp.exp(logits - jnp.max(logits, axis=0, keepdims=True))
-    combine = raised / jnp.sum(raised, axis=0, keepdims=True)
-    dispatch = jnp.exp(logits - marks[:, piece : piece + 1]) / marks[:, piece + 1 : piece + 2]
-    first, second = total[:slots], total[slots:]
-    grads = combine * (first - jnp.sum(combine * first, axis=0, keepdims=True)) + dispatch * second
-    for e in range(out.shape[0]):
-        out[e] = grads
+        combine = shares[:, s]
+        dispatch = jnp.exp(logits[i] - top) / total
+        weights[i] = dispatch
+        part = combine * first[:, s]
+        line = jnp.sum(part, axis=0, keepdims=True)
+        out[i] = part - combine * line + dispatch * second[:, s]
 
 
 def router_part(got, tokens, mine, theirs):
     n = got.shape[0]
     grads = jnp.concatenate([got[e] for e in range(n)], axis=1)
-    part = contract(tokens[...], grads, 1, 1)
+    part = contract(tokens[...], grads, 1, 1, THREE)
     q = part.shape[0] // 4
     low = jnp.concatenate([part[0:q], part[q : 2 * q]], axis=1)
     high = jnp.concatenate([part[2 * q : 3 * q], part[3 * q :]], axis=1)
@@ -267,13 +294,11 @@
     theirs[...] = jnp.where(core == 0, high, low)
 
 
-def token_grads(got, logits, rows, marks, router, out, piece):
+def token_grads(got, weights, rows, router, out):
     left = jnp.transpose(jnp.concatenate([router[...], rows[...]], axis=0))
-    top, total = marks[:, piece : piece + 1], marks[:, piece + 1 : piece + 2]
     for e in range(got.shape[0]):
-        dispatch = jnp.exp(logits[e] - top) / total
-        right = jnp.concatenate([got[e], dispatch], axis=0)
-        out[:, e * LANES : (e + 1) * LANES] = contract(left, right, 1, 0)
+        right = jnp.concatenate([got[e], weights[e]], axis=0)
+        out[:, e * LANES : (e + 1) * LANES] = contract(left, right, 1, 0, THREE)
 
 
 def add_copies(mine, theirs, out):
@@ -330,9 +355,11 @@
     partner = [(i, i ^ 1) for i in range(n_seq)]
     groups = [[2 * k + c for k in range(chips)] for c in range(2)]
     turned = router.T
+    spread = (n_exp, slots, LANES)
     to_owner = [
-        ((2 * k + c) * n_exp + f, (2 * (2 * f + b) + c) * n_exp + e)
-        for (b, e), k in seats(n_exp).items()
+        ((2 * seat(b, e, f) + c) * n_exp + f, (2 * (2 * f + b) + c) * n_exp + e)
+        for b in range(2)
+        for e in range(n_exp)
         for c in range(2)
         for f in range(n_exp)
     ]
@@ -341,27 +368,46 @@
     def to_partner(values):
         return lax.ppermute(values, S, partner)
 
-    sent = run(logit_parts, (n_exp, slots, LANES), turned, tokens)
-    sent, own = run(
-        add_spread, [(n_exp, slots, LANES), (slots, LANES)], exchange(sent, E)
-    )
+    any_spec = pl.BlockSpec(memory_space=pl.ANY)
+    vmem_spec = pl.BlockSpec(memory_space=pltpu.VMEM)
+    limit = pltpu.CompilerParams(vmem_limit_bytes=40 * 1024 * 1024)
+    sent = pl.pallas_call(
+        logit_parts,
+        out_shape=jax.ShapeDtypeStruct(spread, F32),
+        in_specs=[any_spec, any_spec],
+        out_specs=vmem_spec,
+        scratch_shapes=[
+            pltpu.VMEM(turned.shape, F32),
+            pltpu.VMEM((4, rows_block, local_tokens // 4), F32),
+            pltpu.SemaphoreType.DMA((5,)),
+        ],
+        compiler_params=pltpu.CompilerParams(vmem_limit_bytes=60 * 1024 * 1024),
+    )(turned, tokens)
+    sent = run(add_spread, spread, exchange(sent, E))
+    sent, w_in, w_out = lax.optimization_barrier((sent, w_in, w_out))
     logits = exchange(sent, E)
-    half = experts // 2
-
-    def split(w):
-        own = lax.dynamic_slice_in_dim(w, half * core, half, 0)
-        return own, to_partner(lax.dynamic_slice_in_dim(w, half * (1 - core), half, 0))
-
-    own_in, near_in = split(w_in)
-    own_out, near_out = split(w_out)
-    logits, own_in, own_out, near_in, near_out = lax.optimization_barrier(
-        (logits, own_in, own_out, near_in, near_out)
-    )
-    weights = (own_in, own_out, near_in, near_out)
+    half = (experts // 2,) + w_in.shape[1:]
+    own_in, own_out, far_in, far_out = pl.pallas_call(
+        split_weights,
+        out_shape=[jax.ShapeDtypeStruct(half, F32)] * 4,
+        in_specs=[any_spec, any_spec],
+        out_specs=[vmem_spec, vmem_spec, any_spec, any_spec],
+        scratch_shapes=[pltpu.SemaphoreType.DMA((4,))],
+        compiler_params=limit,
+    )(w_in, w_out)
+    logits, own_in, own_out, far_in, far_out = lax.optimization_barrier(
+        (logits, own_in, own_out, far_in, far_out)
+    )
+    weights = (own_in, own_out, to_partner(far_in), to_partner(far_out))
 
     tiles = (chips, 8, LANES)
-    mine, near = run(
-        partial_rows, [tiles, tiles], logits, tokens, grad_out, scratch=[(2,) + tiles]
+    mine, near, shares = run(
+        partial_rows,
+        [tiles, tiles, (slots, local_tokens)],
+        logits,
+        tokens,
+        grad_out,
+        scratch=[(2,) + tiles],
     )
     sent = run(functools.partial(merge_cores, piece=piece), tiles, mine, to_partner(near))
     tile = run(
@@ -383,48 +429,37 @@
     sent = run(copies, tiles, lax.ppermute(tile, (S, E), from_owner))
     mine = exchange(sent, S, groups)
     near = to_partner(mine)
-    sent, rows, marks = run(
+    sent, weights, rows = run(
         width_products,
-        [(n_exp, 2 * slots, LANES), (slots, rows_block), (slots, LANES)],
+        [spread, spread, (slots, rows_block)],
         mine,
         near,
         tokens,
         grad_out,
-        scratch=[(slots, rows_block)],
-    )
-    sent = run(
-        functools.partial(logit_grads, piece=piece),
-        (n_exp, slots, LANES),
-        exchange(sent, E),
-        own,
-        marks,
-    )
+        logits,
+        shares,
+        scratch=[(slots, rows_block), (slots, LANES)],
+    )
+    sent = run(add_spread, spread, exchange(sent, E))
+    sent, full, held = lax.optimization_barrier((sent, full, held))
     grads = exchange(sent, E)
+    grad_w_in, grad_w_out = run(
+        weight_grads,
+        [w_in.shape, w_out.shape],
+        full,
+        to_partner(full),
+        held,
+        to_partner(held),
+    )
+    grads, grad_w_in, grad_w_out = lax.optimization_barrier((grads, grad_w_in, grad_w_out))
     fold = (rows_block // 4, 2 * slots)
     near, theirs = run(router_part, [fold, fold], grads, tokens)
     sent = run(add_copies, (chips,) + fold, near, to_partner(theirs))
-    near_full = to_partner(full)
-    near_held = to_partner(held)
-    sent, grads, full, near_full, near_held = lax.optimization_barrier(
-        (sent, grads, full, near_full, near_held)
-    )
-    got = exchange(sent, S, groups)
-    grad_w_in, grad_w_out = run(
-        weight_grads, [w_in.shape, w_out.shape], full, near_full, held, near_held
-    )
+    got, weights, rows = lax.optimization_barrier((exchange(sent, S, groups), weights, rows))
+    near = run(add_all, fold, got)
     grad_tokens = run(
-        functools.partial(token_grads, piece=piece),
-        (rows_block, local_tokens),
-        grads,
-        logits,
-        rows,
-        marks,
-        turned,
-    )
-    got, grad_w_in, grad_w_out, grad_tokens = lax.optimization_barrier(
-        (got, grad_w_in, grad_w_out, grad_tokens)
-    )
-    near = run(add_all, fold, got)
+        token_grads, (rows_block, local_tokens), grads, weights, rows, turned
+    )
     grad_router = run(unfold, (slots, rows_block), near, to_partner(near)).T
     return (grad_tokens, grad_router, grad_w_in, grad_w_out)
 

time: 163 us -> 159 us (0.975)
  waiting for transfers between devices: 20.2 us -> 13.9 us
  local copies, waits for them, and re-layouts: 2.2 us -> 6.49 us
  starting transfers between devices: 31 us -> 28.1 us
  Pallas kernels: 14.2 us -> 16.2 us
    all_to_all x2, waiting for transfers between devices: 12.3 us -> 3.06 us  [exchange(): lax.all_to_all(blocks, axis, 0, 0, axis_index_groups=groups, tiled=True)]
    unnamed x8 -> x16, local copies, waits for them, and re-layouts: 0.02 us -> 6.49 us
    pallas_call x0 -> x2, Pallas kernels: none -> 3.85 us  [the longest x1 2.85 us: per_device(): pl.pallas_call(logit_parts, out_shape=jax.ShapeDtypeStruct(spread, F32),...]
    ppermute x8, starting transfers between devices: 22.1 us -> 18.8 us  [to_partner(): return lax.ppermute(values, S, partner)]
    ppermute x1, waiting for transfers between devices: 1.63 us -> 4.63 us  [per_device(): lax.ppermute(tile, (S, E), to_owner)]
    dynamic_slice x2 -> x0, local copies, waits for them, and re-layouts: 2.18 us -> none  [split(): lax.dynamic_slice_in_dim(w, half * (1 - core), half, 0)]
    pallas_call x17 -> x16, Pallas kernels: 14.2 us -> 12.3 us  [run(): pl.pallas_call(kernel, out_shape=[jax.ShapeDtypeStruct(s, F32) for s in s...]
where the time goes in v5:
time: 159 us; the launch traced here: 158 us
  blocking collectives  92.7 us (58%)
  starting transfers between devices  28.1 us (18%)
  Pallas kernels  16.2 us (10%)
  waiting for transfers between devices  13.9 us (9%)
  local copies, waits for them, and re-layouts  6.49 us (4%)
    all_to_all x7, blocking collectives, exchange(): lax.all_to_all(blocks, axis, 0, 0, axis_index_groups=groups, tiled=True)  92.7 us
    ppermute x8, starting transfers between devices, to_partner(): return lax.ppermute(values, S, partner)  18.8 us
    pallas_call x16, Pallas kernels, run(): pl.pallas_call(kernel, out_shape=[jax.ShapeDtypeStruct(s, F32) for s in s...  12.3 us
    all_to_all x2, starting transfers between devices, exchange(): lax.all_to_all(blocks, axis, 0, 0, axis_index_groups=groups, tiled=True)  6.83 us
    unnamed x16, local copies, waits for them, and re-layouts  6.49 us
    ppermute x1, waiting for transfers between devices, per_device(): lax.ppermute(tile, (S, E), to_owner)  4.63 us
    ppermute x8, waiting for transfers between devices, to_partner(): return lax.ppermute(values, S, partner)  3.74 us
  transfers between devices with their start and end apart: 12, of which 8 were waited for; matrix products, arithmetic and copies ran while one was open for 0% of the time, Pallas kernels for 4%

profile of v5, /device:TPU:1, one launch (start us, length us, event | category | flops | bytes accessed | tf_op | source)
XLA Modules:
  0.0 158.1 jit_solution(15400631822270671296)
XLA Ops:
  0.6 2.9 %shard_map.84 = f32[8,64,128]{2,1,0:T(8,128)} custom-call(f32[64,192]{1,0:T(8,128)} %bitcast.2, f32[192,1024]{1,0:T(8,128)} %tokens.7), custom_call_target="tpu_custom_call" | custom-call | tf_op jit(solution)/shard_map/pallas_call | solution.py:374
  3.5 15.1 %all_to_all.45.got = f32[8,64,128]{2,1,0:T(8,128)S(1)} all-to-all(f32[8,64,128]{2,1,0:T(8,128)} %shard_map.84), channel_id=1, replica_groups=mesh['seq'=32,'expert'=8] {'expert'}, dimensions={0} | all-to-all | bytes 524288 | tf_op jit(solution)/shard_map/all_to_all | solution.py:29
  19.3 3.4 %all-to-all-start.1 = ((f32[8,64,128]{2,1,0:T(8,128)}), f32[8,64,128]{2,1,0:T(8,128)S(1)}, u32[]{:S(2)}, u32[]{:S(2)}) async-start(f32[8,64,128]{2,1,0:T(8,128)} %shard_map.85), calls=%async_computation.1 | async-start | bytes 524288 | tf_op jit(solution)/shard_map/all_to_all | solution.py:29
  22.8 1.7 %copy-done.3 = f32[4,48,3072]{2,1,0:T(8,128)S(1)} copy-done((f32[4,48,3072]{2,1,0:T(8,128)S(1)}, f32[4,48,3072]{2,1,0:T(8,128)}, u32[]{:S(2)}) %copy-start.3) | copy-done | bytes 2359320
  24.4 1.7 %copy-done.4 = f32[4,48,3072]{2,1,0:T(8,128)S(1)} copy-done((f32[4,48,3072]{2,1,0:T(8,128)S(1)}, f32[4,48,3072]{2,1,0:T(8,128)}, u32[]{:S(2)}) %copy-start.4) | copy-done | bytes 2359320
  26.1 1.0 shard_map.86
  27.1 1.0 copy-done.6
  28.1 1.0 copy-done.7
  29.1 1.4 all-to-all-done.1.got.logits
  30.6 3.0 %collective-permute-start.2 = (f32[2,48,3072]{2,1,0:T(8,128)}, f32[2,48,3072]{2,1,0:T(8,128)S(1)}, u32[]{:S(2)}, u32[]{:S(2)}) collective-permute-start(f32[2,48,3072]{2,1,0:T(8,128)} %copy-done.7), channel_id=1, source_target_pairs={{0,8},{8,0},{16,24},{24,16},{32,40},{40,32},{48,56},{56,48},{64,72... | collective-permute-start | bytes 3538952 | tf_op jit(solution)/shard_map/ppermute | solution.py:369
  33.6 1.1 copy-done.1
  34.7 1.4 shard_map.87
  36.8 1.1 collective-permute-done.near
  38.0 15.5 %all_to_all.46.got = f32[16,8,128]{2,1,0:T(8,128)S(1)} all-to-all(f32[16,8,128]{2,1,0:T(8,128)S(1)} %shard_map.88), channel_id=1, replica_groups={{0,16,32,48,64,80,96,112,128,144,160,176,192,208,224,240},{8,24,40,56,7..., dimensions={0} | all-to-all | bytes 131072 | tf_op jit(solution)/shard_map/all_to_all | solution.py:29
  54.5 4.6 %collective-permute-done.1.got = f32[8,128]{1,0:T(8,128)S(1)} collective-permute-done((f32[8,128]{1,0:T(8,128)S(1)}, f32[8,128]{1,0:T(8,128)S(1)}, u32[]{:S(2)}, u32[]{:S(2)}) %collective-permute-start.1) | collective-permute-done | bytes 4128 | tf_op jit(solution)/shard_map/ppermute | solution.py:421
  59.1 1.3 shard_map.90
  60.4 11.8 %all_to_all.47.got = f32[16,8,256]{2,1,0:T(8,128)S(1)} all-to-all(f32[16,8,256]{2,1,0:T(8,128)S(1)} %get-tuple-element.53), channel_id=1, replica_groups={{0,16,32,48,64,80,96,112,128,144,160,176,192,208,224,240},{8,24,40,56,7..., dimensions={0} | all-to-all | bytes 262144 | tf_op jit(solution)/shard_map/all_to_all | solution.py:29
  72.2 10.5 %all_to_all.48.got = f32[16,8,256]{2,1,0:T(8,128)S(1)} all-to-all(f32[16,8,256]{2,1,0:T(8,128)S(1)} %shard_map.91), channel_id=1, replica_groups={{0,16,32,48,64,80,96,112,128,144,160,176,192,208,224,240},{8,24,40,56,7..., dimensions={0} | all-to-all | bytes 262144 | tf_op jit(solution)/shard_map/all_to_all | solution.py:29
  82.7 1.1 shard_map.92
  83.9 1.5 collective-permute-start.4
  85.4 2.5 %collective-permute-done.4.tile = f32[8,128]{1,0:T(8,128)S(1)} collective-permute-done((f32[8,128]{1,0:T(8,128)S(1)}, f32[8,128]{1,0:T(8,128)S(1)}, u32[]{:S(2)}, u32[]{:S(2)}) %collective-permute-start.4) | collective-permute-done | bytes 4128 | tf_op jit(solution)/shard_map/ppermute | solution.py:429
  87.9 14.0 %all_to_all.49.mine = f32[16,8,128]{2,1,0:T(8,128)S(1)} all-to-all(f32[16,8,128]{2,1,0:T(8,128)S(1)} %shard_map.93), channel_id=1, replica_groups={{0,16,32,48,64,80,96,112,128,144,160,176,192,208,224,240},{8,24,40,56,7..., dimensions={0} | all-to-all | bytes 131072 | tf_op jit(solution)/shard_map/all_to_all | solution.py:29
  101.9 7.5 %collective-permute-start.5 = (f32[16,8,128]{2,1,0:T(8,128)S(1)}, f32[16,8,128]{2,1,0:T(8,128)S(1)}, u32[]{:S(2)}, u32[]{:S(2)}) collective-permute-start(f32[16,8,128]{2,1,0:T(8,128)S(1)} %all_to_all.49.mine), channel_id=1, source_target_pairs={{0,8},{8,0},{16,24},{24,16},{32,40},{40,32},{48,56},{56,48},{64,72... | collective-permute-start | bytes 196616 | tf_op jit(solution)/shard_map/ppermute | solution.py:369
  111.2 11.9 %all_to_all.50.got = f32[8,64,128]{2,1,0:T(8,128)S(1)} all-to-all(f32[8,64,128]{2,1,0:T(8,128)S(1)} %get-tuple-element.57), channel_id=1, replica_groups=mesh['seq'=32,'expert'=8] {'expert'}, dimensions={0} | all-to-all | bytes 524288 | tf_op jit(solution)/shard_map/all_to_all | solution.py:29
  123.9 3.4 %all-to-all-start.7 = ((f32[8,64,128]{2,1,0:T(8,128)}), f32[8,64,128]{2,1,0:T(8,128)S(1)}, u32[]{:S(2)}, u32[]{:S(2)}) async-start(f32[8,64,128]{2,1,0:T(8,128)} %shard_map.95), calls=%async_computation.7 | async-start | bytes 524288 | tf_op jit(solution)/shard_map/all_to_all | solution.py:29
  127.3 1.9 %collective-permute-start.6 = (f32[8,3072]{1,0:T(8,128)S(1)}, f32[8,3072]{1,0:T(8,128)S(1)}, u32[]{:S(2)}, u32[]{:S(2)}) collective-permute-start(f32[8,3072]{1,0:T(8,128)S(1)} %get-tuple-element.60.full), channel_id=1, source_target_pairs={{0,8},{8,0},{16,24},{24,16},{32,40},{40,32},{48,56},{56,48},{64,72... | collective-permute-start | bytes 294920 | tf_op jit(solution)/shard_map/ppermute | solution.py:369
  130.4 3.0 %shard_map.96 = (f32[4,48,3072]{2,1,0:T(8,128)}, f32[4,48,3072]{2,1,0:T(8,128)}) custom-call(f32[8,3072]{1,0:T(8,128)S(1)} %get-tuple-element.60.full, f32[8,3072]{1,0:T(8,128)S(1)} %collective-permute-done.6.near_full, f32[8,128]{1,0:T(8,128)S(1)} %get-tuple-element.61.keep, f32[8,128]{1,0:T(8,128)S(1)} %collective-permute-done.7.near_keep), custom_call_target="tpu_custom_call" | custom-call | bytes 4923392 | tf_op jit(solution)/shard_map/pallas_call | solution.py:37
  133.4 1.6 %all-to-all-done.7.got = f32[8,64,128]{2,1,0:T(8,128)S(1)} async-done(((f32[8,64,128]{2,1,0:T(8,128)}), f32[8,64,128]{2,1,0:T(8,128)S(1)}, u32[]{:S(2)}, u32[]{:S(2)}) %all-to-all-start.7) | async-done | bytes 262176 | tf_op jit(solution)/shard_map/all_to_all | solution.py:29
  135.6 2.9 %collective-permute-start.8 = (f32[48,128]{1,0:T(8,128)S(1)}, f32[48,128]{1,0:T(8,128)S(1)}, u32[]{:S(2)}, u32[]{:S(2)}) collective-permute-start(f32[48,128]{1,0:T(8,128)S(1)} %get-tuple-element.66), channel_id=1, source_target_pairs={{0,8},{8,0},{16,24},{24,16},{32,40},{40,32},{48,56},{56,48},{64,72... | collective-permute-start | bytes 73736 | tf_op jit(solution)/shard_map/ppermute | solution.py:369
  139.3 13.9 %all_to_all.51.got = f32[16,48,128]{2,1,0:T(8,128)S(1)} all-to-all(f32[16,48,128]{2,1,0:T(8,128)S(1)} %shard_map.98), channel_id=1, replica_groups={{0,16,32,48,64,80,96,112,128,144,160,176,192,208,224,240},{8,24,40,56,7..., dimensions={0} | all-to-all | bytes 786432 | tf_op jit(solution)/shard_map/all_to_all | solution.py:29
  153.3 2.6 %collective-permute-start.9 = (f32[48,128]{1,0:T(8,128)S(1)}, f32[48,128]{1,0:T(8,128)S(1)}, u32[]{:S(2)}, u32[]{:S(2)}) collective-permute-start(f32[48,128]{1,0:T(8,128)S(1)} %shard_map.100.mine), channel_id=1, source_target_pairs={{0,8},{8,0},{16,24},{24,16},{32,40},{40,32},{48,56},{56,48},{64,72... | collective-permute-start | bytes 73736 | tf_op jit(solution)/shard_map/ppermute | solution.py:369
  155.9 1.4 shard_map.99
  (33 shorter events, 8.5 us)
Async XLA Ops:
  19.3 11.2 %all-to-all-start.1 = ((f32[8,64,128]{2,1,0:T(8,128)}), f32[8,64,128]{2,1,0:T(8,128)S(1)}, u32[]{:S(2)}, u32[]{:S(2)}) async-start(f32[8,64,128]{2,1,0:T(8,128)} %shard_map.85), calls=%async_computation.1 | async-start | bytes 524288 | tf_op jit(solution)/shard_map/all_to_all | solution.py:29
  22.8 1.7 %copy-start.3 = (f32[4,48,3072]{2,1,0:T(8,128)S(1)}, f32[4,48,3072]{2,1,0:T(8,128)}, u32[]{:S(2)}) copy-start(f32[4,48,3072]{2,1,0:T(8,128)} %w_in) | copy-start | bytes 7077892
  24.4 1.7 %copy-start.4 = (f32[4,48,3072]{2,1,0:T(8,128)S(1)}, f32[4,48,3072]{2,1,0:T(8,128)}, u32[]{:S(2)}) copy-start(f32[4,48,3072]{2,1,0:T(8,128)} %w_out) | copy-start | bytes 7077892
  26.1 7.5 %copy-start = (f32[192,1024]{1,0:T(8,128)S(1)}, f32[192,1024]{1,0:T(8,128)}, u32[]{:S(2)}) copy-start(f32[192,1024]{1,0:T(8,128)} %tokens.7) | copy-start | bytes 2359300
  27.1 1.0 copy-start.6
  28.1 1.0 copy-start.7
  30.6 28.6 %collective-permute-start.2 = (f32[2,48,3072]{2,1,0:T(8,128)}, f32[2,48,3072]{2,1,0:T(8,128)S(1)}, u32[]{:S(2)}, u32[]{:S(2)}) collective-permute-start(f32[2,48,3072]{2,1,0:T(8,128)} %copy-done.7), channel_id=1, source_target_pairs={{0,8},{8,0},{16,24},{24,16},{32,40},{40,32},{48,56},{56,48},{64,72... | collective-permute-start | bytes 3538952 | tf_op jit(solution)/shard_map/ppermute | solution.py:369
  33.6 25.5 %collective-permute-start.3 = (f32[2,48,3072]{2,1,0:T(8,128)}, f32[2,48,3072]{2,1,0:T(8,128)S(1)}, u32[]{:S(2)}, u32[]{:S(2)}) collective-permute-start(f32[2,48,3072]{2,1,0:T(8,128)} %copy-done.6), channel_id=1, source_target_pairs={{0,8},{8,0},{16,24},{24,16},{32,40},{40,32},{48,56},{56,48},{64,72... | collective-permute-start | bytes 3538952 | tf_op jit(solution)/shard_map/ppermute | solution.py:369
  33.6 1.1 copy-start.1
  36.2 1.7 %collective-permute-start = (f32[16,8,128]{2,1,0:T(8,128)S(1)}, f32[16,8,128]{2,1,0:T(8,128)S(1)}, u32[]{:S(2)}, u32[]{:S(2)}) collective-permute-start(f32[16,8,128]{2,1,0:T(8,128)S(1)} %get-tuple-element.48), channel_id=1, source_target_pairs={{0,8},{8,0},{16,24},{24,16},{32,40},{40,32},{48,56},{56,48},{64,72... | collective-permute-start | bytes 196616 | tf_op jit(solution)/shard_map/ppermute | solution.py:369
  53.6 5.5 %collective-permute-start.1 = (f32[8,128]{1,0:T(8,128)S(1)}, f32[8,128]{1,0:T(8,128)S(1)}, u32[]{:S(2)}, u32[]{:S(2)}) collective-permute-start(f32[8,128]{1,0:T(8,128)S(1)} %shard_map.89), channel_id=1, source_target_pairs={{80,0},{241,32},{34,64},{195,96},{132,128},{37,160},{182,192},{87,... | collective-permute-start | bytes 12296 | tf_op jit(solution)/shard_map/ppermute | solution.py:421
  82.7 27.6 %copy-start.2 = (f32[192,1024]{1,0:T(8,128)S(1)}, f32[192,1024]{1,0:T(8,128)}, u32[]{:S(2)}) copy-start(f32[192,1024]{1,0:T(8,128)} %grad_out.3) | copy-start | bytes 2359300
  83.9 4.0 %collective-permute-start.4 = (f32[8,128]{1,0:T(8,128)S(1)}, f32[8,128]{1,0:T(8,128)S(1)}, u32[]{:S(2)}, u32[]{:S(2)}) collective-permute-start(f32[8,128]{1,0:T(8,128)S(1)} %get-tuple-element.55), channel_id=1, source_target_pairs={{0,80},{32,241},{64,34},{96,195},{128,132},{160,37},{192,182},{224... | collective-permute-start | bytes 12296 | tf_op jit(solution)/shard_map/ppermute | solution.py:429
  101.9 8.4 %collective-permute-start.5 = (f32[16,8,128]{2,1,0:T(8,128)S(1)}, f32[16,8,128]{2,1,0:T(8,128)S(1)}, u32[]{:S(2)}, u32[]{:S(2)}) collective-permute-start(f32[16,8,128]{2,1,0:T(8,128)S(1)} %all_to_all.49.mine), channel_id=1, source_target_pairs={{0,8},{8,0},{16,24},{24,16},{32,40},{40,32},{48,56},{56,48},{64,72... | collective-permute-start | bytes 196616 | tf_op jit(solution)/shard_map/ppermute | solution.py:369
  123.9 11.1 %all-to-all-start.7 = ((f32[8,64,128]{2,1,0:T(8,128)}), f32[8,64,128]{2,1,0:T(8,128)S(1)}, u32[]{:S(2)}, u32[]{:S(2)}) async-start(f32[8,64,128]{2,1,0:T(8,128)} %shard_map.95), calls=%async_computation.7 | async-start | bytes 524288 | tf_op jit(solution)/shard_map/all_to_all | solution.py:29
  127.3 3.1 %collective-permute-start.6 = (f32[8,3072]{1,0:T(8,128)S(1)}, f32[8,3072]{1,0:T(8,128)S(1)}, u32[]{:S(2)}, u32[]{:S(2)}) collective-permute-start(f32[8,3072]{1,0:T(8,128)S(1)} %get-tuple-element.60.full), channel_id=1, source_target_pairs={{0,8},{8,0},{16,24},{24,16},{32,40},{40,32},{48,56},{56,48},{64,72... | collective-permute-start | bytes 294920 | tf_op jit(solution)/shard_map/ppermute | solution.py:369
  129.2 1.2 collective-permute-start.7
  135.0 20.9 %copy-start.5 = (f32[192,64]{0,1:T(8,128)S(1)}, f32[192,64]{0,1:T(8,128)}, u32[]{:S(2)}) copy-start(f32[192,64]{0,1:T(8,128)} %param.6) | copy-start | bytes 147460
  135.6 3.8 %collective-permute-start.8 = (f32[48,128]{1,0:T(8,128)S(1)}, f32[48,128]{1,0:T(8,128)S(1)}, u32[]{:S(2)}, u32[]{:S(2)}) collective-permute-start(f32[48,128]{1,0:T(8,128)S(1)} %get-tuple-element.66), channel_id=1, source_target_pairs={{0,8},{8,0},{16,24},{24,16},{32,40},{40,32},{48,56},{56,48},{64,72... | collective-permute-start | bytes 73736 | tf_op jit(solution)/shard_map/ppermute | solution.py:369
  153.3 4.1 %collective-permute-start.9 = (f32[48,128]{1,0:T(8,128)S(1)}, f32[48,128]{1,0:T(8,128)S(1)}, u32[]{:S(2)}, u32[]{:S(2)}) collective-permute-start(f32[48,128]{1,0:T(8,128)S(1)} %shard_map.100.mine), channel_id=1, source_target_pairs={{0,8},{8,0},{16,24},{24,16},{32,40},{40,32},{48,56},{56,48},{64,72... | collective-permute-start | bytes 73736 | tf_op jit(solution)/shard_map/ppermute | solution.py:369

commit v6 on v5

--- a/solution.py
+++ b/solution.py
@@ -80,9 +80,9 @@
     return [(b, e, seat(b, e, column)) for b in range(2) for e in range(n)]
 
 
-def logit_parts(router, tokens, out, left, right, sems):
-    n = right.shape[0]
-    cut = right.shape[2]
+def logit_parts(router, tokens, out, left, right, parts, sems, stores):
+    n, _, cut = right.shape
+    each = cut // LANES
     copies = [pltpu.make_async_copy(router, left, sems.at[n])]
     for i in range(n):
         block = tokens.at[:, pl.ds(i * cut, cut)]
@@ -90,21 +90,27 @@
     for copy in copies:
         copy.start()
     copies[0].wait()
+    moves = []
     for i in range(n):
         copies[i + 1].wait()
         part = contract(left[...], right[i], 1, 0)
-        for j in range(cut // LANES):
-            out[i * (cut // LANES) + j] = part[:, j * LANES : (j + 1) * LANES]
-
-
-def split_weights(w_in, w_out, own_in, own_out, far_in, far_out, sems):
+        for j in range(each):
+            parts[i * each + j] = part[:, j * LANES : (j + 1) * LANES]
+        s = pl.ds(i * each, each)
+        moves.append(pltpu.make_async_copy(parts.at[s], out.at[s], stores.at[i]))
+        moves[i].start()
+    for move in moves:
+        move.wait()
+
+
+def stage(w_in, w_out, tokens, grad_out, far_in, far_out, own_in, own_out, x, g, sems):
     core = core_index()
     half = own_in.shape[0]
-    copies = []
-    for i, (whole, own, far) in enumerate(((w_in, own_in, far_in), (w_out, own_out, far_out))):
-        for j, (part, place) in enumerate(((far, 1 - core), (own, core))):
-            block = whole.at[pl.ds(half * place, half)]
-            copies.append(pltpu.make_async_copy(block, part, sems.at[2 * i + j]))
+    pairs = [(tokens, x), (grad_out, g)]
+    for whole, own, far in ((w_in, own_in, far_in), (w_out, own_out, far_out)):
+        pairs.append((whole.at[pl.ds(half * (1 - core), half)], far))
+        pairs.append((whole.at[pl.ds(half * core, half)], own))
+    copies = [pltpu.make_async_copy(a, b, sems.at[i]) for i, (a, b) in enumerate(pairs)]
     for copy in copies:
         copy.start()
     for copy in copies:
@@ -368,36 +374,43 @@
     def to_partner(values):
         return lax.ppermute(values, S, partner)
 
-    any_spec = pl.BlockSpec(memory_space=pl.ANY)
+    def in_hbm(values):
+        return pltpu.with_memory_space_constraint(values, pltpu.HBM)
+
+    far_spec = pl.BlockSpec(memory_space=pltpu.HBM)
     vmem_spec = pl.BlockSpec(memory_space=pltpu.VMEM)
     limit = pltpu.CompilerParams(vmem_limit_bytes=40 * 1024 * 1024)
     sent = pl.pallas_call(
         logit_parts,
-        out_shape=jax.ShapeDtypeStruct(spread, F32),
-        in_specs=[any_spec, any_spec],
-        out_specs=vmem_spec,
+        out_shape=pltpu.HBM(spread, F32),
+        in_specs=[far_spec, far_spec],
+        out_specs=far_spec,
         scratch_shapes=[
             pltpu.VMEM(turned.shape, F32),
             pltpu.VMEM((4, rows_block, local_tokens // 4), F32),
+            pltpu.VMEM(spread, F32),
             pltpu.SemaphoreType.DMA((5,)),
+            pltpu.SemaphoreType.DMA((4,)),
         ],
-        compiler_params=pltpu.CompilerParams(vmem_limit_bytes=60 * 1024 * 1024),
-    )(turned, tokens)
-    sent = run(add_spread, spread, exchange(sent, E))
-    sent, w_in, w_out = lax.optimization_barrier((sent, w_in, w_out))
-    logits = exchange(sent, E)
+        compiler_params=limit,
+    )(in_hbm(turned), in_hbm(tokens))
+    sent, w_in, w_out, grad_out = lax.optimization_barrier((sent, w_in, w_out, grad_out))
+    got = exchange(sent, E)
     half = (experts // 2,) + w_in.shape[1:]
-    own_in, own_out, far_in, far_out = pl.pallas_call(
-        split_weights,
-        out_shape=[jax.ShapeDtypeStruct(half, F32)] * 4,
-        in_specs=[any_spec, any_spec],
-        out_specs=[vmem_spec, vmem_spec, any_spec, any_spec],
-        scratch_shapes=[pltpu.SemaphoreType.DMA((4,))],
+    staged = pl.pallas_call(
+        stage,
+        out_shape=[pltpu.HBM(half, F32)] * 2
+        + [pltpu.VMEM(half, F32)] * 2
+        + [pltpu.VMEM(tokens.shape, F32)] * 2,
+        in_specs=[far_spec] * 4,
+        out_specs=[far_spec] * 2 + [vmem_spec] * 4,
+        scratch_shapes=[pltpu.SemaphoreType.DMA((6,))],
         compiler_params=limit,
-    )(w_in, w_out)
-    logits, own_in, own_out, far_in, far_out = lax.optimization_barrier(
-        (logits, own_in, own_out, far_in, far_out)
-    )
+    )(in_hbm(w_in), in_hbm(w_out), in_hbm(tokens), in_hbm(grad_out))
+    got, far_in, far_out, own_in, own_out, tokens, grad_out = lax.optimization_barrier(
+        (got, *staged)
+    )
+    logits = exchange(run(add_spread, spread, got), E)
     weights = (own_in, own_out, to_partner(far_in), to_partner(far_out))
 
     tiles = (chips, 8, LANES)

time: 159 us -> 225 us (1.42)
  Pallas kernels: 16.2 us -> 87 us
  local copies, waits for them, and re-layouts: 6.49 us -> 0.88 us
  starting transfers between devices: 28.1 us -> 31.6 us
    pallas_call x2, Pallas kernels: 3.85 us -> 75.4 us  [the longest x1 72.6 us: per_device(): pl.pallas_call(stage, out_shape=[pltpu.HBM(half, F32)] * 2 + [pltpu.VMEM(...]
    unnamed x16 -> x6, local copies, waits for them, and re-layouts: 6.49 us -> 0.88 us
    all_to_all x2, starting transfers between devices: 6.83 us -> 10.9 us  [exchange(): lax.all_to_all(blocks, axis, 0, 0, axis_index_groups=groups, tiled=True)]
  transfers between devices with their start and end apart: 12 -> 12, of which waited for: 8 -> 7; matrix products, arithmetic and copies ran while one was open for 0% -> 0% of each run, Pallas kernels for 4% -> 35%
where the time goes in v6:
time: 225 us; the launch traced here: 224 us
  blocking collectives  92 us (41%)
  Pallas kernels  87 us (39%)
  starting transfers between devices  31.6 us (14%)
  waiting for transfers between devices  12.3 us (5%)
    all_to_all x7, blocking collectives, exchange(): lax.all_to_all(blocks, axis, 0, 0, axis_index_groups=groups, tiled=True)  92 us
    pallas_call x1, Pallas kernels, per_device(): pl.pallas_call(stage, out_shape=[pltpu.HBM(half, F32)] * 2 + [pltpu.VMEM(...  72.6 us
    ppermute x8, starting transfers between devices, to_partner(): return lax.ppermute(values, S, partner)  18.2 us
    pallas_call x16, Pallas kernels, run(): pl.pallas_call(kernel, out_shape=[jax.ShapeDtypeStruct(s, F32) for s in s...  11.6 us
    all_to_all x2, starting transfers between devices, exchange(): lax.all_to_all(blocks, axis, 0, 0, axis_index_groups=groups, tiled=True)  10.9 us
    ppermute x1, waiting for transfers between devices, per_device(): lax.ppermute(tile, (S, E), to_owner)  4.63 us
  transfers between devices with their start and end apart: 12, of which 7 were waited for; matrix products, arithmetic and copies ran while one was open for 0% of the time, Pallas kernels for 35%

profile of v6, /device:TPU:1, one launch (start us, length us, event | category | flops | bytes accessed | tf_op | source)
XLA Modules:
  0.0 224.4 jit_solution(17147495650877877087)
XLA Ops:
  0.6 2.8 %shard_map.84 = f32[8,64,128]{2,1,0:T(8,128)} custom-call(f32[64,192]{1,0:T(8,128)} %bitcast.2, f32[192,1024]{1,0:T(8,128)} %tokens.3), custom_call_target="tpu_custom_call" | custom-call | tf_op jit(solution)/shard_map/pallas_call | solution.py:383
  3.4 7.5 %all-to-all-start = ((f32[8,64,128]{2,1,0:T(8,128)}), f32[8,64,128]{2,1,0:T(8,128)S(1)}, u32[]{:S(2)}, u32[]{:S(2)}) async-start(f32[8,64,128]{2,1,0:T(8,128)} %shard_map.84), calls=%async_computation | async-start | bytes 524288 | tf_op jit(solution)/shard_map/all_to_all | solution.py:29
  10.9 72.6 %shard_map.85 = (f32[2,48,3072]{2,1,0:T(8,128)}, f32[2,48,3072]{2,1,0:T(8,128)}, f32[2,48,3072]{2,1,0:T(8,128)S(1)}, f32[2,48,3072]{2,1,0:T(8,128)S(1)}, f32[192...) custom-call(f32[4,48,3072]{2,1,0:T(8,128)} %w_in, f32[4,48,3072]{2,1,0:T(8,128)} %w_out, f32[192,1024]{1,0:T(8,128)} %tokens.3, ...), custom_call_target="tpu_custom_call" | custom-call | tf_op jit(solution)/shard_map/pallas_call | solution.py:400
  83.6 0.9 copy-done
  84.5 1.0 collective-permute-start.2
  85.5 14.6 %all_to_all.45.got.logits = f32[8,64,128]{2,1,0:T(8,128)S(1)} all-to-all(f32[8,64,128]{2,1,0:T(8,128)S(1)} %shard_map.86), channel_id=1, replica_groups=mesh['seq'=32,'expert'=8] {'expert'}, dimensions={0} | all-to-all | bytes 524288 | tf_op jit(solution)/shard_map/all_to_all | solution.py:29
  100.1 1.4 shard_map.87
  101.6 2.0 collective-permute-start
  103.5 0.9 collective-permute-done.near
  104.5 15.5 %all_to_all.46.got = f32[16,8,128]{2,1,0:T(8,128)S(1)} all-to-all(f32[16,8,128]{2,1,0:T(8,128)S(1)} %shard_map.88), channel_id=1, replica_groups={{0,16,32,48,64,80,96,112,128,144,160,176,192,208,224,240},{8,24,40,56,7..., dimensions={0} | all-to-all | bytes 131072 | tf_op jit(solution)/shard_map/all_to_all | solution.py:29
  120.2 0.9 collective-permute-start.1
  121.1 4.6 %collective-permute-done.1.got = f32[8,128]{1,0:T(8,128)S(1)} collective-permute-done((f32[8,128]{1,0:T(8,128)S(1)}, f32[8,128]{1,0:T(8,128)S(1)}, u32[]{:S(2)}, u32[]{:S(2)}) %collective-permute-start.1) | collective-permute-done | bytes 4128 | tf_op jit(solution)/shard_map/ppermute | solution.py:434
  125.7 1.2 shard_map.90
  126.9 11.8 %all_to_all.47.got = f32[16,8,256]{2,1,0:T(8,128)S(1)} all-to-all(f32[16,8,256]{2,1,0:T(8,128)S(1)} %get-tuple-element.63), channel_id=1, replica_groups={{0,16,32,48,64,80,96,112,128,144,160,176,192,208,224,240},{8,24,40,56,7..., dimensions={0} | all-to-all | bytes 262144 | tf_op jit(solution)/shard_map/all_to_all | solution.py:29
  138.7 10.5 %all_to_all.48.got = f32[16,8,256]{2,1,0:T(8,128)S(1)} all-to-all(f32[16,8,256]{2,1,0:T(8,128)S(1)} %shard_map.91), channel_id=1, replica_groups={{0,16,32,48,64,80,96,112,128,144,160,176,192,208,224,240},{8,24,40,56,7..., dimensions={0} | all-to-all | bytes 262144 | tf_op jit(solution)/shard_map/all_to_all | solution.py:29
  149.2 1.2 shard_map.92
  150.4 1.5 collective-permute-start.4
  151.9 2.5 %collective-permute-done.4.tile = f32[8,128]{1,0:T(8,128)S(1)} collective-permute-done((f32[8,128]{1,0:T(8,128)S(1)}, f32[8,128]{1,0:T(8,128)S(1)}, u32[]{:S(2)}, u32[]{:S(2)}) %collective-permute-start.4) | collective-permute-done | bytes 4128 | tf_op jit(solution)/shard_map/ppermute | solution.py:442
  154.4 14.0 %all_to_all.49.mine = f32[16,8,128]{2,1,0:T(8,128)S(1)} all-to-all(f32[16,8,128]{2,1,0:T(8,128)S(1)} %shard_map.93), channel_id=1, replica_groups={{0,16,32,48,64,80,96,112,128,144,160,176,192,208,224,240},{8,24,40,56,7..., dimensions={0} | all-to-all | bytes 131072 | tf_op jit(solution)/shard_map/all_to_all | solution.py:29
  168.4 7.5 %collective-permute-start.5 = (f32[16,8,128]{2,1,0:T(8,128)S(1)}, f32[16,8,128]{2,1,0:T(8,128)S(1)}, u32[]{:S(2)}, u32[]{:S(2)}) collective-permute-start(f32[16,8,128]{2,1,0:T(8,128)S(1)} %all_to_all.49.mine), channel_id=1, source_target_pairs={{0,8},{8,0},{16,24},{24,16},{32,40},{40,32},{48,56},{56,48},{64,72... | collective-permute-start | bytes 196616 | tf_op jit(solution)/shard_map/ppermute | solution.py:375
  175.9 0.9 collective-permute-done.5.near
  176.8 0.9 shard_map.94
  177.7 11.7 %all_to_all.50.got = f32[8,64,128]{2,1,0:T(8,128)S(1)} all-to-all(f32[8,64,128]{2,1,0:T(8,128)S(1)} %get-tuple-element.67), channel_id=1, replica_groups=mesh['seq'=32,'expert'=8] {'expert'}, dimensions={0} | all-to-all | bytes 524288 | tf_op jit(solution)/shard_map/all_to_all | solution.py:29
  190.2 3.4 %all-to-all-start.7 = ((f32[8,64,128]{2,1,0:T(8,128)}), f32[8,64,128]{2,1,0:T(8,128)S(1)}, u32[]{:S(2)}, u32[]{:S(2)}) async-start(f32[8,64,128]{2,1,0:T(8,128)} %shard_map.95), calls=%async_computation.7 | async-start | bytes 524288 | tf_op jit(solution)/shard_map/all_to_all | solution.py:29
  193.6 1.9 collective-permute-start.6
  195.7 0.9 collective-permute-done.7.near_keep
  196.6 3.0 %shard_map.96 = (f32[4,48,3072]{2,1,0:T(8,128)}, f32[4,48,3072]{2,1,0:T(8,128)}) custom-call(f32[8,3072]{1,0:T(8,128)S(1)} %get-tuple-element.70.full, f32[8,3072]{1,0:T(8,128)S(1)} %collective-permute-done.6.near_full, f32[8,128]{1,0:T(8,128)S(1)} %get-tuple-element.71.keep, f32[8,128]{1,0:T(8,128)S(1)} %collective-permute-done.7.near_keep), custom_call_target="tpu_custom_call" | custom-call | bytes 4923392 | tf_op jit(solution)/shard_map/pallas_call | solution.py:37
  199.7 1.6 all-to-all-done.7.got
  201.8 2.9 %collective-permute-start.8 = (f32[48,128]{1,0:T(8,128)S(1)}, f32[48,128]{1,0:T(8,128)S(1)}, u32[]{:S(2)}, u32[]{:S(2)}) collective-permute-start(f32[48,128]{1,0:T(8,128)S(1)} %get-tuple-element.76), channel_id=1, source_target_pairs={{0,8},{8,0},{16,24},{24,16},{32,40},{40,32},{48,56},{56,48},{64,72... | collective-permute-start | bytes 73736 | tf_op jit(solution)/shard_map/ppermute | solution.py:375
  205.6 13.9 %all_to_all.51.got = f32[16,48,128]{2,1,0:T(8,128)S(1)} all-to-all(f32[16,48,128]{2,1,0:T(8,128)S(1)} %shard_map.98), channel_id=1, replica_groups={{0,16,32,48,64,80,96,112,128,144,160,176,192,208,224,240},{8,24,40,56,7..., dimensions={0} | all-to-all | bytes 786432 | tf_op jit(solution)/shard_map/all_to_all | solution.py:29
  219.5 2.6 %collective-permute-start.9 = (f32[48,128]{1,0:T(8,128)S(1)}, f32[48,128]{1,0:T(8,128)S(1)}, u32[]{:S(2)}, u32[]{:S(2)}) collective-permute-start(f32[48,128]{1,0:T(8,128)S(1)} %shard_map.100.mine), channel_id=1, source_target_pairs={{0,8},{8,0},{16,24},{24,16},{32,40},{40,32},{48,56},{56,48},{64,72... | collective-permute-start | bytes 73736 | tf_op jit(solution)/shard_map/ppermute | solution.py:375
  222.2 1.4 shard_map.99
  (23 shorter events, 3.7 us)
Async XLA Ops:
  3.4 81.0 %all-to-all-start = ((f32[8,64,128]{2,1,0:T(8,128)}), f32[8,64,128]{2,1,0:T(8,128)S(1)}, u32[]{:S(2)}, u32[]{:S(2)}) async-start(f32[8,64,128]{2,1,0:T(8,128)} %shard_map.84), calls=%async_computation | async-start | bytes 524288 | tf_op jit(solution)/shard_map/all_to_all | solution.py:29
  83.6 0.9 copy-start
  84.5 15.7 %copy-start.1 = (f32[192,1024]{1,0:T(8,128)S(1)}, f32[192,1024]{1,0:T(8,128)}, u32[]{:S(2)}) copy-start(f32[192,1024]{1,0:T(8,128)} %copy-done) | copy-start | bytes 2359300
  84.5 41.2 %collective-permute-start.2 = (f32[2,48,3072]{2,1,0:T(8,128)}, f32[2,48,3072]{2,1,0:T(8,128)S(1)}, u32[]{:S(2)}, u32[]{:S(2)}) collective-permute-start(f32[2,48,3072]{2,1,0:T(8,128)} %get-tuple-element.61), channel_id=1, source_target_pairs={{0,8},{8,0},{16,24},{24,16},{32,40},{40,32},{48,56},{56,48},{64,72... | collective-permute-start | bytes 3538952 | tf_op jit(solution)/shard_map/ppermute | solution.py:375
  85.4 40.3 %collective-permute-start.3 = (f32[2,48,3072]{2,1,0:T(8,128)}, f32[2,48,3072]{2,1,0:T(8,128)S(1)}, u32[]{:S(2)}, u32[]{:S(2)}) collective-permute-start(f32[2,48,3072]{2,1,0:T(8,128)} %get-tuple-element.62), channel_id=1, source_target_pairs={{0,8},{8,0},{16,24},{24,16},{32,40},{40,32},{48,56},{56,48},{64,72... | collective-permute-start | bytes 3538952 | tf_op jit(solution)/shard_map/ppermute | solution.py:375
  101.6 2.9 %collective-permute-start = (f32[16,8,128]{2,1,0:T(8,128)S(1)}, f32[16,8,128]{2,1,0:T(8,128)S(1)}, u32[]{:S(2)}, u32[]{:S(2)}) collective-permute-start(f32[16,8,128]{2,1,0:T(8,128)S(1)} %get-tuple-element.58), channel_id=1, source_target_pairs={{0,8},{8,0},{16,24},{24,16},{32,40},{40,32},{48,56},{56,48},{64,72... | collective-permute-start | bytes 196616 | tf_op jit(solution)/shard_map/ppermute | solution.py:375
  120.2 5.5 %collective-permute-start.1 = (f32[8,128]{1,0:T(8,128)S(1)}, f32[8,128]{1,0:T(8,128)S(1)}, u32[]{:S(2)}, u32[]{:S(2)}) collective-permute-start(f32[8,128]{1,0:T(8,128)S(1)} %shard_map.89), channel_id=1, source_target_pairs={{80,0},{241,32},{34,64},{195,96},{132,128},{37,160},{182,192},{87,... | collective-permute-start | bytes 12296 | tf_op jit(solution)/shard_map/ppermute | solution.py:434
  150.4 4.0 %collective-permute-start.4 = (f32[8,128]{1,0:T(8,128)S(1)}, f32[8,128]{1,0:T(8,128)S(1)}, u32[]{:S(2)}, u32[]{:S(2)}) collective-permute-start(f32[8,128]{1,0:T(8,128)S(1)} %get-tuple-element.65), channel_id=1, source_target_pairs={{0,80},{32,241},{64,34},{96,195},{128,132},{160,37},{192,182},{224... | collective-permute-start | bytes 12296 | tf_op jit(solution)/shard_map/ppermute | solution.py:442
  168.4 8.4 %collective-permute-start.5 = (f32[16,8,128]{2,1,0:T(8,128)S(1)}, f32[16,8,128]{2,1,0:T(8,128)S(1)}, u32[]{:S(2)}, u32[]{:S(2)}) collective-permute-start(f32[16,8,128]{2,1,0:T(8,128)S(1)} %all_to_all.49.mine), channel_id=1, source_target_pairs={{0,8},{8,0},{16,24},{24,16},{32,40},{40,32},{48,56},{56,48},{64,72... | collective-permute-start | bytes 196616 | tf_op jit(solution)/shard_map/ppermute | solution.py:375
  190.2 11.1 %all-to-all-start.7 = ((f32[8,64,128]{2,1,0:T(8,128)}), f32[8,64,128]{2,1,0:T(8,128)S(1)}, u32[]{:S(2)}, u32[]{:S(2)}) async-start(f32[8,64,128]{2,1,0:T(8,128)} %shard_map.95), calls=%async_computation.7 | async-start | bytes 524288 | tf_op jit(solution)/shard_map/all_to_all | solution.py:29
  193.6 3.1 %collective-permute-start.6 = (f32[8,3072]{1,0:T(8,128)S(1)}, f32[8,3072]{1,0:T(8,128)S(1)}, u32[]{:S(2)}, u32[]{:S(2)}) collective-permute-start(f32[8,3072]{1,0:T(8,128)S(1)} %get-tuple-element.70.full), channel_id=1, source_target_pairs={{0,8},{8,0},{16,24},{24,16},{32,40},{40,32},{48,56},{56,48},{64,72... | collective-permute-start | bytes 294920 | tf_op jit(solution)/shard_map/ppermute | solution.py:375
  195.5 1.2 collective-permute-start.7
  201.3 20.9 %copy-start.2 = (f32[192,64]{0,1:T(8,128)S(1)}, f32[192,64]{0,1:T(8,128)}, u32[]{:S(2)}) copy-start(f32[192,64]{0,1:T(8,128)} %param.6) | copy-start | bytes 147460
  201.8 3.8 %collective-permute-start.8 = (f32[48,128]{1,0:T(8,128)S(1)}, f32[48,128]{1,0:T(8,128)S(1)}, u32[]{:S(2)}, u32[]{:S(2)}) collective-permute-start(f32[48,128]{1,0:T(8,128)S(1)} %get-tuple-element.76), channel_id=1, source_target_pairs={{0,8},{8,0},{16,24},{24,16},{32,40},{40,32},{48,56},{56,48},{64,72... | collective-permute-start | bytes 73736 | tf_op jit(solution)/shard_map/ppermute | solution.py:375
  219.5 4.1 %collective-permute-start.9 = (f32[48,128]{1,0:T(8,128)S(1)}, f32[48,128]{1,0:T(8,128)S(1)}, u32[]{:S(2)}, u32[]{:S(2)}) collective-permute-start(f32[48,128]{1,0:T(8,128)S(1)} %shard_map.100.mine), channel_id=1, source_target_pairs={{0,8},{8,0},{16,24},{24,16},{32,40},{40,32},{48,56},{56,48},{64,72... | collective-permute-start | bytes 73736 | tf_op jit(solution)/shard_map/ppermute | solution.py:375

commit v7 on v6

--- a/solution.py
+++ b/solution.py
@@ -103,17 +103,27 @@
         move.wait()
 
 
-def stage(w_in, w_out, tokens, grad_out, far_in, far_out, own_in, own_out, x, g, sems):
+def stage(w_in, w_out, tokens, grad_out, far_in, far_out, own_in, own_out, x, g, held, sems):
     core = core_index()
     half = own_in.shape[0]
-    pairs = [(tokens, x), (grad_out, g)]
-    for whole, own, far in ((w_in, own_in, far_in), (w_out, own_out, far_out)):
-        pairs.append((whole.at[pl.ds(half * (1 - core), half)], far))
-        pairs.append((whole.at[pl.ds(half * core, half)], own))
+    far = pl.ds(half * (1 - core), half)
+    near = pl.ds(half * core, half)
+    pairs = [
+        (w_in.at[far], held.at[0]),
+        (w_out.at[far], held.at[1]),
+        (grad_out, g),
+        (tokens, x),
+        (w_in.at[near], own_in),
+        (w_out.at[near], own_out),
+    ]
     copies = [pltpu.make_async_copy(a, b, sems.at[i]) for i, (a, b) in enumerate(pairs)]
     for copy in copies:
         copy.start()
-    for copy in copies:
+    for i, out in enumerate((far_in, far_out)):
+        copies[i].wait()
+        copies.append(pltpu.make_async_copy(held.at[i], out, sems.at[6 + i]))
+        copies[-1].start()
+    for copy in copies[2:]:
         copy.wait()
 
 
@@ -404,7 +414,7 @@
         + [pltpu.VMEM(tokens.shape, F32)] * 2,
         in_specs=[far_spec] * 4,
         out_specs=[far_spec] * 2 + [vmem_spec] * 4,
-        scratch_shapes=[pltpu.SemaphoreType.DMA((6,))],
+        scratch_shapes=[pltpu.VMEM((2,) + half, F32), pltpu.SemaphoreType.DMA((8,))],
         compiler_params=limit,
     )(in_hbm(w_in), in_hbm(w_out), in_hbm(tokens), in_hbm(grad_out))
     got, far_in, far_out, own_in, own_out, tokens, grad_out = lax.optimization_barrier(

time: 225 us -> 156 us (0.69)
  Pallas kernels: 87 us -> 18.1 us
  blocking collectives: 92 us -> 87.9 us
  waiting for transfers between devices: 12.3 us -> 15.3 us
    pallas_call x1, Pallas kernels: 72.6 us -> 3.73 us  [per_device(): pl.pallas_call(stage, out_shape=[pltpu.HBM(half, F32)] * 2 + [pltpu.VMEM(...]
    all_to_all x7, blocking collectives: 92 us -> 87.9 us  [exchange(): lax.all_to_all(blocks, axis, 0, 0, axis_index_groups=groups, tiled=True)]
    all_to_all x2, waiting for transfers between devices: 1.63 us -> 4.64 us  [exchange(): lax.all_to_all(blocks, axis, 0, 0, axis_index_groups=groups, tiled=True)]
  transfers between devices with their start and end apart: 12 -> 12, of which waited for: 7 -> 8; matrix products, arithmetic and copies ran while one was open for 0% -> 0% of each run, Pallas kernels for 35% -> 6%
where the time goes in v7:
time: 156 us
  blocking collectives  87.9 us (56%)
  starting transfers between devices  32.6 us (21%)
  Pallas kernels  18.1 us (12%)
  waiting for transfers between devices  15.3 us (10%)
    all_to_all x7, blocking collectives, exchange(): lax.all_to_all(blocks, axis, 0, 0, axis_index_groups=groups, tiled=True)  87.9 us
    ppermute x8, starting transfers between devices, to_partner(): return lax.ppermute(values, S, partner)  19.3 us
    pallas_call x16, Pallas kernels, run(): pl.pallas_call(kernel, out_shape=[jax.ShapeDtypeStruct(s, F32) for s in s...  11.5 us
    all_to_all x2, starting transfers between devices, exchange(): lax.all_to_all(blocks, axis, 0, 0, axis_index_groups=groups, tiled=True)  10.9 us
    all_to_all x2, waiting for transfers between devices, exchange(): lax.all_to_all(blocks, axis, 0, 0, axis_index_groups=groups, tiled=True)  4.64 us
    ppermute x1, waiting for transfers between devices, per_device(): lax.ppermute(tile, (S, E), to_owner)  4.63 us
    pallas_call x1, Pallas kernels, per_device(): pl.pallas_call(stage, out_shape=[pltpu.HBM(half, F32)] * 2 + [pltpu.VMEM(...  3.73 us
    ppermute x8, waiting for transfers between devices, to_partner(): return lax.ppermute(values, S, partner)  3.55 us
  transfers between devices with their start and end apart: 12, of which 8 were waited for; matrix products, arithmetic and copies ran while one was open for 0% of the time, Pallas kernels for 6%

profile of v7, /device:TPU:1, one launch (start us, length us, event | category | flops | bytes accessed | tf_op | source)
XLA Modules:
  0.0 155.5 jit_solution(8853655321471240099)
XLA Ops:
  0.6 2.8 %shard_map.84 = f32[8,64,128]{2,1,0:T(8,128)} custom-call(f32[64,192]{1,0:T(8,128)} %bitcast.2, f32[192,1024]{1,0:T(8,128)} %tokens.3), custom_call_target="tpu_custom_call" | custom-call | tf_op jit(solution)/shard_map/pallas_call | solution.py:393
  3.4 7.5 %all-to-all-start = ((f32[8,64,128]{2,1,0:T(8,128)}), f32[8,64,128]{2,1,0:T(8,128)S(1)}, u32[]{:S(2)}, u32[]{:S(2)}) async-start(f32[8,64,128]{2,1,0:T(8,128)} %shard_map.84), calls=%async_computation | async-start | bytes 524288 | tf_op jit(solution)/shard_map/all_to_all | solution.py:29
  10.9 3.7 %shard_map.85 = (f32[2,48,3072]{2,1,0:T(8,128)}, f32[2,48,3072]{2,1,0:T(8,128)}, f32[2,48,3072]{2,1,0:T(8,128)S(1)}, f32[2,48,3072]{2,1,0:T(8,128)S(1)}, f32[192...) custom-call(f32[4,48,3072]{2,1,0:T(8,128)} %w_in, f32[4,48,3072]{2,1,0:T(8,128)} %w_out, f32[192,1024]{1,0:T(8,128)} %tokens.3, ...), custom_call_target="tpu_custom_call" | custom-call | tf_op jit(solution)/shard_map/pallas_call | solution.py:410
  15.6 3.0 %all-to-all-done.got = f32[8,64,128]{2,1,0:T(8,128)S(1)} async-done(((f32[8,64,128]{2,1,0:T(8,128)}), f32[8,64,128]{2,1,0:T(8,128)S(1)}, u32[]{:S(2)}, u32[]{:S(2)}) %all-to-all-start) | async-done | bytes 262176 | tf_op jit(solution)/shard_map/all_to_all | solution.py:29
  18.6 2.1 %collective-permute-start.2 = (f32[2,48,3072]{2,1,0:T(8,128)}, f32[2,48,3072]{2,1,0:T(8,128)S(1)}, u32[]{:S(2)}, u32[]{:S(2)}) collective-permute-start(f32[2,48,3072]{2,1,0:T(8,128)} %get-tuple-element.61), channel_id=1, source_target_pairs={{0,8},{8,0},{16,24},{24,16},{32,40},{40,32},{48,56},{56,48},{64,72... | collective-permute-start | bytes 3538952 | tf_op jit(solution)/shard_map/ppermute | solution.py:385
  20.7 10.5 %all_to_all.45.got.logits = f32[8,64,128]{2,1,0:T(8,128)S(1)} all-to-all(f32[8,64,128]{2,1,0:T(8,128)S(1)} %shard_map.86), channel_id=1, replica_groups=mesh['seq'=32,'expert'=8] {'expert'}, dimensions={0} | all-to-all | bytes 524288 | tf_op jit(solution)/shard_map/all_to_all | solution.py:29
  31.2 1.4 shard_map.87
  32.7 2.0 %collective-permute-start = (f32[16,8,128]{2,1,0:T(8,128)S(1)}, f32[16,8,128]{2,1,0:T(8,128)S(1)}, u32[]{:S(2)}, u32[]{:S(2)}) collective-permute-start(f32[16,8,128]{2,1,0:T(8,128)S(1)} %get-tuple-element.58), channel_id=1, source_target_pairs={{0,8},{8,0},{16,24},{24,16},{32,40},{40,32},{48,56},{56,48},{64,72... | collective-permute-start | bytes 196616 | tf_op jit(solution)/shard_map/ppermute | solution.py:385
  34.6 0.9 collective-permute-done.near
  35.7 15.5 %all_to_all.46.got = f32[16,8,128]{2,1,0:T(8,128)S(1)} all-to-all(f32[16,8,128]{2,1,0:T(8,128)S(1)} %shard_map.88), channel_id=1, replica_groups={{0,16,32,48,64,80,96,112,128,144,160,176,192,208,224,240},{8,24,40,56,7..., dimensions={0} | all-to-all | bytes 131072 | tf_op jit(solution)/shard_map/all_to_all | solution.py:29
  51.3 0.9 collective-permute-start.1
  52.2 4.6 %collective-permute-done.1.got = f32[8,128]{1,0:T(8,128)S(1)} collective-permute-done((f32[8,128]{1,0:T(8,128)S(1)}, f32[8,128]{1,0:T(8,128)S(1)}, u32[]{:S(2)}, u32[]{:S(2)}) %collective-permute-start.1) | collective-permute-done | bytes 4128 | tf_op jit(solution)/shard_map/ppermute | solution.py:444
  56.8 1.2 shard_map.90
  58.0 11.8 %all_to_all.47.got = f32[16,8,256]{2,1,0:T(8,128)S(1)} all-to-all(f32[16,8,256]{2,1,0:T(8,128)S(1)} %get-tuple-element.63), channel_id=1, replica_groups={{0,16,32,48,64,80,96,112,128,144,160,176,192,208,224,240},{8,24,40,56,7..., dimensions={0} | all-to-all | bytes 262144 | tf_op jit(solution)/shard_map/all_to_all | solution.py:29
  69.8 10.5 %all_to_all.48.got = f32[16,8,256]{2,1,0:T(8,128)S(1)} all-to-all(f32[16,8,256]{2,1,0:T(8,128)S(1)} %shard_map.91), channel_id=1, replica_groups={{0,16,32,48,64,80,96,112,128,144,160,176,192,208,224,240},{8,24,40,56,7..., dimensions={0} | all-to-all | bytes 262144 | tf_op jit(solution)/shard_map/all_to_all | solution.py:29
  80.3 1.2 shard_map.92
  81.5 1.5 collective-permute-start.4
  83.0 2.5 %collective-permute-done.4.tile = f32[8,128]{1,0:T(8,128)S(1)} collective-permute-done((f32[8,128]{1,0:T(8,128)S(1)}, f32[8,128]{1,0:T(8,128)S(1)}, u32[]{:S(2)}, u32[]{:S(2)}) %collective-permute-start.4) | collective-permute-done | bytes 4128 | tf_op jit(solution)/shard_map/ppermute | solution.py:452
  85.5 14.0 %all_to_all.49.mine = f32[16,8,128]{2,1,0:T(8,128)S(1)} all-to-all(f32[16,8,128]{2,1,0:T(8,128)S(1)} %shard_map.93), channel_id=1, replica_groups={{0,16,32,48,64,80,96,112,128,144,160,176,192,208,224,240},{8,24,40,56,7..., dimensions={0} | all-to-all | bytes 131072 | tf_op jit(solution)/shard_map/all_to_all | solution.py:29
  99.5 7.5 %collective-permute-start.5 = (f32[16,8,128]{2,1,0:T(8,128)S(1)}, f32[16,8,128]{2,1,0:T(8,128)S(1)}, u32[]{:S(2)}, u32[]{:S(2)}) collective-permute-start(f32[16,8,128]{2,1,0:T(8,128)S(1)} %all_to_all.49.mine), channel_id=1, source_target_pairs={{0,8},{8,0},{16,24},{24,16},{32,40},{40,32},{48,56},{56,48},{64,72... | collective-permute-start | bytes 196616 | tf_op jit(solution)/shard_map/ppermute | solution.py:385
  107.0 0.9 collective-permute-done.5.near
  107.9 0.9 shard_map.94
  108.9 11.7 %all_to_all.50.got = f32[8,64,128]{2,1,0:T(8,128)S(1)} all-to-all(f32[8,64,128]{2,1,0:T(8,128)S(1)} %get-tuple-element.67), channel_id=1, replica_groups=mesh['seq'=32,'expert'=8] {'expert'}, dimensions={0} | all-to-all | bytes 524288 | tf_op jit(solution)/shard_map/all_to_all | solution.py:29
  121.3 3.4 %all-to-all-start.7 = ((f32[8,64,128]{2,1,0:T(8,128)}), f32[8,64,128]{2,1,0:T(8,128)S(1)}, u32[]{:S(2)}, u32[]{:S(2)}) async-start(f32[8,64,128]{2,1,0:T(8,128)} %shard_map.95), calls=%async_computation.7 | async-start | bytes 524288 | tf_op jit(solution)/shard_map/all_to_all | solution.py:29
  124.7 1.9 %collective-permute-start.6 = (f32[8,3072]{1,0:T(8,128)S(1)}, f32[8,3072]{1,0:T(8,128)S(1)}, u32[]{:S(2)}, u32[]{:S(2)}) collective-permute-start(f32[8,3072]{1,0:T(8,128)S(1)} %get-tuple-element.70.full), channel_id=1, source_target_pairs={{0,8},{8,0},{16,24},{24,16},{32,40},{40,32},{48,56},{56,48},{64,72... | collective-permute-start | bytes 294920 | tf_op jit(solution)/shard_map/ppermute | solution.py:385
  126.9 0.9 collective-permute-done.7.near_keep
  127.7 3.0 %shard_map.96 = (f32[4,48,3072]{2,1,0:T(8,128)}, f32[4,48,3072]{2,1,0:T(8,128)}) custom-call(f32[8,3072]{1,0:T(8,128)S(1)} %get-tuple-element.70.full, f32[8,3072]{1,0:T(8,128)S(1)} %collective-permute-done.6.near_full, f32[8,128]{1,0:T(8,128)S(1)} %get-tuple-element.71.keep, f32[8,128]{1,0:T(8,128)S(1)} %collective-permute-done.7.near_keep), custom_call_target="tpu_custom_call" | custom-call | bytes 4923392 | tf_op jit(solution)/shard_map/pallas_call | solution.py:37
  130.8 1.6 %all-to-all-done.7.got = f32[8,64,128]{2,1,0:T(8,128)S(1)} async-done(((f32[8,64,128]{2,1,0:T(8,128)}), f32[8,64,128]{2,1,0:T(8,128)S(1)}, u32[]{:S(2)}, u32[]{:S(2)}) %all-to-all-start.7) | async-done | bytes 262176 | tf_op jit(solution)/shard_map/all_to_all | solution.py:29
  132.9 2.9 %collective-permute-start.8 = (f32[48,128]{1,0:T(8,128)S(1)}, f32[48,128]{1,0:T(8,128)S(1)}, u32[]{:S(2)}, u32[]{:S(2)}) collective-permute-start(f32[48,128]{1,0:T(8,128)S(1)} %get-tuple-element.76), channel_id=1, source_target_pairs={{0,8},{8,0},{16,24},{24,16},{32,40},{40,32},{48,56},{56,48},{64,72... | collective-permute-start | bytes 73736 | tf_op jit(solution)/shard_map/ppermute | solution.py:385
  136.7 13.9 %all_to_all.51.got = f32[16,48,128]{2,1,0:T(8,128)S(1)} all-to-all(f32[16,48,128]{2,1,0:T(8,128)S(1)} %shard_map.98), channel_id=1, replica_groups={{0,16,32,48,64,80,96,112,128,144,160,176,192,208,224,240},{8,24,40,56,7..., dimensions={0} | all-to-all | bytes 786432 | tf_op jit(solution)/shard_map/all_to_all | solution.py:29
  150.6 2.6 %collective-permute-start.9 = (f32[48,128]{1,0:T(8,128)S(1)}, f32[48,128]{1,0:T(8,128)S(1)}, u32[]{:S(2)}, u32[]{:S(2)}) collective-permute-start(f32[48,128]{1,0:T(8,128)S(1)} %shard_map.100.mine), channel_id=1, source_target_pairs={{0,8},{8,0},{16,24},{24,16},{32,40},{40,32},{48,56},{56,48},{64,72... | collective-permute-start | bytes 73736 | tf_op jit(solution)/shard_map/ppermute | solution.py:385
  153.3 1.4 shard_map.99
  (23 shorter events, 4.4 us)
Async XLA Ops:
  3.4 15.1 %all-to-all-start = ((f32[8,64,128]{2,1,0:T(8,128)}), f32[8,64,128]{2,1,0:T(8,128)S(1)}, u32[]{:S(2)}, u32[]{:S(2)}) async-start(f32[8,64,128]{2,1,0:T(8,128)} %shard_map.84), calls=%async_computation | async-start | bytes 524288 | tf_op jit(solution)/shard_map/all_to_all | solution.py:29
  14.7 0.9 copy-start
  18.6 12.7 %copy-start.1 = (f32[192,1024]{1,0:T(8,128)S(1)}, f32[192,1024]{1,0:T(8,128)}, u32[]{:S(2)}) copy-start(f32[192,1024]{1,0:T(8,128)} %copy-done) | copy-start | bytes 2359300
  18.6 38.2 %collective-permute-start.2 = (f32[2,48,3072]{2,1,0:T(8,128)}, f32[2,48,3072]{2,1,0:T(8,128)S(1)}, u32[]{:S(2)}, u32[]{:S(2)}) collective-permute-start(f32[2,48,3072]{2,1,0:T(8,128)} %get-tuple-element.61), channel_id=1, source_target_pairs={{0,8},{8,0},{16,24},{24,16},{32,40},{40,32},{48,56},{56,48},{64,72... | collective-permute-start | bytes 3538952 | tf_op jit(solution)/shard_map/ppermute | solution.py:385
  20.7 36.1 %collective-permute-start.3 = (f32[2,48,3072]{2,1,0:T(8,128)}, f32[2,48,3072]{2,1,0:T(8,128)S(1)}, u32[]{:S(2)}, u32[]{:S(2)}) collective-permute-start(f32[2,48,3072]{2,1,0:T(8,128)} %get-tuple-element.62), channel_id=1, source_target_pairs={{0,8},{8,0},{16,24},{24,16},{32,40},{40,32},{48,56},{56,48},{64,72... | collective-permute-start | bytes 3538952 | tf_op jit(solution)/shard_map/ppermute | solution.py:385
  32.7 2.9 %collective-permute-start = (f32[16,8,128]{2,1,0:T(8,128)S(1)}, f32[16,8,128]{2,1,0:T(8,128)S(1)}, u32[]{:S(2)}, u32[]{:S(2)}) collective-permute-start(f32[16,8,128]{2,1,0:T(8,128)S(1)} %get-tuple-element.58), channel_id=1, source_target_pairs={{0,8},{8,0},{16,24},{24,16},{32,40},{40,32},{48,56},{56,48},{64,72... | collective-permute-start | bytes 196616 | tf_op jit(solution)/shard_map/ppermute | solution.py:385
  51.3 5.5 %collective-permute-start.1 = (f32[8,128]{1,0:T(8,128)S(1)}, f32[8,128]{1,0:T(8,128)S(1)}, u32[]{:S(2)}, u32[]{:S(2)}) collective-permute-start(f32[8,128]{1,0:T(8,128)S(1)} %shard_map.89), channel_id=1, source_target_pairs={{80,0},{241,32},{34,64},{195,96},{132,128},{37,160},{182,192},{87,... | collective-permute-start | bytes 12296 | tf_op jit(solution)/shard_map/ppermute | solution.py:444
  81.5 4.0 %collective-permute-start.4 = (f32[8,128]{1,0:T(8,128)S(1)}, f32[8,128]{1,0:T(8,128)S(1)}, u32[]{:S(2)}, u32[]{:S(2)}) collective-permute-start(f32[8,128]{1,0:T(8,128)S(1)} %get-tuple-element.65), channel_id=1, source_target_pairs={{0,80},{32,241},{64,34},{96,195},{128,132},{160,37},{192,182},{224... | collective-permute-start | bytes 12296 | tf_op jit(solution)/shard_map/ppermute | solution.py:452
  99.5 8.4 %collective-permute-start.5 = (f32[16,8,128]{2,1,0:T(8,128)S(1)}, f32[16,8,128]{2,1,0:T(8,128)S(1)}, u32[]{:S(2)}, u32[]{:S(2)}) collective-permute-start(f32[16,8,128]{2,1,0:T(8,128)S(1)} %all_to_all.49.mine), channel_id=1, source_target_pairs={{0,8},{8,0},{16,24},{24,16},{32,40},{40,32},{48,56},{56,48},{64,72... | collective-permute-start | bytes 196616 | tf_op jit(solution)/shard_map/ppermute | solution.py:385
  121.3 11.1 %all-to-all-start.7 = ((f32[8,64,128]{2,1,0:T(8,128)}), f32[8,64,128]{2,1,0:T(8,128)S(1)}, u32[]{:S(2)}, u32[]{:S(2)}) async-start(f32[8,64,128]{2,1,0:T(8,128)} %shard_map.95), calls=%async_computation.7 | async-start | bytes 524288 | tf_op jit(solution)/shard_map/all_to_all | solution.py:29
  124.7 3.1 %collective-permute-start.6 = (f32[8,3072]{1,0:T(8,128)S(1)}, f32[8,3072]{1,0:T(8,128)S(1)}, u32[]{:S(2)}, u32[]{:S(2)}) collective-permute-start(f32[8,3072]{1,0:T(8,128)S(1)} %get-tuple-element.70.full), channel_id=1, source_target_pairs={{0,8},{8,0},{16,24},{24,16},{32,40},{40,32},{48,56},{56,48},{64,72... | collective-permute-start | bytes 294920 | tf_op jit(solution)/shard_map/ppermute | solution.py:385
  126.6 1.2 collective-permute-start.7
  132.4 20.9 %copy-start.2 = (f32[192,64]{0,1:T(8,128)S(1)}, f32[192,64]{0,1:T(8,128)}, u32[]{:S(2)}) copy-start(f32[192,64]{0,1:T(8,128)} %param.6) | copy-start | bytes 147460
  132.9 3.8 %collective-permute-start.8 = (f32[48,128]{1,0:T(8,128)S(1)}, f32[48,128]{1,0:T(8,128)S(1)}, u32[]{:S(2)}, u32[]{:S(2)}) collective-permute-start(f32[48,128]{1,0:T(8,128)S(1)} %get-tuple-element.76), channel_id=1, source_target_pairs={{0,8},{8,0},{16,24},{24,16},{32,40},{40,32},{48,56},{56,48},{64,72... | collective-permute-start | bytes 73736 | tf_op jit(solution)/shard_map/ppermute | solution.py:385
  150.6 4.1 %collective-permute-start.9 = (f32[48,128]{1,0:T(8,128)S(1)}, f32[48,128]{1,0:T(8,128)S(1)}, u32[]{:S(2)}, u32[]{:S(2)}) collective-permute-start(f32[48,128]{1,0:T(8,128)S(1)} %shard_map.100.mine), channel_id=1, source_target_pairs={{0,8},{8,0},{16,24},{24,16},{32,40},{40,32},{48,56},{56,48},{64,72... | collective-permute-start | bytes 73736 | tf_op jit(solution)/shard_map/ppermute | solution.py:385

commit v8 on v7

--- a/solution.py
+++ b/solution.py
@@ -103,7 +103,7 @@
         move.wait()
 
 
-def stage(w_in, w_out, tokens, grad_out, far_in, far_out, own_in, own_out, x, g, held, sems):
+def stage(w_in, w_out, tokens, far_in, far_out, own_in, own_out, x, held, sems):
     core = core_index()
     half = own_in.shape[0]
     far = pl.ds(half * (1 - core), half)
@@ -111,7 +111,6 @@
     pairs = [
         (w_in.at[far], held.at[0]),
         (w_out.at[far], held.at[1]),
-        (grad_out, g),
         (tokens, x),
         (w_in.at[near], own_in),
         (w_out.at[near], own_out),
@@ -121,7 +120,7 @@
         copy.start()
     for i, out in enumerate((far_in, far_out)):
         copies[i].wait()
-        copies.append(pltpu.make_async_copy(held.at[i], out, sems.at[6 + i]))
+        copies.append(pltpu.make_async_copy(held.at[i], out, sems.at[5 + i]))
         copies[-1].start()
     for copy in copies[2:]:
         copy.wait()
@@ -404,22 +403,20 @@
         ],
         compiler_params=limit,
     )(in_hbm(turned), in_hbm(tokens))
-    sent, w_in, w_out, grad_out = lax.optimization_barrier((sent, w_in, w_out, grad_out))
+    sent, w_in, w_out = lax.optimization_barrier((sent, w_in, w_out))
     got = exchange(sent, E)
     half = (experts // 2,) + w_in.shape[1:]
     staged = pl.pallas_call(
         stage,
         out_shape=[pltpu.HBM(half, F32)] * 2
         + [pltpu.VMEM(half, F32)] * 2
-        + [pltpu.VMEM(tokens.shape, F32)] * 2,
-        in_specs=[far_spec] * 4,
-        out_specs=[far_spec] * 2 + [vmem_spec] * 4,
-        scratch_shapes=[pltpu.VMEM((2,) + half, F32), pltpu.SemaphoreType.DMA((8,))],
+        + [pltpu.VMEM(tokens.shape, F32)],
+        in_specs=[far_spec] * 3,
+        out_specs=[far_spec] * 2 + [vmem_spec] * 3,
+        scratch_shapes=[pltpu.VMEM((2,) + half, F32), pltpu.SemaphoreType.DMA((7,))],
         compiler_params=limit,
-    )(in_hbm(w_in), in_hbm(w_out), in_hbm(tokens), in_hbm(grad_out))
-    got, far_in, far_out, own_in, own_out, tokens, grad_out = lax.optimization_barrier(
-        (got, *staged)
-    )
+    )(in_hbm(w_in), in_hbm(w_out), in_hbm(tokens))
+    got, far_in, far_out, own_in, own_out, tokens = lax.optimization_barrier((got, *staged))
     logits = exchange(run(add_spread, spread, got), E)
     weights = (own_in, own_out, to_partner(far_in), to_partner(far_out))
 
@@ -449,7 +446,18 @@
     tile, full = run(
         slot_rows, [(8, LANES), (8, hidden)], exchange(sent, S, groups), held, *weights
     )
-    sent = run(copies, tiles, lax.ppermute(tile, (S, E), from_owner))
+    grad_w_in, grad_w_out = run(
+        weight_grads,
+        [w_in.shape, w_out.shape],
+        full,
+        to_partner(full),
+        held,
+        to_partner(held),
+    )
+    tile, grad_w_in, grad_w_out = lax.optimization_barrier(
+        (lax.ppermute(tile, (S, E), from_owner), grad_w_in, grad_w_out)
+    )
+    sent = run(copies, tiles, tile)
     mine = exchange(sent, S, groups)
     near = to_partner(mine)
     sent, weights, rows = run(
@@ -464,17 +472,7 @@
         scratch=[(slots, rows_block), (slots, LANES)],
     )
     sent = run(add_spread, spread, exchange(sent, E))
-    sent, full, held = lax.optimization_barrier((sent, full, held))
     grads = exchange(sent, E)
-    grad_w_in, grad_w_out = run(
-        weight_grads,
-        [w_in.shape, w_out.shape],
-        full,
-        to_partner(full),
-        held,
-        to_partner(held),
-    )
-    grads, grad_w_in, grad_w_out = lax.optimization_barrier((grads, grad_w_in, grad_w_out))
     fold = (rows_block // 4, 2 * slots)
     near, theirs = run(router_part, [fold, fold], grads, tokens)
     sent = run(add_copies, (chips,) + fold, near, to_partner(theirs))

time: 156 us -> 155 us (level)
  blocking collectives: 87.9 us -> 97.9 us
  starting transfers between devices: 32.6 us -> 27.6 us
  waiting for transfers between devices: 15.3 us -> 11.4 us
    all_to_all x7 -> x8, blocking collectives: 87.9 us -> 97.9 us  [exchange(): lax.all_to_all(blocks, axis, 0, 0, axis_index_groups=groups, tiled=True)]
    all_to_all x2 -> x1, starting transfers between devices: 10.9 us -> 7.49 us  [exchange(): lax.all_to_all(blocks, axis, 0, 0, axis_index_groups=groups, tiled=True)]
    ppermute x1, waiting for transfers between devices: 2.46 us -> 0.01 us  [per_device(): lax.ppermute(tile, (S, E), from_owner)]
    ppermute x8, starting transfers between devices: 19.3 us -> 17.7 us  [to_partner(): return lax.ppermute(values, S, partner)]
    all_to_all x2 -> x1, waiting for transfers between devices: 4.64 us -> 4.14 us  [exchange(): lax.all_to_all(blocks, axis, 0, 0, axis_index_groups=groups, tiled=True)]
  transfers between devices with their start and end apart: 12 -> 11, of which waited for: 8 -> 5; matrix products, arithmetic and copies ran while one was open for 0% -> 0% of each run, Pallas kernels for 6% -> 6%
where the time goes in v8:
time: 155 us
  blocking collectives  97.9 us (63%)
  starting transfers between devices  27.6 us (18%)
  Pallas kernels  17.2 us (11%)
  waiting for transfers between devices  11.4 us (7%)
    all_to_all x8, blocking collectives, exchange(): lax.all_to_all(blocks, axis, 0, 0, axis_index_groups=groups, tiled=True)  97.9 us
    ppermute x8, starting transfers between devices, to_partner(): return lax.ppermute(values, S, partner)  17.7 us
    pallas_call x16, Pallas kernels, run(): pl.pallas_call(kernel, out_shape=[jax.ShapeDtypeStruct(s, F32) for s in s...  10.9 us
    all_to_all x1, starting transfers between devices, exchange(): lax.all_to_all(blocks, axis, 0, 0, axis_index_groups=groups, tiled=True)  7.49 us
    ppermute x1, waiting for transfers between devices, per_device(): lax.ppermute(tile, (S, E), to_owner)  4.63 us
    all_to_all x1, waiting for transfers between devices, exchange(): lax.all_to_all(blocks, axis, 0, 0, axis_index_groups=groups, tiled=True)  4.14 us
    pallas_call x1, Pallas kernels, per_device(): pl.pallas_call(stage, out_shape=[pltpu.HBM(half, F32)] * 2 + [pltpu.VMEM(...  3.49 us
  transfers between devices with their start and end apart: 11, of which 5 were waited for; matrix products, arithmetic and copies ran while one was open for 0% of the time, Pallas kernels for 6%

profile of v8, /device:TPU:1, one launch (start us, length us, event | category | flops | bytes accessed | tf_op | source)
XLA Modules:
  0.0 154.8 jit_solution(1861631112380305275)
XLA Ops:
  0.6 2.8 %shard_map.84 = f32[8,64,128]{2,1,0:T(8,128)} custom-call(f32[64,192]{1,0:T(8,128)} %bitcast.2, f32[192,1024]{1,0:T(8,128)} %tokens.3), custom_call_target="tpu_custom_call" | custom-call | tf_op jit(solution)/shard_map/pallas_call | solution.py:392
  3.5 7.5 %all-to-all-start = ((f32[8,64,128]{2,1,0:T(8,128)}), f32[8,64,128]{2,1,0:T(8,128)S(1)}, u32[]{:S(2)}, u32[]{:S(2)}) async-start(f32[8,64,128]{2,1,0:T(8,128)} %shard_map.84), calls=%async_computation | async-start | bytes 524288 | tf_op jit(solution)/shard_map/all_to_all | solution.py:29
  10.9 3.5 %shard_map.85 = (f32[2,48,3072]{2,1,0:T(8,128)}, f32[2,48,3072]{2,1,0:T(8,128)}, f32[2,48,3072]{2,1,0:T(8,128)S(1)}, f32[2,48,3072]{2,1,0:T(8,128)S(1)}, f32[192,1024]{1,0:T(8,128)S(1)}) custom-call(f32[4,48,3072]{2,1,0:T(8,128)} %w_in, f32[4,48,3072]{2,1,0:T(8,128)} %w_out, f32[192,1024]{1,0:T(8,128)} %tokens.3), custom_call_target="tpu_custom_call" | custom-call | tf_op jit(solution)/shard_map/pallas_call | solution.py:409
  14.4 4.1 %all-to-all-done.got = f32[8,64,128]{2,1,0:T(8,128)S(1)} async-done(((f32[8,64,128]{2,1,0:T(8,128)}), f32[8,64,128]{2,1,0:T(8,128)S(1)}, u32[]{:S(2)}, u32[]{:S(2)}) %all-to-all-start) | async-done | bytes 262176 | tf_op jit(solution)/shard_map/all_to_all | solution.py:29
  18.6 2.1 %collective-permute-start.2 = (f32[2,48,3072]{2,1,0:T(8,128)}, f32[2,48,3072]{2,1,0:T(8,128)S(1)}, u32[]{:S(2)}, u32[]{:S(2)}) collective-permute-start(f32[2,48,3072]{2,1,0:T(8,128)} %get-tuple-element.52), channel_id=1, source_target_pairs={{0,8},{8,0},{16,24},{24,16},{32,40},{40,32},{48,56},{56,48},{64,72... | collective-permute-start | bytes 3538952 | tf_op jit(solution)/shard_map/ppermute | solution.py:384
  20.7 10.4 %all_to_all.45.got.logits = f32[8,64,128]{2,1,0:T(8,128)S(1)} all-to-all(f32[8,64,128]{2,1,0:T(8,128)S(1)} %shard_map.86), channel_id=1, replica_groups=mesh['seq'=32,'expert'=8] {'expert'}, dimensions={0} | all-to-all | bytes 524288 | tf_op jit(solution)/shard_map/all_to_all | solution.py:29
  31.1 1.4 shard_map.87
  32.5 1.9 %collective-permute-start = (f32[16,8,128]{2,1,0:T(8,128)S(1)}, f32[16,8,128]{2,1,0:T(8,128)S(1)}, u32[]{:S(2)}, u32[]{:S(2)}) collective-permute-start(f32[16,8,128]{2,1,0:T(8,128)S(1)} %get-tuple-element.49), channel_id=1, source_target_pairs={{0,8},{8,0},{16,24},{24,16},{32,40},{40,32},{48,56},{56,48},{64,72... | collective-permute-start | bytes 196616 | tf_op jit(solution)/shard_map/ppermute | solution.py:384
  34.4 0.9 collective-permute-done.near
  35.4 15.5 %all_to_all.46.got = f32[16,8,128]{2,1,0:T(8,128)S(1)} all-to-all(f32[16,8,128]{2,1,0:T(8,128)S(1)} %shard_map.88), channel_id=1, replica_groups={{0,16,32,48,64,80,96,112,128,144,160,176,192,208,224,240},{8,24,40,56,7..., dimensions={0} | all-to-all | bytes 131072 | tf_op jit(solution)/shard_map/all_to_all | solution.py:29
  51.0 0.9 collective-permute-start.1
  51.9 4.6 %collective-permute-done.1.got = f32[8,128]{1,0:T(8,128)S(1)} collective-permute-done((f32[8,128]{1,0:T(8,128)S(1)}, f32[8,128]{1,0:T(8,128)S(1)}, u32[]{:S(2)}, u32[]{:S(2)}) %collective-permute-start.1) | collective-permute-done | bytes 4128 | tf_op jit(solution)/shard_map/ppermute | solution.py:441
  56.6 1.2 shard_map.90
  57.8 11.8 %all_to_all.47.got = f32[16,8,256]{2,1,0:T(8,128)S(1)} all-to-all(f32[16,8,256]{2,1,0:T(8,128)S(1)} %get-tuple-element.54), channel_id=1, replica_groups={{0,16,32,48,64,80,96,112,128,144,160,176,192,208,224,240},{8,24,40,56,7..., dimensions={0} | all-to-all | bytes 262144 | tf_op jit(solution)/shard_map/all_to_all | solution.py:29
  69.6 10.5 %all_to_all.48.got = f32[16,8,256]{2,1,0:T(8,128)S(1)} all-to-all(f32[16,8,256]{2,1,0:T(8,128)S(1)} %shard_map.91), channel_id=1, replica_groups={{0,16,32,48,64,80,96,112,128,144,160,176,192,208,224,240},{8,24,40,56,7..., dimensions={0} | all-to-all | bytes 262144 | tf_op jit(solution)/shard_map/all_to_all | solution.py:29
  80.1 1.2 shard_map.92
  81.3 5.2 %collective-permute-start.5 = (f32[8,3072]{1,0:T(8,128)S(1)}, f32[8,3072]{1,0:T(8,128)S(1)}, u32[]{:S(2)}, u32[]{:S(2)}) collective-permute-start(f32[8,3072]{1,0:T(8,128)S(1)} %get-tuple-element.57.full), channel_id=1, source_target_pairs={{0,8},{8,0},{16,24},{24,16},{32,40},{40,32},{48,56},{56,48},{64,72... | collective-permute-start | bytes 294920 | tf_op jit(solution)/shard_map/ppermute | solution.py:384
  86.6 1.5 collective-permute-start.4
  88.1 3.0 %shard_map.93 = (f32[4,48,3072]{2,1,0:T(8,128)}, f32[4,48,3072]{2,1,0:T(8,128)}) custom-call(f32[8,3072]{1,0:T(8,128)S(1)} %get-tuple-element.57.full, f32[8,3072]{1,0:T(8,128)S(1)} %collective-permute-done.5.near_full, f32[8,128]{1,0:T(8,128)S(1)} %get-tuple-element.55.keep, f32[8,128]{1,0:T(8,128)S(1)} %collective-permute-done.6.near_keep), custom_call_target="tpu_custom_call" | custom-call | bytes 4923392 | tf_op jit(solution)/shard_map/pallas_call | solution.py:37
  91.1 13.2 %all_to_all.49.mine = f32[16,8,128]{2,1,0:T(8,128)S(1)} all-to-all(f32[16,8,128]{2,1,0:T(8,128)S(1)} %shard_map.94), channel_id=1, replica_groups={{0,16,32,48,64,80,96,112,128,144,160,176,192,208,224,240},{8,24,40,56,7..., dimensions={0} | all-to-all | bytes 131072 | tf_op jit(solution)/shard_map/all_to_all | solution.py:29
  104.3 3.1 %collective-permute-start.7 = (f32[16,8,128]{2,1,0:T(8,128)S(1)}, f32[16,8,128]{2,1,0:T(8,128)S(1)}, u32[]{:S(2)}, u32[]{:S(2)}) collective-permute-start(f32[16,8,128]{2,1,0:T(8,128)S(1)} %all_to_all.49.mine), channel_id=1, source_target_pairs={{0,8},{8,0},{16,24},{24,16},{32,40},{40,32},{48,56},{56,48},{64,72... | collective-permute-start | bytes 196616 | tf_op jit(solution)/shard_map/ppermute | solution.py:384
  107.4 0.9 collective-permute-done.7.near
  108.3 0.9 shard_map.95
  109.2 12.2 %all_to_all.50.got = f32[8,64,128]{2,1,0:T(8,128)S(1)} all-to-all(f32[8,64,128]{2,1,0:T(8,128)S(1)} %get-tuple-element.62), channel_id=1, replica_groups=mesh['seq'=32,'expert'=8] {'expert'}, dimensions={0} | all-to-all | bytes 524288 | tf_op jit(solution)/shard_map/all_to_all | solution.py:29
  121.4 10.5 %all_to_all.51.got = f32[8,64,128]{2,1,0:T(8,128)S(1)} all-to-all(f32[8,64,128]{2,1,0:T(8,128)S(1)} %shard_map.96), channel_id=1, replica_groups=mesh['seq'=32,'expert'=8] {'expert'}, dimensions={0} | all-to-all | bytes 524288 | tf_op jit(solution)/shard_map/all_to_all | solution.py:29
  132.0 0.5 shard_map.97
  132.5 2.7 %collective-permute-start.8 = (f32[48,128]{1,0:T(8,128)S(1)}, f32[48,128]{1,0:T(8,128)S(1)}, u32[]{:S(2)}, u32[]{:S(2)}) collective-permute-start(f32[48,128]{1,0:T(8,128)S(1)} %get-tuple-element.64), channel_id=1, source_target_pairs={{0,8},{8,0},{16,24},{24,16},{32,40},{40,32},{48,56},{56,48},{64,72... | collective-permute-start | bytes 73736 | tf_op jit(solution)/shard_map/ppermute | solution.py:384
  135.2 0.8 collective-permute-done.8.theirs
  136.1 13.9 %all_to_all.52.got = f32[16,48,128]{2,1,0:T(8,128)S(1)} all-to-all(f32[16,48,128]{2,1,0:T(8,128)S(1)} %shard_map.98), channel_id=1, replica_groups={{0,16,32,48,64,80,96,112,128,144,160,176,192,208,224,240},{8,24,40,56,7..., dimensions={0} | all-to-all | bytes 786432 | tf_op jit(solution)/shard_map/all_to_all | solution.py:29
  150.0 2.6 %collective-permute-start.9 = (f32[48,128]{1,0:T(8,128)S(1)}, f32[48,128]{1,0:T(8,128)S(1)}, u32[]{:S(2)}, u32[]{:S(2)}) collective-permute-start(f32[48,128]{1,0:T(8,128)S(1)} %shard_map.100.mine), channel_id=1, source_target_pairs={{0,8},{8,0},{16,24},{24,16},{32,40},{40,32},{48,56},{56,48},{64,72... | collective-permute-start | bytes 73736 | tf_op jit(solution)/shard_map/ppermute | solution.py:384
  152.6 1.4 shard_map.99
  154.0 0.8 shard_map.101
  (20 shorter events, 0.5 us)
Async XLA Ops:
  3.5 15.1 %all-to-all-start = ((f32[8,64,128]{2,1,0:T(8,128)}), f32[8,64,128]{2,1,0:T(8,128)S(1)}, u32[]{:S(2)}, u32[]{:S(2)}) async-start(f32[8,64,128]{2,1,0:T(8,128)} %shard_map.84), calls=%async_computation | async-start | bytes 524288 | tf_op jit(solution)/shard_map/all_to_all | solution.py:29
  18.6 12.5 %copy-start = (f32[192,1024]{1,0:T(8,128)S(1)}, f32[192,1024]{1,0:T(8,128)}, u32[]{:S(2)}) copy-start(f32[192,1024]{1,0:T(8,128)} %grad_out.3) | copy-start | bytes 2359300
  18.6 38.0 %collective-permute-start.2 = (f32[2,48,3072]{2,1,0:T(8,128)}, f32[2,48,3072]{2,1,0:T(8,128)S(1)}, u32[]{:S(2)}, u32[]{:S(2)}) collective-permute-start(f32[2,48,3072]{2,1,0:T(8,128)} %get-tuple-element.52), channel_id=1, source_target_pairs={{0,8},{8,0},{16,24},{24,16},{32,40},{40,32},{48,56},{56,48},{64,72... | collective-permute-start | bytes 3538952 | tf_op jit(solution)/shard_map/ppermute | solution.py:384
  20.7 35.9 %collective-permute-start.3 = (f32[2,48,3072]{2,1,0:T(8,128)}, f32[2,48,3072]{2,1,0:T(8,128)S(1)}, u32[]{:S(2)}, u32[]{:S(2)}) collective-permute-start(f32[2,48,3072]{2,1,0:T(8,128)} %get-tuple-element.53), channel_id=1, source_target_pairs={{0,8},{8,0},{16,24},{24,16},{32,40},{40,32},{48,56},{56,48},{64,72... | collective-permute-start | bytes 3538952 | tf_op jit(solution)/shard_map/ppermute | solution.py:384
  32.5 2.8 %collective-permute-start = (f32[16,8,128]{2,1,0:T(8,128)S(1)}, f32[16,8,128]{2,1,0:T(8,128)S(1)}, u32[]{:S(2)}, u32[]{:S(2)}) collective-permute-start(f32[16,8,128]{2,1,0:T(8,128)S(1)} %get-tuple-element.49), channel_id=1, source_target_pairs={{0,8},{8,0},{16,24},{24,16},{32,40},{40,32},{48,56},{56,48},{64,72... | collective-permute-start | bytes 196616 | tf_op jit(solution)/shard_map/ppermute | solution.py:384
  51.0 5.5 %collective-permute-start.1 = (f32[8,128]{1,0:T(8,128)S(1)}, f32[8,128]{1,0:T(8,128)S(1)}, u32[]{:S(2)}, u32[]{:S(2)}) collective-permute-start(f32[8,128]{1,0:T(8,128)S(1)} %shard_map.89), channel_id=1, source_target_pairs={{80,0},{241,32},{34,64},{195,96},{132,128},{37,160},{182,192},{87,... | collective-permute-start | bytes 12296 | tf_op jit(solution)/shard_map/ppermute | solution.py:441
  81.3 6.8 %collective-permute-start.5 = (f32[8,3072]{1,0:T(8,128)S(1)}, f32[8,3072]{1,0:T(8,128)S(1)}, u32[]{:S(2)}, u32[]{:S(2)}) collective-permute-start(f32[8,3072]{1,0:T(8,128)S(1)} %get-tuple-element.57.full), channel_id=1, source_target_pairs={{0,8},{8,0},{16,24},{24,16},{32,40},{40,32},{48,56},{56,48},{64,72... | collective-permute-start | bytes 294920 | tf_op jit(solution)/shard_map/ppermute | solution.py:384
  86.5 1.6 %collective-permute-start.6 = (f32[8,128]{1,0:T(8,128)S(1)}, f32[8,128]{1,0:T(8,128)S(1)}, u32[]{:S(2)}, u32[]{:S(2)}) collective-permute-start(f32[8,128]{1,0:T(8,128)S(1)} %get-tuple-element.55.keep), channel_id=1, source_target_pairs={{0,8},{8,0},{16,24},{24,16},{32,40},{40,32},{48,56},{56,48},{64,72... | collective-permute-start | bytes 12296 | tf_op jit(solution)/shard_map/ppermute | solution.py:384
  86.6 4.5 %collective-permute-start.4 = (f32[8,128]{1,0:T(8,128)S(1)}, f32[8,128]{1,0:T(8,128)S(1)}, u32[]{:S(2)}, u32[]{:S(2)}) collective-permute-start(f32[8,128]{1,0:T(8,128)S(1)} %get-tuple-element.56), channel_id=1, source_target_pairs={{0,80},{32,241},{64,34},{96,195},{128,132},{160,37},{192,182},{224... | collective-permute-start | bytes 12296 | tf_op jit(solution)/shard_map/ppermute | solution.py:458
  104.3 4.0 %collective-permute-start.7 = (f32[16,8,128]{2,1,0:T(8,128)S(1)}, f32[16,8,128]{2,1,0:T(8,128)S(1)}, u32[]{:S(2)}, u32[]{:S(2)}) collective-permute-start(f32[16,8,128]{2,1,0:T(8,128)S(1)} %all_to_all.49.mine), channel_id=1, source_target_pairs={{0,8},{8,0},{16,24},{24,16},{32,40},{40,32},{48,56},{56,48},{64,72... | collective-permute-start | bytes 196616 | tf_op jit(solution)/shard_map/ppermute | solution.py:384
  132.0 20.7 %copy-start.1 = (f32[192,64]{0,1:T(8,128)S(1)}, f32[192,64]{0,1:T(8,128)}, u32[]{:S(2)}) copy-start(f32[192,64]{0,1:T(8,128)} %param.6) | copy-start | bytes 147460
  132.5 3.5 %collective-permute-start.8 = (f32[48,128]{1,0:T(8,128)S(1)}, f32[48,128]{1,0:T(8,128)S(1)}, u32[]{:S(2)}, u32[]{:S(2)}) collective-permute-start(f32[48,128]{1,0:T(8,128)S(1)} %get-tuple-element.64), channel_id=1, source_target_pairs={{0,8},{8,0},{16,24},{24,16},{32,40},{40,32},{48,56},{56,48},{64,72... | collective-permute-start | bytes 73736 | tf_op jit(solution)/shard_map/ppermute | solution.py:384
  150.0 4.1 %collective-permute-start.9 = (f32[48,128]{1,0:T(8,128)S(1)}, f32[48,128]{1,0:T(8,128)S(1)}, u32[]{:S(2)}, u32[]{:S(2)}) collective-permute-start(f32[48,128]{1,0:T(8,128)S(1)} %shard_map.100.mine), channel_id=1, source_target_pairs={{0,8},{8,0},{16,24},{24,16},{32,40},{40,32},{48,56},{56,48},{64,72... | collective-permute-start | bytes 73736 | tf_op jit(solution)/shard_map/ppermute | solution.py:384

commit v9 on v8

--- a/solution.py
+++ b/solution.py
@@ -336,27 +336,40 @@
         out[:, (2 * i + 1) * q : (2 * i + 2) * q] = turned[h:]
 
 
-def weight_grads(full, near_full, keep, near_keep, grad_in, grad_out):
-    w = grad_in.shape[1]
-    hidden = grad_in.shape[2]
-    core = core_index()
+def weight_grads(values, held, grad_in, grad_out, part_in, part_out, sems, first):
+    w, hidden = part_in.shape[1:]
+    core = core_index()
+    base = 2 * core if first else 2 - 2 * core
+    tile = held[...]
+    cols = jnp.transpose(jnp.where(core == 0, tile[:, 0:w], tile[:, w : 2 * w]))
     step = 512
-    for base, values, held in ((2 * core, full, keep), (2 - 2 * core, near_full, near_keep)):
-        held = held[...]
-        part = jnp.where(core == 0, held[:, 0:w], held[:, w : 2 * w])
-        cols = jnp.transpose(part)
-        for a in range(2):
+    copies = []
+    for a in range(2):
+        i, j = 2 * a, 2 * a + 1
+        for n, (part, out, r, q) in enumerate(
+            ((part_out, grad_out, 4, 0), (part_in, grad_in, 0, 4))
+        ):
             for h in range(0, hidden, step):
                 s = slice(h, h + step)
-                i, j = 2 * a, 2 * a + 1
-                grad_out[base + a, :, s] = (
-                    cols[:, 4 + i : 5 + i] * values[i : i + 1, s]
-                    + cols[:, 4 + j : 5 + j] * values[j : j + 1, s]
+                part[a, :, s] = (
+                    cols[:, r + i : r + i + 1] * values[q + i : q + i + 1, s]
+                    + cols[:, r + j : r + j + 1] * values[q + j : q + j + 1, s]
                 )
-                grad_in[base + a, :, s] = (
-                    cols[:, i : i + 1] * values[4 + i : 5 + i, s]
-                    + cols[:, j : j + 1] * values[4 + j : 5 + j, s]
-                )
+            copy = pltpu.make_async_copy(part.at[a], out.at[base + a], sems.at[2 * a + n])
+            copy.start()
+            copies.append(copy)
+    for copy in copies:
+        copy.wait()
+
+
+def own_weight_grads(full, held, grad_in, grad_out, full_on, held_on, part_in, part_out, sems):
+    full_on[...] = full[...]
+    held_on[...] = held[...]
+    weight_grads(full, held, grad_in, grad_out, part_in, part_out, sems, True)
+
+
+def near_weight_grads(full, held, _, __, grad_in, grad_out, part_in, part_out, sems):
+    weight_grads(full, held, grad_in, grad_out, part_in, part_out, sems, False)
 
 
 def per_device(tokens, router, w_in, w_out, grad_out):
@@ -396,10 +409,10 @@
         out_specs=far_spec,
         scratch_shapes=[
             pltpu.VMEM(turned.shape, F32),
-            pltpu.VMEM((4, rows_block, local_tokens // 4), F32),
+            pltpu.VMEM((1, rows_block, local_tokens), F32),
             pltpu.VMEM(spread, F32),
-            pltpu.SemaphoreType.DMA((5,)),
-            pltpu.SemaphoreType.DMA((4,)),
+            pltpu.SemaphoreType.DMA((2,)),
+            pltpu.SemaphoreType.DMA((1,)),
         ],
         compiler_params=limit,
     )(in_hbm(turned), in_hbm(tokens))
@@ -446,20 +459,24 @@
     tile, full = run(
         slot_rows, [(8, LANES), (8, hidden)], exchange(sent, S, groups), held, *weights
     )
-    grad_w_in, grad_w_out = run(
-        weight_grads,
-        [w_in.shape, w_out.shape],
-        full,
-        to_partner(full),
-        held,
-        to_partner(held),
-    )
-    tile, grad_w_in, grad_w_out = lax.optimization_barrier(
-        (lax.ppermute(tile, (S, E), from_owner), grad_w_in, grad_w_out)
-    )
-    sent = run(copies, tiles, tile)
-    mine = exchange(sent, S, groups)
-    near = to_partner(mine)
+    parts = [pltpu.VMEM(half, F32)] * 2 + [pltpu.SemaphoreType.DMA((4,))]
+    whole = [pltpu.HBM(w_in.shape, F32)] * 2
+    *w_grads, full, held = pl.pallas_call(
+        own_weight_grads,
+        out_shape=whole + [jax.ShapeDtypeStruct(v.shape, F32) for v in (full, held)],
+        in_specs=[vmem_spec] * 2,
+        out_specs=[far_spec] * 2 + [vmem_spec] * 2,
+        scratch_shapes=parts,
+        compiler_params=limit,
+    )(full, held)
+    tile, full, held, *w_grads = lax.optimization_barrier(
+        (lax.ppermute(tile, (S, E), from_owner), full, held, *w_grads)
+    )
+    mine = exchange(run(copies, tiles, tile), S, groups)
+    mine, full, held = lax.optimization_barrier((mine, full, held))
+    near, full, held = lax.optimization_barrier(
+        (to_partner(mine), to_partner(full), to_partner(held))
+    )
     sent, weights, rows = run(
         width_products,
         [spread, spread, (slots, rows_block)],
@@ -475,7 +492,17 @@
     grads = exchange(sent, E)
     fold = (rows_block // 4, 2 * slots)
     near, theirs = run(router_part, [fold, fold], grads, tokens)
-    sent = run(add_copies, (chips,) + fold, near, to_partner(theirs))
+    w_grads = pl.pallas_call(
+        near_weight_grads,
+        out_shape=whole,
+        in_specs=[vmem_spec] * 2 + [far_spec] * 2,
+        out_specs=[far_spec] * 2,
+        scratch_shapes=parts,
+        input_output_aliases={2: 0, 3: 1},
+        compiler_params=limit,
+    )(full, held, *(in_hbm(g) for g in w_grads))
+    theirs, grad_w_in, grad_w_out = lax.optimization_barrier((to_partner(theirs), *w_grads))
+    sent = run(add_copies, (chips,) + fold, near, theirs)
     got, weights, rows = lax.optimization_barrier((exchange(sent, S, groups), weights, rows))
     near = run(add_all, fold, got)
     grad_tokens = run(

time: 155 us -> 157 us (1.013)
    pallas_call x0 -> x2, Pallas kernels: none -> 3.88 us  [the longest x1 1.95 us: per_device(): pl.pallas_call(own_weight_grads, out_shape=whole + [jax.ShapeDtypeStruct(...]
    pallas_call x16 -> x15, Pallas kernels: 10.9 us -> 7.83 us  [run(): pl.pallas_call(kernel, out_shape=[jax.ShapeDtypeStruct(s, F32) for s in s...]
  transfers between devices with their start and end apart: 11 -> 11, of which waited for: 5 -> 5; matrix products, arithmetic and copies ran while one was open for 0% -> 0% of each run, Pallas kernels for 6% -> 7%
where the time goes in v9:
time: 157 us; the launch traced here: 156 us
  blocking collectives  99.2 us (63%)
  starting transfers between devices  26.4 us (17%)
  Pallas kernels  17.7 us (11%)
  waiting for transfers between devices  11 us (7%)
    all_to_all x8, blocking collectives, exchange(): lax.all_to_all(blocks, axis, 0, 0, axis_index_groups=groups, tiled=True)  99.2 us
    ppermute x8, starting transfers between devices, to_partner(): return lax.ppermute(values, S, partner)  16.4 us
    pallas_call x15, Pallas kernels, run(): pl.pallas_call(kernel, out_shape=[jax.ShapeDtypeStruct(s, F32) for s in s...  7.83 us
    all_to_all x1, starting transfers between devices, exchange(): lax.all_to_all(blocks, axis, 0, 0, axis_index_groups=groups, tiled=True)  7.49 us
    ppermute x1, waiting for transfers between devices, per_device(): lax.ppermute(tile, (S, E), to_owner)  4.63 us
    all_to_all x1, waiting for transfers between devices, exchange(): lax.all_to_all(blocks, axis, 0, 0, axis_index_groups=groups, tiled=True)  4.14 us
    pallas_call x1, Pallas kernels, per_device(): pl.pallas_call(stage, out_shape=[pltpu.HBM(half, F32)] * 2 + [pltpu.VMEM(...  3.49 us
  transfers between devices with their start and end apart: 11, of which 5 were waited for; matrix products, arithmetic and copies ran while one was open for 0% of the time, Pallas kernels for 7%

profile of v9, /device:TPU:1, one launch (start us, length us, event | category | flops | bytes accessed | tf_op | source)
XLA Modules:
  0.0 156.1 jit_solution(13348097967510916987)
XLA Ops:
  0.6 2.5 %shard_map.84 = f32[8,64,128]{2,1,0:T(8,128)} custom-call(f32[64,192]{1,0:T(8,128)} %bitcast.2, f32[192,1024]{1,0:T(8,128)} %tokens.3), custom_call_target="tpu_custom_call" | custom-call | tf_op jit(solution)/shard_map/pallas_call | solution.py:405
  3.1 7.5 %all-to-all-start = ((f32[8,64,128]{2,1,0:T(8,128)}), f32[8,64,128]{2,1,0:T(8,128)S(1)}, u32[]{:S(2)}, u32[]{:S(2)}) async-start(f32[8,64,128]{2,1,0:T(8,128)} %shard_map.84), calls=%async_computation | async-start | bytes 524288 | tf_op jit(solution)/shard_map/all_to_all | solution.py:29
  10.6 3.5 %shard_map.85 = (f32[2,48,3072]{2,1,0:T(8,128)}, f32[2,48,3072]{2,1,0:T(8,128)}, f32[2,48,3072]{2,1,0:T(8,128)S(1)}, f32[2,48,3072]{2,1,0:T(8,128)S(1)}, f32[192,1024]{1,0:T(8,128)S(1)}) custom-call(f32[4,48,3072]{2,1,0:T(8,128)} %w_in, f32[4,48,3072]{2,1,0:T(8,128)} %w_out, f32[192,1024]{1,0:T(8,128)} %tokens.3), custom_call_target="tpu_custom_call" | custom-call | tf_op jit(solution)/shard_map/pallas_call | solution.py:422
  14.1 4.1 %all-to-all-done.got = f32[8,64,128]{2,1,0:T(8,128)S(1)} async-done(((f32[8,64,128]{2,1,0:T(8,128)}), f32[8,64,128]{2,1,0:T(8,128)S(1)}, u32[]{:S(2)}, u32[]{:S(2)}) %all-to-all-start) | async-done | bytes 262176 | tf_op jit(solution)/shard_map/all_to_all | solution.py:29
  18.2 2.1 %collective-permute-start.2 = (f32[2,48,3072]{2,1,0:T(8,128)}, f32[2,48,3072]{2,1,0:T(8,128)S(1)}, u32[]{:S(2)}, u32[]{:S(2)}) collective-permute-start(f32[2,48,3072]{2,1,0:T(8,128)} %get-tuple-element.67), channel_id=1, source_target_pairs={{0,8},{8,0},{16,24},{24,16},{32,40},{40,32},{48,56},{56,48},{64,72... | collective-permute-start | bytes 3538952 | tf_op jit(solution)/shard_map/ppermute | solution.py:397
  20.4 10.4 %all_to_all.45.got.logits = f32[8,64,128]{2,1,0:T(8,128)S(1)} all-to-all(f32[8,64,128]{2,1,0:T(8,128)S(1)} %shard_map.86), channel_id=1, replica_groups=mesh['seq'=32,'expert'=8] {'expert'}, dimensions={0} | all-to-all | bytes 524288 | tf_op jit(solution)/shard_map/all_to_all | solution.py:29
  30.7 1.1 copy-done
  31.9 1.4 shard_map.87
  33.3 1.9 %collective-permute-start = (f32[16,8,128]{2,1,0:T(8,128)S(1)}, f32[16,8,128]{2,1,0:T(8,128)S(1)}, u32[]{:S(2)}, u32[]{:S(2)}) collective-permute-start(f32[16,8,128]{2,1,0:T(8,128)S(1)} %get-tuple-element.64), channel_id=1, source_target_pairs={{0,8},{8,0},{16,24},{24,16},{32,40},{40,32},{48,56},{56,48},{64,72... | collective-permute-start | bytes 196616 | tf_op jit(solution)/shard_map/ppermute | solution.py:397
  35.2 0.9 collective-permute-done.near
  36.2 15.5 %all_to_all.46.got = f32[16,8,128]{2,1,0:T(8,128)S(1)} all-to-all(f32[16,8,128]{2,1,0:T(8,128)S(1)} %shard_map.88), channel_id=1, replica_groups={{0,16,32,48,64,80,96,112,128,144,160,176,192,208,224,240},{8,24,40,56,7..., dimensions={0} | all-to-all | bytes 131072 | tf_op jit(solution)/shard_map/all_to_all | solution.py:29
  51.8 0.9 collective-permute-start.1
  52.7 4.6 %collective-permute-done.1.got = f32[8,128]{1,0:T(8,128)S(1)} collective-permute-done((f32[8,128]{1,0:T(8,128)S(1)}, f32[8,128]{1,0:T(8,128)S(1)}, u32[]{:S(2)}, u32[]{:S(2)}) %collective-permute-start.1) | collective-permute-done | bytes 4128 | tf_op jit(solution)/shard_map/ppermute | solution.py:454
  57.4 1.2 shard_map.90
  58.6 11.8 %all_to_all.47.got = f32[16,8,256]{2,1,0:T(8,128)S(1)} all-to-all(f32[16,8,256]{2,1,0:T(8,128)S(1)} %get-tuple-element.69), channel_id=1, replica_groups={{0,16,32,48,64,80,96,112,128,144,160,176,192,208,224,240},{8,24,40,56,7..., dimensions={0} | all-to-all | bytes 262144 | tf_op jit(solution)/shard_map/all_to_all | solution.py:29
  70.4 10.5 %all_to_all.48.got = f32[16,8,256]{2,1,0:T(8,128)S(1)} all-to-all(f32[16,8,256]{2,1,0:T(8,128)S(1)} %shard_map.91), channel_id=1, replica_groups={{0,16,32,48,64,80,96,112,128,144,160,176,192,208,224,240},{8,24,40,56,7..., dimensions={0} | all-to-all | bytes 262144 | tf_op jit(solution)/shard_map/all_to_all | solution.py:29
  80.9 1.2 shard_map.92
  82.1 1.5 collective-permute-start.4
  83.6 1.9 %shard_map.93 = (f32[4,48,3072]{2,1,0:T(8,128)}, f32[4,48,3072]{2,1,0:T(8,128)}, f32[8,3072]{1,0:T(8,128)S(1)}, f32[8,128]{1,0:T(8,128)S(1)}) custom-call(f32[8,3072]{1,0:T(8,128)S(1)} %get-tuple-element.72.full, f32[8,128]{1,0:T(8,128)S(1)} %get-tuple-element.70.keep.held), custom_call_target="tpu_custom_call" | custom-call | tf_op jit(solution)/shard_map/pallas_call | solution.py:464
  86.1 14.0 %all_to_all.49.mine = f32[16,8,128]{2,1,0:T(8,128)S(1)} all-to-all(f32[16,8,128]{2,1,0:T(8,128)S(1)} %shard_map.94), channel_id=1, replica_groups={{0,16,32,48,64,80,96,112,128,144,160,176,192,208,224,240},{8,24,40,56,7..., dimensions={0} | all-to-all | bytes 131072 | tf_op jit(solution)/shard_map/all_to_all | solution.py:29
  100.1 7.5 %collective-permute-start.6 = (f32[8,3072]{1,0:T(8,128)S(1)}, f32[8,3072]{1,0:T(8,128)S(1)}, u32[]{:S(2)}, u32[]{:S(2)}) collective-permute-start(f32[8,3072]{1,0:T(8,128)S(1)} %get-tuple-element.81), channel_id=1, source_target_pairs={{0,8},{8,0},{16,24},{24,16},{32,40},{40,32},{48,56},{56,48},{64,72... | collective-permute-start | bytes 294920 | tf_op jit(solution)/shard_map/ppermute | solution.py:397
  108.1 0.8 collective-permute-done.7.held
  108.9 0.9 shard_map.95
  109.9 11.7 %all_to_all.50.got = f32[8,64,128]{2,1,0:T(8,128)S(1)} all-to-all(f32[8,64,128]{2,1,0:T(8,128)S(1)} %get-tuple-element.85), channel_id=1, replica_groups=mesh['seq'=32,'expert'=8] {'expert'}, dimensions={0} | all-to-all | bytes 524288 | tf_op jit(solution)/shard_map/all_to_all | solution.py:29
  121.6 10.5 %all_to_all.51.got = f32[8,64,128]{2,1,0:T(8,128)S(1)} all-to-all(f32[8,64,128]{2,1,0:T(8,128)S(1)} %shard_map.96), channel_id=1, replica_groups=mesh['seq'=32,'expert'=8] {'expert'}, dimensions={0} | all-to-all | bytes 524288 | tf_op jit(solution)/shard_map/all_to_all | solution.py:29
  132.1 0.5 shard_map.97
  132.7 2.7 %collective-permute-start.8 = (f32[48,128]{1,0:T(8,128)S(1)}, f32[48,128]{1,0:T(8,128)S(1)}, u32[]{:S(2)}, u32[]{:S(2)}) collective-permute-start(f32[48,128]{1,0:T(8,128)S(1)} %get-tuple-element.87), channel_id=1, source_target_pairs={{0,8},{8,0},{16,24},{24,16},{32,40},{40,32},{48,56},{56,48},{64,72... | collective-permute-start | bytes 73736 | tf_op jit(solution)/shard_map/ppermute | solution.py:397
  135.3 1.9 %shard_map.98 = (f32[4,48,3072]{2,1,0:T(8,128)}, f32[4,48,3072]{2,1,0:T(8,128)}) custom-call(f32[8,3072]{1,0:T(8,128)S(1)} %collective-permute-done.6.full, f32[8,128]{1,0:T(8,128)S(1)} %collective-permute-done.7.held, f32[4,48,3072]{2,1,0:T(8,128)} %get-tuple-element.90._, ...), custom_call_target="tpu_custom_call", output_to_operand_aliasing={{0}: (2, {}), {1}: (3, {})} | custom-call | tf_op jit(solution)/shard_map/pallas_call | solution.py:495
  137.3 14.8 %all_to_all.52.got = f32[16,48,128]{2,1,0:T(8,128)S(1)} all-to-all(f32[16,48,128]{2,1,0:T(8,128)S(1)} %shard_map.99), channel_id=1, replica_groups={{0,16,32,48,64,80,96,112,128,144,160,176,192,208,224,240},{8,24,40,56,7..., dimensions={0} | all-to-all | bytes 786432 | tf_op jit(solution)/shard_map/all_to_all | solution.py:29
  152.1 1.8 %collective-permute-start.9 = (f32[48,128]{1,0:T(8,128)S(1)}, f32[48,128]{1,0:T(8,128)S(1)}, u32[]{:S(2)}, u32[]{:S(2)}) collective-permute-start(f32[48,128]{1,0:T(8,128)S(1)} %shard_map.101.mine), channel_id=1, source_target_pairs={{0,8},{8,0},{16,24},{24,16},{32,40},{40,32},{48,56},{56,48},{64,72... | collective-permute-start | bytes 73736 | tf_op jit(solution)/shard_map/ppermute | solution.py:397
  153.9 1.4 shard_map.100
  155.3 0.8 shard_map.102
  (23 shorter events, 1.4 us)
Async XLA Ops:
  3.1 15.1 %all-to-all-start = ((f32[8,64,128]{2,1,0:T(8,128)}), f32[8,64,128]{2,1,0:T(8,128)S(1)}, u32[]{:S(2)}, u32[]{:S(2)}) async-start(f32[8,64,128]{2,1,0:T(8,128)} %shard_map.84), calls=%async_computation | async-start | bytes 524288 | tf_op jit(solution)/shard_map/all_to_all | solution.py:29
  18.2 39.1 %collective-permute-start.2 = (f32[2,48,3072]{2,1,0:T(8,128)}, f32[2,48,3072]{2,1,0:T(8,128)S(1)}, u32[]{:S(2)}, u32[]{:S(2)}) collective-permute-start(f32[2,48,3072]{2,1,0:T(8,128)} %get-tuple-element.67), channel_id=1, source_target_pairs={{0,8},{8,0},{16,24},{24,16},{32,40},{40,32},{48,56},{56,48},{64,72... | collective-permute-start | bytes 3538952 | tf_op jit(solution)/shard_map/ppermute | solution.py:397
  20.3 37.0 %collective-permute-start.3 = (f32[2,48,3072]{2,1,0:T(8,128)}, f32[2,48,3072]{2,1,0:T(8,128)S(1)}, u32[]{:S(2)}, u32[]{:S(2)}) collective-permute-start(f32[2,48,3072]{2,1,0:T(8,128)} %get-tuple-element.68), channel_id=1, source_target_pairs={{0,8},{8,0},{16,24},{24,16},{32,40},{40,32},{48,56},{56,48},{64,72... | collective-permute-start | bytes 3538952 | tf_op jit(solution)/shard_map/ppermute | solution.py:397
  30.7 1.1 copy-start
  33.3 2.8 %collective-permute-start = (f32[16,8,128]{2,1,0:T(8,128)S(1)}, f32[16,8,128]{2,1,0:T(8,128)S(1)}, u32[]{:S(2)}, u32[]{:S(2)}) collective-permute-start(f32[16,8,128]{2,1,0:T(8,128)S(1)} %get-tuple-element.64), channel_id=1, source_target_pairs={{0,8},{8,0},{16,24},{24,16},{32,40},{40,32},{48,56},{56,48},{64,72... | collective-permute-start | bytes 196616 | tf_op jit(solution)/shard_map/ppermute | solution.py:397
  51.8 5.5 %collective-permute-start.1 = (f32[8,128]{1,0:T(8,128)S(1)}, f32[8,128]{1,0:T(8,128)S(1)}, u32[]{:S(2)}, u32[]{:S(2)}) collective-permute-start(f32[8,128]{1,0:T(8,128)S(1)} %shard_map.89), channel_id=1, source_target_pairs={{80,0},{241,32},{34,64},{195,96},{132,128},{37,160},{182,192},{87,... | collective-permute-start | bytes 12296 | tf_op jit(solution)/shard_map/ppermute | solution.py:454
  80.9 28.0 %copy-start.1 = (f32[192,1024]{1,0:T(8,128)S(1)}, f32[192,1024]{1,0:T(8,128)}, u32[]{:S(2)}) copy-start(f32[192,1024]{1,0:T(8,128)} %grad_out.3) | copy-start | bytes 2359300
  82.1 4.0 %collective-permute-start.4 = (f32[8,128]{1,0:T(8,128)S(1)}, f32[8,128]{1,0:T(8,128)S(1)}, u32[]{:S(2)}, u32[]{:S(2)}) collective-permute-start(f32[8,128]{1,0:T(8,128)S(1)} %get-tuple-element.71), channel_id=1, source_target_pairs={{0,80},{32,241},{64,34},{96,195},{128,132},{160,37},{192,182},{224... | collective-permute-start | bytes 12296 | tf_op jit(solution)/shard_map/ppermute | solution.py:473
  100.1 8.8 %collective-permute-start.6 = (f32[8,3072]{1,0:T(8,128)S(1)}, f32[8,3072]{1,0:T(8,128)S(1)}, u32[]{:S(2)}, u32[]{:S(2)}) collective-permute-start(f32[8,3072]{1,0:T(8,128)S(1)} %get-tuple-element.81), channel_id=1, source_target_pairs={{0,8},{8,0},{16,24},{24,16},{32,40},{40,32},{48,56},{56,48},{64,72... | collective-permute-start | bytes 294920 | tf_op jit(solution)/shard_map/ppermute | solution.py:397
  107.6 1.3 collective-permute-start.5
  107.6 1.3 collective-permute-start.7
  132.7 21.3 %copy-start.2 = (f32[192,64]{0,1:T(8,128)S(1)}, f32[192,64]{0,1:T(8,128)}, u32[]{:S(2)}) copy-start(f32[192,64]{0,1:T(8,128)} %param.6) | copy-start | bytes 147460
  132.7 4.6 %collective-permute-start.8 = (f32[48,128]{1,0:T(8,128)S(1)}, f32[48,128]{1,0:T(8,128)S(1)}, u32[]{:S(2)}, u32[]{:S(2)}) collective-permute-start(f32[48,128]{1,0:T(8,128)S(1)} %get-tuple-element.87), channel_id=1, source_target_pairs={{0,8},{8,0},{16,24},{24,16},{32,40},{40,32},{48,56},{56,48},{64,72... | collective-permute-start | bytes 73736 | tf_op jit(solution)/shard_map/ppermute | solution.py:397
  152.1 3.2 %collective-permute-start.9 = (f32[48,128]{1,0:T(8,128)S(1)}, f32[48,128]{1,0:T(8,128)S(1)}, u32[]{:S(2)}, u32[]{:S(2)}) collective-permute-start(f32[48,128]{1,0:T(8,128)S(1)} %shard_map.101.mine), channel_id=1, source_target_pairs={{0,8},{8,0},{16,24},{24,16},{32,40},{40,32},{48,56},{56,48},{64,72... | collective-permute-start | bytes 73736 | tf_op jit(solution)/shard_map/ppermute | solution.py:397

commit v10 on v8

--- a/solution.py
+++ b/solution.py
@@ -40,7 +40,7 @@
         in_specs=[spec] * len(values),
         out_specs=[spec] * len(shapes),
         scratch_shapes=[pltpu.VMEM(s, F32) for s in scratch],
-        compiler_params=pltpu.CompilerParams(vmem_limit_bytes=40 * 1024 * 1024),
+        compiler_params=pltpu.CompilerParams(vmem_limit_bytes=16 * 1024 * 1024),
         cost_estimate=pl.CostEstimate(flops=flops, bytes_accessed=size, transcendentals=0),
     )(*values)
     return out[0] if single else out
@@ -80,49 +80,41 @@
     return [(b, e, seat(b, e, column)) for b in range(2) for e in range(n)]
 
 
-def logit_parts(router, tokens, out, left, right, parts, sems, stores):
-    n, _, cut = right.shape
-    each = cut // LANES
-    copies = [pltpu.make_async_copy(router, left, sems.at[n])]
-    for i in range(n):
-        block = tokens.at[:, pl.ds(i * cut, cut)]
-        copies.append(pltpu.make_async_copy(block, right.at[i], sems.at[i]))
-    for copy in copies:
-        copy.start()
-    copies[0].wait()
-    moves = []
-    for i in range(n):
-        copies[i + 1].wait()
-        part = contract(left[...], right[i], 1, 0)
-        for j in range(each):
-            parts[i * each + j] = part[:, j * LANES : (j + 1) * LANES]
-        s = pl.ds(i * each, each)
-        moves.append(pltpu.make_async_copy(parts.at[s], out.at[s], stores.at[i]))
-        moves[i].start()
-    for move in moves:
-        move.wait()
-
-
-def stage(w_in, w_out, tokens, far_in, far_out, own_in, own_out, x, held, sems):
-    core = core_index()
-    half = own_in.shape[0]
-    far = pl.ds(half * (1 - core), half)
-    near = pl.ds(half * core, half)
+def start_up(router, tokens, w_in, w_out, out, x, far_in, far_out, left, held, sems):
+    half = held.shape[1]
+    far = pl.ds(half * (1 - core_index()), half)
     pairs = [
+        (router, left),
+        (tokens, x),
         (w_in.at[far], held.at[0]),
         (w_out.at[far], held.at[1]),
-        (tokens, x),
-        (w_in.at[near], own_in),
-        (w_out.at[near], own_out),
     ]
     copies = [pltpu.make_async_copy(a, b, sems.at[i]) for i, (a, b) in enumerate(pairs)]
     for copy in copies:
         copy.start()
-    for i, out in enumerate((far_in, far_out)):
-        copies[i].wait()
-        copies.append(pltpu.make_async_copy(held.at[i], out, sems.at[5 + i]))
+    copies[0].wait()
+    copies[1].wait()
+    for i, place in enumerate((far_in, far_out)):
+        copies[2 + i].wait()
+        copies.append(pltpu.make_async_copy(held.at[i], place, sems.at[4 + i]))
         copies[-1].start()
-    for copy in copies[2:]:
+    part = contract(left[...], x[...], 1, 0)
+    for i in range(out.shape[0]):
+        out[i] = part[:, i * LANES : (i + 1) * LANES]
+    for copy in copies[4:]:
+        copy.wait()
+
+
+def load_own(w_in, w_out, own_in, own_out, sems):
+    half = own_in.shape[0]
+    own = pl.ds(half * core_index(), half)
+    copies = [
+        pltpu.make_async_copy(w_in.at[own], own_in, sems.at[0]),
+        pltpu.make_async_copy(w_out.at[own], own_out, sems.at[1]),
+    ]
+    for copy in copies:
+        copy.start()
+    for copy in copies:
         copy.wait()
 
 
@@ -388,37 +380,27 @@
 
     far_spec = pl.BlockSpec(memory_space=pltpu.HBM)
     vmem_spec = pl.BlockSpec(memory_space=pltpu.VMEM)
-    limit = pltpu.CompilerParams(vmem_limit_bytes=40 * 1024 * 1024)
-    sent = pl.pallas_call(
-        logit_parts,
-        out_shape=pltpu.HBM(spread, F32),
-        in_specs=[far_spec, far_spec],
-        out_specs=far_spec,
+    limit = pltpu.CompilerParams(vmem_limit_bytes=16 * 1024 * 1024)
+    half = (experts // 2,) + w_in.shape[1:]
+    sent, tokens, far_in, far_out = pl.pallas_call(
+        start_up,
+        out_shape=[
+            pltpu.VMEM(spread, F32),
+            pltpu.VMEM(tokens.shape, F32),
+            pltpu.HBM(half, F32),
+            pltpu.HBM(half, F32),
+        ],
+        in_specs=[far_spec] * 4,
+        out_specs=[vmem_spec] * 2 + [far_spec] * 2,
         scratch_shapes=[
             pltpu.VMEM(turned.shape, F32),
-            pltpu.VMEM((4, rows_block, local_tokens // 4), F32),
-            pltpu.VMEM(spread, F32),
-            pltpu.SemaphoreType.DMA((5,)),
-            pltpu.SemaphoreType.DMA((4,)),
+            pltpu.VMEM((2,) + half, F32),
+            pltpu.SemaphoreType.DMA((6,)),
         ],
         compiler_params=limit,
-    )(in_hbm(turned), in_hbm(tokens))
-    sent, w_in, w_out = lax.optimization_barrier((sent, w_in, w_out))
-    got = exchange(sent, E)
-    half = (experts // 2,) + w_in.shape[1:]
-    staged = pl.pallas_call(
-        stage,
-        out_shape=[pltpu.HBM(half, F32)] * 2
-        + [pltpu.VMEM(half, F32)] * 2
-        + [pltpu.VMEM(tokens.shape, F32)],
-        in_specs=[far_spec] * 3,
-        out_specs=[far_spec] * 2 + [vmem_spec] * 3,
-        scratch_shapes=[pltpu.VMEM((2,) + half, F32), pltpu.SemaphoreType.DMA((7,))],
-        compiler_params=limit,
-    )(in_hbm(w_in), in_hbm(w_out), in_hbm(tokens))
-    got, far_in, far_out, own_in, own_out, tokens = lax.optimization_barrier((got, *staged))
-    logits = exchange(run(add_spread, spread, got), E)
-    weights = (own_in, own_out, to_partner(far_in), to_partner(far_out))
+    )(in_hbm(turned), in_hbm(tokens), in_hbm(w_in), in_hbm(w_out))
+    near_in, near_out = to_partner(far_in), to_partner(far_out)
+    logits = exchange(run(add_spread, spread, exchange(sent, E)), E)
 
     tiles = (chips, 8, LANES)
     mine, near, shares = run(
@@ -433,12 +415,25 @@
     tile = run(
         functools.partial(merge_chips, piece=piece), (8, LANES), exchange(sent, S, groups)
     )
+    tile, w_in, w_out = lax.optimization_barrier((tile, w_in, w_out))
+    own_in, own_out = pl.pallas_call(
+        load_own,
+        out_shape=[pltpu.VMEM(half, F32)] * 2,
+        in_specs=[far_spec] * 2,
+        out_specs=[vmem_spec] * 2,
+        scratch_shapes=[pltpu.SemaphoreType.DMA((2,))],
+        compiler_params=limit,
+    )(in_hbm(w_in), in_hbm(w_out))
+    tile, own_in, own_out = lax.optimization_barrier(
+        (lax.ppermute(tile, (S, E), to_owner), own_in, own_out)
+    )
+    weights = (own_in, own_out, near_in, near_out)
     share = hidden // chips
     cut = -(-share // LANES) * LANES
     sent, held = run(
         hidden_parts,
         [(chips, 8, cut), (8, LANES)],
-        lax.ppermute(tile, (S, E), to_owner),
+        tile,
         *weights,
         scratch=[(8, hidden)],
     )

time: 155 us -> 156 us (level)
  blocking collectives: 97.9 us -> 111 us
  waiting for transfers between devices: 11.4 us -> 5.65 us
  starting transfers between devices: 27.6 us -> 22.3 us
    all_to_all x8 -> x9, blocking collectives: 97.9 us -> 111 us  [exchange(): lax.all_to_all(blocks, axis, 0, 0, axis_index_groups=groups, tiled=True)]
    all_to_all x1 -> x0, starting transfers between devices: 7.49 us -> none  [exchange(): lax.all_to_all(blocks, axis, 0, 0, axis_index_groups=groups, tiled=True)]
    all_to_all x1 -> x0, waiting for transfers between devices: 4.14 us -> none  [exchange(): lax.all_to_all(blocks, axis, 0, 0, axis_index_groups=groups, tiled=True)]
    ppermute x8, starting transfers between devices: 17.7 us -> 19.9 us  [to_partner(): return lax.ppermute(values, S, partner)]
    pallas_call x2, Pallas kernels: 6.31 us -> 4.64 us  [the longest x1 3 us: per_device(): pl.pallas_call(start_up, out_shape=[pltpu.VMEM(spread, F32), pltpu.VMEM(t...]
    ppermute x1, waiting for transfers between devices: 4.63 us -> 2.98 us  [per_device(): lax.ppermute(tile, (S, E), to_owner)]
  transfers between devices with their start and end apart: 11 -> 10, of which waited for: 5 -> 4; matrix products, arithmetic and copies ran while one was open for 0% -> 0% of each run, Pallas kernels for 6% -> 5%
where the time goes in v10:
time: 156 us; the launch traced here: 155 us
  blocking collectives  111 us (71%)
  starting transfers between devices  22.3 us (14%)
  Pallas kernels  15.8 us (10%)
  waiting for transfers between devices  5.65 us (4%)
    all_to_all x9, blocking collectives, exchange(): lax.all_to_all(blocks, axis, 0, 0, axis_index_groups=groups, tiled=True)  111 us
    ppermute x8, starting transfers between devices, to_partner(): return lax.ppermute(values, S, partner)  19.9 us
    pallas_call x16, Pallas kernels, run(): pl.pallas_call(kernel, out_shape=[jax.ShapeDtypeStruct(s, F32) for s in s...  11.1 us
  transfers between devices with their start and end apart: 10, of which 4 were waited for; matrix products, arithmetic and copies ran while one was open for 0% of the time, Pallas kernels for 5%

profile of v10, /device:TPU:1, one launch (start us, length us, event | category | flops | bytes accessed | tf_op | source)
XLA Modules:
  0.0 155.1 jit_solution(16344594518631464886)
XLA Ops:
  0.6 3.0 %shard_map.84 = (f32[8,64,128]{2,1,0:T(8,128)S(1)}, f32[192,1024]{1,0:T(8,128)S(1)}, f32[2,48,3072]{2,1,0:T(8,128)}, f32[2,48,3072]{2,1,0:T(8,128)}) custom-call(f32[64,192]{1,0:T(8,128)} %bitcast.2, f32[192,1024]{1,0:T(8,128)} %tokens.1, f32[4,48,3072]{2,1,0:T(8,128)} %w_in.2, f32[4,48,3072]{2,1,0:T(8,128)} %w_out.2), custom_call_target="tpu_custom_call" | custom-call | tf_op jit(solution)/shard_map/pallas_call | solution.py:385
  3.7 3.3 %collective-permute-start.2 = (f32[2,48,3072]{2,1,0:T(8,128)}, f32[2,48,3072]{2,1,0:T(8,128)S(1)}, u32[]{:S(2)}, u32[]{:S(2)}) collective-permute-start(f32[2,48,3072]{2,1,0:T(8,128)} %get-tuple-element.48), channel_id=1, source_target_pairs={{0,8},{8,0},{16,24},{24,16},{32,40},{40,32},{48,56},{56,48},{64,72... | collective-permute-start | bytes 3538952 | tf_op jit(solution)/shard_map/ppermute | solution.py:376
  7.1 12.6 %all_to_all.45.got = f32[8,64,128]{2,1,0:T(8,128)S(1)} all-to-all(f32[8,64,128]{2,1,0:T(8,128)S(1)} %get-tuple-element.36), channel_id=1, replica_groups=mesh['seq'=32,'expert'=8] {'expert'}, dimensions={0} | all-to-all | bytes 524288 | tf_op jit(solution)/shard_map/all_to_all | solution.py:29
  19.7 10.5 %all_to_all.46.got.logits = f32[8,64,128]{2,1,0:T(8,128)S(1)} all-to-all(f32[8,64,128]{2,1,0:T(8,128)S(1)} %shard_map.85), channel_id=1, replica_groups=mesh['seq'=32,'expert'=8] {'expert'}, dimensions={0} | all-to-all | bytes 524288 | tf_op jit(solution)/shard_map/all_to_all | solution.py:29
  30.2 1.4 shard_map.86
  31.7 2.7 %collective-permute-start = (f32[16,8,128]{2,1,0:T(8,128)S(1)}, f32[16,8,128]{2,1,0:T(8,128)S(1)}, u32[]{:S(2)}, u32[]{:S(2)}) collective-permute-start(f32[16,8,128]{2,1,0:T(8,128)S(1)} %get-tuple-element.39), channel_id=1, source_target_pairs={{0,8},{8,0},{16,24},{24,16},{32,40},{40,32},{48,56},{56,48},{64,72... | collective-permute-start | bytes 196616 | tf_op jit(solution)/shard_map/ppermute | solution.py:376
  34.4 0.9 collective-permute-done.near
  35.3 0.1 shard_map.87
  35.4 15.5 %all_to_all.47.got = f32[16,8,128]{2,1,0:T(8,128)S(1)} all-to-all(f32[16,8,128]{2,1,0:T(8,128)S(1)} %shard_map.87), channel_id=1, replica_groups={{0,16,32,48,64,80,96,112,128,144,160,176,192,208,224,240},{8,24,40,56,7..., dimensions={0} | all-to-all | bytes 131072 | tf_op jit(solution)/shard_map/all_to_all | solution.py:29
  51.0 0.9 collective-permute-start.1
  52.0 1.6 %shard_map.89 = (f32[2,48,3072]{2,1,0:T(8,128)S(1)}, f32[2,48,3072]{2,1,0:T(8,128)S(1)}) custom-call(f32[4,48,3072]{2,1,0:T(8,128)} %w_in.2, f32[4,48,3072]{2,1,0:T(8,128)} %w_out.2), custom_call_target="tpu_custom_call" | custom-call | tf_op jit(solution)/shard_map/pallas_call | solution.py:419
  53.6 3.0 %collective-permute-done.1.got = f32[8,128]{1,0:T(8,128)S(1)} collective-permute-done((f32[8,128]{1,0:T(8,128)S(1)}, f32[8,128]{1,0:T(8,128)S(1)}, u32[]{:S(2)}, u32[]{:S(2)}) %collective-permute-start.1) | collective-permute-done | bytes 4128 | tf_op jit(solution)/shard_map/ppermute | solution.py:428
  56.6 1.3 shard_map.90
  57.9 11.8 %all_to_all.48.got = f32[16,8,256]{2,1,0:T(8,128)S(1)} all-to-all(f32[16,8,256]{2,1,0:T(8,128)S(1)} %get-tuple-element.50), channel_id=1, replica_groups={{0,16,32,48,64,80,96,112,128,144,160,176,192,208,224,240},{8,24,40,56,7..., dimensions={0} | all-to-all | bytes 262144 | tf_op jit(solution)/shard_map/all_to_all | solution.py:29
  69.8 10.5 %all_to_all.49.got = f32[16,8,256]{2,1,0:T(8,128)S(1)} all-to-all(f32[16,8,256]{2,1,0:T(8,128)S(1)} %shard_map.91), channel_id=1, replica_groups={{0,16,32,48,64,80,96,112,128,144,160,176,192,208,224,240},{8,24,40,56,7..., dimensions={0} | all-to-all | bytes 262144 | tf_op jit(solution)/shard_map/all_to_all | solution.py:29
  80.3 1.2 shard_map.92
  81.5 5.2 %collective-permute-start.5 = (f32[8,3072]{1,0:T(8,128)S(1)}, f32[8,3072]{1,0:T(8,128)S(1)}, u32[]{:S(2)}, u32[]{:S(2)}) collective-permute-start(f32[8,3072]{1,0:T(8,128)S(1)} %get-tuple-element.53.full), channel_id=1, source_target_pairs={{0,8},{8,0},{16,24},{24,16},{32,40},{40,32},{48,56},{56,48},{64,72... | collective-permute-start | bytes 294920 | tf_op jit(solution)/shard_map/ppermute | solution.py:376
  86.8 1.5 collective-permute-start.4
  88.3 3.0 %shard_map.93 = (f32[4,48,3072]{2,1,0:T(8,128)}, f32[4,48,3072]{2,1,0:T(8,128)}) custom-call(f32[8,3072]{1,0:T(8,128)S(1)} %get-tuple-element.53.full, f32[8,3072]{1,0:T(8,128)S(1)} %collective-permute-done.5.near_full, f32[8,128]{1,0:T(8,128)S(1)} %get-tuple-element.51.keep, f32[8,128]{1,0:T(8,128)S(1)} %collective-permute-done.6.near_keep), custom_call_target="tpu_custom_call" | custom-call | bytes 4923392 | tf_op jit(solution)/shard_map/pallas_call | solution.py:37
  91.3 13.2 %all_to_all.50.mine = f32[16,8,128]{2,1,0:T(8,128)S(1)} all-to-all(f32[16,8,128]{2,1,0:T(8,128)S(1)} %shard_map.94), channel_id=1, replica_groups={{0,16,32,48,64,80,96,112,128,144,160,176,192,208,224,240},{8,24,40,56,7..., dimensions={0} | all-to-all | bytes 131072 | tf_op jit(solution)/shard_map/all_to_all | solution.py:29
  104.5 3.1 %collective-permute-start.7 = (f32[16,8,128]{2,1,0:T(8,128)S(1)}, f32[16,8,128]{2,1,0:T(8,128)S(1)}, u32[]{:S(2)}, u32[]{:S(2)}) collective-permute-start(f32[16,8,128]{2,1,0:T(8,128)S(1)} %all_to_all.50.mine), channel_id=1, source_target_pairs={{0,8},{8,0},{16,24},{24,16},{32,40},{40,32},{48,56},{56,48},{64,72... | collective-permute-start | bytes 196616 | tf_op jit(solution)/shard_map/ppermute | solution.py:376
  107.6 0.9 collective-permute-done.7.near
  108.5 0.9 shard_map.95
  109.4 12.2 %all_to_all.51.got = f32[8,64,128]{2,1,0:T(8,128)S(1)} all-to-all(f32[8,64,128]{2,1,0:T(8,128)S(1)} %get-tuple-element.58), channel_id=1, replica_groups=mesh['seq'=32,'expert'=8] {'expert'}, dimensions={0} | all-to-all | bytes 524288 | tf_op jit(solution)/shard_map/all_to_all | solution.py:29
  121.7 10.5 %all_to_all.52.got = f32[8,64,128]{2,1,0:T(8,128)S(1)} all-to-all(f32[8,64,128]{2,1,0:T(8,128)S(1)} %shard_map.96), channel_id=1, replica_groups=mesh['seq'=32,'expert'=8] {'expert'}, dimensions={0} | all-to-all | bytes 524288 | tf_op jit(solution)/shard_map/all_to_all | solution.py:29
  132.2 0.5 shard_map.97
  132.7 2.7 %collective-permute-start.8 = (f32[48,128]{1,0:T(8,128)S(1)}, f32[48,128]{1,0:T(8,128)S(1)}, u32[]{:S(2)}, u32[]{:S(2)}) collective-permute-start(f32[48,128]{1,0:T(8,128)S(1)} %get-tuple-element.60), channel_id=1, source_target_pairs={{0,8},{8,0},{16,24},{24,16},{32,40},{40,32},{48,56},{56,48},{64,72... | collective-permute-start | bytes 73736 | tf_op jit(solution)/shard_map/ppermute | solution.py:376
  135.4 0.8 collective-permute-done.8.theirs
  136.3 13.9 %all_to_all.53.got = f32[16,48,128]{2,1,0:T(8,128)S(1)} all-to-all(f32[16,48,128]{2,1,0:T(8,128)S(1)} %shard_map.98), channel_id=1, replica_groups={{0,16,32,48,64,80,96,112,128,144,160,176,192,208,224,240},{8,24,40,56,7..., dimensions={0} | all-to-all | bytes 786432 | tf_op jit(solution)/shard_map/all_to_all | solution.py:29
  150.2 2.6 %collective-permute-start.9 = (f32[48,128]{1,0:T(8,128)S(1)}, f32[48,128]{1,0:T(8,128)S(1)}, u32[]{:S(2)}, u32[]{:S(2)}) collective-permute-start(f32[48,128]{1,0:T(8,128)S(1)} %shard_map.100.mine), channel_id=1, source_target_pairs={{0,8},{8,0},{16,24},{24,16},{32,40},{40,32},{48,56},{56,48},{64,72... | collective-permute-start | bytes 73736 | tf_op jit(solution)/shard_map/ppermute | solution.py:376
  152.9 1.4 shard_map.99
  154.3 0.8 shard_map.101
  (19 shorter events, 0.4 us)
Async XLA Ops:
  3.6 26.6 %copy-start = (f32[192,1024]{1,0:T(8,128)S(1)}, f32[192,1024]{1,0:T(8,128)}, u32[]{:S(2)}) copy-start(f32[192,1024]{1,0:T(8,128)} %grad_out.3) | copy-start | bytes 2359300
  3.7 52.9 %collective-permute-start.2 = (f32[2,48,3072]{2,1,0:T(8,128)}, f32[2,48,3072]{2,1,0:T(8,128)S(1)}, u32[]{:S(2)}, u32[]{:S(2)}) collective-permute-start(f32[2,48,3072]{2,1,0:T(8,128)} %get-tuple-element.48), channel_id=1, source_target_pairs={{0,8},{8,0},{16,24},{24,16},{32,40},{40,32},{48,56},{56,48},{64,72... | collective-permute-start | bytes 3538952 | tf_op jit(solution)/shard_map/ppermute | solution.py:376
  7.0 49.6 %collective-permute-start.3 = (f32[2,48,3072]{2,1,0:T(8,128)}, f32[2,48,3072]{2,1,0:T(8,128)S(1)}, u32[]{:S(2)}, u32[]{:S(2)}) collective-permute-start(f32[2,48,3072]{2,1,0:T(8,128)} %get-tuple-element.49), channel_id=1, source_target_pairs={{0,8},{8,0},{16,24},{24,16},{32,40},{40,32},{48,56},{56,48},{64,72... | collective-permute-start | bytes 3538952 | tf_op jit(solution)/shard_map/ppermute | solution.py:376
  31.7 3.6 %collective-permute-start = (f32[16,8,128]{2,1,0:T(8,128)S(1)}, f32[16,8,128]{2,1,0:T(8,128)S(1)}, u32[]{:S(2)}, u32[]{:S(2)}) collective-permute-start(f32[16,8,128]{2,1,0:T(8,128)S(1)} %get-tuple-element.39), channel_id=1, source_target_pairs={{0,8},{8,0},{16,24},{24,16},{32,40},{40,32},{48,56},{56,48},{64,72... | collective-permute-start | bytes 196616 | tf_op jit(solution)/shard_map/ppermute | solution.py:376
  51.0 5.5 %collective-permute-start.1 = (f32[8,128]{1,0:T(8,128)S(1)}, f32[8,128]{1,0:T(8,128)S(1)}, u32[]{:S(2)}, u32[]{:S(2)}) collective-permute-start(f32[8,128]{1,0:T(8,128)S(1)} %shard_map.88), channel_id=1, source_target_pairs={{80,0},{241,32},{34,64},{195,96},{132,128},{37,160},{182,192},{87,... | collective-permute-start | bytes 12296 | tf_op jit(solution)/shard_map/ppermute | solution.py:428
  81.5 6.8 %collective-permute-start.5 = (f32[8,3072]{1,0:T(8,128)S(1)}, f32[8,3072]{1,0:T(8,128)S(1)}, u32[]{:S(2)}, u32[]{:S(2)}) collective-permute-start(f32[8,3072]{1,0:T(8,128)S(1)} %get-tuple-element.53.full), channel_id=1, source_target_pairs={{0,8},{8,0},{16,24},{24,16},{32,40},{40,32},{48,56},{56,48},{64,72... | collective-permute-start | bytes 294920 | tf_op jit(solution)/shard_map/ppermute | solution.py:376
  86.7 1.6 %collective-permute-start.6 = (f32[8,128]{1,0:T(8,128)S(1)}, f32[8,128]{1,0:T(8,128)S(1)}, u32[]{:S(2)}, u32[]{:S(2)}) collective-permute-start(f32[8,128]{1,0:T(8,128)S(1)} %get-tuple-element.51.keep), channel_id=1, source_target_pairs={{0,8},{8,0},{16,24},{24,16},{32,40},{40,32},{48,56},{56,48},{64,72... | collective-permute-start | bytes 12296 | tf_op jit(solution)/shard_map/ppermute | solution.py:376
  86.8 4.5 %collective-permute-start.4 = (f32[8,128]{1,0:T(8,128)S(1)}, f32[8,128]{1,0:T(8,128)S(1)}, u32[]{:S(2)}, u32[]{:S(2)}) collective-permute-start(f32[8,128]{1,0:T(8,128)S(1)} %get-tuple-element.52), channel_id=1, source_target_pairs={{0,80},{32,241},{64,34},{96,195},{128,132},{160,37},{192,182},{224... | collective-permute-start | bytes 12296 | tf_op jit(solution)/shard_map/ppermute | solution.py:453
  104.5 4.0 %collective-permute-start.7 = (f32[16,8,128]{2,1,0:T(8,128)S(1)}, f32[16,8,128]{2,1,0:T(8,128)S(1)}, u32[]{:S(2)}, u32[]{:S(2)}) collective-permute-start(f32[16,8,128]{2,1,0:T(8,128)S(1)} %all_to_all.50.mine), channel_id=1, source_target_pairs={{0,8},{8,0},{16,24},{24,16},{32,40},{40,32},{48,56},{56,48},{64,72... | collective-permute-start | bytes 196616 | tf_op jit(solution)/shard_map/ppermute | solution.py:376
  132.2 20.7 %copy-start.1 = (f32[192,64]{0,1:T(8,128)S(1)}, f32[192,64]{0,1:T(8,128)}, u32[]{:S(2)}) copy-start(f32[192,64]{0,1:T(8,128)} %param.6) | copy-start | bytes 147460
  132.7 3.5 %collective-permute-start.8 = (f32[48,128]{1,0:T(8,128)S(1)}, f32[48,128]{1,0:T(8,128)S(1)}, u32[]{:S(2)}, u32[]{:S(2)}) collective-permute-start(f32[48,128]{1,0:T(8,128)S(1)} %get-tuple-element.60), channel_id=1, source_target_pairs={{0,8},{8,0},{16,24},{24,16},{32,40},{40,32},{48,56},{56,48},{64,72... | collective-permute-start | bytes 73736 | tf_op jit(solution)/shard_map/ppermute | solution.py:376
  150.2 4.1 %collective-permute-start.9 = (f32[48,128]{1,0:T(8,128)S(1)}, f32[48,128]{1,0:T(8,128)S(1)}, u32[]{:S(2)}, u32[]{:S(2)}) collective-permute-start(f32[48,128]{1,0:T(8,128)S(1)} %shard_map.100.mine), channel_id=1, source_target_pairs={{0,8},{8,0},{16,24},{24,16},{32,40},{40,32},{48,56},{56,48},{64,72... | collective-permute-start | bytes 73736 | tf_op jit(solution)/shard_map/ppermute | solution.py:376

commit v11 on v10

--- a/solution.py
+++ b/solution.py
@@ -80,29 +80,25 @@
     return [(b, e, seat(b, e, column)) for b in range(2) for e in range(n)]
 
 
-def start_up(router, tokens, w_in, w_out, out, x, far_in, far_out, left, held, sems):
-    half = held.shape[1]
+def start_up(router, tokens, w_in, w_out, out, x, away, left, sems):
+    half = away.shape[1]
     far = pl.ds(half * (1 - core_index()), half)
     pairs = [
         (router, left),
         (tokens, x),
-        (w_in.at[far], held.at[0]),
-        (w_out.at[far], held.at[1]),
+        (w_in.at[far], away.at[0]),
+        (w_out.at[far], away.at[1]),
     ]
     copies = [pltpu.make_async_copy(a, b, sems.at[i]) for i, (a, b) in enumerate(pairs)]
     for copy in copies:
         copy.start()
     copies[0].wait()
     copies[1].wait()
-    for i, place in enumerate((far_in, far_out)):
-        copies[2 + i].wait()
-        copies.append(pltpu.make_async_copy(held.at[i], place, sems.at[4 + i]))
-        copies[-1].start()
     part = contract(left[...], x[...], 1, 0)
     for i in range(out.shape[0]):
         out[i] = part[:, i * LANES : (i + 1) * LANES]
-    for copy in copies[4:]:
-        copy.wait()
+    copies[2].wait()
+    copies[3].wait()
 
 
 def load_own(w_in, w_out, own_in, own_out, sems):
@@ -166,7 +162,7 @@
     out[...] = merge([got[k] for k in range(got.shape[0])], piece)
 
 
-def hidden_parts(got, own_in, own_out, near_in, near_out, sent, keep, full):
+def hidden_parts(got, own_in, own_out, others, sent, keep, full):
     w = own_in.shape[1]
     piece = 2 * w
     hidden = own_in.shape[2]
@@ -180,7 +176,7 @@
     own = jnp.where(core == 0, low, high)
     near = jnp.where(core == 0, high, low)
     for a in range(2):
-        for kind, mine, theirs in ((0, own_in, near_in), (1, own_out, near_out)):
+        for kind, mine, theirs in ((0, own_in, others.at[0]), (1, own_out, others.at[1])):
             r = 4 * kind + 2 * a
             values = [
                 jnp.concatenate(
@@ -219,7 +215,7 @@
         out[k] = both
 
 
-def slot_rows(got, keep, own_in, own_out, near_in, near_out, out, full):
+def slot_rows(got, keep, own_in, own_out, others, out, full):
     w = own_in.shape[1]
     piece = 2 * w
     hidden = own_in.shape[2]
@@ -231,7 +227,7 @@
     lane = lane_of((piece, LANES))
     cols = jnp.zeros((piece, LANES), F32)
     for a in range(2):
-        for kind, mine, theirs in ((0, own_out, near_out), (1, own_in, near_in)):
+        for kind, mine, theirs in ((0, own_out, others.at[1]), (1, own_in, others.at[0])):
             r = 4 * kind + 2 * a
             sums = [jnp.zeros((piece, LANES), F32) for _ in range(2)]
             for h in range(0, hidden, LANES):
@@ -246,6 +242,7 @@
     high = jnp.where(core == 0, near, own)
     square = jnp.concatenate([low, high, jnp.zeros((LANES - piece, LANES), F32)], axis=0)
     rows = jnp.transpose(square)[0:8]
+    full[:, hidden:] = keep[...]
     held = swap(keep[...])
     lane = lane_of((8, LANES))
     column = jnp.sum(jnp.where(lane < piece, held * rows, 0.0), axis=1, keepdims=True)
@@ -328,13 +325,13 @@
         out[:, (2 * i + 1) * q : (2 * i + 2) * q] = turned[h:]
 
 
-def weight_grads(full, near_full, keep, near_keep, grad_in, grad_out):
+def weight_grads(full, near, grad_in, grad_out):
     w = grad_in.shape[1]
     hidden = grad_in.shape[2]
     core = core_index()
     step = 512
-    for base, values, held in ((2 * core, full, keep), (2 - 2 * core, near_full, near_keep)):
-        held = held[...]
+    for base, values in ((2 * core, full), (2 - 2 * core, near)):
+        held = values[:, hidden:]
         part = jnp.where(core == 0, held[:, 0:w], held[:, w : 2 * w])
         cols = jnp.transpose(part)
         for a in range(2):
@@ -382,24 +379,19 @@
     vmem_spec = pl.BlockSpec(memory_space=pltpu.VMEM)
     limit = pltpu.CompilerParams(vmem_limit_bytes=16 * 1024 * 1024)
     half = (experts // 2,) + w_in.shape[1:]
-    sent, tokens, far_in, far_out = pl.pallas_call(
+    sent, tokens, away = pl.pallas_call(
         start_up,
         out_shape=[
             pltpu.VMEM(spread, F32),
             pltpu.VMEM(tokens.shape, F32),
-            pltpu.HBM(half, F32),
-            pltpu.HBM(half, F32),
+            pltpu.VMEM((2,) + half, F32),
         ],
         in_specs=[far_spec] * 4,
-        out_specs=[vmem_spec] * 2 + [far_spec] * 2,
-        scratch_shapes=[
-            pltpu.VMEM(turned.shape, F32),
-            pltpu.VMEM((2,) + half, F32),
-            pltpu.SemaphoreType.DMA((6,)),
-        ],
+        out_specs=[vmem_spec] * 3,
+        scratch_shapes=[pltpu.VMEM(turned.shape, F32), pltpu.SemaphoreType.DMA((4,))],
         compiler_params=limit,
     )(in_hbm(turned), in_hbm(tokens), in_hbm(w_in), in_hbm(w_out))
-    near_in, near_out = to_partner(far_in), to_partner(far_out)
+    others = to_partner(away)
     logits = exchange(run(add_spread, spread, exchange(sent, E)), E)
 
     tiles = (chips, 8, LANES)
@@ -427,7 +419,7 @@
     tile, own_in, own_out = lax.optimization_barrier(
         (lax.ppermute(tile, (S, E), to_owner), own_in, own_out)
     )
-    weights = (own_in, own_out, near_in, near_out)
+    weights = (own_in, own_out, others)
     share = hidden // chips
     cut = -(-share // LANES) * LANES
     sent, held = run(
@@ -439,15 +431,10 @@
     )
     sent = run(gate, (chips, 8, cut), exchange(sent, S, groups))
     tile, full = run(
-        slot_rows, [(8, LANES), (8, hidden)], exchange(sent, S, groups), held, *weights
+        slot_rows, [(8, LANES), (8, hidden + LANES)], exchange(sent, S, groups), held, *weights
     )
     grad_w_in, grad_w_out = run(
-        weight_grads,
-        [w_in.shape, w_out.shape],
-        full,
-        to_partner(full),
-        held,
-        to_partner(held),
+        weight_grads, [w_in.shape, w_out.shape], full, to_partner(full)
     )
     tile, grad_w_in, grad_w_out = lax.optimization_barrier(
         (lax.ppermute(tile, (S, E), from_owner), grad_w_in, grad_w_out)

time: 156 us -> 154 us (0.987)
    ppermute x8 -> x6, starting transfers between devices: 19.9 us -> 19 us  [to_partner(): return lax.ppermute(values, S, partner)]
  transfers between devices with their start and end apart: 10 -> 8, of which waited for: 4 -> 4; matrix products, arithmetic and copies ran while one was open for 0% -> 0% of each run, Pallas kernels for 5% -> 5%
where the time goes in v11:
time: 154 us
  blocking collectives  111 us (72%)
  starting transfers between devices  21.4 us (14%)
  Pallas kernels  14.7 us (10%)
  waiting for transfers between devices  5.64 us (4%)
    all_to_all x9, blocking collectives, exchange(): lax.all_to_all(blocks, axis, 0, 0, axis_index_groups=groups, tiled=True)  111 us
    ppermute x6, starting transfers between devices, to_partner(): return lax.ppermute(values, S, partner)  19 us
    pallas_call x16, Pallas kernels, run(): pl.pallas_call(kernel, out_shape=[jax.ShapeDtypeStruct(s, F32) for s in s...  11.1 us
  transfers between devices with their start and end apart: 8, of which 4 were waited for; matrix products, arithmetic and copies ran while one was open for 0% of the time, Pallas kernels for 5%

profile of v11, /device:TPU:1, one launch (start us, length us, event | category | flops | bytes accessed | tf_op | source)
XLA Modules:
  0.0 153.6 jit_solution(9374416364210690664)
XLA Ops:
  0.6 2.0 %shard_map.84 = (f32[8,64,128]{2,1,0:T(8,128)S(1)}, f32[192,1024]{1,0:T(8,128)S(1)}, f32[2,2,48,3072]{3,2,1,0:T(8,128)S(1)}) custom-call(f32[64,192]{1,0:T(8,128)} %bitcast.2, f32[192,1024]{1,0:T(8,128)} %tokens.1, f32[4,48,3072]{2,1,0:T(8,128)} %w_in.2, f32[4,48,3072]{2,1,0:T(8,128)} %w_out.2), custom_call_target="tpu_custom_call" | custom-call | tf_op jit(solution)/shard_map/pallas_call | solution.py:382
  2.7 3.3 %collective-permute-start.2 = (f32[2,2,48,3072]{3,2,1,0:T(8,128)S(1)}, f32[2,2,48,3072]{3,2,1,0:T(8,128)S(1)}, u32[]{:S(2)}, u32[]{:S(2)}) collective-permute-start(f32[2,2,48,3072]{3,2,1,0:T(8,128)S(1)} %get-tuple-element.47), channel_id=1, source_target_pairs={{0,8},{8,0},{16,24},{24,16},{32,40},{40,32},{48,56},{56,48},{64,72... | collective-permute-start | bytes 7077896 | tf_op jit(solution)/shard_map/ppermute | solution.py:373
  6.0 13.3 %all_to_all.45.got = f32[8,64,128]{2,1,0:T(8,128)S(1)} all-to-all(f32[8,64,128]{2,1,0:T(8,128)S(1)} %get-tuple-element.35), channel_id=1, replica_groups=mesh['seq'=32,'expert'=8] {'expert'}, dimensions={0} | all-to-all | bytes 524288 | tf_op jit(solution)/shard_map/all_to_all | solution.py:29
  19.3 10.1 %all_to_all.46.got.logits = f32[8,64,128]{2,1,0:T(8,128)S(1)} all-to-all(f32[8,64,128]{2,1,0:T(8,128)S(1)} %shard_map.85), channel_id=1, replica_groups=mesh['seq'=32,'expert'=8] {'expert'}, dimensions={0} | all-to-all | bytes 524288 | tf_op jit(solution)/shard_map/all_to_all | solution.py:29
  29.4 1.4 shard_map.86
  30.8 2.5 %collective-permute-start = (f32[16,8,128]{2,1,0:T(8,128)S(1)}, f32[16,8,128]{2,1,0:T(8,128)S(1)}, u32[]{:S(2)}, u32[]{:S(2)}) collective-permute-start(f32[16,8,128]{2,1,0:T(8,128)S(1)} %get-tuple-element.38), channel_id=1, source_target_pairs={{0,8},{8,0},{16,24},{24,16},{32,40},{40,32},{48,56},{56,48},{64,72... | collective-permute-start | bytes 196616 | tf_op jit(solution)/shard_map/ppermute | solution.py:373
  33.3 0.9 collective-permute-done.near
  34.2 0.1 shard_map.87
  34.3 15.5 %all_to_all.47.got = f32[16,8,128]{2,1,0:T(8,128)S(1)} all-to-all(f32[16,8,128]{2,1,0:T(8,128)S(1)} %shard_map.87), channel_id=1, replica_groups={{0,16,32,48,64,80,96,112,128,144,160,176,192,208,224,240},{8,24,40,56,7..., dimensions={0} | all-to-all | bytes 131072 | tf_op jit(solution)/shard_map/all_to_all | solution.py:29
  49.9 0.9 collective-permute-start.1
  50.9 1.6 %shard_map.89 = (f32[2,48,3072]{2,1,0:T(8,128)S(1)}, f32[2,48,3072]{2,1,0:T(8,128)S(1)}) custom-call(f32[4,48,3072]{2,1,0:T(8,128)} %w_in.2, f32[4,48,3072]{2,1,0:T(8,128)} %w_out.2), custom_call_target="tpu_custom_call" | custom-call | tf_op jit(solution)/shard_map/pallas_call | solution.py:411
  52.5 3.0 %collective-permute-done.1.got = f32[8,128]{1,0:T(8,128)S(1)} collective-permute-done((f32[8,128]{1,0:T(8,128)S(1)}, f32[8,128]{1,0:T(8,128)S(1)}, u32[]{:S(2)}, u32[]{:S(2)}) %collective-permute-start.1) | collective-permute-done | bytes 4128 | tf_op jit(solution)/shard_map/ppermute | solution.py:420
  55.5 1.3 shard_map.90
  56.8 11.8 %all_to_all.48.got = f32[16,8,256]{2,1,0:T(8,128)S(1)} all-to-all(f32[16,8,256]{2,1,0:T(8,128)S(1)} %get-tuple-element.48), channel_id=1, replica_groups={{0,16,32,48,64,80,96,112,128,144,160,176,192,208,224,240},{8,24,40,56,7..., dimensions={0} | all-to-all | bytes 262144 | tf_op jit(solution)/shard_map/all_to_all | solution.py:29
  68.6 10.5 %all_to_all.49.got = f32[16,8,256]{2,1,0:T(8,128)S(1)} all-to-all(f32[16,8,256]{2,1,0:T(8,128)S(1)} %shard_map.91), channel_id=1, replica_groups={{0,16,32,48,64,80,96,112,128,144,160,176,192,208,224,240},{8,24,40,56,7..., dimensions={0} | all-to-all | bytes 262144 | tf_op jit(solution)/shard_map/all_to_all | solution.py:29
  79.1 1.3 shard_map.92
  80.4 5.2 %collective-permute-start.4 = (f32[8,3200]{1,0:T(8,128)S(1)}, f32[8,3200]{1,0:T(8,128)S(1)}, u32[]{:S(2)}, u32[]{:S(2)}) collective-permute-start(f32[8,3200]{1,0:T(8,128)S(1)} %get-tuple-element.51.full), channel_id=1, source_target_pairs={{0,8},{8,0},{16,24},{24,16},{32,40},{40,32},{48,56},{56,48},{64,72... | collective-permute-start | bytes 307208 | tf_op jit(solution)/shard_map/ppermute | solution.py:373
  85.6 1.5 collective-permute-start.3
  87.1 3.0 %shard_map.93 = (f32[4,48,3072]{2,1,0:T(8,128)}, f32[4,48,3072]{2,1,0:T(8,128)}) custom-call(f32[8,3200]{1,0:T(8,128)S(1)} %get-tuple-element.51.full, f32[8,3200]{1,0:T(8,128)S(1)} %collective-permute-done.4.near), custom_call_target="tpu_custom_call" | custom-call | bytes 4923392 | tf_op jit(solution)/shard_map/pallas_call | solution.py:37
  90.2 13.2 %all_to_all.50.mine = f32[16,8,128]{2,1,0:T(8,128)S(1)} all-to-all(f32[16,8,128]{2,1,0:T(8,128)S(1)} %shard_map.94), channel_id=1, replica_groups={{0,16,32,48,64,80,96,112,128,144,160,176,192,208,224,240},{8,24,40,56,7..., dimensions={0} | all-to-all | bytes 131072 | tf_op jit(solution)/shard_map/all_to_all | solution.py:29
  103.4 2.6 %collective-permute-start.5 = (f32[16,8,128]{2,1,0:T(8,128)S(1)}, f32[16,8,128]{2,1,0:T(8,128)S(1)}, u32[]{:S(2)}, u32[]{:S(2)}) collective-permute-start(f32[16,8,128]{2,1,0:T(8,128)S(1)} %all_to_all.50.mine), channel_id=1, source_target_pairs={{0,8},{8,0},{16,24},{24,16},{32,40},{40,32},{48,56},{56,48},{64,72... | collective-permute-start | bytes 196616 | tf_op jit(solution)/shard_map/ppermute | solution.py:373
  106.0 0.9 collective-permute-done.5.near
  106.9 0.9 shard_map.95
  107.8 12.4 %all_to_all.51.got = f32[8,64,128]{2,1,0:T(8,128)S(1)} all-to-all(f32[8,64,128]{2,1,0:T(8,128)S(1)} %get-tuple-element.56), channel_id=1, replica_groups=mesh['seq'=32,'expert'=8] {'expert'}, dimensions={0} | all-to-all | bytes 524288 | tf_op jit(solution)/shard_map/all_to_all | solution.py:29
  120.2 10.5 %all_to_all.52.got = f32[8,64,128]{2,1,0:T(8,128)S(1)} all-to-all(f32[8,64,128]{2,1,0:T(8,128)S(1)} %shard_map.96), channel_id=1, replica_groups=mesh['seq'=32,'expert'=8] {'expert'}, dimensions={0} | all-to-all | bytes 524288 | tf_op jit(solution)/shard_map/all_to_all | solution.py:29
  130.8 0.5 shard_map.97
  131.3 2.7 %collective-permute-start.6 = (f32[48,128]{1,0:T(8,128)S(1)}, f32[48,128]{1,0:T(8,128)S(1)}, u32[]{:S(2)}, u32[]{:S(2)}) collective-permute-start(f32[48,128]{1,0:T(8,128)S(1)} %get-tuple-element.58), channel_id=1, source_target_pairs={{0,8},{8,0},{16,24},{24,16},{32,40},{40,32},{48,56},{56,48},{64,72... | collective-permute-start | bytes 73736 | tf_op jit(solution)/shard_map/ppermute | solution.py:373
  134.0 0.8 collective-permute-done.6.theirs
  134.9 13.9 %all_to_all.53.got = f32[16,48,128]{2,1,0:T(8,128)S(1)} all-to-all(f32[16,48,128]{2,1,0:T(8,128)S(1)} %shard_map.98), channel_id=1, replica_groups={{0,16,32,48,64,80,96,112,128,144,160,176,192,208,224,240},{8,24,40,56,7..., dimensions={0} | all-to-all | bytes 786432 | tf_op jit(solution)/shard_map/all_to_all | solution.py:29
  148.8 2.6 %collective-permute-start.7 = (f32[48,128]{1,0:T(8,128)S(1)}, f32[48,128]{1,0:T(8,128)S(1)}, u32[]{:S(2)}, u32[]{:S(2)}) collective-permute-start(f32[48,128]{1,0:T(8,128)S(1)} %shard_map.100.mine), channel_id=1, source_target_pairs={{0,8},{8,0},{16,24},{24,16},{32,40},{40,32},{48,56},{56,48},{64,72... | collective-permute-start | bytes 73736 | tf_op jit(solution)/shard_map/ppermute | solution.py:373
  151.4 1.4 shard_map.99
  152.8 0.8 shard_map.101
  (15 shorter events, 0.3 us)
Async XLA Ops:
  0.6 28.7 %copy-start = (f32[192,1024]{1,0:T(8,128)S(1)}, f32[192,1024]{1,0:T(8,128)}, u32[]{:S(2)}) copy-start(f32[192,1024]{1,0:T(8,128)} %grad_out.3) | copy-start | bytes 2359300
  2.7 52.8 %collective-permute-start.2 = (f32[2,2,48,3072]{3,2,1,0:T(8,128)S(1)}, f32[2,2,48,3072]{3,2,1,0:T(8,128)S(1)}, u32[]{:S(2)}, u32[]{:S(2)}) collective-permute-start(f32[2,2,48,3072]{3,2,1,0:T(8,128)S(1)} %get-tuple-element.47), channel_id=1, source_target_pairs={{0,8},{8,0},{16,24},{24,16},{32,40},{40,32},{48,56},{56,48},{64,72... | collective-permute-start | bytes 7077896 | tf_op jit(solution)/shard_map/ppermute | solution.py:373
  30.8 3.4 %collective-permute-start = (f32[16,8,128]{2,1,0:T(8,128)S(1)}, f32[16,8,128]{2,1,0:T(8,128)S(1)}, u32[]{:S(2)}, u32[]{:S(2)}) collective-permute-start(f32[16,8,128]{2,1,0:T(8,128)S(1)} %get-tuple-element.38), channel_id=1, source_target_pairs={{0,8},{8,0},{16,24},{24,16},{32,40},{40,32},{48,56},{56,48},{64,72... | collective-permute-start | bytes 196616 | tf_op jit(solution)/shard_map/ppermute | solution.py:373
  49.9 5.5 %collective-permute-start.1 = (f32[8,128]{1,0:T(8,128)S(1)}, f32[8,128]{1,0:T(8,128)S(1)}, u32[]{:S(2)}, u32[]{:S(2)}) collective-permute-start(f32[8,128]{1,0:T(8,128)S(1)} %shard_map.88), channel_id=1, source_target_pairs={{80,0},{241,32},{34,64},{195,96},{132,128},{37,160},{182,192},{87,... | collective-permute-start | bytes 12296 | tf_op jit(solution)/shard_map/ppermute | solution.py:420
  80.4 6.7 %collective-permute-start.4 = (f32[8,3200]{1,0:T(8,128)S(1)}, f32[8,3200]{1,0:T(8,128)S(1)}, u32[]{:S(2)}, u32[]{:S(2)}) collective-permute-start(f32[8,3200]{1,0:T(8,128)S(1)} %get-tuple-element.51.full), channel_id=1, source_target_pairs={{0,8},{8,0},{16,24},{24,16},{32,40},{40,32},{48,56},{56,48},{64,72... | collective-permute-start | bytes 307208 | tf_op jit(solution)/shard_map/ppermute | solution.py:373
  85.6 4.5 %collective-permute-start.3 = (f32[8,128]{1,0:T(8,128)S(1)}, f32[8,128]{1,0:T(8,128)S(1)}, u32[]{:S(2)}, u32[]{:S(2)}) collective-permute-start(f32[8,128]{1,0:T(8,128)S(1)} %get-tuple-element.50), channel_id=1, source_target_pairs={{0,80},{32,241},{64,34},{96,195},{128,132},{160,37},{192,182},{224... | collective-permute-start | bytes 12296 | tf_op jit(solution)/shard_map/ppermute | solution.py:440
  103.4 3.5 %collective-permute-start.5 = (f32[16,8,128]{2,1,0:T(8,128)S(1)}, f32[16,8,128]{2,1,0:T(8,128)S(1)}, u32[]{:S(2)}, u32[]{:S(2)}) collective-permute-start(f32[16,8,128]{2,1,0:T(8,128)S(1)} %all_to_all.50.mine), channel_id=1, source_target_pairs={{0,8},{8,0},{16,24},{24,16},{32,40},{40,32},{48,56},{56,48},{64,72... | collective-permute-start | bytes 196616 | tf_op jit(solution)/shard_map/ppermute | solution.py:373
  107.8 43.6 %copy-start.1 = (f32[192,64]{0,1:T(8,128)S(1)}, f32[192,64]{0,1:T(8,128)}, u32[]{:S(2)}) copy-start(f32[192,64]{0,1:T(8,128)} %param.6) | copy-start | bytes 147460
  131.3 3.5 %collective-permute-start.6 = (f32[48,128]{1,0:T(8,128)S(1)}, f32[48,128]{1,0:T(8,128)S(1)}, u32[]{:S(2)}, u32[]{:S(2)}) collective-permute-start(f32[48,128]{1,0:T(8,128)S(1)} %get-tuple-element.58), channel_id=1, source_target_pairs={{0,8},{8,0},{16,24},{24,16},{32,40},{40,32},{48,56},{56,48},{64,72... | collective-permute-start | bytes 73736 | tf_op jit(solution)/shard_map/ppermute | solution.py:373
  148.8 4.1 %collective-permute-start.7 = (f32[48,128]{1,0:T(8,128)S(1)}, f32[48,128]{1,0:T(8,128)S(1)}, u32[]{:S(2)}, u32[]{:S(2)}) collective-permute-start(f32[48,128]{1,0:T(8,128)S(1)} %shard_map.100.mine), channel_id=1, source_target_pairs={{0,8},{8,0},{16,24},{24,16},{32,40},{40,32},{48,56},{56,48},{64,72... | collective-permute-start | bytes 73736 | tf_op jit(solution)/shard_map/ppermute | solution.py:373

commit v12 on v11

--- a/solution.py
+++ b/solution.py
@@ -305,10 +305,10 @@
         out[:, e * LANES : (e + 1) * LANES] = contract(left, right, 1, 0, THREE)
 
 
-def add_copies(mine, theirs, out):
-    both = mine[...] + theirs[...]
+def add_copies(a, b, c, d, out):
+    total = (a[...] + b[...]) + (c[...] + d[...])
     for k in range(out.shape[0]):
-        out[k] = both
+        out[k] = total
 
 
 def add_all(got, out):
@@ -457,12 +457,19 @@
     grads = exchange(sent, E)
     fold = (rows_block // 4, 2 * slots)
     near, theirs = run(router_part, [fold, fold], grads, tokens)
-    sent = run(add_copies, (chips,) + fold, near, to_partner(theirs))
-    got, weights, rows = lax.optimization_barrier((exchange(sent, S, groups), weights, rows))
-    near = run(add_all, fold, got)
+    across = n_seq // 2
+    rows_z = [
+        [across * x + 2 * z + c for z in range(across // 2)] for x in range(2) for c in range(2)
+    ]
+    pairs = [near, to_partner(theirs)]
+    pairs.append(lax.ppermute(near, S, [(i, i ^ across) for i in range(n_seq)]))
+    pairs.append(lax.ppermute(theirs, S, [(i, i ^ across ^ 1) for i in range(n_seq)]))
     grad_tokens = run(
         token_grads, (rows_block, local_tokens), grads, weights, rows, turned
     )
+    *pairs, grad_tokens = lax.optimization_barrier((*pairs, grad_tokens))
+    got = exchange(run(add_copies, (across // 2,) + fold, *pairs), S, rows_z)
+    near = run(add_all, fold, got)
     grad_router = run(unfold, (slots, rows_block), near, to_partner(near)).T
     return (grad_tokens, grad_router, grad_w_in, grad_w_out)
 

time: 154 us -> 153 us (level)
  blocking collectives: 111 us -> 109 us
    ppermute x0 -> x2, starting transfers between devices: none -> 4.29 us  [the longest x1 4.19 us: per_device(): lax.ppermute(theirs, S, [(i, i ^ across ^ 1) for i in range(n_seq)])]
    ppermute x6, starting transfers between devices: 19 us -> 15.2 us  [to_partner(): return lax.ppermute(values, S, partner)]
    all_to_all x9, blocking collectives: 111 us -> 109 us  [exchange(): lax.all_to_all(blocks, axis, 0, 0, axis_index_groups=groups, tiled=True)]
  transfers between devices with their start and end apart: 8 -> 10, of which waited for: 4 -> 5; matrix products, arithmetic and copies ran while one was open for 0% -> 0% of each run, Pallas kernels for 5% -> 5%
where the time goes in v12:
time: 153 us
  blocking collectives  109 us (71%)
  starting transfers between devices  21.9 us (14%)
  Pallas kernels  14.7 us (10%)
  waiting for transfers between devices  6.04 us (4%)
    all_to_all x9, blocking collectives, exchange(): lax.all_to_all(blocks, axis, 0, 0, axis_index_groups=groups, tiled=True)  109 us
    ppermute x6, starting transfers between devices, to_partner(): return lax.ppermute(values, S, partner)  15.2 us
    pallas_call x16, Pallas kernels, run(): pl.pallas_call(kernel, out_shape=[jax.ShapeDtypeStruct(s, F32) for s in s...  11.1 us
    ppermute x1, starting transfers between devices, per_device(): lax.ppermute(theirs, S, [(i, i ^ across ^ 1) for i in range(n_seq)])  4.19 us
  transfers between devices with their start and end apart: 10, of which 5 were waited for; matrix products, arithmetic and copies ran while one was open for 0% of the time, Pallas kernels for 5%

profile of v12, /device:TPU:1, one launch (start us, length us, event | category | flops | bytes accessed | tf_op | source)
XLA Modules:
  0.0 152.9 jit_solution(7089666129059962366)
XLA Ops:
  0.6 2.0 %shard_map.84 = (f32[8,64,128]{2,1,0:T(8,128)S(1)}, f32[192,1024]{1,0:T(8,128)S(1)}, f32[2,2,48,3072]{3,2,1,0:T(8,128)S(1)}) custom-call(f32[64,192]{1,0:T(8,128)} %bitcast.2, f32[192,1024]{1,0:T(8,128)} %tokens.1, f32[4,48,3072]{2,1,0:T(8,128)} %w_in.2, f32[4,48,3072]{2,1,0:T(8,128)} %w_out.2), custom_call_target="tpu_custom_call" | custom-call | tf_op jit(solution)/shard_map/pallas_call | solution.py:382
  2.7 3.3 %collective-permute-start.2 = (f32[2,2,48,3072]{3,2,1,0:T(8,128)S(1)}, f32[2,2,48,3072]{3,2,1,0:T(8,128)S(1)}, u32[]{:S(2)}, u32[]{:S(2)}) collective-permute-start(f32[2,2,48,3072]{3,2,1,0:T(8,128)S(1)} %get-tuple-element.49), channel_id=1, source_target_pairs={{0,8},{8,0},{16,24},{24,16},{32,40},{40,32},{48,56},{56,48},{64,72... | collective-permute-start | bytes 7077896 | tf_op jit(solution)/shard_map/ppermute | solution.py:373
  6.0 13.3 %all_to_all.45.got = f32[8,64,128]{2,1,0:T(8,128)S(1)} all-to-all(f32[8,64,128]{2,1,0:T(8,128)S(1)} %get-tuple-element.37), channel_id=1, replica_groups=mesh['seq'=32,'expert'=8] {'expert'}, dimensions={0} | all-to-all | bytes 524288 | tf_op jit(solution)/shard_map/all_to_all | solution.py:29
  19.3 10.1 %all_to_all.46.got.logits = f32[8,64,128]{2,1,0:T(8,128)S(1)} all-to-all(f32[8,64,128]{2,1,0:T(8,128)S(1)} %shard_map.85), channel_id=1, replica_groups=mesh['seq'=32,'expert'=8] {'expert'}, dimensions={0} | all-to-all | bytes 524288 | tf_op jit(solution)/shard_map/all_to_all | solution.py:29
  29.4 1.4 shard_map.86
  30.8 2.5 %collective-permute-start = (f32[16,8,128]{2,1,0:T(8,128)S(1)}, f32[16,8,128]{2,1,0:T(8,128)S(1)}, u32[]{:S(2)}, u32[]{:S(2)}) collective-permute-start(f32[16,8,128]{2,1,0:T(8,128)S(1)} %get-tuple-element.40), channel_id=1, source_target_pairs={{0,8},{8,0},{16,24},{24,16},{32,40},{40,32},{48,56},{56,48},{64,72... | collective-permute-start | bytes 196616 | tf_op jit(solution)/shard_map/ppermute | solution.py:373
  33.3 0.9 collective-permute-done.near
  34.3 15.5 %all_to_all.47.got = f32[16,8,128]{2,1,0:T(8,128)S(1)} all-to-all(f32[16,8,128]{2,1,0:T(8,128)S(1)} %shard_map.87), channel_id=1, replica_groups={{0,16,32,48,64,80,96,112,128,144,160,176,192,208,224,240},{8,24,40,56,7..., dimensions={0} | all-to-all | bytes 131072 | tf_op jit(solution)/shard_map/all_to_all | solution.py:29
  49.9 0.9 collective-permute-start.1
  50.9 1.6 %shard_map.89 = (f32[2,48,3072]{2,1,0:T(8,128)S(1)}, f32[2,48,3072]{2,1,0:T(8,128)S(1)}) custom-call(f32[4,48,3072]{2,1,0:T(8,128)} %w_in.2, f32[4,48,3072]{2,1,0:T(8,128)} %w_out.2), custom_call_target="tpu_custom_call" | custom-call | tf_op jit(solution)/shard_map/pallas_call | solution.py:411
  52.5 3.0 %collective-permute-done.1.got = f32[8,128]{1,0:T(8,128)S(1)} collective-permute-done((f32[8,128]{1,0:T(8,128)S(1)}, f32[8,128]{1,0:T(8,128)S(1)}, u32[]{:S(2)}, u32[]{:S(2)}) %collective-permute-start.1) | collective-permute-done | bytes 4128 | tf_op jit(solution)/shard_map/ppermute | solution.py:420
  55.5 1.3 shard_map.90
  56.8 11.8 %all_to_all.48.got = f32[16,8,256]{2,1,0:T(8,128)S(1)} all-to-all(f32[16,8,256]{2,1,0:T(8,128)S(1)} %get-tuple-element.50), channel_id=1, replica_groups={{0,16,32,48,64,80,96,112,128,144,160,176,192,208,224,240},{8,24,40,56,7..., dimensions={0} | all-to-all | bytes 262144 | tf_op jit(solution)/shard_map/all_to_all | solution.py:29
  68.6 10.5 %all_to_all.49.got = f32[16,8,256]{2,1,0:T(8,128)S(1)} all-to-all(f32[16,8,256]{2,1,0:T(8,128)S(1)} %shard_map.91), channel_id=1, replica_groups={{0,16,32,48,64,80,96,112,128,144,160,176,192,208,224,240},{8,24,40,56,7..., dimensions={0} | all-to-all | bytes 262144 | tf_op jit(solution)/shard_map/all_to_all | solution.py:29
  79.1 1.3 shard_map.92
  80.4 5.2 %collective-permute-start.4 = (f32[8,3200]{1,0:T(8,128)S(1)}, f32[8,3200]{1,0:T(8,128)S(1)}, u32[]{:S(2)}, u32[]{:S(2)}) collective-permute-start(f32[8,3200]{1,0:T(8,128)S(1)} %get-tuple-element.53.full), channel_id=1, source_target_pairs={{0,8},{8,0},{16,24},{24,16},{32,40},{40,32},{48,56},{56,48},{64,72... | collective-permute-start | bytes 307208 | tf_op jit(solution)/shard_map/ppermute | solution.py:373
  85.6 1.5 collective-permute-start.3
  87.1 3.0 %shard_map.93 = (f32[4,48,3072]{2,1,0:T(8,128)}, f32[4,48,3072]{2,1,0:T(8,128)}) custom-call(f32[8,3200]{1,0:T(8,128)S(1)} %get-tuple-element.53.full, f32[8,3200]{1,0:T(8,128)S(1)} %collective-permute-done.4.near), custom_call_target="tpu_custom_call" | custom-call | bytes 4923392 | tf_op jit(solution)/shard_map/pallas_call | solution.py:37
  90.2 13.2 %all_to_all.50.mine = f32[16,8,128]{2,1,0:T(8,128)S(1)} all-to-all(f32[16,8,128]{2,1,0:T(8,128)S(1)} %shard_map.94), channel_id=1, replica_groups={{0,16,32,48,64,80,96,112,128,144,160,176,192,208,224,240},{8,24,40,56,7..., dimensions={0} | all-to-all | bytes 131072 | tf_op jit(solution)/shard_map/all_to_all | solution.py:29
  103.4 2.6 %collective-permute-start.5 = (f32[16,8,128]{2,1,0:T(8,128)S(1)}, f32[16,8,128]{2,1,0:T(8,128)S(1)}, u32[]{:S(2)}, u32[]{:S(2)}) collective-permute-start(f32[16,8,128]{2,1,0:T(8,128)S(1)} %all_to_all.50.mine), channel_id=1, source_target_pairs={{0,8},{8,0},{16,24},{24,16},{32,40},{40,32},{48,56},{56,48},{64,72... | collective-permute-start | bytes 196616 | tf_op jit(solution)/shard_map/ppermute | solution.py:373
  106.0 0.9 collective-permute-done.5.near
  106.9 0.9 shard_map.95
  107.8 12.3 %all_to_all.51.got = f32[8,64,128]{2,1,0:T(8,128)S(1)} all-to-all(f32[8,64,128]{2,1,0:T(8,128)S(1)} %get-tuple-element.58), channel_id=1, replica_groups=mesh['seq'=32,'expert'=8] {'expert'}, dimensions={0} | all-to-all | bytes 524288 | tf_op jit(solution)/shard_map/all_to_all | solution.py:29
  120.1 10.5 %all_to_all.52.got = f32[8,64,128]{2,1,0:T(8,128)S(1)} all-to-all(f32[8,64,128]{2,1,0:T(8,128)S(1)} %shard_map.96), channel_id=1, replica_groups=mesh['seq'=32,'expert'=8] {'expert'}, dimensions={0} | all-to-all | bytes 524288 | tf_op jit(solution)/shard_map/all_to_all | solution.py:29
  130.6 0.5 shard_map.97
  131.3 4.2 %collective-permute-start.8 = (f32[48,128]{1,0:T(8,128)S(1)}, f32[48,128]{1,0:T(8,128)S(1)}, u32[]{:S(2)}, u32[]{:S(2)}) collective-permute-start(f32[48,128]{1,0:T(8,128)S(1)} %get-tuple-element.60), channel_id=1, source_target_pairs={{0,136},{8,128},{16,152},{24,144},{32,168},{40,160},{48,184},{56,1... | collective-permute-start | bytes 73736 | tf_op jit(solution)/shard_map/ppermute | solution.py:466
  135.5 1.4 shard_map.98
  136.9 0.4 collective-permute-done.8.d
  137.3 12.4 %all_to_all.53.got = f32[8,48,128]{2,1,0:T(8,128)S(1)} all-to-all(f32[8,48,128]{2,1,0:T(8,128)S(1)} %shard_map.99), channel_id=1, replica_groups={{0,16,32,48,64,80,96,112},{8,24,40,56,72,88,104,120},{128,144,160,176,1..., dimensions={0} | all-to-all | bytes 393216 | tf_op jit(solution)/shard_map/all_to_all | solution.py:29
  149.7 1.5 %collective-permute-start.9 = (f32[48,128]{1,0:T(8,128)S(1)}, f32[48,128]{1,0:T(8,128)S(1)}, u32[]{:S(2)}, u32[]{:S(2)}) collective-permute-start(f32[48,128]{1,0:T(8,128)S(1)} %shard_map.100.mine), channel_id=1, source_target_pairs={{0,8},{8,0},{16,24},{24,16},{32,40},{40,32},{48,56},{56,48},{64,72... | collective-permute-start | bytes 73736 | tf_op jit(solution)/shard_map/ppermute | solution.py:373
  151.2 0.8 collective-permute-done.9.theirs
  152.1 0.8 shard_map.101
  (19 shorter events, 0.5 us)
Async XLA Ops:
  0.6 28.7 %copy-start = (f32[192,1024]{1,0:T(8,128)S(1)}, f32[192,1024]{1,0:T(8,128)}, u32[]{:S(2)}) copy-start(f32[192,1024]{1,0:T(8,128)} %grad_out.3) | copy-start | bytes 2359300
  2.7 52.8 %collective-permute-start.2 = (f32[2,2,48,3072]{3,2,1,0:T(8,128)S(1)}, f32[2,2,48,3072]{3,2,1,0:T(8,128)S(1)}, u32[]{:S(2)}, u32[]{:S(2)}) collective-permute-start(f32[2,2,48,3072]{3,2,1,0:T(8,128)S(1)} %get-tuple-element.49), channel_id=1, source_target_pairs={{0,8},{8,0},{16,24},{24,16},{32,40},{40,32},{48,56},{56,48},{64,72... | collective-permute-start | bytes 7077896 | tf_op jit(solution)/shard_map/ppermute | solution.py:373
  30.8 3.4 %collective-permute-start = (f32[16,8,128]{2,1,0:T(8,128)S(1)}, f32[16,8,128]{2,1,0:T(8,128)S(1)}, u32[]{:S(2)}, u32[]{:S(2)}) collective-permute-start(f32[16,8,128]{2,1,0:T(8,128)S(1)} %get-tuple-element.40), channel_id=1, source_target_pairs={{0,8},{8,0},{16,24},{24,16},{32,40},{40,32},{48,56},{56,48},{64,72... | collective-permute-start | bytes 196616 | tf_op jit(solution)/shard_map/ppermute | solution.py:373
  49.9 5.5 %collective-permute-start.1 = (f32[8,128]{1,0:T(8,128)S(1)}, f32[8,128]{1,0:T(8,128)S(1)}, u32[]{:S(2)}, u32[]{:S(2)}) collective-permute-start(f32[8,128]{1,0:T(8,128)S(1)} %shard_map.88), channel_id=1, source_target_pairs={{80,0},{241,32},{34,64},{195,96},{132,128},{37,160},{182,192},{87,... | collective-permute-start | bytes 12296 | tf_op jit(solution)/shard_map/ppermute | solution.py:420
  80.4 6.7 %collective-permute-start.4 = (f32[8,3200]{1,0:T(8,128)S(1)}, f32[8,3200]{1,0:T(8,128)S(1)}, u32[]{:S(2)}, u32[]{:S(2)}) collective-permute-start(f32[8,3200]{1,0:T(8,128)S(1)} %get-tuple-element.53.full), channel_id=1, source_target_pairs={{0,8},{8,0},{16,24},{24,16},{32,40},{40,32},{48,56},{56,48},{64,72... | collective-permute-start | bytes 307208 | tf_op jit(solution)/shard_map/ppermute | solution.py:373
  85.6 4.5 %collective-permute-start.3 = (f32[8,128]{1,0:T(8,128)S(1)}, f32[8,128]{1,0:T(8,128)S(1)}, u32[]{:S(2)}, u32[]{:S(2)}) collective-permute-start(f32[8,128]{1,0:T(8,128)S(1)} %get-tuple-element.52), channel_id=1, source_target_pairs={{0,80},{32,241},{64,34},{96,195},{128,132},{160,37},{192,182},{224... | collective-permute-start | bytes 12296 | tf_op jit(solution)/shard_map/ppermute | solution.py:440
  103.4 3.5 %collective-permute-start.5 = (f32[16,8,128]{2,1,0:T(8,128)S(1)}, f32[16,8,128]{2,1,0:T(8,128)S(1)}, u32[]{:S(2)}, u32[]{:S(2)}) collective-permute-start(f32[16,8,128]{2,1,0:T(8,128)S(1)} %all_to_all.50.mine), channel_id=1, source_target_pairs={{0,8},{8,0},{16,24},{24,16},{32,40},{40,32},{48,56},{56,48},{64,72... | collective-permute-start | bytes 196616 | tf_op jit(solution)/shard_map/ppermute | solution.py:373
  106.9 28.6 %copy-start.1 = (f32[192,64]{0,1:T(8,128)S(1)}, f32[192,64]{0,1:T(8,128)}, u32[]{:S(2)}) copy-start(f32[192,64]{0,1:T(8,128)} %param.6) | copy-start | bytes 147460
  131.2 5.7 %collective-permute-start.7 = (f32[48,128]{1,0:T(8,128)S(1)}, f32[48,128]{1,0:T(8,128)S(1)}, u32[]{:S(2)}, u32[]{:S(2)}) collective-permute-start(f32[48,128]{1,0:T(8,128)S(1)} %get-tuple-element.64.a), channel_id=1, source_target_pairs={{0,128},{8,136},{16,144},{24,152},{32,160},{40,168},{48,176},{56,1... | collective-permute-start | bytes 73736 | tf_op jit(solution)/shard_map/ppermute | solution.py:465
  131.3 6.0 %collective-permute-start.8 = (f32[48,128]{1,0:T(8,128)S(1)}, f32[48,128]{1,0:T(8,128)S(1)}, u32[]{:S(2)}, u32[]{:S(2)}) collective-permute-start(f32[48,128]{1,0:T(8,128)S(1)} %get-tuple-element.60), channel_id=1, source_target_pairs={{0,136},{8,128},{16,152},{24,144},{32,168},{40,160},{48,184},{56,1... | collective-permute-start | bytes 73736 | tf_op jit(solution)/shard_map/ppermute | solution.py:466
  135.5 1.8 %collective-permute-start.6 = (f32[48,128]{1,0:T(8,128)S(1)}, f32[48,128]{1,0:T(8,128)S(1)}, u32[]{:S(2)}, u32[]{:S(2)}) collective-permute-start(f32[48,128]{1,0:T(8,128)S(1)} %get-tuple-element.60), channel_id=1, source_target_pairs={{0,8},{8,0},{16,24},{24,16},{32,40},{40,32},{48,56},{56,48},{64,72... | collective-permute-start | bytes 73736 | tf_op jit(solution)/shard_map/ppermute | solution.py:373
  149.7 2.4 %collective-permute-start.9 = (f32[48,128]{1,0:T(8,128)S(1)}, f32[48,128]{1,0:T(8,128)S(1)}, u32[]{:S(2)}, u32[]{:S(2)}) collective-permute-start(f32[48,128]{1,0:T(8,128)S(1)} %shard_map.100.mine), channel_id=1, source_target_pairs={{0,8},{8,0},{16,24},{24,16},{32,40},{40,32},{48,56},{56,48},{64,72... | collective-permute-start | bytes 73736 | tf_op jit(solution)/shard_map/ppermute | solution.py:373

commit v13 on v12

--- a/solution.py
+++ b/solution.py
@@ -243,10 +243,8 @@
     square = jnp.concatenate([low, high, jnp.zeros((LANES - piece, LANES), F32)], axis=0)
     rows = jnp.transpose(square)[0:8]
     full[:, hidden:] = keep[...]
-    held = swap(keep[...])
-    lane = lane_of((8, LANES))
-    column = jnp.sum(jnp.where(lane < piece, held * rows, 0.0), axis=1, keepdims=True)
-    out[...] = jnp.where(lane < piece, rows, jnp.where(lane == piece + 2, column, held))
+    out[0:8] = jnp.where(lane_of((8, LANES)) < piece, rows, swap(keep[...]))
+    out[8:16] = keep[...]
 
 
 def copies(tile, out):
@@ -255,25 +253,27 @@
         out[k] = value
 
 
-def width_products(mine, near, tokens, grad_out, logits, shares, out, weights, rows, outs, marks):
+def width_products(
+    mine, near, tokens, grad_out, logits, shares, out, weights, rows, outs, ins, marks
+):
     n = out.shape[0]
     piece = rows.shape[1] // 2
     core = core_index()
-    added = []
     for c in range(2):
         for b, e, k in seats(n):
             tile = jnp.where(core == c, mine[k], near[k])
             s, w = slice(8 * e + 4 * c, 8 * e + 4 * c + 4), slice(b * piece, (b + 1) * piece)
             outs[s, w] = tile[0:4, 0:piece]
             rows[s, w] = tile[4:8, 0:piece]
+            ins[s, w] = tile[8:12, 0:piece]
             if b == 0:
                 marks[s] = tile[4:8]
-            else:
-                added.append((s, tile[4:8, piece + 2 : piece + 3]))
-    lane = lane_of((4, LANES))
-    for s, column in added:
-        marks[s] = marks[s] + jnp.where(lane == piece + 2, column, 0.0)
-    top, total, column = (marks[:, piece + i : piece + i + 1] for i in range(3))
+    top, total = (marks[:, piece + i : piece + i + 1] for i in range(2))
+    slots = rows.shape[0]
+    ins[slots:] = jnp.zeros(ins[slots:].shape, F32)
+    cross = contract(rows[...], jnp.transpose(ins[...]), 1, 0)
+    own = lane_of(cross.shape) == lax.broadcasted_iota(jnp.int32, cross.shape, 0)
+    column = jnp.sum(jnp.where(own, cross, 0.0), axis=1, keepdims=True)
     first = contract(outs[...], grad_out[...], 1, 0, THREE)
     second = contract(rows[...], tokens[...], 1, 0) - column
     for i in range(n):
@@ -431,7 +431,7 @@
     )
     sent = run(gate, (chips, 8, cut), exchange(sent, S, groups))
     tile, full = run(
-        slot_rows, [(8, LANES), (8, hidden + LANES)], exchange(sent, S, groups), held, *weights
+        slot_rows, [(16, LANES), (8, hidden + LANES)], exchange(sent, S, groups), held, *weights
     )
     grad_w_in, grad_w_out = run(
         weight_grads, [w_in.shape, w_out.shape], full, to_partner(full)
@@ -439,7 +439,7 @@
     tile, grad_w_in, grad_w_out = lax.optimization_barrier(
         (lax.ppermute(tile, (S, E), from_owner), grad_w_in, grad_w_out)
     )
-    sent = run(copies, tiles, tile)
+    sent = run(copies, (chips, 16, LANES), tile)
     mine = exchange(sent, S, groups)
     near = to_partner(mine)
     sent, weights, rows = run(
@@ -451,7 +451,7 @@
         grad_out,
         logits,
         shares,
-        scratch=[(slots, rows_block), (slots, LANES)],
+        scratch=[(slots, rows_block), (LANES, rows_block), (slots, LANES)],
     )
     sent = run(add_spread, spread, exchange(sent, E))
     grads = exchange(sent, E)

time: 153 us -> 154 us (level)
  no operation moved by 1% of the time
where the time goes in v13:
time: 154 us; the launch traced here: 153 us
  blocking collectives  109 us (71%)
  starting transfers between devices  22.6 us (15%)
  Pallas kernels  14.3 us (9%)
  waiting for transfers between devices  6.26 us (4%)
    all_to_all x9, blocking collectives, exchange(): lax.all_to_all(blocks, axis, 0, 0, axis_index_groups=groups, tiled=True)  109 us
    ppermute x6, starting transfers between devices, to_partner(): return lax.ppermute(values, S, partner)  15.8 us
    pallas_call x16, Pallas kernels, run(): pl.pallas_call(kernel, out_shape=[jax.ShapeDtypeStruct(s, F32) for s in s...  10.6 us
    ppermute x1, starting transfers between devices, per_device(): lax.ppermute(theirs, S, [(i, i ^ across ^ 1) for i in range(n_seq)])  4.06 us
  transfers between devices with their start and end apart: 10, of which 5 were waited for; matrix products, arithmetic and copies ran while one was open for 0% of the time, Pallas kernels for 5%

profile of v13, /device:TPU:1, one launch (start us, length us, event | category | flops | bytes accessed | tf_op | source)
XLA Modules:
  0.0 153.1 jit_solution(16355152196458610640)
XLA Ops:
  0.6 2.0 %shard_map.84 = (f32[8,64,128]{2,1,0:T(8,128)S(1)}, f32[192,1024]{1,0:T(8,128)S(1)}, f32[2,2,48,3072]{3,2,1,0:T(8,128)S(1)}) custom-call(f32[64,192]{1,0:T(8,128)} %bitcast.2, f32[192,1024]{1,0:T(8,128)} %tokens.1, f32[4,48,3072]{2,1,0:T(8,128)} %w_in.2, f32[4,48,3072]{2,1,0:T(8,128)} %w_out.2), custom_call_target="tpu_custom_call" | custom-call | tf_op jit(solution)/shard_map/pallas_call | solution.py:382
  2.7 3.3 %collective-permute-start.2 = (f32[2,2,48,3072]{3,2,1,0:T(8,128)S(1)}, f32[2,2,48,3072]{3,2,1,0:T(8,128)S(1)}, u32[]{:S(2)}, u32[]{:S(2)}) collective-permute-start(f32[2,2,48,3072]{3,2,1,0:T(8,128)S(1)} %get-tuple-element.49), channel_id=1, source_target_pairs={{0,8},{8,0},{16,24},{24,16},{32,40},{40,32},{48,56},{56,48},{64,72... | collective-permute-start | bytes 7077896 | tf_op jit(solution)/shard_map/ppermute | solution.py:373
  6.0 13.3 %all_to_all.45.got = f32[8,64,128]{2,1,0:T(8,128)S(1)} all-to-all(f32[8,64,128]{2,1,0:T(8,128)S(1)} %get-tuple-element.37), channel_id=1, replica_groups=mesh['seq'=32,'expert'=8] {'expert'}, dimensions={0} | all-to-all | bytes 524288 | tf_op jit(solution)/shard_map/all_to_all | solution.py:29
  19.3 10.1 %all_to_all.46.got.logits = f32[8,64,128]{2,1,0:T(8,128)S(1)} all-to-all(f32[8,64,128]{2,1,0:T(8,128)S(1)} %shard_map.85), channel_id=1, replica_groups=mesh['seq'=32,'expert'=8] {'expert'}, dimensions={0} | all-to-all | bytes 524288 | tf_op jit(solution)/shard_map/all_to_all | solution.py:29
  29.4 1.4 shard_map.86
  30.8 2.5 %collective-permute-start = (f32[16,8,128]{2,1,0:T(8,128)S(1)}, f32[16,8,128]{2,1,0:T(8,128)S(1)}, u32[]{:S(2)}, u32[]{:S(2)}) collective-permute-start(f32[16,8,128]{2,1,0:T(8,128)S(1)} %get-tuple-element.40), channel_id=1, source_target_pairs={{0,8},{8,0},{16,24},{24,16},{32,40},{40,32},{48,56},{56,48},{64,72... | collective-permute-start | bytes 196616 | tf_op jit(solution)/shard_map/ppermute | solution.py:373
  33.3 0.9 collective-permute-done.near
  34.3 15.5 %all_to_all.47.got = f32[16,8,128]{2,1,0:T(8,128)S(1)} all-to-all(f32[16,8,128]{2,1,0:T(8,128)S(1)} %shard_map.87), channel_id=1, replica_groups={{0,16,32,48,64,80,96,112,128,144,160,176,192,208,224,240},{8,24,40,56,7..., dimensions={0} | all-to-all | bytes 131072 | tf_op jit(solution)/shard_map/all_to_all | solution.py:29
  49.9 0.9 collective-permute-start.1
  50.8 1.6 %shard_map.89 = (f32[2,48,3072]{2,1,0:T(8,128)S(1)}, f32[2,48,3072]{2,1,0:T(8,128)S(1)}) custom-call(f32[4,48,3072]{2,1,0:T(8,128)} %w_in.2, f32[4,48,3072]{2,1,0:T(8,128)} %w_out.2), custom_call_target="tpu_custom_call" | custom-call | tf_op jit(solution)/shard_map/pallas_call | solution.py:411
  52.5 3.0 %collective-permute-done.1.got = f32[8,128]{1,0:T(8,128)S(1)} collective-permute-done((f32[8,128]{1,0:T(8,128)S(1)}, f32[8,128]{1,0:T(8,128)S(1)}, u32[]{:S(2)}, u32[]{:S(2)}) %collective-permute-start.1) | collective-permute-done | bytes 4128 | tf_op jit(solution)/shard_map/ppermute | solution.py:420
  55.5 1.2 shard_map.90
  56.7 11.8 %all_to_all.48.got = f32[16,8,256]{2,1,0:T(8,128)S(1)} all-to-all(f32[16,8,256]{2,1,0:T(8,128)S(1)} %get-tuple-element.50), channel_id=1, replica_groups={{0,16,32,48,64,80,96,112,128,144,160,176,192,208,224,240},{8,24,40,56,7..., dimensions={0} | all-to-all | bytes 262144 | tf_op jit(solution)/shard_map/all_to_all | solution.py:29
  68.5 10.5 %all_to_all.49.got = f32[16,8,256]{2,1,0:T(8,128)S(1)} all-to-all(f32[16,8,256]{2,1,0:T(8,128)S(1)} %shard_map.91), channel_id=1, replica_groups={{0,16,32,48,64,80,96,112,128,144,160,176,192,208,224,240},{8,24,40,56,7..., dimensions={0} | all-to-all | bytes 262144 | tf_op jit(solution)/shard_map/all_to_all | solution.py:29
  79.0 1.0 shard_map.92
  80.0 5.3 %collective-permute-start.4 = (f32[8,3200]{1,0:T(8,128)S(1)}, f32[8,3200]{1,0:T(8,128)S(1)}, u32[]{:S(2)}, u32[]{:S(2)}) collective-permute-start(f32[8,3200]{1,0:T(8,128)S(1)} %get-tuple-element.53.full), channel_id=1, source_target_pairs={{0,8},{8,0},{16,24},{24,16},{32,40},{40,32},{48,56},{56,48},{64,72... | collective-permute-start | bytes 307208 | tf_op jit(solution)/shard_map/ppermute | solution.py:373
  85.2 1.5 collective-permute-start.3
  86.7 3.0 %shard_map.93 = (f32[4,48,3072]{2,1,0:T(8,128)}, f32[4,48,3072]{2,1,0:T(8,128)}) custom-call(f32[8,3200]{1,0:T(8,128)S(1)} %get-tuple-element.53.full, f32[8,3200]{1,0:T(8,128)S(1)} %collective-permute-done.4.near), custom_call_target="tpu_custom_call" | custom-call | bytes 4923392 | tf_op jit(solution)/shard_map/pallas_call | solution.py:37
  89.8 13.3 %all_to_all.50.mine = f32[16,16,128]{2,1,0:T(8,128)S(1)} all-to-all(f32[16,16,128]{2,1,0:T(8,128)S(1)} %shard_map.94), channel_id=1, replica_groups={{0,16,32,48,64,80,96,112,128,144,160,176,192,208,224,240},{8,24,40,56,7..., dimensions={0} | all-to-all | bytes 262144 | tf_op jit(solution)/shard_map/all_to_all | solution.py:29
  103.1 2.7 %collective-permute-start.5 = (f32[16,16,128]{2,1,0:T(8,128)S(1)}, f32[16,16,128]{2,1,0:T(8,128)S(1)}, u32[]{:S(2)}, u32[]{:S(2)}) collective-permute-start(f32[16,16,128]{2,1,0:T(8,128)S(1)} %all_to_all.50.mine), channel_id=1, source_target_pairs={{0,8},{8,0},{16,24},{24,16},{32,40},{40,32},{48,56},{56,48},{64,72... | collective-permute-start | bytes 393224 | tf_op jit(solution)/shard_map/ppermute | solution.py:373
  105.7 1.0 collective-permute-done.5.near
  106.7 0.9 shard_map.95
  107.7 12.3 %all_to_all.51.got = f32[8,64,128]{2,1,0:T(8,128)S(1)} all-to-all(f32[8,64,128]{2,1,0:T(8,128)S(1)} %get-tuple-element.58), channel_id=1, replica_groups=mesh['seq'=32,'expert'=8] {'expert'}, dimensions={0} | all-to-all | bytes 524288 | tf_op jit(solution)/shard_map/all_to_all | solution.py:29
  120.0 10.5 %all_to_all.52.got = f32[8,64,128]{2,1,0:T(8,128)S(1)} all-to-all(f32[8,64,128]{2,1,0:T(8,128)S(1)} %shard_map.96), channel_id=1, replica_groups=mesh['seq'=32,'expert'=8] {'expert'}, dimensions={0} | all-to-all | bytes 524288 | tf_op jit(solution)/shard_map/all_to_all | solution.py:29
  130.6 0.5 shard_map.97
  131.3 4.1 %collective-permute-start.8 = (f32[48,128]{1,0:T(8,128)S(1)}, f32[48,128]{1,0:T(8,128)S(1)}, u32[]{:S(2)}, u32[]{:S(2)}) collective-permute-start(f32[48,128]{1,0:T(8,128)S(1)} %get-tuple-element.60), channel_id=1, source_target_pairs={{0,136},{8,128},{16,152},{24,144},{32,168},{40,160},{48,184},{56,1... | collective-permute-start | bytes 73736 | tf_op jit(solution)/shard_map/ppermute | solution.py:466
  135.4 1.4 shard_map.98
  136.8 0.5 collective-permute-done.8.d
  137.4 12.0 %all_to_all.53.got = f32[8,48,128]{2,1,0:T(8,128)S(1)} all-to-all(f32[8,48,128]{2,1,0:T(8,128)S(1)} %shard_map.99), channel_id=1, replica_groups={{0,16,32,48,64,80,96,112},{8,24,40,56,72,88,104,120},{128,144,160,176,1..., dimensions={0} | all-to-all | bytes 393216 | tf_op jit(solution)/shard_map/all_to_all | solution.py:29
  149.4 2.1 %collective-permute-start.9 = (f32[48,128]{1,0:T(8,128)S(1)}, f32[48,128]{1,0:T(8,128)S(1)}, u32[]{:S(2)}, u32[]{:S(2)}) collective-permute-start(f32[48,128]{1,0:T(8,128)S(1)} %shard_map.100.mine), channel_id=1, source_target_pairs={{0,8},{8,0},{16,24},{24,16},{32,40},{40,32},{48,56},{56,48},{64,72... | collective-permute-start | bytes 73736 | tf_op jit(solution)/shard_map/ppermute | solution.py:373
  151.5 0.8 collective-permute-done.9.theirs
  152.3 0.8 shard_map.101
  (19 shorter events, 0.6 us)
Async XLA Ops:
  0.6 28.7 %copy-start = (f32[192,1024]{1,0:T(8,128)S(1)}, f32[192,1024]{1,0:T(8,128)}, u32[]{:S(2)}) copy-start(f32[192,1024]{1,0:T(8,128)} %grad_out.3) | copy-start | bytes 2359300
  2.7 52.8 %collective-permute-start.2 = (f32[2,2,48,3072]{3,2,1,0:T(8,128)S(1)}, f32[2,2,48,3072]{3,2,1,0:T(8,128)S(1)}, u32[]{:S(2)}, u32[]{:S(2)}) collective-permute-start(f32[2,2,48,3072]{3,2,1,0:T(8,128)S(1)} %get-tuple-element.49), channel_id=1, source_target_pairs={{0,8},{8,0},{16,24},{24,16},{32,40},{40,32},{48,56},{56,48},{64,72... | collective-permute-start | bytes 7077896 | tf_op jit(solution)/shard_map/ppermute | solution.py:373
  30.8 3.4 %collective-permute-start = (f32[16,8,128]{2,1,0:T(8,128)S(1)}, f32[16,8,128]{2,1,0:T(8,128)S(1)}, u32[]{:S(2)}, u32[]{:S(2)}) collective-permute-start(f32[16,8,128]{2,1,0:T(8,128)S(1)} %get-tuple-element.40), channel_id=1, source_target_pairs={{0,8},{8,0},{16,24},{24,16},{32,40},{40,32},{48,56},{56,48},{64,72... | collective-permute-start | bytes 196616 | tf_op jit(solution)/shard_map/ppermute | solution.py:373
  49.9 5.5 %collective-permute-start.1 = (f32[8,128]{1,0:T(8,128)S(1)}, f32[8,128]{1,0:T(8,128)S(1)}, u32[]{:S(2)}, u32[]{:S(2)}) collective-permute-start(f32[8,128]{1,0:T(8,128)S(1)} %shard_map.88), channel_id=1, source_target_pairs={{80,0},{241,32},{34,64},{195,96},{132,128},{37,160},{182,192},{87,... | collective-permute-start | bytes 12296 | tf_op jit(solution)/shard_map/ppermute | solution.py:420
  80.0 6.8 %collective-permute-start.4 = (f32[8,3200]{1,0:T(8,128)S(1)}, f32[8,3200]{1,0:T(8,128)S(1)}, u32[]{:S(2)}, u32[]{:S(2)}) collective-permute-start(f32[8,3200]{1,0:T(8,128)S(1)} %get-tuple-element.53.full), channel_id=1, source_target_pairs={{0,8},{8,0},{16,24},{24,16},{32,40},{40,32},{48,56},{56,48},{64,72... | collective-permute-start | bytes 307208 | tf_op jit(solution)/shard_map/ppermute | solution.py:373
  85.2 4.5 %collective-permute-start.3 = (f32[16,128]{1,0:T(8,128)S(1)}, f32[16,128]{1,0:T(8,128)S(1)}, u32[]{:S(2)}, u32[]{:S(2)}) collective-permute-start(f32[16,128]{1,0:T(8,128)S(1)} %get-tuple-element.52), channel_id=1, source_target_pairs={{0,80},{32,241},{64,34},{96,195},{128,132},{160,37},{192,182},{224... | collective-permute-start | bytes 24584 | tf_op jit(solution)/shard_map/ppermute | solution.py:440
  103.1 3.6 %collective-permute-start.5 = (f32[16,16,128]{2,1,0:T(8,128)S(1)}, f32[16,16,128]{2,1,0:T(8,128)S(1)}, u32[]{:S(2)}, u32[]{:S(2)}) collective-permute-start(f32[16,16,128]{2,1,0:T(8,128)S(1)} %all_to_all.50.mine), channel_id=1, source_target_pairs={{0,8},{8,0},{16,24},{24,16},{32,40},{40,32},{48,56},{56,48},{64,72... | collective-permute-start | bytes 393224 | tf_op jit(solution)/shard_map/ppermute | solution.py:373
  106.7 28.7 %copy-start.1 = (f32[192,64]{0,1:T(8,128)S(1)}, f32[192,64]{0,1:T(8,128)}, u32[]{:S(2)}) copy-start(f32[192,64]{0,1:T(8,128)} %param.6) | copy-start | bytes 147460
  131.1 5.7 %collective-permute-start.7 = (f32[48,128]{1,0:T(8,128)S(1)}, f32[48,128]{1,0:T(8,128)S(1)}, u32[]{:S(2)}, u32[]{:S(2)}) collective-permute-start(f32[48,128]{1,0:T(8,128)S(1)} %get-tuple-element.64.a), channel_id=1, source_target_pairs={{0,128},{8,136},{16,144},{24,152},{32,160},{40,168},{48,176},{56,1... | collective-permute-start | bytes 73736 | tf_op jit(solution)/shard_map/ppermute | solution.py:465
  131.3 6.0 %collective-permute-start.8 = (f32[48,128]{1,0:T(8,128)S(1)}, f32[48,128]{1,0:T(8,128)S(1)}, u32[]{:S(2)}, u32[]{:S(2)}) collective-permute-start(f32[48,128]{1,0:T(8,128)S(1)} %get-tuple-element.60), channel_id=1, source_target_pairs={{0,136},{8,128},{16,152},{24,144},{32,168},{40,160},{48,184},{56,1... | collective-permute-start | bytes 73736 | tf_op jit(solution)/shard_map/ppermute | solution.py:466
  135.4 1.9 %collective-permute-start.6 = (f32[48,128]{1,0:T(8,128)S(1)}, f32[48,128]{1,0:T(8,128)S(1)}, u32[]{:S(2)}, u32[]{:S(2)}) collective-permute-start(f32[48,128]{1,0:T(8,128)S(1)} %get-tuple-element.60), channel_id=1, source_target_pairs={{0,8},{8,0},{16,24},{24,16},{32,40},{40,32},{48,56},{56,48},{64,72... | collective-permute-start | bytes 73736 | tf_op jit(solution)/shard_map/ppermute | solution.py:373
  149.4 3.0 %collective-permute-start.9 = (f32[48,128]{1,0:T(8,128)S(1)}, f32[48,128]{1,0:T(8,128)S(1)}, u32[]{:S(2)}, u32[]{:S(2)}) collective-permute-start(f32[48,128]{1,0:T(8,128)S(1)} %shard_map.100.mine), channel_id=1, source_target_pairs={{0,8},{8,0},{16,24},{24,16},{32,40},{40,32},{48,56},{56,48},{64,72... | collective-permute-start | bytes 73736 | tf_op jit(solution)/shard_map/ppermute | solution.py:373

commit v14 on v13

--- a/solution.py
+++ b/solution.py
@@ -120,7 +120,7 @@
         out[e] = total
 
 
-def partial_rows(got, tokens, grad_out, mine, near, shares, both):
+def partial_rows(got, tokens, grad_out, sent, shares, both):
     n, slots = got.shape[0], got.shape[1]
     logits = jnp.concatenate([got[e] for e in range(n)], axis=1)
     raised = jnp.exp(logits - jnp.max(logits, axis=0, keepdims=True))
@@ -143,8 +143,8 @@
             both[c, k, 0:4, 0:piece] = rows_in[s, w]
             both[c, k, 4:8, 0:piece] = rows_out[s, w]
     core = core_index()
-    mine[...] = both[core]
-    near[...] = both[1 - core]
+    sent[:, 0:8] = both[core]
+    sent[:, 8:16] = both[1 - core]
 
 
 def merge(parts, piece):
@@ -153,21 +153,18 @@
     return jnp.where(lane_of(rows.shape) == piece, top, rows)
 
 
-def merge_cores(mine, near, out, piece):
-    for k in range(out.shape[0]):
-        out[k] = merge([mine[k], near[k]], piece)
-
-
-def merge_chips(got, out, piece):
-    out[...] = merge([got[k] for k in range(got.shape[0])], piece)
-
-
-def hidden_parts(got, own_in, own_out, others, sent, keep, full):
+def merge_chips(got, mine, near, piece):
+    rows = merge([got[k] for k in range(got.shape[0])], piece)
+    mine[...] = rows[0:8]
+    near[...] = rows[8:16]
+
+
+def hidden_parts(got, other, own_in, own_out, others, sent, keep, full):
     w = own_in.shape[1]
     piece = 2 * w
     hidden = own_in.shape[2]
     core = core_index()
-    rows = got[...]
+    rows = merge([got[...], other[...]], piece)
     scaled = (row_of((8, LANES)) < 4) & (lane_of((8, LANES)) < piece)
     rows = jnp.where(scaled, rows / rows[:, piece + 1 : piece + 2], rows)
     keep[...] = rows
@@ -395,19 +392,18 @@
     logits = exchange(run(add_spread, spread, exchange(sent, E)), E)
 
     tiles = (chips, 8, LANES)
-    mine, near, shares = run(
+    sent, shares = run(
         partial_rows,
-        [tiles, tiles, (slots, local_tokens)],
+        [(chips, 16, LANES), (slots, local_tokens)],
         logits,
         tokens,
         grad_out,
         scratch=[(2,) + tiles],
     )
-    sent = run(functools.partial(merge_cores, piece=piece), tiles, mine, to_partner(near))
-    tile = run(
-        functools.partial(merge_chips, piece=piece), (8, LANES), exchange(sent, S, groups)
-    )
-    tile, w_in, w_out = lax.optimization_barrier((tile, w_in, w_out))
+    tile, other = run(
+        functools.partial(merge_chips, piece=piece), [(8, LANES)] * 2, exchange(sent, S, groups)
+    )
+    tile, other, w_in, w_out = lax.optimization_barrier((tile, other, w_in, w_out))
     own_in, own_out = pl.pallas_call(
         load_own,
         out_shape=[pltpu.VMEM(half, F32)] * 2,
@@ -416,8 +412,14 @@
         scratch_shapes=[pltpu.SemaphoreType.DMA((2,))],
         compiler_params=limit,
     )(in_hbm(w_in), in_hbm(w_out))
-    tile, own_in, own_out = lax.optimization_barrier(
-        (lax.ppermute(tile, (S, E), to_owner), own_in, own_out)
+    crossed = [(here, there ^ n_exp) for here, there in to_owner]
+    tile, other, own_in, own_out = lax.optimization_barrier(
+        (
+            lax.ppermute(tile, (S, E), to_owner),
+            lax.ppermute(other, (S, E), crossed),
+            own_in,
+            own_out,
+        )
     )
     weights = (own_in, own_out, others)
     share = hidden // chips
@@ -426,6 +428,7 @@
         hidden_parts,
         [(chips, 8, cut), (8, LANES)],
         tile,
+        other,
         *weights,
         scratch=[(8, hidden)],
     )

time: 154 us -> 156 us (1.013)
  starting transfers between devices: 22.6 us -> 26 us
  waiting for transfers between devices: 6.26 us -> 3.38 us
  blocking collectives: 109 us -> 111 us
    ppermute x0 -> x1, starting transfers between devices: none -> 6.41 us  [per_device(): lax.ppermute(other, (S, E), crossed)]
    ppermute x1, waiting for transfers between devices: 2.98 us -> 0.01 us  [per_device(): lax.ppermute(tile, (S, E), to_owner)]
    ppermute x6 -> x5, starting transfers between devices: 15.8 us -> 12.9 us  [to_partner(): return lax.ppermute(values, S, partner)]
    pallas_call x16 -> x15, Pallas kernels: 10.6 us -> 10.6 us  [run(): pl.pallas_call(kernel, out_shape=[jax.ShapeDtypeStruct(s, F32) for s in s...]
  transfers between devices with their start and end apart: 10 -> 10, of which waited for: 5 -> 4; matrix products, arithmetic and copies ran while one was open for 0% -> 0% of each run, Pallas kernels for 5% -> 5%
where the time goes in v14:
time: 156 us; the launch traced here: 155 us
  blocking collectives  111 us (71%)
  starting transfers between devices  26 us (17%)
  Pallas kernels  14.3 us (9%)
  waiting for transfers between devices  3.38 us (2%)
    all_to_all x9, blocking collectives, exchange(): lax.all_to_all(blocks, axis, 0, 0, axis_index_groups=groups, tiled=True)  111 us
    ppermute x5, starting transfers between devices, to_partner(): return lax.ppermute(values, S, partner)  12.9 us
    pallas_call x15, Pallas kernels, run(): pl.pallas_call(kernel, out_shape=[jax.ShapeDtypeStruct(s, F32) for s in s...  10.6 us
    ppermute x1, starting transfers between devices, per_device(): lax.ppermute(other, (S, E), crossed)  6.41 us
    ppermute x1, starting transfers between devices, per_device(): lax.ppermute(theirs, S, [(i, i ^ across ^ 1) for i in range(n_seq)])  4.2 us
  transfers between devices with their start and end apart: 10, of which 4 were waited for; matrix products, arithmetic and copies ran while one was open for 0% of the time, Pallas kernels for 5%

profile of v14, /device:TPU:1, one launch (start us, length us, event | category | flops | bytes accessed | tf_op | source)
XLA Modules:
  0.0 155.1 jit_solution(9844912533162920931)
XLA Ops:
  0.6 2.0 %shard_map.84 = (f32[8,64,128]{2,1,0:T(8,128)S(1)}, f32[192,1024]{1,0:T(8,128)S(1)}, f32[2,2,48,3072]{3,2,1,0:T(8,128)S(1)}) custom-call(f32[64,192]{1,0:T(8,128)} %bitcast.2, f32[192,1024]{1,0:T(8,128)} %tokens.1, f32[4,48,3072]{2,1,0:T(8,128)} %w_in.2, f32[4,48,3072]{2,1,0:T(8,128)} %w_out.2), custom_call_target="tpu_custom_call" | custom-call | tf_op jit(solution)/shard_map/pallas_call | solution.py:379
  2.7 3.3 %collective-permute-start.2 = (f32[2,2,48,3072]{3,2,1,0:T(8,128)S(1)}, f32[2,2,48,3072]{3,2,1,0:T(8,128)S(1)}, u32[]{:S(2)}, u32[]{:S(2)}) collective-permute-start(f32[2,2,48,3072]{3,2,1,0:T(8,128)S(1)} %get-tuple-element.55), channel_id=1, source_target_pairs={{0,8},{8,0},{16,24},{24,16},{32,40},{40,32},{48,56},{56,48},{64,72... | collective-permute-start | bytes 7077896 | tf_op jit(solution)/shard_map/ppermute | solution.py:370
  6.0 13.3 %all_to_all.45.got = f32[8,64,128]{2,1,0:T(8,128)S(1)} all-to-all(f32[8,64,128]{2,1,0:T(8,128)S(1)} %get-tuple-element.40), channel_id=1, replica_groups=mesh['seq'=32,'expert'=8] {'expert'}, dimensions={0} | all-to-all | bytes 524288 | tf_op jit(solution)/shard_map/all_to_all | solution.py:29
  19.3 10.1 %all_to_all.46.got.logits = f32[8,64,128]{2,1,0:T(8,128)S(1)} all-to-all(f32[8,64,128]{2,1,0:T(8,128)S(1)} %shard_map.85), channel_id=1, replica_groups=mesh['seq'=32,'expert'=8] {'expert'}, dimensions={0} | all-to-all | bytes 524288 | tf_op jit(solution)/shard_map/all_to_all | solution.py:29
  29.4 1.4 shard_map.86
  30.8 15.5 %all_to_all.47.got = f32[16,16,128]{2,1,0:T(8,128)S(1)} all-to-all(f32[16,16,128]{2,1,0:T(8,128)S(1)} %get-tuple-element.42), channel_id=1, replica_groups={{0,16,32,48,64,80,96,112,128,144,160,176,192,208,224,240},{8,24,40,56,7..., dimensions={0} | all-to-all | bytes 262144 | tf_op jit(solution)/shard_map/all_to_all | solution.py:29
  46.4 0.1 shard_map.87
  46.5 0.9 collective-permute-start
  47.4 6.4 %collective-permute-start.1 = (f32[8,128]{1,0:T(8,128)S(1)}, f32[8,128]{1,0:T(8,128)S(1)}, u32[]{:S(2)}, u32[]{:S(2)}) collective-permute-start(f32[8,128]{1,0:T(8,128)S(1)} %get-tuple-element.46), channel_id=1, source_target_pairs={{80,8},{241,40},{34,72},{195,104},{132,136},{37,168},{182,200},{87... | collective-permute-start | bytes 12296 | tf_op jit(solution)/shard_map/ppermute | solution.py:419
  53.8 1.6 %shard_map.88 = (f32[2,48,3072]{2,1,0:T(8,128)S(1)}, f32[2,48,3072]{2,1,0:T(8,128)S(1)}) custom-call(f32[4,48,3072]{2,1,0:T(8,128)} %w_in.2, f32[4,48,3072]{2,1,0:T(8,128)} %w_out.2), custom_call_target="tpu_custom_call" | custom-call | tf_op jit(solution)/shard_map/pallas_call | solution.py:407
  55.5 1.1 collective-permute-done.1.other
  56.6 1.3 shard_map.89
  57.9 12.3 %all_to_all.48.got = f32[16,8,256]{2,1,0:T(8,128)S(1)} all-to-all(f32[16,8,256]{2,1,0:T(8,128)S(1)} %get-tuple-element.56), channel_id=1, replica_groups={{0,16,32,48,64,80,96,112,128,144,160,176,192,208,224,240},{8,24,40,56,7..., dimensions={0} | all-to-all | bytes 262144 | tf_op jit(solution)/shard_map/all_to_all | solution.py:29
  70.2 10.5 %all_to_all.49.got = f32[16,8,256]{2,1,0:T(8,128)S(1)} all-to-all(f32[16,8,256]{2,1,0:T(8,128)S(1)} %shard_map.90), channel_id=1, replica_groups={{0,16,32,48,64,80,96,112,128,144,160,176,192,208,224,240},{8,24,40,56,7..., dimensions={0} | all-to-all | bytes 262144 | tf_op jit(solution)/shard_map/all_to_all | solution.py:29
  80.7 1.0 shard_map.91
  81.7 4.8 %collective-permute-start.4 = (f32[8,3200]{1,0:T(8,128)S(1)}, f32[8,3200]{1,0:T(8,128)S(1)}, u32[]{:S(2)}, u32[]{:S(2)}) collective-permute-start(f32[8,3200]{1,0:T(8,128)S(1)} %get-tuple-element.59.full), channel_id=1, source_target_pairs={{0,8},{8,0},{16,24},{24,16},{32,40},{40,32},{48,56},{56,48},{64,72... | collective-permute-start | bytes 307208 | tf_op jit(solution)/shard_map/ppermute | solution.py:370
  86.5 1.5 collective-permute-start.3
  88.0 3.0 %shard_map.92 = (f32[4,48,3072]{2,1,0:T(8,128)}, f32[4,48,3072]{2,1,0:T(8,128)}) custom-call(f32[8,3200]{1,0:T(8,128)S(1)} %get-tuple-element.59.full, f32[8,3200]{1,0:T(8,128)S(1)} %collective-permute-done.4.near), custom_call_target="tpu_custom_call" | custom-call | bytes 4923392 | tf_op jit(solution)/shard_map/pallas_call | solution.py:37
  91.0 13.3 %all_to_all.50.mine = f32[16,16,128]{2,1,0:T(8,128)S(1)} all-to-all(f32[16,16,128]{2,1,0:T(8,128)S(1)} %shard_map.93), channel_id=1, replica_groups={{0,16,32,48,64,80,96,112,128,144,160,176,192,208,224,240},{8,24,40,56,7..., dimensions={0} | all-to-all | bytes 262144 | tf_op jit(solution)/shard_map/all_to_all | solution.py:29
  104.3 2.7 %collective-permute-start.5 = (f32[16,16,128]{2,1,0:T(8,128)S(1)}, f32[16,16,128]{2,1,0:T(8,128)S(1)}, u32[]{:S(2)}, u32[]{:S(2)}) collective-permute-start(f32[16,16,128]{2,1,0:T(8,128)S(1)} %all_to_all.50.mine), channel_id=1, source_target_pairs={{0,8},{8,0},{16,24},{24,16},{32,40},{40,32},{48,56},{56,48},{64,72... | collective-permute-start | bytes 393224 | tf_op jit(solution)/shard_map/ppermute | solution.py:370
  107.0 1.0 collective-permute-done.5.near
  108.0 0.9 shard_map.94
  108.9 13.2 %all_to_all.51.got = f32[8,64,128]{2,1,0:T(8,128)S(1)} all-to-all(f32[8,64,128]{2,1,0:T(8,128)S(1)} %get-tuple-element.64), channel_id=1, replica_groups=mesh['seq'=32,'expert'=8] {'expert'}, dimensions={0} | all-to-all | bytes 524288 | tf_op jit(solution)/shard_map/all_to_all | solution.py:29
  122.2 10.5 %all_to_all.52.got = f32[8,64,128]{2,1,0:T(8,128)S(1)} all-to-all(f32[8,64,128]{2,1,0:T(8,128)S(1)} %shard_map.95), channel_id=1, replica_groups=mesh['seq'=32,'expert'=8] {'expert'}, dimensions={0} | all-to-all | bytes 524288 | tf_op jit(solution)/shard_map/all_to_all | solution.py:29
  132.7 0.5 shard_map.96
  133.3 4.2 %collective-permute-start.8 = (f32[48,128]{1,0:T(8,128)S(1)}, f32[48,128]{1,0:T(8,128)S(1)}, u32[]{:S(2)}, u32[]{:S(2)}) collective-permute-start(f32[48,128]{1,0:T(8,128)S(1)} %get-tuple-element.66), channel_id=1, source_target_pairs={{0,136},{8,128},{16,152},{24,144},{32,168},{40,160},{48,184},{56,1... | collective-permute-start | bytes 73736 | tf_op jit(solution)/shard_map/ppermute | solution.py:469
  137.6 1.4 shard_map.97
  139.0 0.4 collective-permute-done.8.d
  139.4 12.0 %all_to_all.53.got = f32[8,48,128]{2,1,0:T(8,128)S(1)} all-to-all(f32[8,48,128]{2,1,0:T(8,128)S(1)} %shard_map.98), channel_id=1, replica_groups={{0,16,32,48,64,80,96,112},{8,24,40,56,72,88,104,120},{128,144,160,176,1..., dimensions={0} | all-to-all | bytes 393216 | tf_op jit(solution)/shard_map/all_to_all | solution.py:29
  151.4 2.1 %collective-permute-start.9 = (f32[48,128]{1,0:T(8,128)S(1)}, f32[48,128]{1,0:T(8,128)S(1)}, u32[]{:S(2)}, u32[]{:S(2)}) collective-permute-start(f32[48,128]{1,0:T(8,128)S(1)} %shard_map.99.mine), channel_id=1, source_target_pairs={{0,8},{8,0},{16,24},{24,16},{32,40},{40,32},{48,56},{56,48},{64,72... | collective-permute-start | bytes 73736 | tf_op jit(solution)/shard_map/ppermute | solution.py:370
  153.5 0.8 collective-permute-done.9.theirs
  154.3 0.8 shard_map.100
  (18 shorter events, 0.3 us)
Async XLA Ops:
  0.6 28.7 %copy-start = (f32[192,1024]{1,0:T(8,128)S(1)}, f32[192,1024]{1,0:T(8,128)}, u32[]{:S(2)}) copy-start(f32[192,1024]{1,0:T(8,128)} %grad_out.3) | copy-start | bytes 2359300
  2.7 54.0 %collective-permute-start.2 = (f32[2,2,48,3072]{3,2,1,0:T(8,128)S(1)}, f32[2,2,48,3072]{3,2,1,0:T(8,128)S(1)}, u32[]{:S(2)}, u32[]{:S(2)}) collective-permute-start(f32[2,2,48,3072]{3,2,1,0:T(8,128)S(1)} %get-tuple-element.55), channel_id=1, source_target_pairs={{0,8},{8,0},{16,24},{24,16},{32,40},{40,32},{48,56},{56,48},{64,72... | collective-permute-start | bytes 7077896 | tf_op jit(solution)/shard_map/ppermute | solution.py:370
  46.5 9.0 %collective-permute-start = (f32[8,128]{1,0:T(8,128)S(1)}, f32[8,128]{1,0:T(8,128)S(1)}, u32[]{:S(2)}, u32[]{:S(2)}) collective-permute-start(f32[8,128]{1,0:T(8,128)S(1)} %get-tuple-element.45), channel_id=1, source_target_pairs={{80,0},{241,32},{34,64},{195,96},{132,128},{37,160},{182,192},{87,... | collective-permute-start | bytes 12296 | tf_op jit(solution)/shard_map/ppermute | solution.py:418
  47.4 9.2 %collective-permute-start.1 = (f32[8,128]{1,0:T(8,128)S(1)}, f32[8,128]{1,0:T(8,128)S(1)}, u32[]{:S(2)}, u32[]{:S(2)}) collective-permute-start(f32[8,128]{1,0:T(8,128)S(1)} %get-tuple-element.46), channel_id=1, source_target_pairs={{80,8},{241,40},{34,72},{195,104},{132,136},{37,168},{182,200},{87... | collective-permute-start | bytes 12296 | tf_op jit(solution)/shard_map/ppermute | solution.py:419
  81.7 6.3 %collective-permute-start.4 = (f32[8,3200]{1,0:T(8,128)S(1)}, f32[8,3200]{1,0:T(8,128)S(1)}, u32[]{:S(2)}, u32[]{:S(2)}) collective-permute-start(f32[8,3200]{1,0:T(8,128)S(1)} %get-tuple-element.59.full), channel_id=1, source_target_pairs={{0,8},{8,0},{16,24},{24,16},{32,40},{40,32},{48,56},{56,48},{64,72... | collective-permute-start | bytes 307208 | tf_op jit(solution)/shard_map/ppermute | solution.py:370
  86.5 4.5 %collective-permute-start.3 = (f32[16,128]{1,0:T(8,128)S(1)}, f32[16,128]{1,0:T(8,128)S(1)}, u32[]{:S(2)}, u32[]{:S(2)}) collective-permute-start(f32[16,128]{1,0:T(8,128)S(1)} %get-tuple-element.58), channel_id=1, source_target_pairs={{0,80},{32,241},{64,34},{96,195},{128,132},{160,37},{192,182},{224... | collective-permute-start | bytes 24584 | tf_op jit(solution)/shard_map/ppermute | solution.py:443
  104.3 3.6 %collective-permute-start.5 = (f32[16,16,128]{2,1,0:T(8,128)S(1)}, f32[16,16,128]{2,1,0:T(8,128)S(1)}, u32[]{:S(2)}, u32[]{:S(2)}) collective-permute-start(f32[16,16,128]{2,1,0:T(8,128)S(1)} %all_to_all.50.mine), channel_id=1, source_target_pairs={{0,8},{8,0},{16,24},{24,16},{32,40},{40,32},{48,56},{56,48},{64,72... | collective-permute-start | bytes 393224 | tf_op jit(solution)/shard_map/ppermute | solution.py:370
  108.0 29.6 %copy-start.1 = (f32[192,64]{0,1:T(8,128)S(1)}, f32[192,64]{0,1:T(8,128)}, u32[]{:S(2)}) copy-start(f32[192,64]{0,1:T(8,128)} %param.6) | copy-start | bytes 147460
  133.2 5.7 %collective-permute-start.7 = (f32[48,128]{1,0:T(8,128)S(1)}, f32[48,128]{1,0:T(8,128)S(1)}, u32[]{:S(2)}, u32[]{:S(2)}) collective-permute-start(f32[48,128]{1,0:T(8,128)S(1)} %get-tuple-element.70.a), channel_id=1, source_target_pairs={{0,128},{8,136},{16,144},{24,152},{32,160},{40,168},{48,176},{56,1... | collective-permute-start | bytes 73736 | tf_op jit(solution)/shard_map/ppermute | solution.py:468
  133.3 6.0 %collective-permute-start.8 = (f32[48,128]{1,0:T(8,128)S(1)}, f32[48,128]{1,0:T(8,128)S(1)}, u32[]{:S(2)}, u32[]{:S(2)}) collective-permute-start(f32[48,128]{1,0:T(8,128)S(1)} %get-tuple-element.66), channel_id=1, source_target_pairs={{0,136},{8,128},{16,152},{24,144},{32,168},{40,160},{48,184},{56,1... | collective-permute-start | bytes 73736 | tf_op jit(solution)/shard_map/ppermute | solution.py:469
  137.5 1.8 %collective-permute-start.6 = (f32[48,128]{1,0:T(8,128)S(1)}, f32[48,128]{1,0:T(8,128)S(1)}, u32[]{:S(2)}, u32[]{:S(2)}) collective-permute-start(f32[48,128]{1,0:T(8,128)S(1)} %get-tuple-element.66), channel_id=1, source_target_pairs={{0,8},{8,0},{16,24},{24,16},{32,40},{40,32},{48,56},{56,48},{64,72... | collective-permute-start | bytes 73736 | tf_op jit(solution)/shard_map/ppermute | solution.py:370
  151.4 3.0 %collective-permute-start.9 = (f32[48,128]{1,0:T(8,128)S(1)}, f32[48,128]{1,0:T(8,128)S(1)}, u32[]{:S(2)}, u32[]{:S(2)}) collective-permute-start(f32[48,128]{1,0:T(8,128)S(1)} %shard_map.99.mine), channel_id=1, source_target_pairs={{0,8},{8,0},{16,24},{24,16},{32,40},{40,32},{48,56},{56,48},{64,72... | collective-permute-start | bytes 73736 | tf_op jit(solution)/shard_map/ppermute | solution.py:370
